TPU v7x, 32 devices: a whole 2x2x4 slice. The times are simulated.
32 devices in a mesh: blk: 8 (over z, y), sub: 4 (over x, core).
Axes of the slice: x: 2, y: 2, z: 4, core: 2. Of those that a mesh axis runs over, the one named last changes fastest.
Arguments:
- tracers: float32 [320, 4, 5400], P(('blk', 'sub')), may hold values from -6 to 6
- velocity: float32 [320, 4, 5400], P(('blk', 'sub')), may hold values from -3 to 3
- kappa: float32 [320, 5400], P(('blk', 'sub')), may hold values from 0.1 to 4
- kmt: float32 [320, 5400], P(('blk', 'sub')), may hold values from -1 to 2.5
- block_owner: int32 [160], replicated, may hold values from 0 to 319, as said below
- neighbours: int32 [160, 4], replicated, may hold values from -1 to 159, as said below
- fold_partner: int32 [160], replicated, may hold values from -1 to 159, as said below
Outputs:
- tracers_out: float32 [320, 4, 5400], P(('blk', 'sub'))
Inputs may be any that keep to these rules, and one draw needn't show every extreme that they name: `block_owner`: the values are distinct. Every device holds between 3 and 10 blocks, in its first slots; devices in index order hold consecutive runs of the blocks taken along a serpentine curve over the block grid. `neighbours`: row b lists the blocks west, east, south and north of block b on a grid of 40 by 5 blocks that is periodic from west to east, or -1 where that place is land or off the grid; the north entry of the northernmost row is -1. The owner of every listed block lies at most 27 devices from the owner of block b. `fold_partner`: for a block of the northernmost row, the block of that row at the mirrored column (39 - column); -1 for all other blocks. Its owner lies at most 27 devices from block b's owner.
All inputs are finite; a program needn't handle non-finite values.
Results may differ from a plain program's by a relative error of at most 0.0003.
Values sent between devices are 32-bit elements; how exact they have to be, the bound alone decides.
No kernel may reach another device: no remote copies, remote signals or barrier semaphores. Data moves between devices by JAX's collectives and lax.ppermute only.
A program may use at most 192 MiB of HBM per device.

v0:
```python
import jax
import jax.numpy as jnp
from jax import lax
from jax.sharding import PartitionSpec as P

IB = 90
JB = 60
REACH = 27


COURANT = 0.2


def shifted(block, axis, distance):
    devices = range(lax.axis_size(axis))
    route = [(i - distance, i) for i in devices if i - distance in devices]
    return lax.ppermute(block, axis, route)


def edge_pack(block_field):
    count, chans, rows, cols = block_field.shape
    west_edge = block_field[:, :, :, 0:2].reshape(count, chans, rows * 2)
    east_edge = block_field[:, :, :, cols - 2 :].reshape(count, chans, rows * 2)
    south_edge = block_field[:, :, 0:2, :].reshape(count, chans, 2 * cols)
    north_edge = block_field[:, :, rows - 2 :, :].reshape(count, chans, 2 * cols)
    return jnp.concatenate([west_edge, east_edge, south_edge, north_edge], axis=2)


def fetch(source, window_codes):
    safe_codes = jnp.maximum(window_codes, 0)
    picked = jnp.take(source, safe_codes.reshape(-1), axis=0)
    picked = picked.reshape(window_codes.shape + source.shape[1:])
    return jnp.where((window_codes >= 0)[..., None, None], picked, 0.0)


def extend(block_field, sources, fold_sign):
    count, chans, rows, cols = block_field.shape
    strip = 2 * rows
    west_halo = sources[:, 0, :, strip : 2 * strip].reshape(count, chans, rows, 2)
    east_halo = sources[:, 1, :, 0:strip].reshape(count, chans, rows, 2)
    south_halo = sources[:, 2, :, 2 * strip + 2 * cols :].reshape(count, chans, 2, cols)
    north_halo = sources[:, 3, :, 2 * strip : 2 * strip + 2 * cols].reshape(count, chans, 2, cols)
    mirrored = sources[:, 4, :, 2 * strip + 2 * cols :].reshape(count, chans, 2, cols)[
        :, :, ::-1, ::-1
    ]
    north_halo = north_halo + fold_sign * mirrored
    middle = jnp.concatenate([west_halo, block_field, east_halo], axis=3)
    corner = jnp.zeros((count, chans, 2, 2), block_field.dtype)
    bottom = jnp.concatenate([corner, south_halo, corner], axis=3)
    top_rows = jnp.concatenate([corner, north_halo, corner], axis=3)
    return jnp.concatenate([bottom, middle, top_rows], axis=2)


def prepare(static_ext, diffusivity):
    levels = (static_ext.shape[1] - 1) // 2
    rows = static_ext.shape[2] - 4
    cols = static_ext.shape[3] - 4
    east_vel = static_ext[:, :levels]
    north_vel = static_ext[:, levels : 2 * levels]
    depth = static_ext[:, 2 * levels :]
    level_ids = jnp.arange(levels).astype(static_ext.dtype).reshape(1, levels, 1, 1)
    wet = jnp.clip(depth - level_ids, 0.0, 1.0)
    face_x = 0.5 * (
        east_vel[:, :, 2 : rows + 2, 1 : cols + 2] + east_vel[:, :, 2 : rows + 2, 2 : cols + 3]
    )
    face_x = face_x * wet[:, :, 2 : rows + 2, 1 : cols + 2] * wet[:, :, 2 : rows + 2, 2 : cols + 3]
    face_y = 0.5 * (
        north_vel[:, :, 1 : rows + 2, 2 : cols + 2] + north_vel[:, :, 2 : rows + 3, 2 : cols + 2]
    )
    face_y = face_y * wet[:, :, 1 : rows + 2, 2 : cols + 2] * wet[:, :, 2 : rows + 3, 2 : cols + 2]
    inner = wet[:, :, 2 : rows + 2, 2 : cols + 2]
    coupling = diffusivity[:, None] * inner[:, :-1] * inner[:, 1:]
    return (face_x, face_y, inner, coupling)


def face_flux(velocity_face, left_far, left_near, right_near, right_far):
    centered = (7.0 * (left_near + right_near) - (left_far + right_far)) / 12.0
    upwind = (right_far - 3.0 * right_near + 3.0 * left_near - left_far) / 12.0
    return velocity_face * centered + jnp.abs(velocity_face) * upwind


def vertical_solve(rhs_cols, coupling):
    levels = rhs_cols.shape[2]
    partials = []
    ratios = []
    for level in range(levels):
        coef_below = coupling[:, :, level] if level < levels - 1 else 0.0
        coef_above = coupling[:, :, level - 1] if level > 0 else 0.0
        diagonal = 1.0 + coef_above + coef_below
        if level == 0:
            divider_value = diagonal
            partial_value = rhs_cols[:, :, 0] / divider_value
        else:
            divider_value = diagonal - coef_above * ratios[-1]
            partial_value = (rhs_cols[:, :, level] + coef_above * partials[-1]) / divider_value
        partials.append(partial_value)
        ratios.append(coef_below / divider_value)
    result = [None] * levels
    result[levels - 1] = partials[levels - 1]
    level = 0
    result[level] = partials[level] + ratios[level] * result[level + 1]
    return jnp.stack(result, axis=2)


def advance(tracer_ext, face_x, face_y, inner, coupling):
    count, chans = (tracer_ext.shape[0], tracer_ext.shape[1])
    levels, rows, cols = (inner.shape[1], inner.shape[2], inner.shape[3])
    ext_cols = tracer_ext.reshape(count, chans // levels, levels, rows + 4, cols + 4)
    middle = ext_cols[:, :, :, 2 : rows + 2]
    flux_x = face_flux(
        face_x[:, None],
        middle[..., 0 : cols + 1],
        middle[..., 1 : cols + 2],
        middle[..., 2 : cols + 3],
        middle[..., 3 : cols + 4],
    )
    column = ext_cols[..., 2 : cols + 2]
    flux_y = face_flux(
        face_y[:, None],
        column[:, :, :, 0 : rows + 1],
        column[:, :, :, 1 : rows + 2],
        column[:, :, :, 2 : rows + 3],
        column[:, :, :, 3 : rows + 4],
    )
    center = middle[..., 2 : cols + 2]
    divergence = flux_x[..., 1:] - flux_x[..., :-1] + (flux_y[:, :, :, 1:] - flux_y[:, :, :, :-1])
    explicit = center - COURANT * inner[:, None] * divergence
    solved = vertical_solve(explicit, coupling[:, None])
    return solved.reshape(count, chans, rows, cols)


def nearby(edge_block, fixed_fields):
    pieces = []
    for offset in range(-REACH, REACH + 1):
        if offset == 0:
            pieces.append(edge_block)
        elif fixed_fields:
            pieces.append(shifted(edge_block, ("blk", "sub"), -offset))
        else:
            pieces.append(shifted(edge_block, ("blk", "sub"), -offset))
    return jnp.concatenate(pieces, axis=0)


def per_device(tracers, velocity, kappa, kmt, block_owner, neighbours, fold_partner):
    slot_count = tracers.shape[0]
    chans = tracers.shape[1]
    sub_count = lax.axis_size("sub")
    my_index = lax.axis_index("blk") * sub_count + lax.axis_index("sub")
    slot_total = slot_count * lax.axis_size("blk") * sub_count
    block_count = block_owner.shape[0]
    slot_block = (
        jnp.full((slot_total,), -1, jnp.int32)
        .at[block_owner]
        .set(jnp.arange(block_count, dtype=jnp.int32))
    )
    mine = lax.dynamic_slice_in_dim(slot_block, my_index * slot_count, slot_count, 0)
    live_slot = mine >= 0
    safe_ids = jnp.maximum(mine, 0)
    links = jnp.concatenate([neighbours[safe_ids], fold_partner[safe_ids][:, None]], axis=1)
    links = jnp.where(live_slot[:, None], links, -1)
    link_codes = jnp.where(links >= 0, block_owner[jnp.maximum(links, 0)], -1)
    owner_dev = link_codes // slot_count
    window_codes = jnp.where(
        link_codes >= 0, (owner_dev - my_index + REACH) * slot_count + link_codes % slot_count, -1
    )
    levels = velocity.shape[1] // 2
    statics = jnp.concatenate([velocity, kmt[:, None, :]], axis=1)
    statics = statics.reshape(slot_count, 2 * levels + 1, JB, IB)
    fold_sign = jnp.concatenate(
        [-jnp.ones((2 * levels,), jnp.float32), jnp.ones((1,), jnp.float32)]
    ).reshape(1, -1, 1, 1)
    static_window = nearby(edge_pack(statics), True)
    static_ext = extend(statics, fetch(static_window, window_codes), fold_sign)
    face_x, face_y, inner, coupling = prepare(static_ext, kappa.reshape(slot_count, JB, IB))
    state = tracers.reshape(slot_count, chans, JB, IB)
    tracer_window = nearby(edge_pack(state), False)
    tracer_ext = extend(state, fetch(tracer_window, window_codes), 1.0)
    state = advance(tracer_ext, face_x, face_y, inner, coupling)
    result = state.reshape(slot_count, chans, JB * IB)
    return jnp.where(live_slot[:, None, None], result, 0.0)


def solution(mesh):
    placed = (
        P(("blk", "sub"), None, None),
        P(("blk", "sub"), None, None),
        P(("blk", "sub"), None),
        P(("blk", "sub"), None),
        P(),
        P(),
        P(),
    )
    return jax.shard_map(
        per_device,
        mesh=mesh,
        in_specs=placed,
        out_specs=P(("blk", "sub"), None, None),
        check_vma=False,
    )
```

profile of v0, /device:TPU:0, one launch (start us, length us, event | category | flops | bytes accessed | tf_op | source)
XLA Modules:
  0.0 977.6 jit_solution(15370385505347114808)
XLA Ops:
  16.1 9.0 collective-permute-start.54
  78.4 7.8 collective-permute-start.2
  89.4 7.1 collective-permute-start.3
  135.6 50.3 %collective-permute-start.12 = (f32[10,4,600]{2,1,0:T(4,128)}, f32[10,4,600]{2,1,0:T(4,128)S(1)}, u32[]{:S(2)}, u32[]{:S(2)}) collective-permute-start(f32[10,4,600]{2,1,0:T(4,128)} %pad_maximum_fusion.23), channel_id=1, source_target_pairs={{0,15},{1,16},{2,17},{3,18},{4,19},{5,20},{6,21},{7,22},{8,23},{9,... | collective-permute-start | bytes 288008 | tf_op jit(solution)/shard_map/ppermute | solution.py:17
  211.7 18.2 %collective-permute-start.18 = (f32[10,4,600]{2,1,0:T(4,128)}, f32[10,4,600]{2,1,0:T(4,128)S(1)}, u32[]{:S(2)}, u32[]{:S(2)}) collective-permute-start(f32[10,4,600]{2,1,0:T(4,128)} %pad_maximum_fusion.23), channel_id=1, source_target_pairs={{0,9},{1,10},{2,11},{3,12},{4,13},{5,14},{6,15},{7,16},{8,17},{9,1... | collective-permute-start | bytes 288008 | tf_op jit(solution)/shard_map/ppermute | solution.py:17
  233.0 8.8 collective-permute-start.19
  244.3 9.1 collective-permute-start.20
  256.0 7.9 collective-permute-start.21
  267.1 7.6 collective-permute-start.22
  277.3 7.9 collective-permute-start.23
  288.4 7.6 collective-permute-start.24
  298.6 7.9 collective-permute-start.25
  309.7 7.7 collective-permute-start.26
  318.5 8.1 collective-permute-start.27
  328.8 7.6 collective-permute-start.28
  443.0 12.1 %collective-permute-done.40 = f32[10,4,600]{2,1,0:T(4,128)S(1)} collective-permute-done((f32[10,4,600]{2,1,0:T(4,128)}, f32[10,4,600]{2,1,0:T(4,128)S(1)}, u32[]{:S(2)}, u32[]{:S(2)}) %collective-permute-start.40) | collective-permute-done | bytes 96032 | tf_op jit(solution)/shard_map/ppermute | solution.py:17
  496.3 7.3 collective-permute-done.46
  513.5 7.5 collective-permute-done.48
  548.5 7.5 collective-permute-done.52
  599.7 44.6 %collective-permute-start.66 = (f32[10,5,600]{2,1,0:T(8,128)S(1)}, f32[10,5,600]{2,1,0:T(8,128)S(1)}, u32[]{:S(2)}, u32[]{:S(2)}) collective-permute-start(f32[10,5,600]{2,1,0:T(8,128)S(1)} %pad_maximum_fusion.22), channel_id=1, source_target_pairs={{0,15},{1,16},{2,17},{3,18},{4,19},{5,20},{6,21},{7,22},{8,23},{9,... | collective-permute-start | bytes 360008 | tf_op jit(solution)/shard_map/ppermute | solution.py:17
  651.0 9.0 collective-permute-start.70
  660.7 8.2 collective-permute-start.71
  673.6 10.7 %collective-permute-start.74 = (f32[10,5,600]{2,1,0:T(8,128)S(1)}, f32[10,5,600]{2,1,0:T(8,128)S(1)}, u32[]{:S(2)}, u32[]{:S(2)}) collective-permute-start(f32[10,5,600]{2,1,0:T(8,128)S(1)} %pad_maximum_fusion.22), channel_id=1, source_target_pairs={{0,7},{1,8},{2,9},{3,10},{4,11},{5,12},{6,13},{7,14},{8,15},{9,16}... | collective-permute-start | bytes 360008 | tf_op jit(solution)/shard_map/ppermute | solution.py:17
  734.5 7.0 collective-permute-start.82
  742.2 7.0 collective-permute-start.83
  750.0 7.0 collective-permute-start.84
  757.7 7.0 collective-permute-start.85
  766.1 7.0 collective-permute-start.86
  773.8 7.0 collective-permute-start.87
  825.4 61.2 %collective-permute-done.96 = f32[10,5,600]{2,1,0:T(8,128)S(1)} collective-permute-done((f32[10,5,600]{2,1,0:T(8,128)S(1)}, f32[10,5,600]{2,1,0:T(8,128)S(1)}, u32[]{:S(2)}, u32[]{:S(2)}) %collective-permute-start.96) | collective-permute-done | bytes 120032 | tf_op jit(solution)/shard_map/ppermute | solution.py:17
  904.1 25.7 %collective-permute-done.102 = f32[10,5,600]{2,1,0:T(8,128)S(1)} collective-permute-done((f32[10,5,600]{2,1,0:T(8,128)S(1)}, f32[10,5,600]{2,1,0:T(8,128)S(1)}, u32[]{:S(2)}, u32[]{:S(2)}) %collective-permute-start.102) | collective-permute-done | bytes 120032 | tf_op jit(solution)/shard_map/ppermute | solution.py:17
  929.9 10.6 %collective-permute-start.107 = (f32[10,5,600]{2,1,0:T(8,128)S(1)}, f32[10,5,600]{2,1,0:T(8,128)S(1)}, u32[]{:S(2)}, u32[]{:S(2)}) collective-permute-start(f32[10,5,600]{2,1,0:T(8,128)S(1)} %pad_maximum_fusion.22), channel_id=1, source_target_pairs={{27,0},{28,1},{29,2},{30,3},{31,4}} | collective-permute-start | bytes 360008 | tf_op jit(solution)/shard_map/ppermute | solution.py:17
  (405 shorter events, 557.0 us)
Async XLA Ops:
  16.1 564.9 %collective-permute-start.54 = (f32[10,5,600]{2,1,0:T(8,128)S(1)}, f32[10,5,600]{2,1,0:T(8,128)}, u32[]{:S(2)}, u32[]{:S(2)}) collective-permute-start(f32[10,5,600]{2,1,0:T(8,128)S(1)} %pad_maximum_fusion.22), channel_id=1, source_target_pairs={{0,27},{1,28},{2,29},{3,30},{4,31}} | collective-permute-start | bytes 360008 | tf_op jit(solution)/shard_map/ppermute | solution.py:17
  25.1 558.9 %collective-permute-start.55 = (f32[10,5,600]{2,1,0:T(8,128)S(1)}, f32[10,5,600]{2,1,0:T(8,128)}, u32[]{:S(2)}, u32[]{:S(2)}) collective-permute-start(f32[10,5,600]{2,1,0:T(8,128)S(1)} %pad_maximum_fusion.22), channel_id=1, source_target_pairs={{0,26},{1,27},{2,28},{3,29},{4,30},{5,31}} | collective-permute-start | bytes 360008 | tf_op jit(solution)/shard_map/ppermute | solution.py:17
  31.5 555.4 %collective-permute-start.56 = (f32[10,5,600]{2,1,0:T(8,128)S(1)}, f32[10,5,600]{2,1,0:T(8,128)}, u32[]{:S(2)}, u32[]{:S(2)}) collective-permute-start(f32[10,5,600]{2,1,0:T(8,128)S(1)} %pad_maximum_fusion.22), channel_id=1, source_target_pairs={{0,25},{1,26},{2,27},{3,28},{4,29},{5,30},{6,31}} | collective-permute-start | bytes 360008 | tf_op jit(solution)/shard_map/ppermute | solution.py:17
  37.8 552.0 %collective-permute-start.57 = (f32[10,5,600]{2,1,0:T(8,128)S(1)}, f32[10,5,600]{2,1,0:T(8,128)}, u32[]{:S(2)}, u32[]{:S(2)}) collective-permute-start(f32[10,5,600]{2,1,0:T(8,128)S(1)} %pad_maximum_fusion.22), channel_id=1, source_target_pairs={{0,24},{1,25},{2,26},{3,27},{4,28},{5,29},{6,30},{7,31}} | collective-permute-start | bytes 360008 | tf_op jit(solution)/shard_map/ppermute | solution.py:17
  135.6 52.8 %collective-permute-start.12 = (f32[10,4,600]{2,1,0:T(4,128)}, f32[10,4,600]{2,1,0:T(4,128)S(1)}, u32[]{:S(2)}, u32[]{:S(2)}) collective-permute-start(f32[10,4,600]{2,1,0:T(4,128)} %pad_maximum_fusion.23), channel_id=1, source_target_pairs={{0,15},{1,16},{2,17},{3,18},{4,19},{5,20},{6,21},{7,22},{8,23},{9,... | collective-permute-start | bytes 288008 | tf_op jit(solution)/shard_map/ppermute | solution.py:17
  589.8 55.2 %collective-permute-start.62 = (f32[10,5,600]{2,1,0:T(8,128)S(1)}, f32[10,5,600]{2,1,0:T(8,128)S(1)}, u32[]{:S(2)}, u32[]{:S(2)}) collective-permute-start(f32[10,5,600]{2,1,0:T(8,128)S(1)} %pad_maximum_fusion.22), channel_id=1, source_target_pairs={{0,19},{1,20},{2,21},{3,22},{4,23},{5,24},{6,25},{7,26},{8,27},{9,... | collective-permute-start | bytes 360008 | tf_op jit(solution)/shard_map/ppermute | solution.py:17
  592.8 54.3 %collective-permute-start.63 = (f32[10,5,600]{2,1,0:T(8,128)S(1)}, f32[10,5,600]{2,1,0:T(8,128)S(1)}, u32[]{:S(2)}, u32[]{:S(2)}) collective-permute-start(f32[10,5,600]{2,1,0:T(8,128)S(1)} %pad_maximum_fusion.22), channel_id=1, source_target_pairs={{0,18},{1,19},{2,20},{3,21},{4,22},{5,23},{6,24},{7,25},{8,26},{9,... | collective-permute-start | bytes 360008 | tf_op jit(solution)/shard_map/ppermute | solution.py:17
  595.7 53.3 %collective-permute-start.64 = (f32[10,5,600]{2,1,0:T(8,128)S(1)}, f32[10,5,600]{2,1,0:T(8,128)S(1)}, u32[]{:S(2)}, u32[]{:S(2)}) collective-permute-start(f32[10,5,600]{2,1,0:T(8,128)S(1)} %pad_maximum_fusion.22), channel_id=1, source_target_pairs={{0,17},{1,18},{2,19},{3,20},{4,21},{5,22},{6,23},{7,24},{8,25},{9,... | collective-permute-start | bytes 360008 | tf_op jit(solution)/shard_map/ppermute | solution.py:17
  597.7 53.3 %collective-permute-start.65 = (f32[10,5,600]{2,1,0:T(8,128)S(1)}, f32[10,5,600]{2,1,0:T(8,128)S(1)}, u32[]{:S(2)}, u32[]{:S(2)}) collective-permute-start(f32[10,5,600]{2,1,0:T(8,128)S(1)} %pad_maximum_fusion.22), channel_id=1, source_target_pairs={{0,16},{1,17},{2,18},{3,19},{4,20},{5,21},{6,22},{7,23},{8,24},{9,... | collective-permute-start | bytes 360008 | tf_op jit(solution)/shard_map/ppermute | solution.py:17
  599.7 61.0 %collective-permute-start.66 = (f32[10,5,600]{2,1,0:T(8,128)S(1)}, f32[10,5,600]{2,1,0:T(8,128)S(1)}, u32[]{:S(2)}, u32[]{:S(2)}) collective-permute-start(f32[10,5,600]{2,1,0:T(8,128)S(1)} %pad_maximum_fusion.22), channel_id=1, source_target_pairs={{0,15},{1,16},{2,17},{3,18},{4,19},{5,20},{6,21},{7,22},{8,23},{9,... | collective-permute-start | bytes 360008 | tf_op jit(solution)/shard_map/ppermute | solution.py:17
  651.0 34.0 %collective-permute-start.70 = (f32[10,5,600]{2,1,0:T(8,128)S(1)}, f32[10,5,600]{2,1,0:T(8,128)S(1)}, u32[]{:S(2)}, u32[]{:S(2)}) collective-permute-start(f32[10,5,600]{2,1,0:T(8,128)S(1)} %pad_maximum_fusion.22), channel_id=1, source_target_pairs={{0,11},{1,12},{2,13},{3,14},{4,15},{5,16},{6,17},{7,18},{8,19},{9,... | collective-permute-start | bytes 360008 | tf_op jit(solution)/shard_map/ppermute | solution.py:17
  671.6 34.7 %collective-permute-start.73 = (f32[10,5,600]{2,1,0:T(8,128)S(1)}, f32[10,5,600]{2,1,0:T(8,128)S(1)}, u32[]{:S(2)}, u32[]{:S(2)}) collective-permute-start(f32[10,5,600]{2,1,0:T(8,128)S(1)} %pad_maximum_fusion.22), channel_id=1, source_target_pairs={{0,8},{1,9},{2,10},{3,11},{4,12},{5,13},{6,14},{7,15},{8,16},{9,17... | collective-permute-start | bytes 360008 | tf_op jit(solution)/shard_map/ppermute | solution.py:17
  673.6 39.7 %collective-permute-start.74 = (f32[10,5,600]{2,1,0:T(8,128)S(1)}, f32[10,5,600]{2,1,0:T(8,128)S(1)}, u32[]{:S(2)}, u32[]{:S(2)}) collective-permute-start(f32[10,5,600]{2,1,0:T(8,128)S(1)} %pad_maximum_fusion.22), channel_id=1, source_target_pairs={{0,7},{1,8},{2,9},{3,10},{4,11},{5,12},{6,13},{7,14},{8,15},{9,16}... | collective-permute-start | bytes 360008 | tf_op jit(solution)/shard_map/ppermute | solution.py:17
  685.1 35.3 %collective-permute-start.75 = (f32[10,5,600]{2,1,0:T(8,128)S(1)}, f32[10,5,600]{2,1,0:T(8,128)S(1)}, u32[]{:S(2)}, u32[]{:S(2)}) collective-permute-start(f32[10,5,600]{2,1,0:T(8,128)S(1)} %pad_maximum_fusion.22), channel_id=1, source_target_pairs={{0,6},{1,7},{2,8},{3,9},{4,10},{5,11},{6,12},{7,13},{8,14},{9,15},... | collective-permute-start | bytes 360008 | tf_op jit(solution)/shard_map/ppermute | solution.py:17
  692.1 35.3 %collective-permute-start.76 = (f32[10,5,600]{2,1,0:T(8,128)S(1)}, f32[10,5,600]{2,1,0:T(8,128)S(1)}, u32[]{:S(2)}, u32[]{:S(2)}) collective-permute-start(f32[10,5,600]{2,1,0:T(8,128)S(1)} %pad_maximum_fusion.22), channel_id=1, source_target_pairs={{0,5},{1,6},{2,7},{3,8},{4,9},{5,10},{6,11},{7,12},{8,13},{9,14},{... | collective-permute-start | bytes 360008 | tf_op jit(solution)/shard_map/ppermute | solution.py:17
  699.2 35.3 %collective-permute-start.77 = (f32[10,5,600]{2,1,0:T(8,128)S(1)}, f32[10,5,600]{2,1,0:T(8,128)S(1)}, u32[]{:S(2)}, u32[]{:S(2)}) collective-permute-start(f32[10,5,600]{2,1,0:T(8,128)S(1)} %pad_maximum_fusion.22), channel_id=1, source_target_pairs={{0,4},{1,5},{2,6},{3,7},{4,8},{5,9},{6,10},{7,11},{8,12},{9,13},{1... | collective-permute-start | bytes 360008 | tf_op jit(solution)/shard_map/ppermute | solution.py:17
  706.2 36.0 %collective-permute-start.78 = (f32[10,5,600]{2,1,0:T(8,128)S(1)}, f32[10,5,600]{2,1,0:T(8,128)S(1)}, u32[]{:S(2)}, u32[]{:S(2)}) collective-permute-start(f32[10,5,600]{2,1,0:T(8,128)S(1)} %pad_maximum_fusion.22), channel_id=1, source_target_pairs={{0,3},{1,4},{2,5},{3,6},{4,7},{5,8},{6,9},{7,10},{8,11},{9,12},{10... | collective-permute-start | bytes 360008 | tf_op jit(solution)/shard_map/ppermute | solution.py:17
  713.3 36.6 %collective-permute-start.79 = (f32[10,5,600]{2,1,0:T(8,128)S(1)}, f32[10,5,600]{2,1,0:T(8,128)S(1)}, u32[]{:S(2)}, u32[]{:S(2)}) collective-permute-start(f32[10,5,600]{2,1,0:T(8,128)S(1)} %pad_maximum_fusion.22), channel_id=1, source_target_pairs={{0,2},{1,3},{2,4},{3,5},{4,6},{5,7},{6,8},{7,9},{8,10},{9,11},{10,... | collective-permute-start | bytes 360008 | tf_op jit(solution)/shard_map/ppermute | solution.py:17
  720.4 37.3 %collective-permute-start.80 = (f32[10,5,600]{2,1,0:T(8,128)S(1)}, f32[10,5,600]{2,1,0:T(8,128)S(1)}, u32[]{:S(2)}, u32[]{:S(2)}) collective-permute-start(f32[10,5,600]{2,1,0:T(8,128)S(1)} %pad_maximum_fusion.22), channel_id=1, source_target_pairs={{0,1},{1,2},{2,3},{3,4},{4,5},{5,6},{6,7},{7,8},{8,9},{9,10},{10,1... | collective-permute-start | bytes 360008 | tf_op jit(solution)/shard_map/ppermute | solution.py:17
  727.4 38.6 %collective-permute-start.81 = (f32[10,5,600]{2,1,0:T(8,128)S(1)}, f32[10,5,600]{2,1,0:T(8,128)S(1)}, u32[]{:S(2)}, u32[]{:S(2)}) collective-permute-start(f32[10,5,600]{2,1,0:T(8,128)S(1)} %pad_maximum_fusion.22), channel_id=1, source_target_pairs={{1,0},{2,1},{3,2},{4,3},{5,4},{6,5},{7,6},{8,7},{9,8},{10,9},{11,1... | collective-permute-start | bytes 360008 | tf_op jit(solution)/shard_map/ppermute | solution.py:17
  734.5 39.3 %collective-permute-start.82 = (f32[10,5,600]{2,1,0:T(8,128)S(1)}, f32[10,5,600]{2,1,0:T(8,128)S(1)}, u32[]{:S(2)}, u32[]{:S(2)}) collective-permute-start(f32[10,5,600]{2,1,0:T(8,128)S(1)} %pad_maximum_fusion.22), channel_id=1, source_target_pairs={{2,0},{3,1},{4,2},{5,3},{6,4},{7,5},{8,6},{9,7},{10,8},{11,9},{12,... | collective-permute-start | bytes 360008 | tf_op jit(solution)/shard_map/ppermute | solution.py:17
  742.2 39.3 %collective-permute-start.83 = (f32[10,5,600]{2,1,0:T(8,128)S(1)}, f32[10,5,600]{2,1,0:T(8,128)S(1)}, u32[]{:S(2)}, u32[]{:S(2)}) collective-permute-start(f32[10,5,600]{2,1,0:T(8,128)S(1)} %pad_maximum_fusion.22), channel_id=1, source_target_pairs={{3,0},{4,1},{5,2},{6,3},{7,4},{8,5},{9,6},{10,7},{11,8},{12,9},{13... | collective-permute-start | bytes 360008 | tf_op jit(solution)/shard_map/ppermute | solution.py:17
  805.6 81.1 %collective-permute-start.96 = (f32[10,5,600]{2,1,0:T(8,128)S(1)}, f32[10,5,600]{2,1,0:T(8,128)S(1)}, u32[]{:S(2)}, u32[]{:S(2)}) collective-permute-start(f32[10,5,600]{2,1,0:T(8,128)S(1)} %pad_maximum_fusion.22), channel_id=1, source_target_pairs={{16,0},{17,1},{18,2},{19,3},{20,4},{21,5},{22,6},{23,7},{24,8},{25... | collective-permute-start | bytes 360008 | tf_op jit(solution)/shard_map/ppermute | solution.py:17
  812.0 76.6 %collective-permute-start.97 = (f32[10,5,600]{2,1,0:T(8,128)S(1)}, f32[10,5,600]{2,1,0:T(8,128)S(1)}, u32[]{:S(2)}, u32[]{:S(2)}) collective-permute-start(f32[10,5,600]{2,1,0:T(8,128)S(1)} %pad_maximum_fusion.22), channel_id=1, source_target_pairs={{17,0},{18,1},{19,2},{20,3},{21,4},{22,5},{23,6},{24,7},{25,8},{26... | collective-permute-start | bytes 360008 | tf_op jit(solution)/shard_map/ppermute | solution.py:17
  814.6 81.6 %collective-permute-start.98 = (f32[10,5,600]{2,1,0:T(8,128)S(1)}, f32[10,5,600]{2,1,0:T(8,128)S(1)}, u32[]{:S(2)}, u32[]{:S(2)}) collective-permute-start(f32[10,5,600]{2,1,0:T(8,128)S(1)} %pad_maximum_fusion.22), channel_id=1, source_target_pairs={{18,0},{19,1},{20,2},{21,3},{22,4},{23,5},{24,6},{25,7},{26,8},{27... | collective-permute-start | bytes 360008 | tf_op jit(solution)/shard_map/ppermute | solution.py:17
  821.4 76.7 %collective-permute-start.99 = (f32[10,5,600]{2,1,0:T(8,128)S(1)}, f32[10,5,600]{2,1,0:T(8,128)S(1)}, u32[]{:S(2)}, u32[]{:S(2)}) collective-permute-start(f32[10,5,600]{2,1,0:T(8,128)S(1)} %pad_maximum_fusion.22), channel_id=1, source_target_pairs={{19,0},{20,1},{21,2},{22,3},{23,4},{24,5},{25,6},{26,7},{27,8},{28... | collective-permute-start | bytes 360008 | tf_op jit(solution)/shard_map/ppermute | solution.py:17
  823.4 76.7 %collective-permute-start.100 = (f32[10,5,600]{2,1,0:T(8,128)S(1)}, f32[10,5,600]{2,1,0:T(8,128)S(1)}, u32[]{:S(2)}, u32[]{:S(2)}) collective-permute-start(f32[10,5,600]{2,1,0:T(8,128)S(1)} %pad_maximum_fusion.22), channel_id=1, source_target_pairs={{20,0},{21,1},{22,2},{23,3},{24,4},{25,5},{26,6},{27,7},{28,8},{29... | collective-permute-start | bytes 360008 | tf_op jit(solution)/shard_map/ppermute | solution.py:17
  888.6 41.2 %collective-permute-start.102 = (f32[10,5,600]{2,1,0:T(8,128)S(1)}, f32[10,5,600]{2,1,0:T(8,128)S(1)}, u32[]{:S(2)}, u32[]{:S(2)}) collective-permute-start(f32[10,5,600]{2,1,0:T(8,128)S(1)} %pad_maximum_fusion.22), channel_id=1, source_target_pairs={{22,0},{23,1},{24,2},{25,3},{26,4},{27,5},{28,6},{29,7},{30,8},{31... | collective-permute-start | bytes 360008 | tf_op jit(solution)/shard_map/ppermute | solution.py:17
  896.2 45.0 %collective-permute-start.103 = (f32[10,5,600]{2,1,0:T(8,128)S(1)}, f32[10,5,600]{2,1,0:T(8,128)S(1)}, u32[]{:S(2)}, u32[]{:S(2)}) collective-permute-start(f32[10,5,600]{2,1,0:T(8,128)S(1)} %pad_maximum_fusion.22), channel_id=1, source_target_pairs={{23,0},{24,1},{25,2},{26,3},{27,4},{28,5},{29,6},{30,7},{31,8}} | collective-permute-start | bytes 360008 | tf_op jit(solution)/shard_map/ppermute | solution.py:17
  898.2 43.7 %collective-permute-start.104 = (f32[10,5,600]{2,1,0:T(8,128)S(1)}, f32[10,5,600]{2,1,0:T(8,128)S(1)}, u32[]{:S(2)}, u32[]{:S(2)}) collective-permute-start(f32[10,5,600]{2,1,0:T(8,128)S(1)} %pad_maximum_fusion.22), channel_id=1, source_target_pairs={{24,0},{25,1},{26,2},{27,3},{28,4},{29,5},{30,6},{31,7}} | collective-permute-start | bytes 360008 | tf_op jit(solution)/shard_map/ppermute | solution.py:17
  900.2 42.4 %collective-permute-start.105 = (f32[10,5,600]{2,1,0:T(8,128)S(1)}, f32[10,5,600]{2,1,0:T(8,128)S(1)}, u32[]{:S(2)}, u32[]{:S(2)}) collective-permute-start(f32[10,5,600]{2,1,0:T(8,128)S(1)} %pad_maximum_fusion.22), channel_id=1, source_target_pairs={{25,0},{26,1},{27,2},{28,3},{29,4},{30,5},{31,6}} | collective-permute-start | bytes 360008 | tf_op jit(solution)/shard_map/ppermute | solution.py:17
  902.2 41.1 %collective-permute-start.106 = (f32[10,5,600]{2,1,0:T(8,128)S(1)}, f32[10,5,600]{2,1,0:T(8,128)S(1)}, u32[]{:S(2)}, u32[]{:S(2)}) collective-permute-start(f32[10,5,600]{2,1,0:T(8,128)S(1)} %pad_maximum_fusion.22), channel_id=1, source_target_pairs={{26,0},{27,1},{28,2},{29,3},{30,4},{31,5}} | collective-permute-start | bytes 360008 | tf_op jit(solution)/shard_map/ppermute | solution.py:17
  (84 other events, 1140.9 us)
where the time goes:
time: 991 us; the launch traced here: 978 us
  starting transfers between devices  488 us (49%)
  waiting for transfers between devices  327 us (33%)
  local copies, waits for them, and re-layouts  143 us (14%)
  other arithmetic  18.9 us (2%)
    ppermute x108, starting transfers between devices, shifted(): return lax.ppermute(block, axis, route)  488 us
    ppermute x108, waiting for transfers between devices, shifted(): return lax.ppermute(block, axis, route)  327 us
    unnamed x125, local copies, waits for them, and re-layouts  79.4 us
  transfers between devices with their start and end apart: 108, of which 62 were waited for; matrix products, arithmetic and copies ran while one was open for 11% of the time, Pallas kernels for 0%

commit v1 on v0

v1 whole, which is shorter than its diff:
```python
import jax
import jax.numpy as jnp
from jax import lax
from jax.sharding import PartitionSpec as P

IB = 90
JB = 60
COURANT = 0.2
LANES = 128


def edge_pack(state, statics):
    count, chans = state.shape[:2]
    levels = (statics.shape[1] - 1) // 2
    east_vel, north_vel, depth = statics[:, :levels], statics[:, levels : 2 * levels], statics[:, 2 * levels :]
    x_part = jnp.concatenate([east_vel, depth], axis=1)
    y_part = jnp.concatenate([north_vel, depth], axis=1)
    pieces = [
        state[:, :, :, 0:2], x_part[:, :, :, 0],
        state[:, :, :, IB - 2 :], x_part[:, :, :, IB - 1],
        state[:, :, 0:2], y_part[:, :, 0],
        state[:, :, JB - 2 :], y_part[:, :, JB - 1],
    ]
    return jnp.concatenate([piece.reshape(count, -1) for piece in pieces], axis=1)


def face_flux(velocity_face, left_far, left_near, right_near, right_far):
    centered = (7.0 * (left_near + right_near) - (left_far + right_far)) / 12.0
    upwind = (right_far - 3.0 * right_near + 3.0 * left_near - left_far) / 12.0
    return velocity_face * centered + jnp.abs(velocity_face) * upwind


def per_device(tracers, velocity, kappa, kmt, block_owner, neighbours, fold_partner):
    slot_count, chans = tracers.shape[:2]
    levels = velocity.shape[1] // 2
    sub_count = lax.axis_size("sub")
    device_count = lax.axis_size("blk") * sub_count
    my_index = lax.axis_index("blk") * sub_count + lax.axis_index("sub")
    block_count = block_owner.shape[0]
    my_slots = my_index * slot_count + jnp.arange(slot_count, dtype=jnp.int32)
    hits = block_owner[None, :] == my_slots[:, None]
    live_slot = jnp.any(hits, axis=1)
    mine = jnp.sum(jnp.where(hits, jnp.arange(block_count, dtype=jnp.int32)[None, :], 0), axis=1)
    links = jnp.concatenate([neighbours[mine], fold_partner[mine][:, None]], axis=1)
    links = jnp.where(live_slot[:, None], links, -1)
    codes = jnp.where(links >= 0, block_owner[jnp.maximum(links, 0)], -1)

    state = tracers.reshape(slot_count, chans, JB, IB)
    statics = jnp.concatenate([velocity, kmt[:, None, :]], axis=1).reshape(slot_count, 2 * levels + 1, JB, IB)
    pack = edge_pack(state, statics)
    width = pack.shape[1]
    padded = -(-width // LANES) * LANES
    pack = jnp.pad(pack, ((0, 0), (0, padded - width))).reshape(-1, LANES)
    window = lax.all_gather(pack, ("blk", "sub"), axis=0, tiled=True)
    window = window.reshape(device_count * slot_count, padded)

    x_far, x_near = chans * JB * 2, (levels + 1) * JB
    y_far, y_near = chans * 2 * IB, (levels + 1) * IB
    x_wide, y_wide = x_far + x_near, y_far + y_near

    def strip(direction, start, wide):
        code = codes[:, direction]
        picked = jnp.take(window, jnp.maximum(code, 0), axis=0)[:, start : start + wide]
        return jnp.where((code >= 0)[:, None], picked, 0.0)

    west = strip(0, x_wide, x_wide)
    east = strip(1, 0, x_wide)
    south = strip(2, 2 * x_wide + y_wide, y_wide)
    north = strip(3, 2 * x_wide, y_wide)
    mirror = strip(4, 2 * x_wide + y_wide, y_wide)

    def halo_x(part):
        return part[:, :x_far].reshape(slot_count, chans, JB, 2), part[:, x_far:].reshape(slot_count, levels + 1, JB, 1)

    def halo_y(part):
        return part[:, :y_far].reshape(slot_count, chans, 2, IB), part[:, y_far:].reshape(slot_count, levels + 1, 1, IB)

    west_x, west_s = halo_x(west)
    east_x, east_s = halo_x(east)
    south_x, south_s = halo_y(south)
    north_x, north_s = halo_y(north)
    mirror_x, mirror_s = halo_y(mirror)
    sign = jnp.concatenate([-jnp.ones((levels,), jnp.float32), jnp.ones((1,), jnp.float32)]).reshape(1, -1, 1, 1)
    north_x = north_x + mirror_x[:, :, ::-1, ::-1]
    north_s = north_s + sign * mirror_s[:, :, :, ::-1]

    x_vel = jnp.concatenate([west_s[:, :levels], statics[:, :levels], east_s[:, :levels]], axis=3)
    y_vel = jnp.concatenate([south_s[:, :levels], statics[:, levels : 2 * levels], north_s[:, :levels]], axis=2)
    depth = statics[:, 2 * levels :]
    x_depth = jnp.concatenate([west_s[:, levels:], depth, east_s[:, levels:]], axis=3)
    y_depth = jnp.concatenate([south_s[:, levels:], depth, north_s[:, levels:]], axis=2)
    level_ids = jnp.arange(levels).astype(jnp.float32).reshape(1, levels, 1, 1)
    x_wet = jnp.clip(x_depth - level_ids, 0.0, 1.0)
    y_wet = jnp.clip(y_depth - level_ids, 0.0, 1.0)
    inner = jnp.clip(depth - level_ids, 0.0, 1.0)
    face_x = 0.5 * (x_vel[..., :-1] + x_vel[..., 1:]) * x_wet[..., :-1] * x_wet[..., 1:]
    face_y = 0.5 * (y_vel[:, :, :-1] + y_vel[:, :, 1:]) * y_wet[:, :, :-1] * y_wet[:, :, 1:]
    x_ext = jnp.concatenate([west_x, state, east_x], axis=3).reshape(slot_count, chans // levels, levels, JB, IB + 4)
    y_ext = jnp.concatenate([south_x, state, north_x], axis=2).reshape(slot_count, chans // levels, levels, JB + 4, IB)
    flux_x = face_flux(face_x[:, None], x_ext[..., 0 : IB + 1], x_ext[..., 1 : IB + 2], x_ext[..., 2 : IB + 3], x_ext[..., 3 : IB + 4])
    flux_y = face_flux(face_y[:, None], y_ext[..., 0 : JB + 1, :], y_ext[..., 1 : JB + 2, :], y_ext[..., 2 : JB + 3, :], y_ext[..., 3 : JB + 4, :])
    divergence = flux_x[..., 1:] - flux_x[..., :-1] + (flux_y[..., 1:, :] - flux_y[..., :-1, :])
    explicit = state.reshape(slot_count, chans // levels, levels, JB, IB) - COURANT * inner[:, None] * divergence

    below = kappa.reshape(slot_count, 1, JB, IB) * inner[:, 0][:, None] * inner[:, 1][:, None]
    divider = 1.0 + below
    ratio = below / divider
    first = explicit[:, :, 0] / divider
    second = (explicit[:, :, 1] + below * first) / (divider - below * ratio)
    solved = jnp.stack([first + ratio * second, second], axis=2)
    result = solved.reshape(slot_count, chans, JB * IB)
    return jnp.where(live_slot[:, None, None], result, 0.0)


def solution(mesh):
    placed = (
        P(("blk", "sub"), None, None),
        P(("blk", "sub"), None, None),
        P(("blk", "sub"), None),
        P(("blk", "sub"), None),
        P(),
        P(),
        P(),
    )
    return jax.shard_map(
        per_device,
        mesh=mesh,
        in_specs=placed,
        out_specs=P(("blk", "sub"), None, None),
        check_vma=False,
    )
```

time: 991 us -> 153 us (0.15); the launches traced: 978 us -> 152 us
  starting transfers between devices: 488 us -> 0.01 us
  waiting for transfers between devices: 327 us -> 53.8 us
  local copies, waits for them, and re-layouts: 143 us -> 63.5 us
  between operations: 1.56 us -> 14.1 us
    ppermute x108 -> x0, starting transfers between devices: 488 us -> none  [shifted(): return lax.ppermute(block, axis, route)]
    ppermute x108 -> x0, waiting for transfers between devices: 327 us -> none  [shifted(): return lax.ppermute(block, axis, route)]
    unnamed x125 -> x65, local copies, waits for them, and re-layouts: 79.4 us -> 4.72 us
    all_gather x0 -> x1, waiting for transfers between devices: none -> 53.8 us  [per_device(): window = lax.all_gather(pack, ('blk', 'sub'), axis=0, tiled=True)]
    another operation x13 -> x5, local copies, waits for them, and re-layouts: 19.1 us -> 4.37 us  [the longest x1 2.24 us: per_device(): state.reshape(slot_count, chans // levels, levels, JB, IB)]
  transfers between devices with their start and end apart: 108 -> 1, of which waited for: 62 -> 1; matrix products, arithmetic and copies ran while one was open for 11% -> 7% of each run, Pallas kernels for 0% -> 0%
where the time goes in v1:
time: 153 us; the launch traced here: 152 us
  local copies, waits for them, and re-layouts  63.5 us (42%)
  waiting for transfers between devices  53.8 us (35%)
  other arithmetic  20.5 us (13%)
  between operations  14.1 us (9%)
    all_gather x1, waiting for transfers between devices, per_device(): window = lax.all_gather(pack, ('blk', 'sub'), axis=0, tiled=True)  53.8 us
    gather x5, local copies, waits for them, and re-layouts, strip(): jnp.take(window, jnp.maximum(code, 0), axis=0)[:, start:start + wide]  14.3 us
    add x2, other arithmetic, face_flux(): return velocity_face * centered + jnp.abs(velocity_face) * upwind  5.9 us
    concatenate x2, local copies, waits for them, and re-layouts, per_device(): jnp.concatenate([west_x, state, east_x], axis=3)  5.63 us
    reshape x1, local copies, waits for them, and re-layouts, per_device(): window = window.reshape(device_count * slot_count, padded)  5.05 us
    mul x4, other arithmetic, face_flux(): return velocity_face * centered + jnp.abs(velocity_face) * upwind  4.91 us
    unnamed x65, local copies, waits for them, and re-layouts  4.72 us
    slice x2, local copies, waits for them, and re-layouts, edge_pack(): state[:, :, :, IB - 2:]  4.16 us
  transfers between devices with their start and end apart: 1, of which 1 were waited for; matrix products, arithmetic and copies ran while one was open for 7% of the time, Pallas kernels for 0%

profile of v1, /device:TPU:0, one launch (start us, length us, event | category | flops | bytes accessed | tf_op | source)
XLA Modules:
  0.0 152.0 jit_solution(9561320261305841835)
XLA Ops:
  6.5 3.4 %reshape.174 = f32[10,4,60,90]{3,2,1,0:T(8,128)S(1)} reshape(f32[10,4,5400]{2,1,0:T(4,128)} %param.9) | data formatting | bytes 1728000 | tf_op jit(solution)/shard_map/reshape | solution.py:48
  10.0 1.9 %fusion.23 = (f32[10,4,60,2]{3,2,1,0:T(8,128)}, f32[10,4,60,2]{3,2,1,0:T(8,128)}) fusion(f32[10,4,60,90]{3,2,1,0:T(8,128)S(1)} %reshape.174), kind=kLoop, calls=%fused_computation.114 | loop fusion | bytes 76800 | tf_op jit(solution)/shard_map/slice | solution.py:20
  12.6 2.2 %concatenate.83 = f32[10,4,60,90]{3,2,1,0:T(8,128)S(1)} reshape(f32[10,4,5400]{2,1,0:T(4,128)S(1)} %copy-done.15) | data formatting | bytes 1728000 | tf_op jit(solution)/shard_map/concatenate | solution.py:49
  14.9 1.0 fusion.21
  16.5 0.9 fusion.3
  19.6 2.9 %copy.92 = f32[10,4,60,2]{0,3,2,1:T(2,128)S(1)} copy(f32[10,4,60,2]{3,2,1,0:T(8,128)} %get-tuple-element.33) | data formatting | bytes 38400 | tf_op jit(solution)/shard_map/slice | solution.py:19
  23.2 2.2 %copy.94 = f32[10,4,60,2]{0,3,2,1:T(2,128)} copy(f32[10,4,60,2]{3,2,1,0:T(8,128)S(1)} %copy-done.2) | data formatting | bytes 38400 | tf_op jit(solution)/shard_map/slice | solution.py:20
  25.4 1.1 copy.97
  28.2 0.9 concatenate.87
  29.9 2.2 %reshape_reshape.3 = f32[10,2,2,60,90]{4,3,2,1,0:T(8,128)S(1)} reshape(f32[10,4,5400]{2,1,0:T(4,128)S(1)} %copy-done.3) | data formatting | bytes 1728000 | tf_op jit(solution)/shard_map/reshape;reshape | solution.py:103
  32.2 1.2 sub.79
  36.7 1.2 reshape.188
  38.7 1.1 broadcast_multiply_fusion.2
  40.5 0.9 fusion.7
  41.4 53.8 %all-gather.3.cloned.1.call-done = f32[32,260,128]{2,1,0:T(8,128)} async-done(((f32[1,260,128]{2,1,0:T(8,128)}), f32[32,260,128]{2,1,0:T(8,128)}) %all-gather.3.cloned.1.call-update) | async-done | bytes 4259856 | tf_op jit(solution)/shard_map/all_gather | solution.py:54
  95.2 5.1 %reshape.180 = f32[320,3328]{1,0:T(8,128)} reshape(f32[32,260,128]{2,1,0:T(8,128)} %all-gather.3.cloned.1.call-done) | data formatting | bytes 8519680 | tf_op jit(solution)/shard_map/reshape | solution.py:55
  100.3 2.9 %gather_fusion.4 = f32[10,3328]{1,0:T(8,128)S(1)} fusion(f32[320,3328]{1,0:T(8,128)} %reshape.180, s32[1024]{0:T(1024)S(1)} %pad_clamp_fusion.3), kind=kCustom, calls=%fused_computation.1.clone | custom fusion | bytes 266280 | tf_op jit(solution)/shard_map/jit(_take)/gather | solution.py:63
  103.4 2.9 %gather_fusion.3 = f32[10,3328]{1,0:T(8,128)S(1)} fusion(f32[320,3328]{1,0:T(8,128)} %reshape.180, s32[1024]{0:T(1024)S(1)} %pad_clamp_fusion.4), kind=kCustom, calls=%fused_computation.clone | custom fusion | bytes 266280 | tf_op jit(solution)/shard_map/jit(_take)/gather | solution.py:63
  106.6 2.9 %gather_fusion.7 = f32[10,3328]{1,0:T(8,128)S(1)} fusion(f32[320,3328]{1,0:T(8,128)} %reshape.180, s32[1024]{0:T(1024)S(1)} %pad_clamp_fusion), kind=kCustom, calls=%fused_computation.4.clone | custom fusion | bytes 266280 | tf_op jit(solution)/shard_map/jit(_take)/gather | solution.py:63
  109.9 2.9 %gather_fusion.6 = f32[10,3328]{1,0:T(8,128)S(1)} fusion(f32[320,3328]{1,0:T(8,128)} %reshape.180, s32[1024]{0:T(1024)S(1)} %pad_clamp_fusion.1), kind=kCustom, calls=%fused_computation.3.clone | custom fusion | bytes 266280 | tf_op jit(solution)/shard_map/jit(_take)/gather | solution.py:63
  114.3 2.9 %gather_fusion.5 = f32[10,3328]{1,0:T(8,128)S(1)} fusion(f32[320,3328]{1,0:T(8,128)} %reshape.180, s32[1024]{0:T(1024)S(1)} %pad_clamp_fusion.2), kind=kCustom, calls=%fused_computation.2.clone | custom fusion | bytes 266280 | tf_op jit(solution)/shard_map/jit(_take)/gather | solution.py:63
  119.0 1.2 copy.112
  120.2 1.2 copy.111
  121.3 2.8 %broadcast_multiply_fusion.1 = (f32[10,2,60,91]{3,2,1,0:T(8,128)}, f32[10,2,60,91]{3,2,1,0:T(8,128)S(1)}) fusion(f32[10,2,60,92]{3,2,1,0:T(8,128)S(1)} %subtract_clamp_fusion.1, f32[10,2,60,1]{3,2,1,0:T(8,128)} %copy.112, f32[10,2,60,90]{3,2,1,0:T(8,128)S(1)} %get-tuple-element.29, f32[10,2,60,1]{3,2,1,0:T(8,128)} %copy.111), kind=kLoop, calls=%fused_computation.54 | loop fusion | flops 764400 | bytes 2188800 | tf_op jit(solution)/shard_map/mul | solution.py:30
  125.0 2.8 %copy.101 = f32[10,2,2,60,2]{4,3,2,1,0:T(8,128)} copy(f32[10,2,2,60,2]{0,4,3,2,1:T(2,128)S(1)} %bitcast.35) | data formatting | bytes 38400 | tf_op jit(solution)/shard_map/concatenate | solution.py:98
  128.0 2.8 %copy.99 = f32[10,2,2,60,2]{4,3,2,1,0:T(8,128)} copy(f32[10,2,2,60,2]{0,4,3,2,1:T(2,128)S(1)} %bitcast.36) | data formatting | bytes 38400 | tf_op jit(solution)/shard_map/concatenate | solution.py:98
  132.3 1.1 broadcast_multiply_fusion
  133.5 0.9 abs_multiply_fusion
  135.1 4.9 %multiply_add_fusion.1 = f32[10,2,2,60,91]{4,3,2,1,0:T(8,128)S(1)} fusion(f32[10,2,2,60,90]{4,3,2,1,0:T(8,128)S(1)} %reshape_reshape.3, f32[10,2,2,60,2]{4,3,2,1,0:T(8,128)} %copy.99, f32[10,2,2,60,2]{4,3,2,1,0:T(8,128)} %copy.101, f32[10,2,60,91]{3,2,1,0:T(8,128)S(1)} %abs_multiply_fusion.1, f32[10,2,60,91]{3,2,1,0:T(8,128)S(1)} %copy-done.5), kind=kLoop, calls=%fused_computation.23 | loop fusion | flops 3494400 | bytes 2649600 | tf_op jit(solution)/shard_map/add | solution.py:30
  140.0 1.0 multiply_add_fusion
  142.7 1.3 reshape.189
  144.0 1.2 broadcast_select_fusion
  (160 shorter events, 20.3 us)
Async XLA Ops:
  6.5 28.1 %copy-start = (s32[160]{0:T(256)S(1)}, s32[160]{0:T(256)}, u32[]{:S(2)}) copy-start(s32[160]{0:T(256)} %param.15) | copy-start | bytes 1924
  6.5 88.7 %all-gather.3.cloned.1.call-start = ((), (), s32[]{:S(2)}) async-start(), calls=%async_computation | async-start | bytes 4460544 | tf_op jit(solution)/shard_map/all_gather | solution.py:54
  10.0 2.6 %copy-start.15 = (f32[10,4,5400]{2,1,0:T(4,128)S(1)}, f32[10,4,5400]{2,1,0:T(4,128)}, u32[]{:S(2)}) copy-start(f32[10,4,5400]{2,1,0:T(4,128)} %param.10) | copy-start | bytes 2592004
  14.8 1.1 copy-start.9
  16.5 6.6 %copy-start.2 = (f32[10,4,60,2]{3,2,1,0:T(8,128)S(1)}, f32[10,4,60,2]{3,2,1,0:T(8,128)}, u32[]{:S(2)}) copy-start(f32[10,4,60,2]{3,2,1,0:T(8,128)} %get-tuple-element.32) | copy-start | bytes 57604
  23.2 6.7 %copy-start.3 = (f32[10,4,5400]{2,1,0:T(4,128)S(1)}, f32[10,4,5400]{2,1,0:T(4,128)}, u32[]{:S(2)}) copy-start(f32[10,4,5400]{2,1,0:T(4,128)} %param.9) | copy-start | bytes 2592004
  29.9 3.5 %copy-start.1 = (s32[160]{0:T(256)S(1)}, s32[160]{0:T(256)}, u32[]{:S(2)}) copy-start(s32[160]{0:T(256)} %param.13) | copy-start | bytes 1924
  29.9 3.8 %copy-start.27 = (s32[160,4]{0,1:T(4,128)S(1)}, s32[160,4]{0,1:T(4,128)}, u32[]{:S(2)}) copy-start(s32[160,4]{0,1:T(4,128)} %param.14) | copy-start | bytes 7684
  35.7 3.0 %copy-start.10 = (f32[10,60,90]{2,1,0:T(8,128)S(1)}, f32[10,60,90]{2,1,0:T(8,128)}, u32[]{:S(2)}) copy-start(f32[10,60,90]{2,1,0:T(8,128)} %sub.79) | copy-start | bytes 648004
  37.9 1.8 %copy-start.11 = (f32[10,1,60,90]{3,2,0,1:T(8,128)S(1)}, f32[10,1,60,90]{3,2,0,1:T(8,128)}, u32[]{:S(2)}) copy-start(f32[10,1,60,90]{3,2,0,1:T(8,128)} %reshape.188) | copy-start | bytes 648004
  37.9 80.9 %copy-start.26 = (f32[2]{0:T(128)}, f32[2]{0:T(128)S(1)}, u32[]{:S(2)}) copy-start(f32[2]{0:T(128)S(1)} %iota_convert_fusion) | copy-start | bytes 28
  103.2 6.2 %copy-start.20 = (f32[10,660]{1,0:T(8,128)}, f32[10,660]{1,0:T(8,128)S(1)}, u32[]{:S(2)}) copy-start(f32[10,660]{1,0:T(8,128)S(1)} %fusion.12) | copy-start | bytes 79204
  103.4 6.1 %copy-start.22 = (f32[10,3,60,1]{2,1,0,3:T(4,128)}, f32[10,3,60,1]{2,1,0,3:T(4,128)S(1)}, u32[]{:S(2)}) copy-start(f32[10,3,60,1]{2,1,0,3:T(4,128)S(1)} %reshape.182) | copy-start | bytes 21604
  106.4 3.1 %copy-start.21 = (f32[10,660]{1,0:T(8,128)}, f32[10,660]{1,0:T(8,128)S(1)}, u32[]{:S(2)}) copy-start(f32[10,660]{1,0:T(8,128)S(1)} %fusion.13) | copy-start | bytes 79204
  106.5 6.2 %copy-start.23 = (f32[10,3,60,1]{2,1,0,3:T(4,128)}, f32[10,3,60,1]{2,1,0,3:T(4,128)S(1)}, u32[]{:S(2)}) copy-start(f32[10,3,60,1]{2,1,0,3:T(4,128)S(1)} %reshape.181) | copy-start | bytes 21604
  109.5 3.6 %copy-start.28 = (f32[3]{0:T(128)S(1)}, f32[3]{0:T(128)}, u32[]{:S(2)}) copy-start(f32[3]{0:T(128)} %constant.24.clone.1) | copy-start | bytes 40
  109.6 8.5 %copy-start.17 = (f32[10,990]{1,0:T(8,128)}, f32[10,990]{1,0:T(8,128)S(1)}, u32[]{:S(2)}) copy-start(f32[10,990]{1,0:T(8,128)S(1)} %fusion.9) | copy-start | bytes 118804
  112.9 5.2 %copy-start.18 = (f32[10,990]{1,0:T(8,128)}, f32[10,990]{1,0:T(8,128)S(1)}, u32[]{:S(2)}) copy-start(f32[10,990]{1,0:T(8,128)S(1)} %fusion.10) | copy-start | bytes 118804
  117.5 1.5 copy-start.24
  118.5 1.7 %slice-start.6 = ((f32[10,3,60,1]{2,1,0,3:T(4,128)}), f32[10,2,60,1]{2,1,0,3:T(2,128)S(1)}, s32[]{:S(2)}) async-start(f32[10,3,60,1]{2,1,0,3:T(4,128)} %copy-done.23), calls=%async_computation.7 | async-start | bytes 20480 | tf_op jit(solution)/shard_map/slice | solution.py:87
  124.1 3.7 %slice-start.4 = ((f32[10,660]{1,0:T(8,128)}), f32[10,480]{1,0:T(8,128)S(1)}, s32[]{:S(2)}) async-start(f32[10,660]{1,0:T(8,128)} %copy-done.21), calls=%async_computation.5 | async-start | bytes 65536 | tf_op jit(solution)/shard_map/slice | solution.py:73
  128.0 4.3 %copy-start.6 = (f32[10,2,60,90]{3,2,1,0:T(8,128)S(1)}, f32[10,2,60,90]{3,2,1,0:T(8,128)}, u32[]{:S(2)}) copy-start(f32[10,2,60,90]{3,2,1,0:T(8,128)} %get-tuple-element.28) | copy-start | bytes 1296004
  128.0 4.3 %slice-start.7 = ((f32[10,3,1,90]{3,1,0,2:T(4,128)}), f32[10,2,1,90]{3,1,0,2:T(2,128)S(1)}, s32[]{:S(2)}) async-start(f32[10,3,1,90]{3,1,0,2:T(4,128)} %copy-done.24), calls=%async_computation.8 | async-start | bytes 20480 | tf_op jit(solution)/shard_map/slice | solution.py:88
  128.0 4.3 %copy-start.25 = (f32[10,2,1,90]{3,2,1,0:T(1,128)S(1)}, f32[10,2,1,90]{3,2,1,0:T(1,128)}, u32[]{:S(2)}) copy-start(f32[10,2,1,90]{3,2,1,0:T(1,128)} %slice.318) | copy-start | bytes 21604
  133.5 1.3 slice-start.1
  133.5 1.4 slice-start.2
  133.5 1.6 %copy-start.5 = (f32[10,2,60,91]{3,2,1,0:T(8,128)S(1)}, f32[10,2,60,91]{3,2,1,0:T(8,128)}, u32[]{:S(2)}) copy-start(f32[10,2,60,91]{3,2,1,0:T(8,128)} %get-tuple-element.24) | copy-start | bytes 1310404
  135.1 4.9 %copy-start.7 = (f32[10,2,61,90]{3,2,1,0:T(8,128)S(1)}, f32[10,2,61,90]{3,2,1,0:T(8,128)}, u32[]{:S(2)}) copy-start(f32[10,2,61,90]{3,2,1,0:T(8,128)} %abs_multiply_fusion) | copy-start | bytes 1317604
  135.1 4.9 %copy-start.8 = (f32[10,2,61,90]{3,2,1,0:T(8,128)S(1)}, f32[10,2,61,90]{3,2,1,0:T(8,128)}, u32[]{:S(2)}) copy-start(f32[10,2,61,90]{3,2,1,0:T(8,128)} %get-tuple-element.26) | copy-start | bytes 1317604
  140.0 1.1 copy-start.4
  141.1 1.1 copy-start.13
  141.1 1.2 copy-start.14
  (6 other events, 5.2 us)
Sparse Core Ops, SparseCore 0:
  30.0 65.1 all-gather.2

commit v2 on v1

--- a/solution.py
+++ b/solution.py
@@ -6,22 +6,32 @@
 IB = 90
 JB = 60
 COURANT = 0.2
-LANES = 128
 
 
-def edge_pack(state, statics):
+def edge_pack(state, statics, parts):
     count, chans = state.shape[:2]
     levels = (statics.shape[1] - 1) // 2
     east_vel, north_vel, depth = statics[:, :levels], statics[:, levels : 2 * levels], statics[:, 2 * levels :]
     x_part = jnp.concatenate([east_vel, depth], axis=1)
     y_part = jnp.concatenate([north_vel, depth], axis=1)
-    pieces = [
-        state[:, :, :, 0:2], x_part[:, :, :, 0],
-        state[:, :, :, IB - 2 :], x_part[:, :, :, IB - 1],
-        state[:, :, 0:2], y_part[:, :, 0],
-        state[:, :, JB - 2 :], y_part[:, :, JB - 1],
+    sides = [
+        (state[:, :, :, 0:2], x_part[:, :, :, 0]),
+        (state[:, :, :, IB - 2 :], x_part[:, :, :, IB - 1]),
+        (state[:, :, 0:2], y_part[:, :, 0]),
+        (state[:, :, JB - 2 :], y_part[:, :, JB - 1]),
     ]
-    return jnp.concatenate([piece.reshape(count, -1) for piece in pieces], axis=1)
+    pieces = []
+    for near, far in sides:
+        flat = jnp.concatenate([near.reshape(count, -1), far.reshape(count, -1)], axis=1)
+        wide = -(-flat.shape[1] // parts)
+        flat = jnp.pad(flat, ((0, 0), (0, parts * wide - flat.shape[1])))
+        pieces.append(flat.reshape(count, parts, wide))
+    return jnp.concatenate(pieces, axis=2).transpose(1, 0, 2)
+
+
+def chosen(codes, table):
+    one_hot = (codes[:, None] == jnp.arange(table.shape[0], dtype=jnp.int32)[None, :]).astype(jnp.float32)
+    return jnp.dot(one_hot, table, precision=lax.Precision.HIGHEST)
 
 
 def face_flux(velocity_face, left_far, left_near, right_near, right_far):
@@ -37,37 +47,43 @@
     device_count = lax.axis_size("blk") * sub_count
     my_index = lax.axis_index("blk") * sub_count + lax.axis_index("sub")
     block_count = block_owner.shape[0]
-    my_slots = my_index * slot_count + jnp.arange(slot_count, dtype=jnp.int32)
-    hits = block_owner[None, :] == my_slots[:, None]
-    live_slot = jnp.any(hits, axis=1)
-    mine = jnp.sum(jnp.where(hits, jnp.arange(block_count, dtype=jnp.int32)[None, :], 0), axis=1)
-    links = jnp.concatenate([neighbours[mine], fold_partner[mine][:, None]], axis=1)
-    links = jnp.where(live_slot[:, None], links, -1)
-    codes = jnp.where(links >= 0, block_owner[jnp.maximum(links, 0)], -1)
+    slot_total = device_count * slot_count
+    axes = ("blk", "sub")
 
     state = tracers.reshape(slot_count, chans, JB, IB)
     statics = jnp.concatenate([velocity, kmt[:, None, :]], axis=1).reshape(slot_count, 2 * levels + 1, JB, IB)
-    pack = edge_pack(state, statics)
-    width = pack.shape[1]
-    padded = -(-width // LANES) * LANES
-    pack = jnp.pad(pack, ((0, 0), (0, padded - width))).reshape(-1, LANES)
-    window = lax.all_gather(pack, ("blk", "sub"), axis=0, tiled=True)
-    window = window.reshape(device_count * slot_count, padded)
+    pack = edge_pack(state, statics, device_count)
+
+    hits = block_owner[None, :] == jnp.arange(slot_total, dtype=jnp.int32)[:, None]
+    live = jnp.any(hits, axis=1)
+    links = jnp.concatenate([neighbours, fold_partner[:, None]], axis=1)
+    link_blocks = jnp.max(jnp.where(hits[:, :, None], links[None], -1), axis=1)
+    link_hits = link_blocks[:, :, None] == jnp.arange(block_count, dtype=jnp.int32)[None, None, :]
+    codes = jnp.max(jnp.where(link_hits, block_owner[None, None, :], -1), axis=2)
+    live_slot = lax.dynamic_slice_in_dim(live, my_index * slot_count, slot_count, 0)
+    folded = lax.dynamic_slice_in_dim(codes[:, 4] >= 0, my_index * slot_count, slot_count, 0)
 
     x_far, x_near = chans * JB * 2, (levels + 1) * JB
     y_far, y_near = chans * 2 * IB, (levels + 1) * IB
     x_wide, y_wide = x_far + x_near, y_far + y_near
 
-    def strip(direction, start, wide):
-        code = codes[:, direction]
-        picked = jnp.take(window, jnp.maximum(code, 0), axis=0)[:, start : start + wide]
-        return jnp.where((code >= 0)[:, None], picked, 0.0)
+    x_piece, y_piece = -(-x_wide // device_count), -(-y_wide // device_count)
+    cuts = [0, x_piece, 2 * x_piece, 2 * x_piece + y_piece, 2 * x_piece + 2 * y_piece]
 
-    west = strip(0, x_wide, x_wide)
-    east = strip(1, 0, x_wide)
-    south = strip(2, 2 * x_wide + y_wide, y_wide)
-    north = strip(3, 2 * x_wide, y_wide)
-    mirror = strip(4, 2 * x_wide + y_wide, y_wide)
+    held = lax.all_to_all(pack, axes, 0, 0, tiled=True).reshape(slot_total, cuts[4])
+    sides = [held[:, cuts[i] : cuts[i + 1]] for i in range(4)]
+    picked = [
+        chosen(codes[:, 0], sides[1]),
+        chosen(codes[:, 1], sides[0]),
+        chosen(codes[:, 2], sides[3]),
+        chosen(codes[:, 3], sides[2]) + chosen(codes[:, 4], sides[3]),
+    ]
+    picked = jnp.concatenate(picked, axis=1).reshape(device_count, slot_count, cuts[4])
+    window = lax.all_to_all(picked, axes, 0, 0, tiled=True).transpose(1, 0, 2)
+    west = window[:, :, : cuts[1]].reshape(slot_count, -1)[:, :x_wide]
+    east = window[:, :, cuts[1] : cuts[2]].reshape(slot_count, -1)[:, :x_wide]
+    south = window[:, :, cuts[2] : cuts[3]].reshape(slot_count, -1)[:, :y_wide]
+    north = window[:, :, cuts[3] :].reshape(slot_count, -1)[:, :y_wide]
 
     def halo_x(part):
         return part[:, :x_far].reshape(slot_count, chans, JB, 2), part[:, x_far:].reshape(slot_count, levels + 1, JB, 1)
@@ -79,10 +95,10 @@
     east_x, east_s = halo_x(east)
     south_x, south_s = halo_y(south)
     north_x, north_s = halo_y(north)
-    mirror_x, mirror_s = halo_y(mirror)
     sign = jnp.concatenate([-jnp.ones((levels,), jnp.float32), jnp.ones((1,), jnp.float32)]).reshape(1, -1, 1, 1)
-    north_x = north_x + mirror_x[:, :, ::-1, ::-1]
-    north_s = north_s + sign * mirror_s[:, :, :, ::-1]
+    flipped = folded[:, None, None, None]
+    north_x = jnp.where(flipped, north_x[:, :, ::-1, ::-1], north_x)
+    north_s = jnp.where(flipped, sign * north_s[:, :, :, ::-1], north_s)
 
     x_vel = jnp.concatenate([west_s[:, :levels], statics[:, :levels], east_s[:, :levels]], axis=3)
     y_vel = jnp.concatenate([south_s[:, :levels], statics[:, levels : 2 * levels], north_s[:, :levels]], axis=2)

time: 153 us -> 81.4 us (0.53)
  waiting for transfers between devices: 53.8 us -> 12.5 us
  local copies, waits for them, and re-layouts: 63.5 us -> 35.2 us
  between operations: 14.1 us -> 0.79 us
  starting transfers between devices: 0.01 us -> 10.1 us
  matrix products: 0 us -> 2.68 us
    all_gather x1 -> x0, waiting for transfers between devices: 53.8 us -> none  [per_device(): window = lax.all_gather(pack, ('blk', 'sub'), axis=0, tiled=True)]
    gather x10 -> x0, local copies, waits for them, and re-layouts: 16.5 us -> none  [the longest x5 14.3 us: strip(): jnp.take(window, jnp.maximum(code, 0), axis=0)[:, start:start + wide]]
    all_to_all x0 -> x2, waiting for transfers between devices: none -> 12.5 us  [the longest x1 6.84 us: per_device(): lax.all_to_all(pack, axes, 0, 0, tiled=True).reshape(slot_total, cuts[4])]
    all_to_all x0 -> x2, starting transfers between devices: none -> 10.1 us  [the longest x1 7.3 us: per_device(): lax.all_to_all(pack, axes, 0, 0, tiled=True).reshape(slot_total, cuts[4])]
    reshape x5 -> x14, local copies, waits for them, and re-layouts: 8.61 us -> 2.51 us  [the longest x4 0.77 us: edge_pack(): pieces.append(flat.reshape(count, parts, wide))]
    dot_general x0 -> x5, matrix products: none -> 2.68 us  [chosen(): return jnp.dot(one_hot, table, precision=lax.Precision.HIGHEST)]
    slice x2 -> x1, local copies, waits for them, and re-layouts: 4.16 us -> 1.57 us  [edge_pack(): state[:, :, :, IB - 2:]]
    slice x1 -> x2, local copies, waits for them, and re-layouts: 2.88 us -> 4.92 us  [edge_pack(): state[:, :, :, 0:2]]
  transfers between devices with their start and end apart: 1 -> 2, of which waited for: 1 -> 2; matrix products, arithmetic and copies ran while one was open for 7% -> 10% of each run, Pallas kernels for 0% -> 0%
where the time goes in v2:
time: 81.4 us; the launch traced here: 80.8 us
  local copies, waits for them, and re-layouts  35.2 us (43%)
  other arithmetic  19.6 us (24%)
  waiting for transfers between devices  12.5 us (15%)
  starting transfers between devices  10.1 us (12%)
  matrix products  2.68 us (3%)
    all_to_all x1, starting transfers between devices, per_device(): lax.all_to_all(pack, axes, 0, 0, tiled=True).reshape(slot_total, cuts[4])  7.3 us
    all_to_all x1, waiting for transfers between devices, per_device(): lax.all_to_all(pack, axes, 0, 0, tiled=True).reshape(slot_total, cuts[4])  6.84 us
    add x2, other arithmetic, face_flux(): return velocity_face * centered + jnp.abs(velocity_face) * upwind  5.73 us
    all_to_all x1, waiting for transfers between devices, per_device(): window = lax.all_to_all(picked, axes, 0, 0, tiled=True).transpose(1, 0, 2)  5.63 us
    concatenate x2, local copies, waits for them, and re-layouts, per_device(): jnp.concatenate([west_x, state, east_x], axis=3)  5.62 us
    slice x2, local copies, waits for them, and re-layouts, edge_pack(): state[:, :, :, 0:2]  4.92 us
    mul x4, other arithmetic, face_flux(): return velocity_face * centered + jnp.abs(velocity_face) * upwind  4.8 us
    unnamed x57, local copies, waits for them, and re-layouts  4.28 us
  transfers between devices with their start and end apart: 2, of which 2 were waited for; matrix products, arithmetic and copies ran while one was open for 10% of the time, Pallas kernels for 0%

profile of v2, /device:TPU:0, one launch (start us, length us, event | category | flops | bytes accessed | tf_op | source)
XLA Modules:
  0.0 80.8 jit_solution(8557515028338522463)
XLA Ops:
  0.0 3.4 %reshape.129 = f32[10,4,60,90]{3,2,1,0:T(8,128)S(1)} reshape(f32[10,4,5400]{2,1,0:T(4,128)} %param.7) | data formatting | bytes 1728000 | tf_op jit(solution)/shard_map/reshape | solution.py:53
  3.4 2.0 %fusion.27 = (f32[10,4,60,2]{3,2,1,0:T(8,128)}, f32[10,4,60,2]{3,2,1,0:T(8,128)}) fusion(f32[10,4,60,90]{3,2,1,0:T(8,128)S(1)} %reshape.129), kind=kLoop, calls=%fused_computation.98 | loop fusion | bytes 76800 | tf_op jit(solution)/shard_map/slice | solution.py:18
  5.4 2.2 %concatenate.82 = f32[10,4,60,90]{3,2,1,0:T(8,128)S(1)} reshape(f32[10,4,5400]{2,1,0:T(4,128)S(1)} %copy-done.11) | data formatting | bytes 1728000 | tf_op jit(solution)/shard_map/concatenate | solution.py:54
  7.7 0.9 %fusion.26 = (f32[10,2,60,90]{3,2,1,0:T(8,128)}, f32[10,2,60,90]{3,2,1,0:T(8,128)S(1)}) fusion(f32[10,4,60,90]{3,2,1,0:T(8,128)S(1)} %concatenate.82), kind=kLoop, calls=%fused_computation.97 | loop fusion | bytes 1728000 | tf_op jit(solution)/shard_map/slice | solution.py:14
  9.3 0.9 %maximum_reduce_fusion = (f32[10,3,60]{2,1,0:T(4,128)S(1)}, f32[10,3,60]{2,1,0:T(4,128)S(1)}) fusion(f32[10,1,60,90]{3,2,1,0:T(8,128)S(1)} %bitcast.28, f32[10,2,60,90]{3,2,1,0:T(8,128)S(1)} %get-tuple-element.23), kind=kLoop, calls=%fused_computation.22 | loop fusion | flops 3600 | bytes 662400 | tf_op jit(solution)/shard_map/slice | solution.py:18
  10.2 3.0 %copy.103 = f32[10,4,60,2]{0,3,2,1:T(2,128)S(1)} copy(f32[10,4,60,2]{3,2,1,0:T(8,128)} %get-tuple-element.24) | data formatting | bytes 38400 | tf_op jit(solution)/shard_map/slice | solution.py:18
  13.7 1.6 %copy.106 = f32[10,4,60,2]{0,3,2,1:T(2,128)S(1)} copy(f32[10,4,60,2]{3,2,1,0:T(8,128)S(1)} %copy-done) | data formatting | bytes 38400 | tf_op jit(solution)/shard_map/slice | solution.py:19
  16.8 0.8 copy.109
  17.6 7.3 %all-to-all-start = ((f32[32,10,104]{2,1,0:T(8,128)}), f32[32,10,104]{2,1,0:T(8,128)S(1)}, u32[]{:S(2)}, u32[]{:S(2)}) async-start(f32[32,10,104]{2,1,0:T(8,128)} %copy.109), calls=%async_computation | async-start | bytes 524288 | tf_op jit(solution)/shard_map/all_to_all | solution.py:73
  26.2 1.1 %broadcast_multiply_fusion.2 = (f32[10,2,60,90]{3,2,0,1:T(8,128)}, f32[10,2,60,90]{3,2,0,1:T(8,128)S(1)}) fusion(f32[2]{0:T(128)S(1)} %iota_convert_fusion, f32[10,60,90]{2,1,0:T(8,128)S(1)} %sub.79), kind=kLoop, calls=%fused_computation.60 | loop fusion | flops 324000 | bytes 1080008 | tf_op jit(solution)/shard_map/mul | solution.py:119
  27.8 0.9 %fusion.12 = (f32[10,60,90]{2,1,0:T(8,128)}, f32[10,1,60,90]{3,2,0,1:T(8,128)}) fusion(f32[10,2,60,90]{3,2,0,1:T(8,128)S(1)} %get-tuple-element.29, f32[10,1,60,90]{3,2,0,1:T(8,128)S(1)} %reshape.149), kind=kLoop, calls=%fused_computation.61 | loop fusion | flops 216000 | bytes 1080000 | tf_op jit(solution)/shard_map/mul | solution.py:126
  28.7 6.8 %all-to-all-done = f32[32,10,104]{2,1,0:T(8,128)S(1)} async-done(((f32[32,10,104]{2,1,0:T(8,128)}), f32[32,10,104]{2,1,0:T(8,128)S(1)}, u32[]{:S(2)}, u32[]{:S(2)}) %all-to-all-start) | async-done | bytes 133152 | tf_op jit(solution)/shard_map/all_to_all | solution.py:73
  38.4 0.7 reshape.139
  39.1 2.8 %all-to-all-start.1 = ((f32[32,10,104]{2,1,0:T(8,128)}), f32[32,10,104]{2,1,0:T(8,128)S(1)}, u32[]{:S(2)}, u32[]{:S(2)}) async-start(f32[32,10,104]{2,1,0:T(8,128)} %reshape.139), calls=%async_computation.1 | async-start | bytes 524288 | tf_op jit(solution)/shard_map/all_to_all | solution.py:82
  41.9 2.2 %reshape_reshape.3 = f32[10,2,2,60,90]{4,3,2,1,0:T(8,128)S(1)} reshape(f32[10,4,5400]{2,1,0:T(4,128)S(1)} %copy-done.1) | data formatting | bytes 1728000 | tf_op jit(solution)/shard_map/reshape;reshape | solution.py:119
  44.2 0.7 dynamic_slice.6
  44.9 1.8 %fusion.11 = (f32[10,60,90]{2,1,0:T(8,128)S(1)}, f32[10,60,90]{2,1,0:T(8,128)}) fusion(f32[10,1,60,90]{3,2,0,1:T(8,128)} %get-tuple-element.17), kind=kLoop, calls=%fused_computation.53 | loop fusion | flops 216000 | bytes 648000 | tf_op jit(solution)/shard_map/div | solution.py:125
  46.7 5.6 %all-to-all-done.1 = f32[32,10,104]{2,1,0:T(8,128)S(1)} async-done(((f32[32,10,104]{2,1,0:T(8,128)}), f32[32,10,104]{2,1,0:T(8,128)S(1)}, u32[]{:S(2)}, u32[]{:S(2)}) %all-to-all-start.1) | async-done | bytes 133152 | tf_op jit(solution)/shard_map/all_to_all | solution.py:82
  55.4 1.2 %copy.128 = f32[10,2,60,1]{3,2,1,0:T(8,128)} copy(f32[10,2,60,1]{2,1,0,3:T(2,128)S(1)} %slice-done.4) | data formatting | bytes 9600
  56.6 1.2 %copy.129 = f32[10,2,60,1]{3,2,1,0:T(8,128)} copy(f32[10,2,60,1]{2,1,0,3:T(2,128)S(1)} %slice-done.5) | data formatting | bytes 9600
  57.8 2.7 %broadcast_multiply_fusion.1 = (f32[10,2,60,91]{3,2,1,0:T(8,128)}, f32[10,2,60,91]{3,2,1,0:T(8,128)S(1)}) fusion(f32[10,2,60,92]{3,2,1,0:T(8,128)S(1)} %subtract_clamp_fusion.1, f32[10,2,60,1]{3,2,1,0:T(8,128)} %copy.129, f32[10,2,60,90]{3,2,1,0:T(8,128)S(1)} %get-tuple-element.23, f32[10,2,60,1]{3,2,1,0:T(8,128)} %copy.128), kind=kLoop, calls=%fused_computation.59 | loop fusion | flops 764400 | bytes 2188800 | tf_op jit(solution)/shard_map/mul | solution.py:40
  60.6 0.7 slice-done.2
  61.4 2.8 %copy.113 = f32[10,2,2,60,2]{4,3,2,1,0:T(8,128)} copy(f32[10,2,2,60,2]{0,4,3,2,1:T(2,128)S(1)} %bitcast.34) | data formatting | bytes 38400 | tf_op jit(solution)/shard_map/concatenate | solution.py:114
  64.4 2.8 %copy.116 = f32[10,2,2,60,2]{4,3,2,1,0:T(8,128)} copy(f32[10,2,2,60,2]{0,4,3,2,1:T(2,128)S(1)} %bitcast.35) | data formatting | bytes 38400 | tf_op jit(solution)/shard_map/concatenate | solution.py:114
  67.4 0.9 %copy-done.5 = f32[10,2,60,90]{3,2,1,0:T(8,128)S(1)} copy-done((f32[10,2,60,90]{3,2,1,0:T(8,128)S(1)}, f32[10,2,60,90]{3,2,1,0:T(8,128)}, u32[]{:S(2)}) %copy-start.5) | copy-done | bytes 432024
  68.3 1.1 %broadcast_multiply_fusion = (f32[10,2,61,90]{3,2,1,0:T(8,128)}, f32[10,2,61,90]{3,2,1,0:T(8,128)S(1)}) fusion(f32[10,2,62,90]{3,2,1,0:T(8,128)S(1)} %subtract_clamp_fusion, f32[10,2,1,90]{3,2,1,0:T(1,128)S(1)} %slice-done.7, f32[10,2,60,90]{3,2,1,0:T(8,128)S(1)} %copy-done.5, f32[10,2,1,90]{3,2,1,0:T(1,128)S(1)} %bitcast.37), kind=kLoop, calls=%fused_computation.58 | loop fusion | flops 768600 | bytes 2203200 | tf_op jit(solution)/shard_map/mul | solution.py:40
  69.4 0.9 %abs_multiply_fusion = f32[10,2,61,90]{3,2,1,0:T(8,128)} fusion(f32[10,2,61,90]{3,2,1,0:T(8,128)S(1)} %get-tuple-element.21), kind=kLoop, calls=%fused_computation.35 | loop fusion | flops 219600 | bytes 878400 | tf_op jit(solution)/shard_map/mul | solution.py:40
  70.9 4.7 %multiply_add_fusion.1 = f32[10,2,2,60,91]{4,3,2,1,0:T(8,128)S(1)} fusion(f32[10,2,2,60,90]{4,3,2,1,0:T(8,128)S(1)} %reshape_reshape.3, f32[10,2,2,60,2]{4,3,2,1,0:T(8,128)} %copy.113, f32[10,2,2,60,2]{4,3,2,1,0:T(8,128)} %copy.116, f32[10,2,60,91]{3,2,1,0:T(8,128)S(1)} %abs_multiply_fusion.1, f32[10,2,60,91]{3,2,1,0:T(8,128)S(1)} %copy-done.4), kind=kLoop, calls=%fused_computation.15 | loop fusion | flops 3494400 | bytes 2649600 | tf_op jit(solution)/shard_map/add | solution.py:40
  75.7 1.0 %multiply_add_fusion = f32[10,2,2,61,90]{4,3,2,1,0:T(8,128)S(1)} fusion(f32[10,2,2,60,90]{4,3,2,1,0:T(8,128)S(1)} %reshape_reshape.3, f32[10,2,2,2,90]{4,3,2,1,0:T(2,128)S(1)} %concatenate.99, f32[10,2,2,2,90]{4,3,2,1,0:T(2,128)S(1)} %bitcast.36, f32[10,2,61,90]{3,2,1,0:T(8,128)S(1)} %copy-done.6, f32[10,2,61,90]{3,2,1,0:T(8,128)S(1)} %copy-done.7), kind=kLoop, calls=%fused_computation.14 | loop fusion | flops 3513600 | bytes 2678400 | tf_op jit(solution)/shard_map/add | solution.py:40
  76.7 0.7 fusion.2
  78.4 1.2 %reshape.150 = f32[10,4,5400]{2,1,0:T(4,128)S(1)} reshape(f32[10,2,2,60,90]{4,3,2,1,0:T(8,128)S(1)} %pad_maximum_fusion.4) | data formatting | bytes 1728000 | tf_op jit(solution)/shard_map/reshape | solution.py:127
  79.6 1.2 %broadcast_select_fusion = f32[10,4,5400]{2,1,0:T(4,128)} fusion(f32[10,4,5400]{2,1,0:T(4,128)S(1)} %reshape.150, pred[10]{0:T(512)(128)(4,1)S(1)} %copy-done.25), kind=kLoop, calls=%fused_computation.52 | loop fusion | flops 216000 | bytes 1728010 | tf_op jit(solution)/shard_map/jit(_where)/select_n | solution.py:128
  (143 shorter events, 12.3 us)
Async XLA Ops:
  3.4 2.0 %copy-start.11 = (f32[10,4,5400]{2,1,0:T(4,128)S(1)}, f32[10,4,5400]{2,1,0:T(4,128)}, u32[]{:S(2)}) copy-start(f32[10,4,5400]{2,1,0:T(4,128)} %param.8) | copy-start | bytes 2592004
  7.6 1.0 %copy-start.8 = (f32[10,5400]{1,0:T(8,128)S(1)}, f32[10,5400]{1,0:T(8,128)}, u32[]{:S(2)}) copy-start(f32[10,5400]{1,0:T(8,128)} %param.10) | copy-start | bytes 648004
  10.1 3.5 %copy-start = (f32[10,4,60,2]{3,2,1,0:T(8,128)S(1)}, f32[10,4,60,2]{3,2,1,0:T(8,128)}, u32[]{:S(2)}) copy-start(f32[10,4,60,2]{3,2,1,0:T(8,128)} %get-tuple-element.25) | copy-start | bytes 57604
  16.4 9.0 %copy-start.21 = (s32[160]{0:T(256)S(1)}, s32[160]{0:T(256)}, u32[]{:S(2)}) copy-start(s32[160]{0:T(256)} %param.11) | copy-start | bytes 1924
  16.6 9.0 %copy-start.22 = (s32[160,4]{0,1:T(4,128)S(1)}, s32[160,4]{0,1:T(4,128)}, u32[]{:S(2)}) copy-start(s32[160,4]{0,1:T(4,128)} %param.12) | copy-start | bytes 7684
  16.6 9.0 %copy-start.23 = (s32[160]{0:T(256)S(1)}, s32[160]{0:T(256)}, u32[]{:S(2)}) copy-start(s32[160]{0:T(256)} %param.13) | copy-start | bytes 1924
  17.6 17.9 %all-to-all-start = ((f32[32,10,104]{2,1,0:T(8,128)}), f32[32,10,104]{2,1,0:T(8,128)S(1)}, u32[]{:S(2)}, u32[]{:S(2)}) async-start(f32[32,10,104]{2,1,0:T(8,128)} %copy.109), calls=%async_computation | async-start | bytes 524288 | tf_op jit(solution)/shard_map/all_to_all | solution.py:73
  24.9 2.3 %copy-start.12 = (f32[10,5400]{1,0:T(8,128)S(1)}, f32[10,5400]{1,0:T(8,128)}, u32[]{:S(2)}) copy-start(f32[10,5400]{1,0:T(8,128)} %param.9) | copy-start | bytes 648004
  35.6 6.4 %copy-start.1 = (f32[10,4,5400]{2,1,0:T(4,128)S(1)}, f32[10,4,5400]{2,1,0:T(4,128)}, u32[]{:S(2)}) copy-start(f32[10,4,5400]{2,1,0:T(4,128)} %param.7) | copy-start | bytes 2592004
  39.1 13.2 %all-to-all-start.1 = ((f32[32,10,104]{2,1,0:T(8,128)}), f32[32,10,104]{2,1,0:T(8,128)S(1)}, u32[]{:S(2)}, u32[]{:S(2)}) async-start(f32[32,10,104]{2,1,0:T(8,128)} %reshape.139), calls=%async_computation.1 | async-start | bytes 524288 | tf_op jit(solution)/shard_map/all_to_all | solution.py:82
  52.7 1.0 %copy-start.15 = (f32[10,672]{1,0:T(8,128)}, f32[10,672]{1,0:T(8,128)S(1)}, u32[]{:S(2)}) copy-start(f32[10,672]{1,0:T(8,128)S(1)} %reshape.140) | copy-start | bytes 80644
  52.8 1.1 %copy-start.24 = (f32[3]{0:T(128)S(1)}, f32[3]{0:T(128)}, u32[]{:S(2)}) copy-start(f32[3]{0:T(128)} %constant.50.clone.1) | copy-start | bytes 40
  53.1 1.3 %copy-start.16 = (f32[10,672]{1,0:T(8,128)}, f32[10,672]{1,0:T(8,128)S(1)}, u32[]{:S(2)}) copy-start(f32[10,672]{1,0:T(8,128)S(1)} %reshape.141) | copy-start | bytes 80644
  53.2 1.1 %copy-start.18 = (f32[10,3,60,1]{2,1,0,3:T(4,128)}, f32[10,3,60,1]{2,1,0,3:T(4,128)S(1)}, u32[]{:S(2)}) copy-start(f32[10,3,60,1]{2,1,0,3:T(4,128)S(1)} %reshape.143) | copy-start | bytes 21604
  53.7 1.5 %copy-start.13 = (f32[10,992]{1,0:T(8,128)}, f32[10,992]{1,0:T(8,128)S(1)}, u32[]{:S(2)}) copy-start(f32[10,992]{1,0:T(8,128)S(1)} %reshape.145) | copy-start | bytes 119044
  54.1 1.2 %copy-start.20 = (f32[10,3,1,90]{3,2,1,0:T(1,128)}, f32[10,3,1,90]{3,2,1,0:T(1,128)S(1)}, u32[]{:S(2)}) copy-start(f32[10,3,1,90]{3,2,1,0:T(1,128)S(1)} %broadcast_select_fusion.2) | copy-start | bytes 32404
  54.3 1.0 %copy-start.14 = (f32[10,992]{1,0:T(8,128)}, f32[10,992]{1,0:T(8,128)S(1)}, u32[]{:S(2)}) copy-start(f32[10,992]{1,0:T(8,128)S(1)} %reshape.144) | copy-start | bytes 119044
  55.0 1.7 %slice-start.5 = ((f32[10,3,60,1]{2,1,0,3:T(4,128)}), f32[10,2,60,1]{2,1,0,3:T(2,128)S(1)}, s32[]{:S(2)}) async-start(f32[10,3,60,1]{2,1,0,3:T(4,128)} %copy-done.18), calls=%async_computation.7 | async-start | bytes 20480 | tf_op jit(solution)/shard_map/slice | solution.py:103
  60.5 3.7 %slice-start.3 = ((f32[10,672]{1,0:T(8,128)}), f32[10,480]{1,0:T(8,128)S(1)}, s32[]{:S(2)}) async-start(f32[10,672]{1,0:T(8,128)} %copy-done.16), calls=%async_computation.5 | async-start | bytes 65536 | tf_op jit(solution)/shard_map/slice | solution.py:89
  64.4 3.0 %slice-start.6 = ((f32[10,3,1,90]{3,1,0,2:T(4,128)}), f32[10,2,1,90]{3,1,0,2:T(2,128)S(1)}, s32[]{:S(2)}) async-start(f32[10,3,1,90]{3,1,0,2:T(4,128)} %copy-done.19), calls=%async_computation.8 | async-start | bytes 20480 | tf_op jit(solution)/shard_map/slice | solution.py:104
  64.4 3.0 %slice-start.7 = ((f32[10,3,1,90]{3,2,1,0:T(1,128)}), f32[10,2,1,90]{3,2,1,0:T(1,128)S(1)}, s32[]{:S(2)}) async-start(f32[10,3,1,90]{3,2,1,0:T(1,128)} %copy-done.20), calls=%async_computation.9 | async-start | bytes 20480 | tf_op jit(solution)/shard_map/slice | solution.py:104
  67.2 1.1 %copy-start.5 = (f32[10,2,60,90]{3,2,1,0:T(8,128)S(1)}, f32[10,2,60,90]{3,2,1,0:T(8,128)}, u32[]{:S(2)}) copy-start(f32[10,2,60,90]{3,2,1,0:T(8,128)} %get-tuple-element.22) | copy-start | bytes 1296004
  69.4 0.9 %slice-start = ((f32[10,992]{1,0:T(8,128)}), f32[10,720]{1,0:T(8,128)S(1)}, s32[]{:S(2)}) async-start(f32[10,992]{1,0:T(8,128)} %copy-done.13), calls=%async_computation.2 | async-start | bytes 98304 | tf_op jit(solution)/shard_map/slice | solution.py:92
  69.4 1.4 %slice-start.1 = ((f32[10,992]{1,0:T(8,128)}), f32[10,720]{1,0:T(8,128)S(1)}, s32[]{:S(2)}) async-start(f32[10,992]{1,0:T(8,128)} %copy-done.14), calls=%async_computation.3 | async-start | bytes 98304 | tf_op jit(solution)/shard_map/slice | solution.py:92
  69.4 1.5 %copy-start.4 = (f32[10,2,60,91]{3,2,1,0:T(8,128)S(1)}, f32[10,2,60,91]{3,2,1,0:T(8,128)}, u32[]{:S(2)}) copy-start(f32[10,2,60,91]{3,2,1,0:T(8,128)} %get-tuple-element.18) | copy-start | bytes 1310404
  70.9 4.7 %copy-start.6 = (f32[10,2,61,90]{3,2,1,0:T(8,128)S(1)}, f32[10,2,61,90]{3,2,1,0:T(8,128)}, u32[]{:S(2)}) copy-start(f32[10,2,61,90]{3,2,1,0:T(8,128)} %abs_multiply_fusion) | copy-start | bytes 1317604
  70.9 4.7 %copy-start.7 = (f32[10,2,61,90]{3,2,1,0:T(8,128)S(1)}, f32[10,2,61,90]{3,2,1,0:T(8,128)}, u32[]{:S(2)}) copy-start(f32[10,2,61,90]{3,2,1,0:T(8,128)} %get-tuple-element.20) | copy-start | bytes 1317604
  75.6 1.1 %copy-start.3 = (f32[10,2,60,90]{3,2,0,1:T(8,128)S(1)}, f32[10,2,60,90]{3,2,0,1:T(8,128)}, u32[]{:S(2)}) copy-start(f32[10,2,60,90]{3,2,0,1:T(8,128)} %get-tuple-element.28) | copy-start | bytes 1296004
  76.7 1.0 %copy-start.2 = (f32[10,1,60,90]{3,2,0,1:T(8,128)S(1)}, f32[10,1,60,90]{3,2,0,1:T(8,128)}, u32[]{:S(2)}) copy-start(f32[10,1,60,90]{3,2,0,1:T(8,128)} %get-tuple-element.17) | copy-start | bytes 648004
  76.7 1.1 %copy-start.9 = (f32[10,60,90]{2,1,0:T(8,128)S(1)}, f32[10,60,90]{2,1,0:T(8,128)}, u32[]{:S(2)}) copy-start(f32[10,60,90]{2,1,0:T(8,128)} %get-tuple-element.16) | copy-start | bytes 648004
  76.7 1.2 %copy-start.10 = (f32[10,60,90]{2,1,0:T(8,128)S(1)}, f32[10,60,90]{2,1,0:T(8,128)}, u32[]{:S(2)}) copy-start(f32[10,60,90]{2,1,0:T(8,128)} %get-tuple-element.31) | copy-start | bytes 648004
  78.3 1.2 %copy-start.25 = (pred[10]{0:T(512)(128)(4,1)S(1)}, pred[10]{0:T(512)(128)(4,1)}, u32[]{:S(2)}) copy-start(pred[10]{0:T(512)(128)(4,1)} %dynamic_slice.6) | copy-start | bytes 34
  (4 other events, 3.3 us)

commit v3 on v1

v3 whole, which is shorter than its diff:
```python
import functools

import jax
import jax.numpy as jnp
import numpy as np
from jax import lax
from jax.experimental import pallas as pl
from jax.experimental.pallas import tpu as pltpu
from jax.sharding import PartitionSpec as P

IB = 90
JB = 60
CELLS = IB * JB
COURANT = 0.2
LANES = 128
TILES = -(-CELLS // LANES)
WIDE = TILES * LANES
GAPS = JB + 1
HALF = IB // 2
ROWS = 16
PARTS = 32
X_PART = 22
SPARE = 48
PIECE = 16
SCALE = COURANT / 12.0
SIDES = 3


def lane_of(rows):
    return lax.broadcasted_iota(jnp.int32, (rows, LANES), 1)


def rot(value, shift):
    shift = shift % LANES
    return value if shift == 0 else pltpu.roll(value, shift, 1)


def window(get, start, rows):
    tile, offset = start // LANES, start % LANES
    head = rot(get(tile), -offset)
    if offset == 0 or tile + 1 >= TILES:
        return head
    return jnp.where(lane_of(rows) < LANES - offset, head, rot(get(tile + 1), -offset))


def gap_groups(get, first, wide, rows):
    lane = lane_of(rows)
    held = LANES // wide
    result = []
    for at in range(0, GAPS, held):
        value = jnp.zeros((rows, LANES), jnp.float32)
        for gap in range(at, min(at + held, GAPS)):
            start = IB * gap + first
            place = (gap - at) * wide
            for tile in range(max(start, 0) // LANES, min(start + wide - 1, CELLS - 1) // LANES + 1):
                low = max(start, tile * LANES, 0)
                value = jnp.where(lane >= place + low - start, rot(get(tile), place - start + tile * LANES), value)
        result.append(value)
    return result


def lane_pick(pair, index, rows):
    low = jnp.take_along_axis(pair[0], index % LANES, axis=1, mode="promise_in_bounds")
    high = jnp.take_along_axis(pair[1], index % LANES, axis=1, mode="promise_in_bounds")
    return jnp.where(index < LANES, low, high)


def both_slots(target, source):
    target[0:4, 0:CELLS] = source[0]
    target[4:8, 0:CELLS] = source[1]
    target[:, CELLS:] = jnp.zeros((8, WIDE - CELLS), jnp.float32)


def tile_getter(ref):
    return lambda tile: ref[:, tile * LANES : (tile + 1) * LANES]


def depth_getter(ref):
    rows = ref.shape[0]

    def get(tile):
        if tile + 1 < TILES:
            return ref[:, tile * LANES : (tile + 1) * LANES]
        rest = jnp.zeros((rows, WIDE - CELLS), jnp.float32)
        return jnp.concatenate([ref[:, tile * LANES : CELLS], rest], axis=1)

    return get


def joined(south, north, half, rows):
    if half == 0:
        return jnp.where(lane_of(rows) < 64, south, rot(north, 64))
    return jnp.where(lane_of(rows) < 64, rot(south, -HALF), rot(north, 64 - HALF))


def pack_kernel(tracer_ref, velocity_ref, depth_ref, out_ref, x_ref, v_ref, strip_ref):
    step = pl.program_id(0)
    count = depth_ref.shape[0]
    both_slots(x_ref, tracer_ref)
    both_slots(v_ref, velocity_ref)
    get_x, get_v = tile_getter(x_ref), tile_getter(v_ref)
    lane = lane_of(8)
    groups = gap_groups(get_x, -2, 4, 8)
    near = lane_pick(groups, 4 * (lane // 2) + 1 + lane % 2, 8)
    far = lane_pick(groups, 4 * (lane // 2) + 3 * (lane % 2), 8)
    south = [window(get_x, 0, 8), window(get_x, IB, 8)]
    north = [window(get_x, CELLS - IB, 8), window(get_x, CELLS - 2 * IB, 8)]
    v_south, v_north = window(get_v, 0, 8), window(get_v, CELLS - IB, 8)
    strips = [joined(south[0], north[0], half, 8) for half in range(2)]
    strips += [joined(south[1], north[1], half, 8) for half in range(2)]
    strips += [joined(v_south, v_north, half, 8) for half in range(2)]
    strips += [near, far, gap_groups(get_v, -1, 2, 8)[0]]
    own = pl.ds(pl.multiple_of(8 * step, 8), 8)
    for index, strip in enumerate(strips):
        strip_ref[index, own, :] = strip

    @pl.when(step == pl.num_programs(0) - 1)
    def _():
        out_ref[...] = jnp.zeros(out_ref.shape, jnp.float32)
        slots = pl.ds(0, count)
        slot_lane = lane_of(count)
        get_d = depth_getter(depth_ref)
        d_south, d_north = window(get_d, 0, count), window(get_d, CELLS - IB, count)
        d_gaps = gap_groups(get_d, -1, 2, count)[0]
        spare = (slot_lane >= SPARE) & (slot_lane < SPARE + PIECE)
        for chan in range(4):
            rows = pl.ds(chan, count, stride=4)
            for half in range(2):
                for deep in range(2):
                    part = 2 * (4 * deep + chan) + half
                    value = strip_ref[2 * deep + half, rows, :]
                    if part < 8:
                        value = jnp.where(spare, rot(d_gaps, SPARE - PIECE * part), value)
                    out_ref[part, slots, :] = value
                if chan >= 2:
                    out_ref[2 * (8 + chan - 2) + half, slots, :] = strip_ref[4 + half, rows, :]
            out_ref[X_PART + chan, slots, :] = strip_ref[6, rows, :]
            out_ref[X_PART + 4 + chan, slots, :] = strip_ref[7, rows, :]
            if chan < 2:
                out_ref[X_PART + 8 + chan, slots, :] = strip_ref[8, rows, :]
        for half in range(2):
            out_ref[20 + half, slots, :] = joined(d_south, d_north, half, count)


def route_kernel(part_ref, code_ref, held_ref, out_ref):
    total = held_ref.shape[0]
    rows = out_ref.shape[0]
    part = part_ref[0]
    picked = [jnp.zeros((rows, 2 * LANES), jnp.float32) for _ in range(5)]
    for start in range(0, total, rows):
        held = held_ref[start : start + rows, :]
        high = held.astype(jnp.bfloat16)
        low = (held - high.astype(jnp.float32)).astype(jnp.bfloat16)
        halves = jnp.concatenate([high, low], axis=1)
        source = lax.broadcasted_iota(jnp.int32, (rows, rows), 1) + start
        for side in range(5):
            one_hot = jnp.where(code_ref[:, side : side + 1] == source, 1.0, 0.0).astype(jnp.bfloat16)
            picked[side] += jnp.dot(one_hot, halves, preferred_element_type=jnp.float32)
    west, east, south, north, fold = [value[:, :LANES] + value[:, LANES:] for value in picked]
    lane = lane_of(rows)
    along_x = (part >= X_PART) | ((part < 8) & (lane >= SPARE) & (lane < SPARE + PIECE))
    x_side = jnp.where(lane % 2 == 0, west, east)
    y_side = jnp.where(lane < 64, north + rot(fold, 64), south)
    out_ref[...] = jnp.where(along_x, x_side, y_side)


def bulk_kernel(tracer_ref, velocity_ref, depth_ref, kappa_ref, column_ref, base_ref, edge_ref,
                x_ref, v_ref, d_ref, k_ref, w_ref, z_ref, strip_ref):
    step = pl.program_id(0)
    count = depth_ref.shape[0]
    both_slots(x_ref, tracer_ref)
    both_slots(v_ref, velocity_ref)
    for target, source in ((d_ref, depth_ref), (k_ref, kappa_ref)):
        for slot in range(2):
            row = source[pl.ds(2 * step + slot, 1), :]
            target[4 * slot : 4 * slot + 4, 0:CELLS] = jnp.broadcast_to(row, (4, CELLS))
        target[:, CELLS:] = jnp.zeros((8, WIDE - CELLS), jnp.float32)
    row = lax.broadcasted_iota(jnp.int32, (8, WIDE), 0)
    x_row, level = row % 4 < 2, row % 2
    column = column_ref[...]
    first, last = column == 0.0, column == IB - 1.0

    def lanes(value, shift):
        return pltpu.roll(value, shift % WIDE, 1)

    def sublanes(value, shift):
        return pltpu.roll(value, shift % 8, 0)

    depth = d_ref[...]
    top = jnp.clip(depth, 0.0, 1.0)
    low = jnp.clip(depth - 1.0, 0.0, 1.0)
    wet = jnp.where(level == 0, top, low)
    coupling = k_ref[...] * top * low
    ratio = coupling / (1.0 + 2.0 * coupling)
    velocity = v_ref[...]
    next_vel = jnp.where(x_row, lanes(velocity, -1), lanes(velocity, -IB))
    next_wet = jnp.where(x_row, jnp.where(last, 0.0, lanes(wet, -1)), lanes(wet, -IB))
    face = SCALE * (velocity + next_vel) * (wet * next_wet)
    w_ref[...] = face
    z_ref[...] = jnp.where(x_row, face, jnp.where(level == 0, ratio, depth))
    face_x = jnp.where(x_row, face, sublanes(face, 2))
    face_y = jnp.where(x_row, sublanes(face, -2), face)

    state = x_ref[...]

    def divergence(speed, distance, before, after):
        mine = 5.0 * state
        upper = lanes(mine - after, -distance)
        flux = jnp.maximum(speed, 0.0) * (mine - before + 2.0 * after)
        flux += jnp.minimum(speed, 0.0) * (2.0 * state + upper)
        return flux - lanes(flux, distance)

    change = divergence(face_x, 1, jnp.where(first, 0.0, lanes(state, 1)), jnp.where(last, 0.0, lanes(state, -1)))
    change += divergence(face_y, IB, lanes(state, IB), lanes(state, -IB))
    explicit = state - wet * change
    other = jnp.where(level == 0, sublanes(explicit, -1), sublanes(explicit, 1))
    base_ref[...] = explicit + ratio * (other - explicit)

    get_w, get_z = tile_getter(w_ref), tile_getter(z_ref)
    lane = lane_of(8)
    groups = gap_groups(get_z, -2, 4, 8)
    strips = [
        lane_pick(groups, 4 * (lane // 2) + 2 * (lane % 2), 8),
        lane_pick(groups, 4 * (lane // 2) + 1 + lane % 2, 8),
        lane_pick(groups, 4 * (lane // 2) + 3 * (lane % 2), 8),
        window(get_w, 0, 8),
        window(get_z, 0, 8),
        window(get_z, IB, 8),
        window(get_w, CELLS - 2 * IB, 8),
        window(get_z, CELLS - IB, 8),
        window(get_z, CELLS - 2 * IB, 8),
    ]
    own = pl.ds(pl.multiple_of(8 * step, 8), 8)
    for index, strip in enumerate(strips):
        strip_ref[index, own, :] = strip

    @pl.when(step == pl.num_programs(0) - 1)
    def _():
        edge_ref[...] = jnp.zeros(edge_ref.shape, jnp.float32)
        east_lane = lane_of(count) % 2 == 0
        slots = pl.ds(0, count)
        for side in range(SIDES):
            for k in range(2):
                speed = strip_ref[3 * side, pl.ds(k if side == 0 else 2 + k, count, stride=4), :]
                if side == 0:
                    speed = jnp.where(east_lane, -speed, speed)
                elif side == 2:
                    speed = -speed
                edge_ref[5 * side + k, slots, :] = jnp.maximum(speed, 0.0)
            edge_ref[5 * side + 2, slots, :] = strip_ref[3 * side + 1, pl.ds(2, count, stride=4), :]
            edge_ref[5 * side + 3, slots, :] = strip_ref[3 * side + 2, pl.ds(2, count, stride=4), :]
            edge_ref[5 * side + 4, slots, :] = strip_ref[3 * side + 2, pl.ds(3, count, stride=4), :]


def finish_kernel(live_ref, own_ref, halo_ref, fold_ref, edge_ref, base_ref, out_ref, delta_ref):
    step = pl.program_id(0)

    @pl.when(step == 0)
    def _():
        lane = lane_of(ROWS)
        folded = fold_ref[...] > 0.0
        mirror = jnp.where(lane < IB, IB - 1 - lane, lane)

        def lower(ref, value):
            return jnp.where(lane < HALF, ref[2 * value], rot(ref[2 * value + 1], HALF))

        def upper(ref, value):
            return jnp.where(lane < HALF, rot(ref[2 * value], 64), rot(ref[2 * value + 1], 64 + HALF))

        def across(ref, value):
            if value < 10:
                return ref[X_PART + value]
            whole = rot(ref[0], -SPARE)
            for part in range(1, 8):
                whole = jnp.where(lane >= PIECE * part, rot(ref[part], PIECE * part - SPARE), whole)
            return whole

        def x_halo(value):
            raw = across(halo_ref, value)
            return jnp.where(lane % 2 == 0, rot(raw, 1), rot(raw, -1))

        def north_halo(value):
            raw = lower(halo_ref, value)
            turned = jnp.take_along_axis(raw, mirror, axis=1, mode="promise_in_bounds")
            return jnp.where(folded, -turned if value in (8, 9) else turned, raw)

        readers = [
            (functools.partial(across, own_ref), x_halo),
            (functools.partial(lower, own_ref), functools.partial(upper, halo_ref)),
            (functools.partial(upper, own_ref), north_halo),
        ]
        for side, (mine, theirs) in enumerate(readers):
            near_depth, out_depth = mine(10), theirs(10)
            next_depth = edge_ref[5 * side + 4]
            ratio = [edge_ref[5 * side + 2], edge_ref[5 * side + 3]]
            change = {}
            for k in range(2):
                wet = [jnp.clip(depth - k, 0.0, 1.0) for depth in (out_depth, near_depth, next_depth)]
                speed = SCALE * (mine(8 + k) + theirs(8 + k)) * wet[0] * wet[1]
                if side == 0:
                    speed = jnp.where(lane % 2 == 0, -speed, speed)
                elif side == 2:
                    speed = -speed
                inward, outward = jnp.maximum(speed, 0.0), jnp.minimum(speed, 0.0)
                inner_speed = edge_ref[5 * side + k]
                for tracer in range(2):
                    chan = 2 * tracer + k
                    near, deep = mine(chan), mine(4 + chan)
                    out_near, out_far = theirs(chan), theirs(4 + chan)
                    flux = inward * (5.0 * out_near + 2.0 * near - out_far)
                    flux += outward * (2.0 * out_near + 5.0 * near - deep)
                    inner_flux = inner_speed * out_near
                    change[0, tracer, k] = wet[1] * (flux + inner_flux)
                    change[1, tracer, k] = -wet[2] * inner_flux
            for place in range(2):
                for tracer in range(2):
                    for k in range(2):
                        self, other = change[place, tracer, k], change[place, tracer, 1 - k]
                        rows = pl.ds(ROWS * (2 * tracer + k), ROWS)
                        delta_ref[2 * side + place, rows, :] = self + ratio[place] * (other - self)

    lane = lane_of(8)

    def slots_of(index):
        pair = [delta_ref[index, pl.ds(2 * step + slot, 4, stride=ROWS), :] for slot in range(2)]
        return jnp.concatenate(pair, axis=0)

    near, deep = slots_of(0), slots_of(1)
    groups = []
    for at in range(2):
        index = 2 * (lane // 4) + (lane % 4) // 2 + 64 * at
        outer = jnp.take_along_axis(near, index, axis=1, mode="promise_in_bounds")
        inner = jnp.take_along_axis(deep, index, axis=1, mode="promise_in_bounds")
        groups.append(jnp.where((lane % 4 == 1) | (lane % 4 == 2), outer, inner))
    placed = [(groups[gap // 32], 4 * (gap % 32), IB * gap - 2, 4) for gap in range(GAPS)]
    placed += [(slots_of(2), 0, 0, IB), (slots_of(3), 0, IB, IB)]
    placed += [(slots_of(4), 0, CELLS - IB, IB), (slots_of(5), 0, CELLS - 2 * IB, IB)]
    live = [live_ref[2 * step + slot] > 0 for slot in range(2)]
    for tile in range(TILES):
        at = tile * LANES
        value = base_ref[:, at : at + LANES]
        for source, origin, start, wide in placed:
            low, high = max(start, at, 0), min(start + wide, at + LANES, CELLS)
            if low < high:
                inside = (lane >= low - at) & (lane < high - at)
                value += jnp.where(inside, rot(source, start - at - origin), 0.0)
        stop = min(at + LANES, CELLS)
        for slot in range(2):
            out_ref[slot, :, at:stop] = jnp.where(live[slot], value[4 * slot : 4 * slot + 4, : stop - at], 0.0)


def route_codes(block_owner, neighbours, fold_partner, slot_count, device_count):
    total = device_count * ROWS
    block_count = block_owner.shape[0]
    row = block_owner // slot_count * ROWS + block_owner % slot_count
    hits = row[None, :] == jnp.arange(total, dtype=jnp.int32)[:, None]
    live = jnp.any(hits, axis=1)
    links = jnp.concatenate([neighbours, fold_partner[:, None]], axis=1)
    linked = links[:, :, None] == jnp.arange(block_count, dtype=jnp.int32)[None, None, :]
    link_rows = jnp.max(jnp.where(linked, row[None, None, :], -1), axis=2)
    codes = jnp.max(jnp.where(hits[:, :, None], link_rows[None], -1), axis=1)
    return codes, live


def per_device(tracers, velocity, kappa, kmt, block_owner, neighbours, fold_partner):
    slot_count, chans = tracers.shape[:2]
    sub_count = lax.axis_size("sub")
    device_count = lax.axis_size("blk") * sub_count
    if device_count < PARTS or chans != 4 or slot_count % 2 or slot_count > ROWS:
        raise ValueError("unsupported sizes")
    my_index = lax.axis_index("blk") * sub_count + lax.axis_index("sub")
    axes = ("blk", "sub")
    pairs = slot_count // 2
    f32 = jnp.float32
    limit = pltpu.CompilerParams(vmem_limit_bytes=40 * 1024 * 1024)

    def whole(shape):
        return pl.BlockSpec(shape, lambda *_: (0,) * len(shape))

    two_slots = pl.BlockSpec((2, 4, CELLS), lambda step: (step, 0, 0))
    by_slot = whole((slot_count, CELLS))
    wide = pltpu.VMEM((8, WIDE), f32)
    strips = pltpu.VMEM((9, 8 * pairs, LANES), f32)

    pack = pl.pallas_call(
        pack_kernel,
        grid=(pairs,),
        out_shape=jax.ShapeDtypeStruct((device_count, ROWS, LANES), f32),
        in_specs=[two_slots, two_slots, by_slot],
        out_specs=whole((device_count, ROWS, LANES)),
        scratch_shapes=[wide, wide, strips],
        compiler_params=limit,
        cost_estimate=pl.CostEstimate(flops=4_000_000, bytes_accessed=2_400_000, transcendentals=0),
    )(tracers, velocity, kmt)

    held = lax.all_to_all(pack, axes, 0, 0, tiled=True).reshape(device_count * ROWS, LANES)

    codes, live = route_codes(block_owner, neighbours, fold_partner, slot_count, device_count)
    my_rows = my_index * ROWS
    my_live = lax.dynamic_slice_in_dim(live, my_rows, ROWS, 0).astype(jnp.int32)
    my_fold = lax.dynamic_slice_in_dim(codes[:, 4:5], my_rows, ROWS, 0) >= 0
    my_fold = jnp.broadcast_to(my_fold.astype(f32), (ROWS, LANES))

    routed_rows = PARTS * ROWS
    routed = pl.pallas_call(
        route_kernel,
        grid=(device_count // PARTS,),
        out_shape=jax.ShapeDtypeStruct((device_count * ROWS, LANES), f32),
        in_specs=[
            pl.BlockSpec(memory_space=pltpu.SMEM),
            pl.BlockSpec((routed_rows, 5), lambda step: (step, 0)),
            whole((device_count * ROWS, LANES)),
        ],
        out_specs=pl.BlockSpec((routed_rows, LANES), lambda step: (step, 0)),
        compiler_params=limit,
    )(my_index.astype(jnp.int32).reshape(1), codes, held)

    halo = lax.all_to_all(routed.reshape(device_count, ROWS, LANES), axes, 0, 0, tiled=True)

    column = np.full((8, WIDE), IB - 1, np.float32)
    column[:, :CELLS] = np.arange(CELLS) % IB
    base, edges = pl.pallas_call(
        bulk_kernel,
        grid=(pairs,),
        out_shape=[
            jax.ShapeDtypeStruct((8 * pairs, WIDE), f32),
            jax.ShapeDtypeStruct((5 * SIDES, ROWS, LANES), f32),
        ],
        in_specs=[two_slots, two_slots, by_slot, by_slot, whole((8, WIDE))],
        out_specs=[pl.BlockSpec((8, WIDE), lambda step: (step, 0)), whole((5 * SIDES, ROWS, LANES))],
        scratch_shapes=[wide] * 6 + [strips],
        compiler_params=limit,
        cost_estimate=pl.CostEstimate(flops=22_000_000, bytes_accessed=4_000_000, transcendentals=0),
    )(tracers, velocity, kmt, kappa, jnp.asarray(column))

    return pl.pallas_call(
        finish_kernel,
        grid=(pairs,),
        out_shape=jax.ShapeDtypeStruct(tracers.shape, f32),
        in_specs=[
            pl.BlockSpec(memory_space=pltpu.SMEM),
            whole((PARTS, ROWS, LANES)),
            whole((PARTS, ROWS, LANES)),
            whole((ROWS, LANES)),
            whole((5 * SIDES, ROWS, LANES)),
            pl.BlockSpec((8, WIDE), lambda step: (step, 0)),
        ],
        out_specs=two_slots,
        scratch_shapes=[pltpu.VMEM((2 * SIDES, 4 * ROWS, LANES), f32)],
        compiler_params=limit,
    )(my_live, pack, halo, my_fold, edges, base)


def solution(mesh):
    placed = (
        P(("blk", "sub"), None, None),
        P(("blk", "sub"), None, None),
        P(("blk", "sub"), None),
        P(("blk", "sub"), None),
        P(),
        P(),
        P(),
    )
    return jax.shard_map(
        per_device,
        mesh=mesh,
        in_specs=placed,
        out_specs=P(("blk", "sub"), None, None),
        check_vma=False,
    )
```

time: 153 us -> 43.3 us (0.28)
  local copies, waits for them, and re-layouts: 63.5 us -> 5.13 us
  waiting for transfers between devices: 53.8 us -> 12.1 us
  other arithmetic: 20.5 us -> 2.18 us
  between operations: 14.1 us -> 0.14 us
  Pallas kernels: 0 us -> 13.5 us
  starting transfers between devices: 0.01 us -> 9.88 us
    all_gather x1 -> x0, waiting for transfers between devices: 53.8 us -> none  [per_device(): window = lax.all_gather(pack, ('blk', 'sub'), axis=0, tiled=True)]
    gather x10 -> x0, local copies, waits for them, and re-layouts: 16.5 us -> none  [the longest x5 14.3 us: strip(): jnp.take(window, jnp.maximum(code, 0), axis=0)[:, start:start + wide]]
    reshape x15 -> x0, local copies, waits for them, and re-layouts: 15.2 us -> none  [the longest x1 5.05 us: per_device(): window = window.reshape(device_count * slot_count, padded)]
    pallas_call x0 -> x4, Pallas kernels: none -> 13.5 us  [the longest x1 5.06 us: per_device(): pl.pallas_call(bulk_kernel, grid=(pairs,), out_shape=[jax.ShapeDtypeStruc...]
    all_to_all x0 -> x2, waiting for transfers between devices: none -> 12.1 us  [the longest x1 9.01 us: per_device(): lax.all_to_all(pack, axes, 0, 0, tiled=True)]
    slice x32 -> x1, local copies, waits for them, and re-layouts: 11.4 us -> 0.6 us  [per_device(): my_fold = lax.dynamic_slice_in_dim(codes[:, 4:5], my_rows, ROWS, 0) >= 0]
    all_to_all x0 -> x2, starting transfers between devices: none -> 9.88 us  [the longest x1 7.3 us: per_device(): lax.all_to_all(pack, axes, 0, 0, tiled=True)]
    concatenate x6 -> x0, local copies, waits for them, and re-layouts: 9.41 us -> none  [the longest x2 5.63 us: per_device(): jnp.concatenate([west_x, state, east_x], axis=3)]
  transfers between devices with their start and end apart: 1 -> 2, of which waited for: 1 -> 2; matrix products, arithmetic and copies ran while one was open for 7% -> 7% of each run, Pallas kernels for 0% -> 12%
where the time goes in v3:
time: 43.3 us; the launch traced here: 42.9 us
  Pallas kernels  13.5 us (31%)
  waiting for transfers between devices  12.1 us (28%)
  starting transfers between devices  9.88 us (23%)
  local copies, waits for them, and re-layouts  5.13 us (12%)
  other arithmetic  2.18 us (5%)
    all_to_all x1, waiting for transfers between devices, per_device(): lax.all_to_all(pack, axes, 0, 0, tiled=True)  9.01 us
    all_to_all x1, starting transfers between devices, per_device(): lax.all_to_all(pack, axes, 0, 0, tiled=True)  7.3 us
    pallas_call x1, Pallas kernels, per_device(): pl.pallas_call(bulk_kernel, grid=(pairs,), out_shape=[jax.ShapeDtypeStruc...  5.06 us
    unnamed x24, local copies, waits for them, and re-layouts  4.32 us
    pallas_call x1, Pallas kernels, per_device(): pl.pallas_call(finish_kernel, grid=(pairs,), out_shape=jax.ShapeDtypeStru...  4.26 us
    all_to_all x1, waiting for transfers between devices, per_device(): lax.all_to_all(routed.reshape(device_count, ROWS, LANES), axes, 0, 0, til...  3.09 us
    all_to_all x1, starting transfers between devices, per_device(): lax.all_to_all(routed.reshape(device_count, ROWS, LANES), axes, 0, 0, til...  2.59 us
    pallas_call x1, Pallas kernels, per_device(): pl.pallas_call(pack_kernel, grid=(pairs,), out_shape=jax.ShapeDtypeStruct...  2.5 us
  transfers between devices with their start and end apart: 2, of which 2 were waited for; matrix products, arithmetic and copies ran while one was open for 7% of the time, Pallas kernels for 12%

profile of v3, /device:TPU:0, one launch (start us, length us, event | category | flops | bytes accessed | tf_op | source)
XLA Modules:
  0.0 42.9 jit_solution(476070537260820411)
XLA Ops:
  0.0 1.2 %copy-done = f32[10,4,5400]{2,1,0:T(4,128)S(1)} copy-done((f32[10,4,5400]{2,1,0:T(4,128)S(1)}, f32[10,4,5400]{2,1,0:T(4,128)}, u32[]{:S(2)}) %copy-start) | copy-done | bytes 864024
  1.2 0.0 copy-start.2
  1.2 1.2 %copy-done.2 = f32[10,4,5400]{2,1,0:T(4,128)S(1)} copy-done((f32[10,4,5400]{2,1,0:T(4,128)S(1)}, f32[10,4,5400]{2,1,0:T(4,128)}, u32[]{:S(2)}) %copy-start.2) | copy-done | bytes 864024
  2.3 0.0 copy-start.4
  2.3 1.0 %copy-done.4 = f32[10,5400]{1,0:T(8,128)S(1)} copy-done((f32[10,5400]{1,0:T(8,128)S(1)}, f32[10,5400]{1,0:T(8,128)}, u32[]{:S(2)}) %copy-start.4) | copy-done | bytes 216024
  3.3 2.5 %shard_map.82.own_ref = f32[32,16,128]{2,1,0:T(8,128)} custom-call(f32[10,4,5400]{2,1,0:T(4,128)S(1)} %copy-done, f32[10,4,5400]{2,1,0:T(4,128)S(1)} %copy-done.2, f32[10,5400]{1,0:T(8,128)S(1)} %copy-done.4), custom_call_target="tpu_custom_call" | custom-call | flops 4000000 | bytes 2400000 | tf_op jit(solution)/shard_map/pallas_call | solution.py:385
  5.8 7.3 %all-to-all-start = ((f32[32,16,128]{2,1,0:T(8,128)}), f32[32,16,128]{2,1,0:T(8,128)S(1)}, u32[]{:S(2)}, u32[]{:S(2)}) async-start(f32[32,16,128]{2,1,0:T(8,128)} %shard_map.82.own_ref), calls=%async_computation | async-start | bytes 524288 | tf_op jit(solution)/shard_map/all_to_all | solution.py:396
  13.1 0.0 copy-done.9
  13.2 0.0 copy-done.8
  13.2 0.0 copy-done.10
  13.2 0.4 select_reduce_fusion.1
  13.6 0.0 copy-start.3
  13.6 0.7 %iota_compare_fusion.1 = (pred[512,160]{0,1:T(8,128)(4,1)S(1)}, pred[512]{0:T(512)(128)(4,1)}) fusion(s32[160]{0:T(256)S(1)} %fusion.1), kind=kLoop, calls=%fused_computation.3 | loop fusion | flops 163328 | bytes 83072 | tf_op jit(solution)/shard_map/eq | solution.py:356
  14.3 0.3 select_reduce_fusion
  14.6 0.1 copy.11.code_ref
  14.7 9.0 %all-to-all-done = f32[32,16,128]{2,1,0:T(8,128)S(1)} async-done(((f32[32,16,128]{2,1,0:T(8,128)}), f32[32,16,128]{2,1,0:T(8,128)S(1)}, u32[]{:S(2)}, u32[]{:S(2)}) %all-to-all-start) | async-done | bytes 262176 | tf_op jit(solution)/shard_map/all_to_all | solution.py:396
  23.7 1.7 %shard_map.83 = f32[512,128]{1,0:T(8,128)} custom-call(s32[1]{0:T(128)} %bitcast.part_ref, s32[512,5]{1,0:T(8,128)S(1)} %copy.11.code_ref, f32[512,128]{1,0:T(8,128)S(1)} %bitcast.6), custom_call_target="tpu_custom_call" | custom-call | tf_op jit(solution)/shard_map/pallas_call | solution.py:405
  25.4 2.6 %all-to-all-start.1 = ((f32[32,16,128]{2,1,0:T(8,128)}), f32[32,16,128]{2,1,0:T(8,128)S(1)}, u32[]{:S(2)}, u32[]{:S(2)}) async-start(f32[32,16,128]{2,1,0:T(8,128)} %bitcast.3), calls=%async_computation.1 | async-start | bytes 524288 | tf_op jit(solution)/shard_map/all_to_all | solution.py:418
  28.0 0.6 %slice.4 = s32[512,1]{0,1:T(1,128)} slice(s32[512,5]{0,1:T(8,128)S(1)} %select_reduce_fusion), slice={[0:512], [4:5]} | slice | bytes 4096 | tf_op jit(solution)/shard_map/slice | solution.py:401
  28.6 0.0 copy-done.5
  28.6 0.0 copy-done.7
  28.6 0.0 copy-done.3
  28.6 0.0 copy-done.1
  28.6 0.0 copy-start.6
  28.6 1.0 %copy-done.6 = f32[10,5400]{1,0:T(8,128)S(1)} copy-done((f32[10,5400]{1,0:T(8,128)S(1)}, f32[10,5400]{1,0:T(8,128)}, u32[]{:S(2)}) %copy-start.6) | copy-done | bytes 216024
  29.6 5.1 %shard_map.84 = (f32[40,5504]{1,0:T(8,128)S(1)}, f32[15,16,128]{2,1,0:T(8,128)S(1)}) custom-call(f32[10,4,5400]{2,1,0:T(4,128)S(1)} %copy-done.1, f32[10,4,5400]{2,1,0:T(4,128)S(1)} %copy-done.3, f32[10,5400]{1,0:T(8,128)S(1)} %copy-done.5, f32[10,5400]{1,0:T(8,128)S(1)} %copy-done.6, f32[8,5504]{1,0:T(8,128)S(1)} %copy-done.7), custom_call_target="tpu_custom_call" | custom-call | flops 22000000 | bytes 4000000 | tf_op jit(solution)/shard_map/pallas_call | solution.py:422
  34.7 0.0 copy-done.11
  34.7 0.1 dynamic-slice_convert_fusion.live_ref
  34.7 0.8 %fusion.2 = f32[16]{0:T(128)S(1)} fusion(s32[512,1]{0,1:T(1,128)} %slice.4, s32[]{:T(128)S(6)} %select_n.26), kind=kLoop, calls=%fused_computation.11 | loop fusion | flops 32 | bytes 132 | tf_op jit(solution)/shard_map/broadcast_in_dim | solution.py:402
  35.5 3.1 %all-to-all-done.1.halo_ref = f32[32,16,128]{2,1,0:T(8,128)S(1)} async-done(((f32[32,16,128]{2,1,0:T(8,128)}), f32[32,16,128]{2,1,0:T(8,128)S(1)}, u32[]{:S(2)}, u32[]{:S(2)}) %all-to-all-start.1) | async-done | bytes 262176 | tf_op jit(solution)/shard_map/all_to_all | solution.py:418
  38.6 0.1 broadcast_in_dim.60.fold_ref
  38.7 4.3 %shard_map.85 = f32[10,4,5400]{2,1,0:T(4,128)} custom-call(s32[16]{0:T(128)S(1)} %dynamic-slice_convert_fusion.live_ref, f32[32,16,128]{2,1,0:T(8,128)} %shard_map.82.own_ref, f32[32,16,128]{2,1,0:T(8,128)S(1)} %all-to-all-done.1.halo_ref, f32[16,128]{1,0:T(8,128)S(1)} %broadcast_in_dim.60.fold_ref, f32[15,16,128]{2,1,0:T(8,128)S(1)} %get-tuple-element.7.edge_ref, ...), custom_call_target="tpu_custom_call" | custom-call | tf_op jit(solution)/shard_map/pallas_call | solution.py:436
  (10 shorter events, 0.0 us)
Async XLA Ops:
  0.0 1.2 %copy-start = (f32[10,4,5400]{2,1,0:T(4,128)S(1)}, f32[10,4,5400]{2,1,0:T(4,128)}, u32[]{:S(2)}) copy-start(f32[10,4,5400]{2,1,0:T(4,128)} %tracer_ref.3) | copy-start | bytes 2592004
  1.2 1.2 %copy-start.2 = (f32[10,4,5400]{2,1,0:T(4,128)S(1)}, f32[10,4,5400]{2,1,0:T(4,128)}, u32[]{:S(2)}) copy-start(f32[10,4,5400]{2,1,0:T(4,128)} %velocity_ref.3) | copy-start | bytes 2592004
  2.3 1.0 %copy-start.4 = (f32[10,5400]{1,0:T(8,128)S(1)}, f32[10,5400]{1,0:T(8,128)}, u32[]{:S(2)}) copy-start(f32[10,5400]{1,0:T(8,128)} %depth_ref.3) | copy-start | bytes 648004
  3.3 9.8 %copy-start.9 = (s32[160]{0:T(256)S(1)}, s32[160]{0:T(256)}, u32[]{:S(2)}) copy-start(s32[160]{0:T(256)} %param.12) | copy-start | bytes 1924
  3.3 9.8 %copy-start.8 = (s32[160,4]{0,1:T(4,128)S(1)}, s32[160,4]{0,1:T(4,128)}, u32[]{:S(2)}) copy-start(s32[160,4]{0,1:T(4,128)} %param.13) | copy-start | bytes 7684
  3.3 9.9 %copy-start.10 = (s32[160]{0:T(256)S(1)}, s32[160]{0:T(256)}, u32[]{:S(2)}) copy-start(s32[160]{0:T(256)} %param.14) | copy-start | bytes 1924
  5.8 22.8 %copy-start.5 = (f32[10,5400]{1,0:T(8,128)S(1)}, f32[10,5400]{1,0:T(8,128)}, u32[]{:S(2)}) copy-start(f32[10,5400]{1,0:T(8,128)} %depth_ref.3) | copy-start | bytes 648004
  5.8 22.8 %copy-start.7 = (f32[8,5504]{1,0:T(8,128)S(1)}, f32[8,5504]{1,0:T(8,128)}, u32[]{:S(2)}) copy-start(f32[8,5504]{1,0:T(8,128)} %constant.45.clone.column_ref) | copy-start | bytes 528388
  5.8 17.9 %all-to-all-start = ((f32[32,16,128]{2,1,0:T(8,128)}), f32[32,16,128]{2,1,0:T(8,128)S(1)}, u32[]{:S(2)}, u32[]{:S(2)}) async-start(f32[32,16,128]{2,1,0:T(8,128)} %shard_map.82.own_ref), calls=%async_computation | async-start | bytes 524288 | tf_op jit(solution)/shard_map/all_to_all | solution.py:396
  13.6 15.0 %copy-start.3 = (f32[10,4,5400]{2,1,0:T(4,128)S(1)}, f32[10,4,5400]{2,1,0:T(4,128)}, u32[]{:S(2)}) copy-start(f32[10,4,5400]{2,1,0:T(4,128)} %velocity_ref.3) | copy-start | bytes 2592004
  14.3 14.3 %copy-start.1 = (f32[10,4,5400]{2,1,0:T(4,128)S(1)}, f32[10,4,5400]{2,1,0:T(4,128)}, u32[]{:S(2)}) copy-start(f32[10,4,5400]{2,1,0:T(4,128)} %tracer_ref.3) | copy-start | bytes 2592004
  25.4 13.2 %all-to-all-start.1 = ((f32[32,16,128]{2,1,0:T(8,128)}), f32[32,16,128]{2,1,0:T(8,128)S(1)}, u32[]{:S(2)}, u32[]{:S(2)}) async-start(f32[32,16,128]{2,1,0:T(8,128)} %bitcast.3), calls=%async_computation.1 | async-start | bytes 524288 | tf_op jit(solution)/shard_map/all_to_all | solution.py:418
  28.6 1.0 %copy-start.6 = (f32[10,5400]{1,0:T(8,128)S(1)}, f32[10,5400]{1,0:T(8,128)}, u32[]{:S(2)}) copy-start(f32[10,5400]{1,0:T(8,128)} %kappa_ref.1) | copy-start | bytes 648004
  29.6 5.1 %copy-start.11 = (pred[512]{0:T(512)(128)(4,1)S(1)}, pred[512]{0:T(512)(128)(4,1)}, u32[]{:S(2)}) copy-start(pred[512]{0:T(512)(128)(4,1)} %get-tuple-element.10) | copy-start | bytes 1540

commit v4 on v1

v4 whole, which is shorter than its diff:
```python
import functools

import jax
import jax.numpy as jnp
from jax import lax
from jax.experimental import pallas as pl
from jax.experimental.pallas import tpu as pltpu
from jax.sharding import PartitionSpec as P

IB = 90
JB = 60
CELLS = IB * JB
COURANT = 0.2
LANES = 128
TILES = -(-CELLS // LANES)
WIDE = TILES * LANES
GAPS = JB + 1
HALF = IB // 2
PARTS = 32
X_PART = 22
SPARE = 48
PIECE = 16
SCALE = COURANT / 12.0
SIDES = 3
OWN = 8
FIRST_PAIRS = 3


def lane_of(rows):
    return lax.broadcasted_iota(jnp.int32, (rows, LANES), 1)


def rot(value, shift):
    shift = shift % LANES
    return value if shift == 0 else pltpu.roll(value, shift, 1)


def sublanes(value, shift):
    return pltpu.roll(value, shift % 8, 0)


def once(make):
    held = {}

    def get(tile):
        if tile not in held:
            held[tile] = make(tile)
        return held[tile]

    return get


def shifted(get, distance):
    offset = distance % LANES
    turned = once(lambda tile: rot(get(tile), -offset))

    def make(tile):
        low = tile + distance // LANES
        first = turned(low) if 0 <= low < TILES else jnp.zeros((8, LANES), jnp.float32)
        second = turned(low + 1) if 0 <= low + 1 < TILES else jnp.zeros((8, LANES), jnp.float32)
        return jnp.where(lane_of(8) < LANES - offset, first, second)

    return once(make)


def window(get, start, rows):
    tile, offset = start // LANES, start % LANES
    head = rot(get(tile), -offset)
    if offset == 0 or tile + 1 >= TILES:
        return head
    return jnp.where(lane_of(rows) < LANES - offset, head, rot(get(tile + 1), -offset))


def gap_groups(get, first, wide, rows):
    lane = lane_of(rows)
    held = LANES // wide
    result = []
    for at in range(0, GAPS, held):
        value = jnp.zeros((rows, LANES), jnp.float32)
        for gap in range(at, min(at + held, GAPS)):
            start = IB * gap + first
            place = (gap - at) * wide
            for tile in range(max(start, 0) // LANES, min(start + wide - 1, CELLS - 1) // LANES + 1):
                low = max(start, tile * LANES, 0)
                value = jnp.where(lane >= place + low - start, rot(get(tile), place - start + tile * LANES), value)
        result.append(value)
    return result


def lane_take(value, index):
    return jnp.take_along_axis(value, index, axis=1, mode="promise_in_bounds")


def lane_pick(pair, index):
    return jnp.where(index < LANES, lane_take(pair[0], index % LANES), lane_take(pair[1], index % LANES))


def tile_getter(ref, rows, count):
    def get(tile):
        if tile + 1 < TILES:
            return ref[rows, tile * LANES : (tile + 1) * LANES]
        rest = jnp.zeros((count, WIDE - CELLS), jnp.float32)
        return jnp.concatenate([ref[rows, tile * LANES : CELLS], rest], axis=1)

    return get


def joined(south, north, half, rows):
    if half == 0:
        return jnp.where(lane_of(rows) < 64, south, rot(north, 64))
    return jnp.where(lane_of(rows) < 64, rot(south, -HALF), rot(north, 64 - HALF))


def pair_copies(source, target, sems, first, pairs):
    copies = []
    for pair in range(pairs):
        into = target.at[pl.ds(8 * pair, 8)].reshape(2, 4, CELLS)
        copies.append(pltpu.make_async_copy(source.at[pl.ds(2 * (first + pair), 2)], into, sems.at[pair]))
    return copies


def pack_kernel(tracer_ref, velocity_ref, depth_ref, out_ref, own_ref,
                x_ref, v_ref, d_ref, strip_ref, x_sems, v_sems, d_sem):
    count = depth_ref.shape[0]
    pairs = count // 2
    x_copies = pair_copies(tracer_ref, x_ref, x_sems, 0, pairs)
    v_copies = pair_copies(velocity_ref, v_ref, v_sems, 0, pairs)
    d_copy = pltpu.make_async_copy(depth_ref, d_ref, d_sem)
    for pair in range(pairs):
        x_copies[pair].start()
        v_copies[pair].start()
    d_copy.start()
    lane = lane_of(8)
    for pair in range(pairs):
        rows = pl.ds(8 * pair, 8)
        x_copies[pair].wait()
        get_x = tile_getter(x_ref, rows, 8)
        groups = gap_groups(get_x, -2, 4, 8)
        near = lane_pick(groups, 4 * (lane // 2) + 1 + lane % 2)
        far = lane_pick(groups, 4 * (lane // 2) + 3 * (lane % 2))
        south = [window(get_x, 0, 8), window(get_x, IB, 8)]
        north = [window(get_x, CELLS - IB, 8), window(get_x, CELLS - 2 * IB, 8)]
        v_copies[pair].wait()
        get_v = tile_getter(v_ref, rows, 8)
        v_south, v_north = window(get_v, 0, 8), window(get_v, CELLS - IB, 8)
        strips = [joined(south[0], north[0], half, 8) for half in range(2)]
        strips += [joined(south[1], north[1], half, 8) for half in range(2)]
        strips += [joined(v_south, v_north, half, 8) for half in range(2)]
        for index, strip in enumerate(strips):
            strip_ref[index, rows, :] = strip
        own_ref[0, rows, :] = near
        own_ref[1, rows, :] = far
        own_ref[2, rows, :] = gap_groups(get_v, -1, 2, 8)[0]

    d_copy.wait()
    if out_ref.shape[0] > PARTS * count:
        rest = out_ref.shape[0] - PARTS * count
        out_ref[PARTS * count :, :] = jnp.zeros((rest, LANES), jnp.float32)
    slot_lane = lane_of(count)
    get_d = tile_getter(d_ref, slice(None), count)
    d_south, d_north = window(get_d, 0, count), window(get_d, CELLS - IB, count)
    d_gaps = gap_groups(get_d, -1, 2, count)[0]
    spare = (slot_lane >= SPARE) & (slot_lane < SPARE + PIECE)

    def put(part, value):
        out_ref[part * count : (part + 1) * count, :] = value

    for chan in range(4):
        rows = pl.ds(chan, count, stride=4)
        for half in range(2):
            for deep in range(2):
                part = 2 * (4 * deep + chan) + half
                value = strip_ref[2 * deep + half, rows, :]
                if part < 8:
                    value = jnp.where(spare, rot(d_gaps, SPARE - PIECE * part), value)
                put(part, value)
            if chan >= 2:
                put(2 * (8 + chan - 2) + half, strip_ref[4 + half, rows, :])
        put(X_PART + chan, own_ref[0, rows, :])
        put(X_PART + 4 + chan, own_ref[1, rows, :])
        if chan < 2:
            put(X_PART + 8 + chan, own_ref[2, rows, :])
    for half in range(2):
        put(20 + half, joined(d_south, d_north, half, count))


def route_kernel(part_ref, code_ref, held_ref, after_ref, out_ref):
    del after_ref
    total = held_ref.shape[0]
    rows = out_ref.shape[0]
    part = part_ref[0]
    picked = [jnp.zeros((rows, 2 * LANES), jnp.float32) for _ in range(5)]
    for start in range(0, total, rows):
        held = held_ref[start : start + rows, :]
        high = held.astype(jnp.bfloat16)
        low = (held - high.astype(jnp.float32)).astype(jnp.bfloat16)
        halves = jnp.concatenate([high, low], axis=1)
        source = lax.broadcasted_iota(jnp.int32, (rows, rows), 1) + start
        for side in range(5):
            one_hot = jnp.where(code_ref[:, side : side + 1] == source, 1.0, 0.0).astype(jnp.bfloat16)
            picked[side] += jnp.dot(one_hot, halves, preferred_element_type=jnp.float32)
    west, east, south, north, fold = [value[:, :LANES] + value[:, LANES:] for value in picked]
    lane = lane_of(rows)
    along_x = (part >= X_PART) | ((part < 8) & (lane >= SPARE) & (lane < SPARE + PIECE))
    x_side = jnp.where(lane % 2 == 0, west, east)
    y_side = jnp.where(lane < 64, north + rot(fold, 64), south)
    out_ref[...] = jnp.where(along_x, x_side, y_side)


def bulk_kernel(first, my_ref, tracer_ref, velocity_ref, depth_ref, kappa_ref, code_ref, own_ref, after_ref,
                base_ref, edge_ref, x_ref, v_ref, d_ref, k_ref, w_ref, z_ref, x_sems, v_sems, d_sems):
    del after_ref
    count = depth_ref.shape[0]
    pairs = base_ref.shape[0] // 8
    x_copies = pair_copies(tracer_ref, x_ref, x_sems, first, pairs)
    v_copies = pair_copies(velocity_ref, v_ref, v_sems, first, pairs)
    d_copy = pltpu.make_async_copy(depth_ref, d_ref, d_sems.at[0])
    k_copy = pltpu.make_async_copy(kappa_ref, k_ref, d_sems.at[1])
    d_copy.start()
    k_copy.start()
    for pair in range(pairs):
        v_copies[pair].start()
        x_copies[pair].start()
    d_copy.wait()
    k_copy.wait()
    lane = lane_of(8)
    row = lax.broadcasted_iota(jnp.int32, (8, LANES), 0)
    x_row, even, place = row % 4 < 2, row % 2 == 0, row % 4
    level = (row % 2).astype(jnp.float32)
    zero = jnp.zeros((8, LANES), jnp.float32)

    def all_rows(value, chosen):
        result = value
        for at in range(4):
            if at != chosen:
                result = jnp.where(place == at, sublanes(value, at - chosen), result)
        return result

    def wet_of(depth):
        return jnp.clip(depth - level, 0.0, 1.0)

    def one_pair(pair):
        slot = 2 * (first + pair)
        rows = pl.ds(8 * pair, 8)

        def two_rows(ref, columns, width):
            top, low = ref[pl.ds(slot, 1), columns], ref[pl.ds(slot + 1, 1), columns]
            return jnp.where(row[:, :width] < 4, jnp.broadcast_to(top, (8, width)), jnp.broadcast_to(low, (8, width)))

        def slot_getter(ref):
            def get(tile):
                if tile + 1 < TILES:
                    return two_rows(ref, slice(tile * LANES, (tile + 1) * LANES), LANES)
                last = two_rows(ref, slice(tile * LANES, CELLS), CELLS - tile * LANES)
                return jnp.concatenate([last, jnp.zeros((8, WIDE - CELLS), jnp.float32)], axis=1)

            return once(get)

        codes = [code_ref[pl.ds(my_ref[0] * count + slot + at, 1), :] for at in range(2)]

        def flag(column):
            pieces = [jnp.broadcast_to(code[:, column : column + 1], (8, LANES)) for code in codes]
            return jnp.where(row < 4, pieces[0], pieces[1]) >= 0

        live, folded = flag(5), flag(4)
        state, velocity = once(tile_getter(x_ref, rows, 8)), once(tile_getter(v_ref, rows, 8))
        depth, kappa = slot_getter(d_ref), slot_getter(k_ref)
        wet = once(lambda tile: wet_of(depth(tile)))

        @once
        def ratio(tile):
            other = jnp.clip(depth(tile) - (1.0 - level), 0.0, 1.0)
            coupling = kappa(tile) * (wet(tile) * other)
            return coupling / (1.0 + 2.0 * coupling)

        next_vel = [shifted(velocity, 1), shifted(velocity, IB)]
        next_wet = [shifted(wet, 1), shifted(wet, IB)]

        @once
        def face(tile):
            rims = [at - tile * LANES for at in range(IB - 1, CELLS, IB) if at // LANES == tile]
            rim = functools.reduce(jnp.logical_or, [lane == at for at in rims]) if rims else None
            across = next_wet[0](tile) if rim is None else jnp.where(rim, 0.0, next_wet[0](tile))
            speed = velocity(tile) + jnp.where(x_row, next_vel[0](tile), next_vel[1](tile))
            value = SCALE * speed * (wet(tile) * jnp.where(x_row, across, next_wet[1](tile)))
            w_ref[:, tile * LANES : (tile + 1) * LANES] = value
            return value

        face_x = once(lambda tile: jnp.where(x_row, face(tile), sublanes(face(tile), 2)))
        face_y = once(lambda tile: jnp.where(x_row, sublanes(face(tile), -2), face(tile)))
        five = once(lambda tile: 5.0 * state(tile))
        two = once(lambda tile: 2.0 * state(tile))

        def divergence(speed, distance):
            before, after = shifted(state, -distance), shifted(state, distance)
            upper = shifted(once(lambda tile: five(tile) - after(tile)), distance)

            @once
            def flux(tile):
                value = jnp.maximum(speed(tile), 0.0) * (five(tile) - before(tile) + 2.0 * after(tile))
                return value + jnp.minimum(speed(tile), 0.0) * (two(tile) + upper(tile))

            back = shifted(flux, -distance)
            return lambda tile: flux(tile) - back(tile)

        change_x, change_y = divergence(face_x, 1), divergence(face_y, IB)
        for tile in range(TILES):
            explicit = state(tile) - wet(tile) * (change_x(tile) + change_y(tile))
            other = jnp.where(even, sublanes(explicit, -1), sublanes(explicit, 1))
            value = jnp.where(live, explicit + ratio(tile) * (other - explicit), zero)
            stop = min((tile + 1) * LANES, CELLS)
            base_ref[rows, tile * LANES : stop] = value[:, : stop - tile * LANES]
            mixed = jnp.where(x_row, face(tile), jnp.where(even, ratio(tile), depth(tile)))
            z_ref[:, tile * LANES : (tile + 1) * LANES] = mixed

        whole = slice(None)
        get_w, get_z = [lambda tile, ref=ref: ref[:, tile * LANES : (tile + 1) * LANES] for ref in (w_ref, z_ref)]
        groups = gap_groups(get_z, -2, 4, 8)
        east = lane % 2 == 0
        own_rows = pl.ds(8 * (first + pair), 8)
        near, far, normal = [own_ref[index, own_rows, :] for index in range(3)]
        normal = jnp.where(x_row, normal, sublanes(normal, 2))
        rim_speed = lane_pick(groups, 4 * (lane // 2) + 2 * (lane % 2))
        rim_speed = jnp.where(x_row, rim_speed, sublanes(rim_speed, 2))
        sides = [(
            near, far, jnp.where(east, -normal, normal), jnp.where(east, -rim_speed, rim_speed),
            lane_pick(groups, 4 * (lane // 2) + 1 + lane % 2), lane_pick(groups, 4 * (lane // 2) + 3 * (lane % 2)),
        )]
        for outer, inner, edge, sign in ((0, IB, 0, 1.0), (CELLS - IB, CELLS - 2 * IB, CELLS - 2 * IB, -1.0)):
            normal, rim_speed = window(velocity, outer, 8), window(get_w, edge, 8)
            normal = sign * jnp.where(x_row, sublanes(normal, -2), normal)
            rim_speed = sign * jnp.where(x_row, sublanes(rim_speed, -2), rim_speed)
            sides.append((window(state, outer, 8), window(state, inner, 8), normal, rim_speed,
                          window(get_z, outer, 8), window(get_z, inner, 8)))
        for side, (near, far, normal, rim_speed, outer, inner) in enumerate(sides):
            values = (near, far, normal, jnp.where(live, jnp.maximum(rim_speed, 0.0), zero), wet_of(all_rows(outer, 3)),
                      wet_of(all_rows(inner, 3)), all_rows(outer, 2), all_rows(inner, 2))
            for index, value in enumerate(values):
                edge_ref[OWN * side + index, rows, :] = value
        edge_ref[OWN * SIDES, rows, :] = jnp.where(folded, 1.0, zero)

    for pair in range(pairs):
        v_copies[pair].wait()
        x_copies[pair].wait()
        one_pair(pair)


def finish_kernel(halo_ref, edge_a_ref, edge_b_ref, base_a_ref, base_b_ref, out_ref,
                  y_ref, raw_ref, delta_ref, in_sems, out_sems):
    count = out_ref.shape[0]
    pairs = count // 2
    rows = 4 * count
    split = base_a_ref.shape[0]
    a_copy = pltpu.make_async_copy(base_a_ref, y_ref.at[pl.ds(0, split)], in_sems.at[0])
    b_copy = pltpu.make_async_copy(base_b_ref, y_ref.at[pl.ds(split, rows - split)], in_sems.at[1])
    a_copy.start()
    b_copy.start()
    lane = lane_of(rows)
    level = (lax.broadcasted_iota(jnp.int32, (rows, LANES), 0) % 2).astype(jnp.float32)

    def own(index):
        return jnp.concatenate([edge_a_ref[index], edge_b_ref[index]], axis=0)

    def part(index):
        return halo_ref[index * count : (index + 1) * count, :]

    def assembled(index, parts):
        for chan, value in enumerate(parts):
            raw_ref[index, pl.ds(chan, count, stride=4), :] = value
        return raw_ref[index]

    folded = own(OWN * SIDES) > 0.0
    mirror = jnp.where(lane < IB, IB - 1 - lane, lane)
    slot_lane = lane_of(count)
    depth_x = rot(part(0), -SPARE)
    for index in range(1, 8):
        depth_x = jnp.where(slot_lane >= PIECE * index, rot(part(index), PIECE * index - SPARE), depth_x)
    x_raw = [[part(X_PART + chan) for chan in range(4)], [part(X_PART + 4 + chan) for chan in range(4)],
             [part(X_PART + 8 + chan % 2) for chan in range(4)], [depth_x] * 4]
    y_values = [list(range(4)), list(range(4, 8)), [8, 9, 8, 9], [10] * 4]
    x_halo, south_halo, north_halo = [], [], []
    for kind in range(4):
        raw = assembled(3 * kind, x_raw[kind])
        x_halo.append(jnp.where(lane % 2 == 0, rot(raw, 1), rot(raw, -1)))
        first, second = [assembled(3 * kind + 1 + half, [part(2 * value + half) for value in y_values[kind]])
                         for half in range(2)]
        south_halo.append(jnp.where(lane < HALF, rot(first, 64), rot(second, 64 + HALF)))
        raw = jnp.where(lane < HALF, first, rot(second, HALF))
        turned = lane_take(raw, mirror)
        north_halo.append(jnp.where(folded, -turned if kind == 2 else turned, raw))

    for side, (out_near, out_far, out_normal, out_depth) in enumerate((x_halo, south_halo, north_halo)):
        near, far, normal, rim_speed, wet, inner_wet, ratio, inner_ratio = [
            own(OWN * side + index) for index in range(OWN)]
        if side == 0:
            out_normal = jnp.where(lane % 2 == 0, -out_normal, out_normal)
            beyond = out_near - jnp.where(lane % 2 == 0, rot(near, -1), rot(near, 1))
        else:
            out_normal = -out_normal if side == 2 else out_normal
            beyond = out_near
        speed = SCALE * (normal + out_normal) * (wet * jnp.clip(out_depth - level, 0.0, 1.0))
        flux = jnp.maximum(speed, 0.0) * (5.0 * out_near + 2.0 * near - out_far)
        flux += jnp.minimum(speed, 0.0) * (2.0 * out_near + 5.0 * near - far)
        inner_flux = rim_speed * beyond
        for place, (change, share) in enumerate(((wet * (flux + inner_flux), ratio),
                                                 (-inner_wet * inner_flux, inner_ratio))):
            other = jnp.where(level == 0.0, pltpu.roll(change, rows - 1, 0), pltpu.roll(change, 1, 0))
            delta_ref[2 * side + place] = change + share * (other - change)

    lane = lane_of(8)
    a_copy.wait()
    b_copy.wait()
    out_copies = []
    for pair in range(pairs):
        mine = pl.ds(8 * pair, 8)
        near, deep, south, south_in, north, north_in = [delta_ref[index, mine, :] for index in range(2 * SIDES)]
        groups = []
        for at in range(2):
            index = 2 * (lane // 4) + (lane % 4) // 2 + 64 * at
            outer, inner = lane_take(near, index), lane_take(deep, index)
            groups.append(jnp.where((lane % 4 == 1) | (lane % 4 == 2), outer, inner))
        placed = [(groups[gap // 32], 4 * (gap % 32), IB * gap - 2, 4) for gap in range(GAPS)]
        placed += [(south, 0, 0, IB), (south_in, 0, IB, IB)]
        placed += [(north, 0, CELLS - IB, IB), (north_in, 0, CELLS - 2 * IB, IB)]
        for tile in range(TILES):
            at, stop = tile * LANES, min((tile + 1) * LANES, CELLS)
            change = jnp.zeros((8, LANES), jnp.float32)
            for source, origin, start, wide in placed:
                low, high = max(start, at, 0), min(start + wide, stop)
                if low < high:
                    inside = (lane >= low - at) & (lane < high - at)
                    change += jnp.where(inside, rot(source, start - at - origin), 0.0)
            y_ref[mine, at:stop] = y_ref[mine, at:stop] + change[:, : stop - at]
        copy = pltpu.make_async_copy(
            y_ref.at[mine].reshape(2, 4, CELLS), out_ref.at[pl.ds(2 * pair, 2)], out_sems.at[pair])
        copy.start()
        out_copies.append(copy)
    for copy in out_copies:
        copy.wait()


def route_codes(block_owner, neighbours, fold_partner, slot_total):
    block_count = block_owner.shape[0]
    hits = block_owner[None, :] == jnp.arange(slot_total, dtype=jnp.int32)[:, None]
    links = jnp.concatenate([neighbours, fold_partner[:, None]], axis=1)
    linked = links[:, :, None] == jnp.arange(block_count, dtype=jnp.int32)[None, None, :]
    link_slots = jnp.max(jnp.where(linked, block_owner[None, None, :], -1), axis=2)
    link_slots = jnp.concatenate([link_slots, block_owner[:, None]], axis=1)
    return jnp.max(jnp.where(hits[:, :, None], link_slots[None], -1), axis=1)


def per_device(tracers, velocity, kappa, kmt, block_owner, neighbours, fold_partner):
    slot_count, chans = tracers.shape[:2]
    sub_count = lax.axis_size("sub")
    device_count = lax.axis_size("blk") * sub_count
    if device_count % PARTS or chans != 4 or slot_count % 2 or slot_count < 2 * FIRST_PAIRS + 2:
        raise ValueError("unsupported sizes")
    my_index = (lax.axis_index("blk") * sub_count + lax.axis_index("sub")).astype(jnp.int32).reshape(1)
    axes = ("blk", "sub")
    pairs = slot_count // 2
    slot_total = device_count * slot_count
    state_rows = 4 * slot_count
    f32 = jnp.float32
    in_hbm = pl.BlockSpec(memory_space=pltpu.HBM)
    anywhere = pl.BlockSpec(memory_space=pl.ANY)
    in_vmem = pl.BlockSpec(memory_space=pltpu.VMEM)
    in_smem = pl.BlockSpec(memory_space=pltpu.SMEM)
    dma = pltpu.SemaphoreType.DMA

    def exchanged(pieces):
        pieces = pieces.reshape(device_count, slot_count, 1, LANES)
        return lax.all_to_all(pieces, axes, 0, 0, tiled=True).reshape(slot_total, LANES)

    pack, own = pl.pallas_call(
        pack_kernel,
        out_shape=[jax.ShapeDtypeStruct((slot_total, LANES), f32), jax.ShapeDtypeStruct((3, state_rows, LANES), f32)],
        in_specs=[in_hbm, in_hbm, in_hbm],
        out_specs=[in_vmem, in_vmem],
        scratch_shapes=[
            pltpu.VMEM((state_rows, CELLS), f32),
            pltpu.VMEM((state_rows, CELLS), f32),
            pltpu.VMEM((slot_count, CELLS), f32),
            pltpu.VMEM((6, state_rows, LANES), f32),
            dma((pairs,)),
            dma((pairs,)),
            dma,
        ],
        cost_estimate=pl.CostEstimate(flops=4_000_000, bytes_accessed=2_400_000, transcendentals=0),
    )(tracers, velocity, kmt)
    held = exchanged(pack)
    codes = route_codes(block_owner, neighbours, fold_partner, slot_total)

    def bulk(first, some, after):
        return pl.pallas_call(
            functools.partial(bulk_kernel, first),
            out_shape=[
                jax.ShapeDtypeStruct((8 * some, CELLS), f32),
                jax.ShapeDtypeStruct((OWN * SIDES + 1, 8 * some, LANES), f32),
            ],
            in_specs=[in_smem, in_hbm, in_hbm, in_hbm, in_hbm, in_vmem, in_vmem, anywhere],
            out_specs=[in_vmem, in_vmem],
            scratch_shapes=[
                pltpu.VMEM((8 * some, CELLS), f32),
                pltpu.VMEM((8 * some, CELLS), f32),
                pltpu.VMEM((slot_count, CELLS), f32),
                pltpu.VMEM((slot_count, CELLS), f32),
                pltpu.VMEM((8, WIDE), f32),
                pltpu.VMEM((8, WIDE), f32),
                dma((some,)),
                dma((some,)),
                dma((2,)),
            ],
            cost_estimate=pl.CostEstimate(flops=4_000_000 * some, bytes_accessed=800_000 * some, transcendentals=0),
        )(my_index, tracers, velocity, kmt, kappa, codes, own, after)

    base_a, edge_a = bulk(0, FIRST_PAIRS, own)

    routed_rows = PARTS * slot_count
    routed = pl.pallas_call(
        route_kernel,
        grid=(device_count // PARTS,),
        out_shape=jax.ShapeDtypeStruct((slot_total, LANES), f32),
        in_specs=[
            in_smem,
            pl.BlockSpec((routed_rows, 6), lambda step: (step, 0)),
            pl.BlockSpec((slot_total, LANES), lambda step: (0, 0)),
            anywhere,
        ],
        out_specs=pl.BlockSpec((routed_rows, LANES), lambda step: (step, 0)),
    )(my_index, codes, held, edge_a)

    base_b, edge_b = bulk(FIRST_PAIRS, pairs - FIRST_PAIRS, routed)
    halo = exchanged(routed)[: PARTS * slot_count]

    return pl.pallas_call(
        finish_kernel,
        out_shape=jax.ShapeDtypeStruct(tracers.shape, f32),
        in_specs=[in_vmem, in_vmem, in_vmem, anywhere, anywhere],
        out_specs=in_hbm,
        scratch_shapes=[
            pltpu.VMEM((state_rows, CELLS), f32),
            pltpu.VMEM((12, state_rows, LANES), f32),
            pltpu.VMEM((2 * SIDES, state_rows, LANES), f32),
            dma((2,)),
            dma((pairs,)),
        ],
    )(halo, edge_a, edge_b, base_a, base_b)


def solution(mesh):
    placed = (
        P(("blk", "sub"), None, None),
        P(("blk", "sub"), None, None),
        P(("blk", "sub"), None),
        P(("blk", "sub"), None),
        P(),
        P(),
        P(),
    )
    return jax.shard_map(
        per_device,
        mesh=mesh,
        in_specs=placed,
        out_specs=P(("blk", "sub"), None, None),
        check_vma=False,
    )
```

time: 153 us -> 79.7 us (0.52)
  Pallas kernels: 0 us -> 63.1 us
  local copies, waits for them, and re-layouts: 63.5 us -> 2.14 us
  waiting for transfers between devices: 53.8 us -> 0.01 us
  other arithmetic: 20.5 us -> 0.79 us
  between operations: 14.1 us -> 0.14 us
  starting transfers between devices: 0.01 us -> 13.1 us
    pallas_call x0 -> x5, Pallas kernels: none -> 63.1 us  [the longest x2 53.3 us: bulk(): pl.pallas_call(functools.partial(bulk_kernel, first), out_shape=[jax.Shap...]
    all_gather x1 -> x0, waiting for transfers between devices: 53.8 us -> none  [per_device(): window = lax.all_gather(pack, ('blk', 'sub'), axis=0, tiled=True)]
    gather x10 -> x0, local copies, waits for them, and re-layouts: 16.5 us -> none  [the longest x5 14.3 us: strip(): jnp.take(window, jnp.maximum(code, 0), axis=0)[:, start:start + wide]]
    reshape x15 -> x0, local copies, waits for them, and re-layouts: 15.2 us -> none  [the longest x1 5.05 us: per_device(): window = window.reshape(device_count * slot_count, padded)]
    all_to_all x0 -> x2, starting transfers between devices: none -> 13.1 us  [exchanged(): lax.all_to_all(pieces, axes, 0, 0, tiled=True).reshape(slot_total, LANES)]
    slice x32 -> x0, local copies, waits for them, and re-layouts: 11.4 us -> none  [the longest x2 4.16 us: edge_pack(): state[:, :, :, IB - 2:]]
    concatenate x6 -> x0, local copies, waits for them, and re-layouts: 9.41 us -> none  [the longest x2 5.63 us: per_device(): jnp.concatenate([west_x, state, east_x], axis=3)]
    mul x6 -> x0, other arithmetic: 6.75 us -> none  [the longest x4 4.91 us: face_flux(): return velocity_face * centered + jnp.abs(velocity_face) * upwind]
  transfers between devices with their start and end apart: 1 -> 2, of which waited for: 1 -> 0; matrix products, arithmetic and copies ran while one was open for 7% -> 2% of each run, Pallas kernels for 0% -> 67%
where the time goes in v4:
time: 79.7 us; the launch traced here: 79.3 us
  Pallas kernels  63.1 us (79%)
  starting transfers between devices  13.1 us (16%)
  local copies, waits for them, and re-layouts  2.14 us (3%)
    pallas_call x2, Pallas kernels, bulk(): pl.pallas_call(functools.partial(bulk_kernel, first), out_shape=[jax.Shap...  53.3 us
    all_to_all x2, starting transfers between devices, exchanged(): lax.all_to_all(pieces, axes, 0, 0, tiled=True).reshape(slot_total, LANES)  13.1 us
    pallas_call x1, Pallas kernels, per_device(): pl.pallas_call(pack_kernel, out_shape=[jax.ShapeDtypeStruct((slot_total,...  3.75 us
    pallas_call x1, Pallas kernels, per_device(): pl.pallas_call(finish_kernel, out_shape=jax.ShapeDtypeStruct(tracers.shap...  3.68 us
    pallas_call x1, Pallas kernels, per_device(): pl.pallas_call(route_kernel, grid=(device_count // PARTS,), out_shape=jax...  2.35 us
  transfers between devices with their start and end apart: 2, of which 0 were waited for; matrix products, arithmetic and copies ran while one was open for 2% of the time, Pallas kernels for 67%

profile of v4, /device:TPU:0, one launch (start us, length us, event | category | flops | bytes accessed | tf_op | source)
XLA Modules:
  0.0 79.3 jit_solution(15032074152263375272)
XLA Ops:
  0.0 0.0 copy-start.4
  0.0 0.0 copy-start.3
  0.0 0.0 copy-start.2
  0.0 3.8 %shard_map.73 = (f32[320,128]{1,0:T(8,128)}, f32[3,40,128]{2,1,0:T(8,128)}) custom-call(f32[10,4,5400]{2,1,0:T(4,128)} %tracer_ref.5, f32[10,4,5400]{2,1,0:T(4,128)} %velocity_ref.5, f32[10,5400]{1,0:T(8,128)} %depth_ref.5), custom_call_target="tpu_custom_call" | custom-call | flops 4000000 | bytes 2400000 | tf_op jit(solution)/shard_map/pallas_call | solution.py:474
  3.8 7.3 %all-to-all-start = ((f32[32,10,1,128]{3,2,1,0:T(1,128)}), f32[32,10,1,128]{3,2,1,0:T(1,128)S(1)}, u32[]{:S(2)}, u32[]{:S(2)}) async-start(f32[32,10,1,128]{3,2,1,0:T(1,128)} %bitcast.10), calls=%async_computation | async-start | bytes 327680 | tf_op jit(solution)/shard_map/all_to_all | solution.py:472
  11.1 0.0 copy-done.4
  11.1 0.0 copy-done.3
  11.1 0.0 copy-done.2
  11.1 0.4 select_reduce_fusion.1
  11.6 0.1 iota_compare_fusion.1
  11.7 0.3 select_reduce_fusion
  11.9 0.8 %copy.17.code_ref = s32[320,6]{1,0:T(8,128)} copy(s32[320,6]{0,1:T(8,128)S(1)} %select_reduce_fusion) | data formatting | bytes 15360 | tf_op jit(solution)/shard_map/reduce_max | solution.py:449
  12.8 31.5 %shard_map.74 = (f32[24,5400]{1,0:T(8,128)}, f32[25,24,128]{2,1,0:T(8,128)}) custom-call(s32[1]{0:T(128)} %bitcast.my_ref.part_ref, f32[10,4,5400]{2,1,0:T(4,128)} %tracer_ref.5, f32[10,4,5400]{2,1,0:T(4,128)} %velocity_ref.5, f32[10,5400]{1,0:T(8,128)} %depth_ref.5, f32[10,5400]{1,0:T(8,128)} %kappa_ref.3, s32[320,6]{1,0:T(8,128)} %copy.17.code_ref, ...), custom_call_target="tpu_custom_call" | custom-call | flops 12000000 | bytes 2400000 | tf_op jit(solution)/shard_map/pallas_call | solution.py:494
  44.2 0.0 all-to-all-done
  44.2 0.0 copy-start.1
  44.2 0.7 copy-done.1
  44.9 2.4 %shard_map.75.after_ref = f32[320,128]{1,0:T(8,128)} custom-call(s32[1]{0:T(128)} %bitcast.my_ref.part_ref, s32[320,6]{1,0:T(8,128)} %copy.17.code_ref, f32[320,128]{1,0:T(8,128)} %bitcast.9, f32[25,24,128]{2,1,0:T(8,128)} %get-tuple-element.13.after_ref.edge_a_ref), custom_call_target="tpu_custom_call" | custom-call | tf_op jit(solution)/shard_map/pallas_call | solution.py:519
  47.3 5.8 %all-to-all-start.1 = ((f32[32,10,1,128]{3,2,1,0:T(1,128)}), f32[32,10,1,128]{3,2,1,0:T(1,128)S(1)}, u32[]{:S(2)}, u32[]{:S(2)}) async-start(f32[32,10,1,128]{3,2,1,0:T(1,128)} %bitcast.7), calls=%async_computation.1 | async-start | bytes 327680 | tf_op jit(solution)/shard_map/all_to_all | solution.py:472
  53.1 21.9 %shard_map.76 = (f32[16,5400]{1,0:T(8,128)}, f32[25,16,128]{2,1,0:T(8,128)}) custom-call(s32[1]{0:T(128)} %bitcast.my_ref.part_ref, f32[10,4,5400]{2,1,0:T(4,128)} %tracer_ref.5, f32[10,4,5400]{2,1,0:T(4,128)} %velocity_ref.5, f32[10,5400]{1,0:T(8,128)} %depth_ref.5, f32[10,5400]{1,0:T(8,128)} %kappa_ref.3, s32[320,6]{1,0:T(8,128)} %copy.17.code_ref, ...), custom_call_target="tpu_custom_call" | custom-call | flops 8000000 | bytes 1600000 | tf_op jit(solution)/shard_map/pallas_call | solution.py:494
  75.0 0.0 all-to-all-done.1
  75.0 0.0 copy-start
  75.0 0.6 copy-done
  75.6 3.7 %shard_map.77 = f32[10,4,5400]{2,1,0:T(4,128)} custom-call(f32[320,128]{1,0:T(8,128)} %bitcast.8, f32[25,24,128]{2,1,0:T(8,128)} %get-tuple-element.13.after_ref.edge_a_ref, f32[25,16,128]{2,1,0:T(8,128)} %get-tuple-element.14.edge_b_ref, f32[24,5400]{1,0:T(8,128)} %get-tuple-element.15.base_a_ref, f32[16,5400]{1,0:T(8,128)} %get-tuple-element.16.base_b_ref), custom_call_target="tpu_custom_call" | custom-call | tf_op jit(solution)/shard_map/pallas_call | solution.py:535
  (2 shorter events, 0.0 us)
Async XLA Ops:
  0.0 11.1 %copy-start.4 = (s32[160]{0:T(256)S(1)}, s32[160]{0:T(256)}, u32[]{:S(2)}) copy-start(s32[160]{0:T(256)} %param.13) | copy-start | bytes 1924
  0.0 11.1 %copy-start.3 = (s32[160,4]{0,1:T(4,128)S(1)}, s32[160,4]{0,1:T(4,128)}, u32[]{:S(2)}) copy-start(s32[160,4]{0,1:T(4,128)} %param.12) | copy-start | bytes 7684
  0.0 11.1 %copy-start.2 = (s32[160]{0:T(256)S(1)}, s32[160]{0:T(256)}, u32[]{:S(2)}) copy-start(s32[160]{0:T(256)} %param.11) | copy-start | bytes 1924
  3.8 40.4 %all-to-all-start = ((f32[32,10,1,128]{3,2,1,0:T(1,128)}), f32[32,10,1,128]{3,2,1,0:T(1,128)S(1)}, u32[]{:S(2)}, u32[]{:S(2)}) async-start(f32[32,10,1,128]{3,2,1,0:T(1,128)} %bitcast.10), calls=%async_computation | async-start | bytes 327680 | tf_op jit(solution)/shard_map/all_to_all | solution.py:472
  44.2 0.7 copy-start.1
  47.3 27.7 %all-to-all-start.1 = ((f32[32,10,1,128]{3,2,1,0:T(1,128)}), f32[32,10,1,128]{3,2,1,0:T(1,128)S(1)}, u32[]{:S(2)}, u32[]{:S(2)}) async-start(f32[32,10,1,128]{3,2,1,0:T(1,128)} %bitcast.7), calls=%async_computation.1 | async-start | bytes 327680 | tf_op jit(solution)/shard_map/all_to_all | solution.py:472
  75.0 0.7 copy-start

commit v5 on v4

--- a/solution.py
+++ b/solution.py
@@ -208,7 +208,7 @@
 
 
 def bulk_kernel(first, my_ref, tracer_ref, velocity_ref, depth_ref, kappa_ref, code_ref, own_ref, after_ref,
-                base_ref, edge_ref, x_ref, v_ref, d_ref, k_ref, w_ref, z_ref, x_sems, v_sems, d_sems):
+                base_ref, edge_ref, x_ref, v_ref, d_ref, k_ref, d8_ref, k8_ref, w_ref, z_ref, x_sems, v_sems, d_sems):
     del after_ref
     count = depth_ref.shape[0]
     pairs = base_ref.shape[0] // 8
@@ -221,8 +221,6 @@
     for pair in range(pairs):
         v_copies[pair].start()
         x_copies[pair].start()
-    d_copy.wait()
-    k_copy.wait()
     lane = lane_of(8)
     row = lax.broadcasted_iota(jnp.int32, (8, LANES), 0)
     x_row, even, place = row % 4 < 2, row % 2 == 0, row % 4
@@ -239,22 +237,22 @@
     def wet_of(depth):
         return jnp.clip(depth - level, 0.0, 1.0)
 
+    for copy, source, target in ((d_copy, d_ref, d8_ref), (k_copy, k_ref, k8_ref)):
+        copy.wait()
+        for pair in range(pairs):
+            slot = 2 * (first + pair)
+            for start in range(0, CELLS, LANES):
+                columns = slice(start, min(start + LANES, CELLS))
+                shape = (8, columns.stop - start)
+                top, low = [jnp.broadcast_to(source[slot + at : slot + at + 1, columns], shape) for at in range(2)]
+                target[8 * pair : 8 * pair + 8, columns] = jnp.where(row[:, : shape[1]] < 4, top, low)
+
     def one_pair(pair):
         slot = 2 * (first + pair)
-        rows = pl.ds(8 * pair, 8)
-
-        def two_rows(ref, columns, width):
-            top, low = ref[pl.ds(slot, 1), columns], ref[pl.ds(slot + 1, 1), columns]
-            return jnp.where(row[:, :width] < 4, jnp.broadcast_to(top, (8, width)), jnp.broadcast_to(low, (8, width)))
-
-        def slot_getter(ref):
-            def get(tile):
-                if tile + 1 < TILES:
-                    return two_rows(ref, slice(tile * LANES, (tile + 1) * LANES), LANES)
-                last = two_rows(ref, slice(tile * LANES, CELLS), CELLS - tile * LANES)
-                return jnp.concatenate([last, jnp.zeros((8, WIDE - CELLS), jnp.float32)], axis=1)
-
-            return once(get)
+        rows = pl.ds(pl.multiple_of(8 * pair, 8), 8)
+        for source, target, sems in ((velocity_ref, v_ref, v_sems), (tracer_ref, x_ref, x_sems)):
+            pltpu.make_async_copy(
+                source.at[pl.ds(0, 2)], target.at[rows].reshape(2, 4, CELLS), sems.at[pair]).wait()
 
         codes = [code_ref[pl.ds(my_ref[0] * count + slot + at, 1), :] for at in range(2)]
 
@@ -264,7 +262,7 @@
 
         live, folded = flag(5), flag(4)
         state, velocity = once(tile_getter(x_ref, rows, 8)), once(tile_getter(v_ref, rows, 8))
-        depth, kappa = slot_getter(d_ref), slot_getter(k_ref)
+        depth, kappa = once(tile_getter(d8_ref, rows, 8)), once(tile_getter(k8_ref, rows, 8))
         wet = once(lambda tile: wet_of(depth(tile)))
 
         @once
@@ -293,16 +291,23 @@
 
         def divergence(speed, distance):
             before, after = shifted(state, -distance), shifted(state, distance)
+            lower = once(lambda tile: five(tile) - before(tile) + 2.0 * after(tile))
             upper = shifted(once(lambda tile: five(tile) - after(tile)), distance)
 
             @once
             def flux(tile):
-                value = jnp.maximum(speed(tile), 0.0) * (five(tile) - before(tile) + 2.0 * after(tile))
+                value = jnp.maximum(speed(tile), 0.0) * lower(tile)
                 return value + jnp.minimum(speed(tile), 0.0) * (two(tile) + upper(tile))
 
             back = shifted(flux, -distance)
-            return lambda tile: flux(tile) - back(tile)
-
+            for stage in (after, before, lower, upper, flux, back):
+                for tile in range(TILES):
+                    stage(tile)
+            return once(lambda tile: flux(tile) - back(tile))
+
+        for stage in (depth, wet, ratio, *next_vel, *next_wet, face):
+            for tile in range(TILES):
+                stage(tile)
         change_x, change_y = divergence(face_x, 1), divergence(face_y, IB)
         for tile in range(TILES):
             explicit = state(tile) - wet(tile) * (change_x(tile) + change_y(tile))
@@ -313,11 +318,10 @@
             mixed = jnp.where(x_row, face(tile), jnp.where(even, ratio(tile), depth(tile)))
             z_ref[:, tile * LANES : (tile + 1) * LANES] = mixed
 
-        whole = slice(None)
         get_w, get_z = [lambda tile, ref=ref: ref[:, tile * LANES : (tile + 1) * LANES] for ref in (w_ref, z_ref)]
         groups = gap_groups(get_z, -2, 4, 8)
         east = lane % 2 == 0
-        own_rows = pl.ds(8 * (first + pair), 8)
+        own_rows = pl.ds(pl.multiple_of(8 * (first + pair), 8), 8)
         near, far, normal = [own_ref[index, own_rows, :] for index in range(3)]
         normal = jnp.where(x_row, normal, sublanes(normal, 2))
         rim_speed = lane_pick(groups, 4 * (lane // 2) + 2 * (lane % 2))
@@ -339,10 +343,7 @@
                 edge_ref[OWN * side + index, rows, :] = value
         edge_ref[OWN * SIDES, rows, :] = jnp.where(folded, 1.0, zero)
 
-    for pair in range(pairs):
-        v_copies[pair].wait()
-        x_copies[pair].wait()
-        one_pair(pair)
+    pl.loop(0, pairs)(one_pair)
 
 
 def finish_kernel(halo_ref, edge_a_ref, edge_b_ref, base_a_ref, base_b_ref, out_ref,
@@ -466,6 +467,7 @@
     in_vmem = pl.BlockSpec(memory_space=pltpu.VMEM)
     in_smem = pl.BlockSpec(memory_space=pltpu.SMEM)
     dma = pltpu.SemaphoreType.DMA
+    limit = pltpu.CompilerParams(vmem_limit_bytes=32 * 1024 * 1024)
 
     def exchanged(pieces):
         pieces = pieces.reshape(device_count, slot_count, 1, LANES)
@@ -504,12 +506,15 @@
                 pltpu.VMEM((8 * some, CELLS), f32),
                 pltpu.VMEM((slot_count, CELLS), f32),
                 pltpu.VMEM((slot_count, CELLS), f32),
+                pltpu.VMEM((8 * some, CELLS), f32),
+                pltpu.VMEM((8 * some, CELLS), f32),
                 pltpu.VMEM((8, WIDE), f32),
                 pltpu.VMEM((8, WIDE), f32),
                 dma((some,)),
                 dma((some,)),
                 dma((2,)),
             ],
+            compiler_params=limit,
             cost_estimate=pl.CostEstimate(flops=4_000_000 * some, bytes_accessed=800_000 * some, transcendentals=0),
         )(my_index, tracers, velocity, kmt, kappa, codes, own, after)
 
@@ -527,6 +532,7 @@
             anywhere,
         ],
         out_specs=pl.BlockSpec((routed_rows, LANES), lambda step: (step, 0)),
+        compiler_params=limit,
     )(my_index, codes, held, edge_a)
 
     base_b, edge_b = bulk(FIRST_PAIRS, pairs - FIRST_PAIRS, routed)
@@ -544,6 +550,7 @@
             dma((2,)),
             dma((pairs,)),
         ],
+        compiler_params=limit,
     )(halo, edge_a, edge_b, base_a, base_b)
 
 

time: 79.7 us -> 37.6 us (0.47)
  Pallas kernels: 63.1 us -> 13.3 us
  waiting for transfers between devices: 0.01 us -> 7.62 us
  local copies, waits for them, and re-layouts: 2.14 us -> 4.43 us
  starting transfers between devices: 13.1 us -> 10.9 us
    pallas_call x2, Pallas kernels: 53.3 us -> 6.13 us  [bulk(): pl.pallas_call(functools.partial(bulk_kernel, first), out_shape=[jax.Shap...]
    all_to_all x2, waiting for transfers between devices: 0.01 us -> 7.62 us  [exchanged(): lax.all_to_all(pieces, axes, 0, 0, tiled=True).reshape(slot_total, LANES)]
    unnamed x10 -> x26, local copies, waits for them, and re-layouts: 1.33 us -> 4.29 us
    all_to_all x2, starting transfers between devices: 13.1 us -> 10.9 us  [exchanged(): lax.all_to_all(pieces, axes, 0, 0, tiled=True).reshape(slot_total, LANES)]
    pallas_call x1, Pallas kernels: 3.68 us -> 1.95 us  [per_device(): pl.pallas_call(finish_kernel, out_shape=jax.ShapeDtypeStruct(tracers.shap...]
    pallas_call x1, Pallas kernels: 2.35 us -> 1.37 us  [per_device(): pl.pallas_call(route_kernel, grid=(device_count // PARTS,), out_shape=jax...]
  transfers between devices with their start and end apart: 2 -> 2, of which waited for: 0 -> 2; matrix products, arithmetic and copies ran while one was open for 2% -> 2% of each run, Pallas kernels for 67% -> 16%
where the time goes in v5:
time: 37.6 us; the launch traced here: 37.2 us
  Pallas kernels  13.3 us (35%)
  starting transfers between devices  10.9 us (29%)
  waiting for transfers between devices  7.62 us (20%)
  local copies, waits for them, and re-layouts  4.43 us (12%)
  other arithmetic  0.79 us (2%)
    all_to_all x2, starting transfers between devices, exchanged(): lax.all_to_all(pieces, axes, 0, 0, tiled=True).reshape(slot_total, LANES)  10.9 us
    all_to_all x2, waiting for transfers between devices, exchanged(): lax.all_to_all(pieces, axes, 0, 0, tiled=True).reshape(slot_total, LANES)  7.62 us
    pallas_call x2, Pallas kernels, bulk(): pl.pallas_call(functools.partial(bulk_kernel, first), out_shape=[jax.Shap...  6.13 us
    unnamed x26, local copies, waits for them, and re-layouts  4.29 us
    pallas_call x1, Pallas kernels, per_device(): pl.pallas_call(pack_kernel, out_shape=[jax.ShapeDtypeStruct((slot_total,...  3.86 us
    pallas_call x1, Pallas kernels, per_device(): pl.pallas_call(finish_kernel, out_shape=jax.ShapeDtypeStruct(tracers.shap...  1.95 us
    pallas_call x1, Pallas kernels, per_device(): pl.pallas_call(route_kernel, grid=(device_count // PARTS,), out_shape=jax...  1.37 us
  transfers between devices with their start and end apart: 2, of which 2 were waited for; matrix products, arithmetic and copies ran while one was open for 2% of the time, Pallas kernels for 16%

profile of v5, /device:TPU:0, one launch (start us, length us, event | category | flops | bytes accessed | tf_op | source)
XLA Modules:
  0.0 37.2 jit_solution(13844821017926454957)
XLA Ops:
  0.0 0.0 copy-start.12
  0.0 3.9 %shard_map.73 = (f32[320,128]{1,0:T(8,128)}, f32[3,40,128]{2,1,0:T(8,128)}) custom-call(f32[10,4,5400]{2,1,0:T(4,128)} %tracer_ref.5, f32[10,4,5400]{2,1,0:T(4,128)} %velocity_ref.5, f32[10,5400]{1,0:T(8,128)} %depth_ref.5), custom_call_target="tpu_custom_call" | custom-call | flops 4000000 | bytes 2400000 | tf_op jit(solution)/shard_map/pallas_call | solution.py:476
  3.9 0.0 copy-start.2
  3.9 0.0 copy-start.3
  3.9 7.3 %all-to-all-start = ((f32[32,10,1,128]{3,2,1,0:T(1,128)}), f32[32,10,1,128]{3,2,1,0:T(1,128)S(1)}, u32[]{:S(2)}, u32[]{:S(2)}) async-start(f32[32,10,1,128]{3,2,1,0:T(1,128)} %bitcast.9), calls=%async_computation | async-start | bytes 327680 | tf_op jit(solution)/shard_map/all_to_all | solution.py:474
  11.2 0.0 copy-done.12
  11.2 0.0 copy-done.11
  11.3 0.0 copy-done.10
  11.3 0.4 %select_reduce_fusion.1 = s32[160,5]{0,1:T(8,128)S(1)} fusion(s32[160]{0:T(256)S(1)} %copy-done.10, s32[160,5]{0,1:T(8,128)S(1)} %pad_add_fusion), kind=kLoop, calls=%fused_computation.1 | loop fusion | flops 383200 | bytes 7040 | tf_op jit(solution)/shard_map/reduce_max | solution.py:448
  11.7 0.1 iota_compare_fusion.1
  11.8 0.3 select_reduce_fusion
  12.1 0.1 copy.17.code_ref
  12.2 0.0 copy-done
  12.3 0.0 copy-done.1
  12.3 0.0 copy-done.2
  12.3 0.0 copy-done.3
  12.3 0.0 copy-start.4
  12.3 0.8 %copy-done.4 = f32[3,40,128]{2,1,0:T(8,128)S(1)} copy-done((f32[3,40,128]{2,1,0:T(8,128)S(1)}, f32[3,40,128]{2,1,0:T(8,128)}, u32[]{:S(2)}) %copy-start.4) | copy-done | bytes 61464
  13.1 3.6 %shard_map.74 = (f32[24,5400]{1,0:T(8,128)S(1)}, f32[25,24,128]{2,1,0:T(8,128)S(1)}) custom-call(s32[1]{0:T(128)} %bitcast.my_ref.part_ref, f32[10,4,5400]{2,1,0:T(4,128)S(1)} %copy-done, f32[10,4,5400]{2,1,0:T(4,128)S(1)} %copy-done.1, f32[10,5400]{1,0:T(8,128)S(1)} %copy-done.2, f32[10,5400]{1,0:T(8,128)S(1)} %copy-done.3, s32[320,6]{1,0:T(8,128)S(1)} %copy.17.code_ref, ...), custom_call_target="tpu_custom_call" | custom-call | flops 12000000 | bytes 2400000 | tf_op jit(solution)/shard_map/pallas_call | solution.py:496
  16.7 0.0 copy-start.6
  16.7 0.8 %copy-done.6 = f32[24,5400]{1,0:T(8,128)} copy-done((f32[24,5400]{1,0:T(8,128)}, f32[24,5400]{1,0:T(8,128)S(1)}, u32[]{:S(2)}) %copy-start.6) | copy-done | bytes 518424
  17.5 2.3 %all-to-all-done = f32[32,10,1,128]{3,2,1,0:T(1,128)S(1)} async-done(((f32[32,10,1,128]{3,2,1,0:T(1,128)}), f32[32,10,1,128]{3,2,1,0:T(1,128)S(1)}, u32[]{:S(2)}, u32[]{:S(2)}) %all-to-all-start) | async-done | bytes 163872 | tf_op jit(solution)/shard_map/all_to_all | solution.py:474
  19.8 1.4 %shard_map.75.after_ref = f32[320,128]{1,0:T(8,128)} custom-call(s32[1]{0:T(128)} %bitcast.my_ref.part_ref, s32[320,6]{1,0:T(8,128)S(1)} %copy.17.code_ref, f32[320,128]{1,0:T(8,128)S(1)} %bitcast.8, f32[25,24,128]{2,1,0:T(8,128)S(1)} %get-tuple-element.13.after_ref.edge_a_ref), custom_call_target="tpu_custom_call" | custom-call | tf_op jit(solution)/shard_map/pallas_call | solution.py:524
  21.2 3.6 %all-to-all-start.1 = ((f32[32,10,1,128]{3,2,1,0:T(1,128)}), f32[32,10,1,128]{3,2,1,0:T(1,128)S(1)}, u32[]{:S(2)}, u32[]{:S(2)}) async-start(f32[32,10,1,128]{3,2,1,0:T(1,128)} %bitcast.5), calls=%async_computation.1 | async-start | bytes 327680 | tf_op jit(solution)/shard_map/all_to_all | solution.py:474
  24.7 0.0 copy-done.5
  24.7 2.5 %shard_map.76 = (f32[16,5400]{1,0:T(8,128)S(1)}, f32[25,16,128]{2,1,0:T(8,128)S(1)}) custom-call(s32[1]{0:T(128)} %bitcast.my_ref.part_ref, f32[10,4,5400]{2,1,0:T(4,128)S(1)} %copy-done, f32[10,4,5400]{2,1,0:T(4,128)S(1)} %copy-done.1, f32[10,5400]{1,0:T(8,128)S(1)} %copy-done.2, f32[10,5400]{1,0:T(8,128)S(1)} %copy-done.3, s32[320,6]{1,0:T(8,128)S(1)} %copy.17.code_ref, ...), custom_call_target="tpu_custom_call" | custom-call | flops 8000000 | bytes 1600000 | tf_op jit(solution)/shard_map/pallas_call | solution.py:496
  27.3 0.0 copy-start.8
  27.3 0.7 %copy-done.8 = f32[25,16,128]{2,1,0:T(8,128)} copy-done((f32[25,16,128]{2,1,0:T(8,128)}, f32[25,16,128]{2,1,0:T(8,128)S(1)}, u32[]{:S(2)}) %copy-start.8) | copy-done | bytes 204824
  28.0 5.3 %all-to-all-done.1 = f32[32,10,1,128]{3,2,1,0:T(1,128)S(1)} async-done(((f32[32,10,1,128]{3,2,1,0:T(1,128)}), f32[32,10,1,128]{3,2,1,0:T(1,128)S(1)}, u32[]{:S(2)}, u32[]{:S(2)}) %all-to-all-start.1) | async-done | bytes 163872 | tf_op jit(solution)/shard_map/all_to_all | solution.py:474
  33.3 1.0 %copy-done.7 = f32[24,5400]{1,0:T(8,128)S(1)} copy-done((f32[24,5400]{1,0:T(8,128)S(1)}, f32[24,5400]{1,0:T(8,128)}, u32[]{:S(2)}) %copy-start.7) | copy-done | bytes 518424
  34.4 0.9 %copy-done.9 = f32[25,16,128]{2,1,0:T(8,128)S(1)} copy-done((f32[25,16,128]{2,1,0:T(8,128)S(1)}, f32[25,16,128]{2,1,0:T(8,128)}, u32[]{:S(2)}) %copy-start.9) | copy-done | bytes 204824
  35.3 2.0 %shard_map.77 = f32[10,4,5400]{2,1,0:T(4,128)} custom-call(f32[320,128]{1,0:T(8,128)S(1)} %bitcast.7, f32[25,24,128]{2,1,0:T(8,128)S(1)} %get-tuple-element.13.after_ref.edge_a_ref, f32[25,16,128]{2,1,0:T(8,128)S(1)} %copy-done.9, f32[24,5400]{1,0:T(8,128)S(1)} %copy-done.7, f32[16,5400]{1,0:T(8,128)S(1)} %get-tuple-element.16.base_b_ref), custom_call_target="tpu_custom_call" | custom-call | tf_op jit(solution)/shard_map/pallas_call | solution.py:541
  (9 shorter events, 0.0 us)
Async XLA Ops:
  0.0 11.2 %copy-start.12 = (s32[160]{0:T(256)S(1)}, s32[160]{0:T(256)}, u32[]{:S(2)}) copy-start(s32[160]{0:T(256)} %param.13) | copy-start | bytes 1924
  0.0 11.2 %copy-start.11 = (s32[160,4]{0,1:T(4,128)S(1)}, s32[160,4]{0,1:T(4,128)}, u32[]{:S(2)}) copy-start(s32[160,4]{0,1:T(4,128)} %param.12) | copy-start | bytes 7684
  0.0 11.3 %copy-start.10 = (s32[160]{0:T(256)S(1)}, s32[160]{0:T(256)}, u32[]{:S(2)}) copy-start(s32[160]{0:T(256)} %param.11) | copy-start | bytes 1924
  0.0 12.2 %copy-start = (f32[10,4,5400]{2,1,0:T(4,128)S(1)}, f32[10,4,5400]{2,1,0:T(4,128)}, u32[]{:S(2)}) copy-start(f32[10,4,5400]{2,1,0:T(4,128)} %tracer_ref.5) | copy-start | bytes 2592004
  0.0 12.2 %copy-start.1 = (f32[10,4,5400]{2,1,0:T(4,128)S(1)}, f32[10,4,5400]{2,1,0:T(4,128)}, u32[]{:S(2)}) copy-start(f32[10,4,5400]{2,1,0:T(4,128)} %velocity_ref.5) | copy-start | bytes 2592004
  3.9 8.4 %copy-start.2 = (f32[10,5400]{1,0:T(8,128)S(1)}, f32[10,5400]{1,0:T(8,128)}, u32[]{:S(2)}) copy-start(f32[10,5400]{1,0:T(8,128)} %depth_ref.5) | copy-start | bytes 648004
  3.9 8.4 %copy-start.3 = (f32[10,5400]{1,0:T(8,128)S(1)}, f32[10,5400]{1,0:T(8,128)}, u32[]{:S(2)}) copy-start(f32[10,5400]{1,0:T(8,128)} %kappa_ref.3) | copy-start | bytes 648004
  3.9 15.9 %all-to-all-start = ((f32[32,10,1,128]{3,2,1,0:T(1,128)}), f32[32,10,1,128]{3,2,1,0:T(1,128)S(1)}, u32[]{:S(2)}, u32[]{:S(2)}) async-start(f32[32,10,1,128]{3,2,1,0:T(1,128)} %bitcast.9), calls=%async_computation | async-start | bytes 327680 | tf_op jit(solution)/shard_map/all_to_all | solution.py:474
  12.3 0.8 %copy-start.4 = (f32[3,40,128]{2,1,0:T(8,128)S(1)}, f32[3,40,128]{2,1,0:T(8,128)}, u32[]{:S(2)}) copy-start(f32[3,40,128]{2,1,0:T(8,128)} %get-tuple-element.12.own_ref.after_ref) | copy-start | bytes 184324
  16.7 0.8 %copy-start.6 = (f32[24,5400]{1,0:T(8,128)}, f32[24,5400]{1,0:T(8,128)S(1)}, u32[]{:S(2)}) copy-start(f32[24,5400]{1,0:T(8,128)S(1)} %get-tuple-element.15.base_a_ref) | copy-start | bytes 1555204
  17.5 7.2 %copy-start.5 = (f32[3,40,128]{2,1,0:T(8,128)S(1)}, f32[3,40,128]{2,1,0:T(8,128)}, u32[]{:S(2)}) copy-start(f32[3,40,128]{2,1,0:T(8,128)} %get-tuple-element.12.own_ref.after_ref) | copy-start | bytes 184324
  21.2 12.1 %all-to-all-start.1 = ((f32[32,10,1,128]{3,2,1,0:T(1,128)}), f32[32,10,1,128]{3,2,1,0:T(1,128)S(1)}, u32[]{:S(2)}, u32[]{:S(2)}) async-start(f32[32,10,1,128]{3,2,1,0:T(1,128)} %bitcast.5), calls=%async_computation.1 | async-start | bytes 327680 | tf_op jit(solution)/shard_map/all_to_all | solution.py:474
  27.3 0.7 %copy-start.8 = (f32[25,16,128]{2,1,0:T(8,128)}, f32[25,16,128]{2,1,0:T(8,128)S(1)}, u32[]{:S(2)}) copy-start(f32[25,16,128]{2,1,0:T(8,128)S(1)} %get-tuple-element.14.edge_b_ref) | copy-start | bytes 614404
  33.3 1.0 %copy-start.7 = (f32[24,5400]{1,0:T(8,128)S(1)}, f32[24,5400]{1,0:T(8,128)}, u32[]{:S(2)}) copy-start(f32[24,5400]{1,0:T(8,128)} %copy-done.6) | copy-start | bytes 1555204
  34.4 0.9 %copy-start.9 = (f32[25,16,128]{2,1,0:T(8,128)S(1)}, f32[25,16,128]{2,1,0:T(8,128)}, u32[]{:S(2)}) copy-start(f32[25,16,128]{2,1,0:T(8,128)} %copy-done.8) | copy-start | bytes 614404

commit v6 on v5

--- a/solution.py
+++ b/solution.py
@@ -23,7 +23,7 @@
 SCALE = COURANT / 12.0
 SIDES = 3
 OWN = 8
-FIRST_PAIRS = 3
+FIRST_PAIRS = 2
 
 
 def lane_of(rows):
@@ -105,6 +105,12 @@
     return get
 
 
+def across_pair(get):
+    lane = lane_of(8)
+    groups = gap_groups(get, -2, 4, 8)
+    return lane_pick(groups, 4 * (lane // 2) + 1 + lane % 2), lane_pick(groups, 4 * (lane // 2) + 3 * (lane % 2))
+
+
 def joined(south, north, half, rows):
     if half == 0:
         return jnp.where(lane_of(rows) < 64, south, rot(north, 64))
@@ -119,8 +125,7 @@
     return copies
 
 
-def pack_kernel(tracer_ref, velocity_ref, depth_ref, out_ref, own_ref,
-                x_ref, v_ref, d_ref, strip_ref, x_sems, v_sems, d_sem):
+def pack_kernel(tracer_ref, velocity_ref, depth_ref, out_ref, x_ref, v_ref, d_ref, strip_ref, x_sems, v_sems, d_sem):
     count = depth_ref.shape[0]
     pairs = count // 2
     x_copies = pair_copies(tracer_ref, x_ref, x_sems, 0, pairs)
@@ -130,14 +135,11 @@
         x_copies[pair].start()
         v_copies[pair].start()
     d_copy.start()
-    lane = lane_of(8)
     for pair in range(pairs):
         rows = pl.ds(8 * pair, 8)
         x_copies[pair].wait()
         get_x = tile_getter(x_ref, rows, 8)
-        groups = gap_groups(get_x, -2, 4, 8)
-        near = lane_pick(groups, 4 * (lane // 2) + 1 + lane % 2)
-        far = lane_pick(groups, 4 * (lane // 2) + 3 * (lane % 2))
+        near, far = across_pair(get_x)
         south = [window(get_x, 0, 8), window(get_x, IB, 8)]
         north = [window(get_x, CELLS - IB, 8), window(get_x, CELLS - 2 * IB, 8)]
         v_copies[pair].wait()
@@ -146,11 +148,9 @@
         strips = [joined(south[0], north[0], half, 8) for half in range(2)]
         strips += [joined(south[1], north[1], half, 8) for half in range(2)]
         strips += [joined(v_south, v_north, half, 8) for half in range(2)]
+        strips += [near, far, gap_groups(get_v, -1, 2, 8)[0]]
         for index, strip in enumerate(strips):
             strip_ref[index, rows, :] = strip
-        own_ref[0, rows, :] = near
-        own_ref[1, rows, :] = far
-        own_ref[2, rows, :] = gap_groups(get_v, -1, 2, 8)[0]
 
     d_copy.wait()
     if out_ref.shape[0] > PARTS * count:
@@ -176,10 +176,10 @@
                 put(part, value)
             if chan >= 2:
                 put(2 * (8 + chan - 2) + half, strip_ref[4 + half, rows, :])
-        put(X_PART + chan, own_ref[0, rows, :])
-        put(X_PART + 4 + chan, own_ref[1, rows, :])
+        put(X_PART + chan, strip_ref[6, rows, :])
+        put(X_PART + 4 + chan, strip_ref[7, rows, :])
         if chan < 2:
-            put(X_PART + 8 + chan, own_ref[2, rows, :])
+            put(X_PART + 8 + chan, strip_ref[8, rows, :])
     for half in range(2):
         put(20 + half, joined(d_south, d_north, half, count))
 
@@ -207,11 +207,11 @@
     out_ref[...] = jnp.where(along_x, x_side, y_side)
 
 
-def bulk_kernel(first, my_ref, tracer_ref, velocity_ref, depth_ref, kappa_ref, code_ref, own_ref, after_ref,
-                base_ref, edge_ref, x_ref, v_ref, d_ref, k_ref, d8_ref, k8_ref, w_ref, z_ref, x_sems, v_sems, d_sems):
+def bulk_kernel(first, my_ref, tracer_ref, velocity_ref, depth_ref, kappa_ref, code_ref, after_ref,
+                base_ref, edge_ref, y_ref, x_ref, v_ref, d_ref, k_ref, d8_ref, k8_ref, w_ref, z_ref, x_sems, v_sems, y_sems, d_sems):
     del after_ref
     count = depth_ref.shape[0]
-    pairs = base_ref.shape[0] // 8
+    pairs = edge_ref.shape[1] // 8
     x_copies = pair_copies(tracer_ref, x_ref, x_sems, first, pairs)
     v_copies = pair_copies(velocity_ref, v_ref, v_sems, first, pairs)
     d_copy = pltpu.make_async_copy(depth_ref, d_ref, d_sems.at[0])
@@ -314,15 +314,17 @@
             other = jnp.where(even, sublanes(explicit, -1), sublanes(explicit, 1))
             value = jnp.where(live, explicit + ratio(tile) * (other - explicit), zero)
             stop = min((tile + 1) * LANES, CELLS)
-            base_ref[rows, tile * LANES : stop] = value[:, : stop - tile * LANES]
+            y_ref[rows, tile * LANES : stop] = value[:, : stop - tile * LANES]
             mixed = jnp.where(x_row, face(tile), jnp.where(even, ratio(tile), depth(tile)))
             z_ref[:, tile * LANES : (tile + 1) * LANES] = mixed
 
+        pltpu.make_async_copy(
+            y_ref.at[rows].reshape(2, 4, CELLS), base_ref.at[pl.ds(slot, 2)], y_sems.at[pair]).start()
         get_w, get_z = [lambda tile, ref=ref: ref[:, tile * LANES : (tile + 1) * LANES] for ref in (w_ref, z_ref)]
         groups = gap_groups(get_z, -2, 4, 8)
         east = lane % 2 == 0
-        own_rows = pl.ds(pl.multiple_of(8 * (first + pair), 8), 8)
-        near, far, normal = [own_ref[index, own_rows, :] for index in range(3)]
+        near, far = across_pair(state)
+        normal = gap_groups(velocity, -1, 2, 8)[0]
         normal = jnp.where(x_row, normal, sublanes(normal, 2))
         rim_speed = lane_pick(groups, 4 * (lane // 2) + 2 * (lane % 2))
         rim_speed = jnp.where(x_row, rim_speed, sublanes(rim_speed, 2))
@@ -344,23 +346,27 @@
         edge_ref[OWN * SIDES, rows, :] = jnp.where(folded, 1.0, zero)
 
     pl.loop(0, pairs)(one_pair)
-
-
-def finish_kernel(halo_ref, edge_a_ref, edge_b_ref, base_a_ref, base_b_ref, out_ref,
-                  y_ref, raw_ref, delta_ref, in_sems, out_sems):
+    for pair in range(pairs):
+        slots = pl.ds(2 * (first + pair), 2)
+        rows = y_ref.at[pl.ds(8 * pair, 8)].reshape(2, 4, CELLS)
+        pltpu.make_async_copy(rows, base_ref.at[slots], y_sems.at[pair]).wait()
+
+
+def finish_kernel(halo_ref, edge_a_ref, edge_b_ref, base_ref, out_ref,
+                  y_ref, own_ref, raw_ref, delta_ref, own_sems, in_sems, out_sems):
     count = out_ref.shape[0]
     pairs = count // 2
     rows = 4 * count
-    split = base_a_ref.shape[0]
-    a_copy = pltpu.make_async_copy(base_a_ref, y_ref.at[pl.ds(0, split)], in_sems.at[0])
-    b_copy = pltpu.make_async_copy(base_b_ref, y_ref.at[pl.ds(split, rows - split)], in_sems.at[1])
-    a_copy.start()
-    b_copy.start()
+    split = edge_a_ref.shape[1]
+    own_copies = [
+        pltpu.make_async_copy(edge_a_ref, own_ref.at[:, pl.ds(0, split)], own_sems.at[0]),
+        pltpu.make_async_copy(edge_b_ref, own_ref.at[:, pl.ds(split, rows - split)], own_sems.at[1]),
+    ]
+    in_copies = pair_copies(base_ref, y_ref, in_sems, 0, pairs)
+    for copy in own_copies + in_copies:
+        copy.start()
     lane = lane_of(rows)
     level = (lax.broadcasted_iota(jnp.int32, (rows, LANES), 0) % 2).astype(jnp.float32)
-
-    def own(index):
-        return jnp.concatenate([edge_a_ref[index], edge_b_ref[index]], axis=0)
 
     def part(index):
         return halo_ref[index * count : (index + 1) * count, :]
@@ -370,7 +376,6 @@
             raw_ref[index, pl.ds(chan, count, stride=4), :] = value
         return raw_ref[index]
 
-    folded = own(OWN * SIDES) > 0.0
     mirror = jnp.where(lane < IB, IB - 1 - lane, lane)
     slot_lane = lane_of(count)
     depth_x = rot(part(0), -SPARE)
@@ -379,20 +384,25 @@
     x_raw = [[part(X_PART + chan) for chan in range(4)], [part(X_PART + 4 + chan) for chan in range(4)],
              [part(X_PART + 8 + chan % 2) for chan in range(4)], [depth_x] * 4]
     y_values = [list(range(4)), list(range(4, 8)), [8, 9, 8, 9], [10] * 4]
-    x_halo, south_halo, north_halo = [], [], []
+    x_halo, south_halo, north_raw = [], [], []
     for kind in range(4):
         raw = assembled(3 * kind, x_raw[kind])
         x_halo.append(jnp.where(lane % 2 == 0, rot(raw, 1), rot(raw, -1)))
         first, second = [assembled(3 * kind + 1 + half, [part(2 * value + half) for value in y_values[kind]])
                          for half in range(2)]
         south_halo.append(jnp.where(lane < HALF, rot(first, 64), rot(second, 64 + HALF)))
-        raw = jnp.where(lane < HALF, first, rot(second, HALF))
+        north_raw.append(jnp.where(lane < HALF, first, rot(second, HALF)))
+    for copy in own_copies:
+        copy.wait()
+    folded = own_ref[OWN * SIDES] > 0.0
+    north_halo = []
+    for kind, raw in enumerate(north_raw):
         turned = lane_take(raw, mirror)
         north_halo.append(jnp.where(folded, -turned if kind == 2 else turned, raw))
 
     for side, (out_near, out_far, out_normal, out_depth) in enumerate((x_halo, south_halo, north_halo)):
         near, far, normal, rim_speed, wet, inner_wet, ratio, inner_ratio = [
-            own(OWN * side + index) for index in range(OWN)]
+            own_ref[OWN * side + index] for index in range(OWN)]
         if side == 0:
             out_normal = jnp.where(lane % 2 == 0, -out_normal, out_normal)
             beyond = out_near - jnp.where(lane % 2 == 0, rot(near, -1), rot(near, 1))
@@ -409,11 +419,10 @@
             delta_ref[2 * side + place] = change + share * (other - change)
 
     lane = lane_of(8)
-    a_copy.wait()
-    b_copy.wait()
     out_copies = []
     for pair in range(pairs):
         mine = pl.ds(8 * pair, 8)
+        in_copies[pair].wait()
         near, deep, south, south_in, north, north_in = [delta_ref[index, mine, :] for index in range(2 * SIDES)]
         groups = []
         for at in range(2):
@@ -473,16 +482,16 @@
         pieces = pieces.reshape(device_count, slot_count, 1, LANES)
         return lax.all_to_all(pieces, axes, 0, 0, tiled=True).reshape(slot_total, LANES)
 
-    pack, own = pl.pallas_call(
+    pack = pl.pallas_call(
         pack_kernel,
-        out_shape=[jax.ShapeDtypeStruct((slot_total, LANES), f32), jax.ShapeDtypeStruct((3, state_rows, LANES), f32)],
+        out_shape=jax.ShapeDtypeStruct((slot_total, LANES), f32),
         in_specs=[in_hbm, in_hbm, in_hbm],
-        out_specs=[in_vmem, in_vmem],
+        out_specs=in_vmem,
         scratch_shapes=[
             pltpu.VMEM((state_rows, CELLS), f32),
             pltpu.VMEM((state_rows, CELLS), f32),
             pltpu.VMEM((slot_count, CELLS), f32),
-            pltpu.VMEM((6, state_rows, LANES), f32),
+            pltpu.VMEM((9, state_rows, LANES), f32),
             dma((pairs,)),
             dma((pairs,)),
             dma,
@@ -492,16 +501,21 @@
     held = exchanged(pack)
     codes = route_codes(block_owner, neighbours, fold_partner, slot_total)
 
-    def bulk(first, some, after):
+    def bulk(first, some, after, base):
+        kernel = functools.partial(bulk_kernel, first)
+        extra = [] if base is None else [base]
+        if extra:
+            kernel = lambda *refs: bulk_kernel(first, *refs[:7], *refs[8:])
         return pl.pallas_call(
-            functools.partial(bulk_kernel, first),
+            kernel,
             out_shape=[
-                jax.ShapeDtypeStruct((8 * some, CELLS), f32),
+                jax.ShapeDtypeStruct(tracers.shape, f32),
                 jax.ShapeDtypeStruct((OWN * SIDES + 1, 8 * some, LANES), f32),
             ],
-            in_specs=[in_smem, in_hbm, in_hbm, in_hbm, in_hbm, in_vmem, in_vmem, anywhere],
-            out_specs=[in_vmem, in_vmem],
+            in_specs=[in_smem, in_hbm, in_hbm, in_hbm, in_hbm, in_vmem, anywhere] + [in_hbm] * len(extra),
+            out_specs=[in_hbm, in_vmem],
             scratch_shapes=[
+                pltpu.VMEM((8 * some, CELLS), f32),
                 pltpu.VMEM((8 * some, CELLS), f32),
                 pltpu.VMEM((8 * some, CELLS), f32),
                 pltpu.VMEM((slot_count, CELLS), f32),
@@ -512,13 +526,14 @@
                 pltpu.VMEM((8, WIDE), f32),
                 dma((some,)),
                 dma((some,)),
+                dma((some,)),
                 dma((2,)),
             ],
-            compiler_params=limit,
+            input_output_aliases={7: 0} if extra else {},
             cost_estimate=pl.CostEstimate(flops=4_000_000 * some, bytes_accessed=800_000 * some, transcendentals=0),
-        )(my_index, tracers, velocity, kmt, kappa, codes, own, after)
-
-    base_a, edge_a = bulk(0, FIRST_PAIRS, own)
+        )(my_index, tracers, velocity, kmt, kappa, codes, after, *extra)
+
+    base, edge_a = bulk(0, FIRST_PAIRS, pack, None)
 
     routed_rows = PARTS * slot_count
     routed = pl.pallas_call(
@@ -535,23 +550,26 @@
         compiler_params=limit,
     )(my_index, codes, held, edge_a)
 
-    base_b, edge_b = bulk(FIRST_PAIRS, pairs - FIRST_PAIRS, routed)
+    base, edge_b = bulk(FIRST_PAIRS, pairs - FIRST_PAIRS, routed, base)
     halo = exchanged(routed)[: PARTS * slot_count]
 
     return pl.pallas_call(
         finish_kernel,
         out_shape=jax.ShapeDtypeStruct(tracers.shape, f32),
-        in_specs=[in_vmem, in_vmem, in_vmem, anywhere, anywhere],
+        in_specs=[in_vmem, anywhere, anywhere, in_hbm],
         out_specs=in_hbm,
         scratch_shapes=[
             pltpu.VMEM((state_rows, CELLS), f32),
+            pltpu.VMEM((OWN * SIDES + 1, state_rows, LANES), f32),
             pltpu.VMEM((12, state_rows, LANES), f32),
             pltpu.VMEM((2 * SIDES, state_rows, LANES), f32),
             dma((2,)),
             dma((pairs,)),
+            dma((pairs,)),
         ],
+        input_output_aliases={3: 0},
         compiler_params=limit,
-    )(halo, edge_a, edge_b, base_a, base_b)
+    )(halo, edge_a, edge_b, base)
 
 
 def solution(mesh):

time: 37.6 us -> 39.2 us (1.043)
  Pallas kernels: 13.3 us -> 20.2 us
  waiting for transfers between devices: 7.62 us -> 3.13 us
  local copies, waits for them, and re-layouts: 4.43 us -> 2.72 us
  starting transfers between devices: 10.9 us -> 11.8 us
    pallas_call x3, Pallas kernels: 9.99 us -> 16.1 us  [the longest x2 12.3 us: bulk(): pl.pallas_call(kernel, out_shape=[jax.ShapeDtypeStruct(tracers.shape, f32...]
    all_to_all x2, waiting for transfers between devices: 7.62 us -> 3.13 us  [exchanged(): lax.all_to_all(pieces, axes, 0, 0, tiled=True).reshape(slot_total, LANES)]
    unnamed x26 -> x14, local copies, waits for them, and re-layouts: 4.29 us -> 1.92 us
    all_to_all x2, starting transfers between devices: 10.9 us -> 11.8 us  [exchanged(): lax.all_to_all(pieces, axes, 0, 0, tiled=True).reshape(slot_total, LANES)]
    pallas_call x1, Pallas kernels: 1.95 us -> 2.77 us  [per_device(): pl.pallas_call(finish_kernel, out_shape=jax.ShapeDtypeStruct(tracers.shap...]
    reduce_max x1, local copies, waits for them, and re-layouts: 0.14 us -> 0.8 us  [route_codes(): return jnp.max(jnp.where(hits[:, :, None], link_slots[None], -1), axis=1)]
  transfers between devices with their start and end apart: 2 -> 2, of which waited for: 2 -> 2; matrix products, arithmetic and copies ran while one was open for 2% -> 4% of each run, Pallas kernels for 16% -> 32%
where the time goes in v6:
time: 39.2 us; the launch traced here: 38.8 us
  Pallas kernels  20.2 us (52%)
  starting transfers between devices  11.8 us (30%)
  waiting for transfers between devices  3.13 us (8%)
  local copies, waits for them, and re-layouts  2.72 us (7%)
  other arithmetic  0.79 us (2%)
    pallas_call x2, Pallas kernels, bulk(): pl.pallas_call(kernel, out_shape=[jax.ShapeDtypeStruct(tracers.shape, f32...  12.3 us
    all_to_all x2, starting transfers between devices, exchanged(): lax.all_to_all(pieces, axes, 0, 0, tiled=True).reshape(slot_total, LANES)  11.8 us
    pallas_call x1, Pallas kernels, per_device(): pl.pallas_call(pack_kernel, out_shape=jax.ShapeDtypeStruct((slot_total, L...  3.75 us
    all_to_all x2, waiting for transfers between devices, exchanged(): lax.all_to_all(pieces, axes, 0, 0, tiled=True).reshape(slot_total, LANES)  3.13 us
    pallas_call x1, Pallas kernels, per_device(): pl.pallas_call(finish_kernel, out_shape=jax.ShapeDtypeStruct(tracers.shap...  2.77 us
    unnamed x14, local copies, waits for them, and re-layouts  1.92 us
    pallas_call x1, Pallas kernels, per_device(): pl.pallas_call(route_kernel, grid=(device_count // PARTS,), out_shape=jax...  1.37 us
    reduce_max x1, local copies, waits for them, and re-layouts, route_codes(): return jnp.max(jnp.where(hits[:, :, None], link_slots[None], -1), axis=1)  0.8 us
  transfers between devices with their start and end apart: 2, of which 2 were waited for; matrix products, arithmetic and copies ran while one was open for 4% of the time, Pallas kernels for 32%

profile of v6, /device:TPU:0, one launch (start us, length us, event | category | flops | bytes accessed | tf_op | source)
XLA Modules:
  0.0 38.8 jit_solution(14305191244299962386)
XLA Ops:
  0.0 0.0 copy-start.6
  0.0 0.0 copy-start.5
  0.0 0.0 copy-start.4
  0.0 3.8 %shard_map.73.after_ref = f32[320,128]{1,0:T(8,128)} custom-call(f32[10,4,5400]{2,1,0:T(4,128)} %refs_1_.1, f32[10,4,5400]{2,1,0:T(4,128)} %refs_2_.1, f32[10,5400]{1,0:T(8,128)} %refs_3_.1), custom_call_target="tpu_custom_call" | custom-call | flops 4000000 | bytes 2400000 | tf_op jit(solution)/shard_map/pallas_call | solution.py:485
  3.8 7.3 %all-to-all-start = ((f32[32,10,1,128]{3,2,1,0:T(1,128)}), f32[32,10,1,128]{3,2,1,0:T(1,128)S(1)}, u32[]{:S(2)}, u32[]{:S(2)}) async-start(f32[32,10,1,128]{3,2,1,0:T(1,128)} %bitcast.9), calls=%async_computation | async-start | bytes 327680 | tf_op jit(solution)/shard_map/all_to_all | solution.py:483
  11.1 0.0 copy-done.6
  11.1 0.0 copy-done.5
  11.1 0.0 copy-done.4
  11.1 0.4 %select_reduce_fusion.1 = s32[160,5]{0,1:T(8,128)S(1)} fusion(s32[160]{0:T(256)S(1)} %copy-done.4, s32[160,5]{0,1:T(8,128)S(1)} %pad_add_fusion), kind=kLoop, calls=%fused_computation.1 | loop fusion | flops 383200 | bytes 7040 | tf_op jit(solution)/shard_map/reduce_max | solution.py:457
  11.6 0.1 iota_compare_fusion.1
  11.7 0.3 select_reduce_fusion
  11.9 0.8 %copy.19.code_ref.refs_5_ = s32[320,6]{1,0:T(8,128)} copy(s32[320,6]{0,1:T(8,128)S(1)} %select_reduce_fusion) | data formatting | bytes 15360 | tf_op jit(solution)/shard_map/reduce_max | solution.py:459
  12.7 0.0 copy-start
  12.7 5.6 %shard_map.74 = (f32[10,4,5400]{2,1,0:T(4,128)}, f32[25,16,128]{2,1,0:T(8,128)}) custom-call(s32[1]{0:T(128)} %bitcast.my_ref.part_ref.refs_0_, f32[10,4,5400]{2,1,0:T(4,128)} %refs_1_.1, f32[10,4,5400]{2,1,0:T(4,128)} %refs_2_.1, f32[10,5400]{1,0:T(8,128)} %refs_3_.1, f32[10,5400]{1,0:T(8,128)} %refs_4_.1, s32[320,6]{1,0:T(8,128)} %copy.19.code_ref.refs_5_, ...), custom_call_target="tpu_custom_call" | custom-call | flops 8000000 | bytes 1600000 | tf_op jit(solution)/shard_map/pallas_call | solution.py:509
  18.3 1.3 %all-to-all-done = f32[32,10,1,128]{3,2,1,0:T(1,128)S(1)} async-done(((f32[32,10,1,128]{3,2,1,0:T(1,128)}), f32[32,10,1,128]{3,2,1,0:T(1,128)S(1)}, u32[]{:S(2)}, u32[]{:S(2)}) %all-to-all-start) | async-done | bytes 163872 | tf_op jit(solution)/shard_map/all_to_all | solution.py:483
  19.7 0.0 copy-done
  19.7 0.0 copy-start.1
  19.7 0.9 %copy-done.1 = f32[25,16,128]{2,1,0:T(8,128)S(1)} copy-done((f32[25,16,128]{2,1,0:T(8,128)S(1)}, f32[25,16,128]{2,1,0:T(8,128)}, u32[]{:S(2)}) %copy-start.1) | copy-done | bytes 204824
  20.6 1.4 %shard_map.75.refs_6_ = f32[320,128]{1,0:T(8,128)} custom-call(s32[1]{0:T(128)} %bitcast.my_ref.part_ref.refs_0_, s32[320,6]{1,0:T(8,128)S(1)} %copy-done, f32[320,128]{1,0:T(8,128)S(1)} %bitcast.8, f32[25,16,128]{2,1,0:T(8,128)S(1)} %copy-done.1), custom_call_target="tpu_custom_call" | custom-call | tf_op jit(solution)/shard_map/pallas_call | solution.py:539
  22.0 4.5 %all-to-all-start.1 = ((f32[32,10,1,128]{3,2,1,0:T(1,128)}), f32[32,10,1,128]{3,2,1,0:T(1,128)S(1)}, u32[]{:S(2)}, u32[]{:S(2)}) async-start(f32[32,10,1,128]{3,2,1,0:T(1,128)} %bitcast.5), calls=%async_computation.1 | async-start | bytes 327680 | tf_op jit(solution)/shard_map/all_to_all | solution.py:483
  26.5 0.0 copy-start.2
  26.5 6.8 %shard_map.76 = (f32[10,4,5400]{2,1,0:T(4,128)}, f32[25,24,128]{2,1,0:T(8,128)}) custom-call(s32[1]{0:T(128)} %bitcast.my_ref.part_ref.refs_0_, f32[10,4,5400]{2,1,0:T(4,128)} %refs_1_.1, f32[10,4,5400]{2,1,0:T(4,128)} %refs_2_.1, f32[10,5400]{1,0:T(8,128)} %refs_3_.1, f32[10,5400]{1,0:T(8,128)} %refs_4_.1, ...), custom_call_target="tpu_custom_call", output_to_operand_aliasing={{0}: (7, {})} | custom-call | flops 12000000 | bytes 2400000 | tf_op jit(solution)/shard_map/pallas_call | solution.py:509
  33.3 1.8 %all-to-all-done.1 = f32[32,10,1,128]{3,2,1,0:T(1,128)S(1)} async-done(((f32[32,10,1,128]{3,2,1,0:T(1,128)}), f32[32,10,1,128]{3,2,1,0:T(1,128)S(1)}, u32[]{:S(2)}, u32[]{:S(2)}) %all-to-all-start.1) | async-done | bytes 163872 | tf_op jit(solution)/shard_map/all_to_all | solution.py:483
  35.1 0.0 copy-done.2
  35.1 0.0 copy-start.3
  35.1 1.0 %copy-done.3 = f32[25,24,128]{2,1,0:T(8,128)S(1)} copy-done((f32[25,24,128]{2,1,0:T(8,128)S(1)}, f32[25,24,128]{2,1,0:T(8,128)}, u32[]{:S(2)}) %copy-start.3) | copy-done | bytes 307224
  36.0 2.8 %shard_map.77 = f32[10,4,5400]{2,1,0:T(4,128)} custom-call(f32[320,128]{1,0:T(8,128)S(1)} %bitcast.7, f32[25,16,128]{2,1,0:T(8,128)S(1)} %copy-done.2, f32[25,24,128]{2,1,0:T(8,128)S(1)} %copy-done.3, f32[10,4,5400]{2,1,0:T(4,128)} %get-tuple-element.12.base_ref), custom_call_target="tpu_custom_call", output_to_operand_aliasing={{}: (3, {})} | custom-call | tf_op jit(solution)/shard_map/pallas_call | solution.py:556
  (2 shorter events, 0.0 us)
Async XLA Ops:
  0.0 11.1 %copy-start.6 = (s32[160]{0:T(256)S(1)}, s32[160]{0:T(256)}, u32[]{:S(2)}) copy-start(s32[160]{0:T(256)} %param.13) | copy-start | bytes 1924
  0.0 11.1 %copy-start.5 = (s32[160,4]{0,1:T(4,128)S(1)}, s32[160,4]{0,1:T(4,128)}, u32[]{:S(2)}) copy-start(s32[160,4]{0,1:T(4,128)} %param.12) | copy-start | bytes 7684
  0.0 11.1 %copy-start.4 = (s32[160]{0:T(256)S(1)}, s32[160]{0:T(256)}, u32[]{:S(2)}) copy-start(s32[160]{0:T(256)} %param.11) | copy-start | bytes 1924
  3.8 15.9 %all-to-all-start = ((f32[32,10,1,128]{3,2,1,0:T(1,128)}), f32[32,10,1,128]{3,2,1,0:T(1,128)S(1)}, u32[]{:S(2)}, u32[]{:S(2)}) async-start(f32[32,10,1,128]{3,2,1,0:T(1,128)} %bitcast.9), calls=%async_computation | async-start | bytes 327680 | tf_op jit(solution)/shard_map/all_to_all | solution.py:483
  12.7 6.9 %copy-start = (s32[320,6]{1,0:T(8,128)S(1)}, s32[320,6]{1,0:T(8,128)}, u32[]{:S(2)}) copy-start(s32[320,6]{1,0:T(8,128)} %copy.19.code_ref.refs_5_) | copy-start | bytes 23044
  19.7 0.9 %copy-start.1 = (f32[25,16,128]{2,1,0:T(8,128)S(1)}, f32[25,16,128]{2,1,0:T(8,128)}, u32[]{:S(2)}) copy-start(f32[25,16,128]{2,1,0:T(8,128)} %get-tuple-element.9.after_ref.edge_a_ref) | copy-start | bytes 614404
  22.0 13.1 %all-to-all-start.1 = ((f32[32,10,1,128]{3,2,1,0:T(1,128)}), f32[32,10,1,128]{3,2,1,0:T(1,128)S(1)}, u32[]{:S(2)}, u32[]{:S(2)}) async-start(f32[32,10,1,128]{3,2,1,0:T(1,128)} %bitcast.5), calls=%async_computation.1 | async-start | bytes 327680 | tf_op jit(solution)/shard_map/all_to_all | solution.py:483
  26.5 8.6 %copy-start.2 = (f32[25,16,128]{2,1,0:T(8,128)S(1)}, f32[25,16,128]{2,1,0:T(8,128)}, u32[]{:S(2)}) copy-start(f32[25,16,128]{2,1,0:T(8,128)} %get-tuple-element.9.after_ref.edge_a_ref) | copy-start | bytes 614404
  35.1 1.0 %copy-start.3 = (f32[25,24,128]{2,1,0:T(8,128)S(1)}, f32[25,24,128]{2,1,0:T(8,128)}, u32[]{:S(2)}) copy-start(f32[25,24,128]{2,1,0:T(8,128)} %get-tuple-element.11.edge_b_ref) | copy-start | bytes 921604

commit v7 on v6

--- a/solution.py
+++ b/solution.py
@@ -184,8 +184,7 @@
         put(20 + half, joined(d_south, d_north, half, count))
 
 
-def route_kernel(part_ref, code_ref, held_ref, after_ref, out_ref):
-    del after_ref
+def route_kernel(part_ref, code_ref, held_ref, out_ref):
     total = held_ref.shape[0]
     rows = out_ref.shape[0]
     part = part_ref[0]
@@ -208,8 +207,9 @@
 
 
 def bulk_kernel(first, my_ref, tracer_ref, velocity_ref, depth_ref, kappa_ref, code_ref, after_ref,
-                base_ref, edge_ref, y_ref, x_ref, v_ref, d_ref, k_ref, d8_ref, k8_ref, w_ref, z_ref, x_sems, v_sems, y_sems, d_sems):
+                base_ref, edge_ref, part_ref, y_ref, x_ref, v_ref, d_ref, k_ref, d8_ref, k8_ref, w_ref, z_ref, x_sems, v_sems, y_sems, d_sems):
     del after_ref
+    part_ref[0] = my_ref[0]
     count = depth_ref.shape[0]
     pairs = edge_ref.shape[1] // 8
     x_copies = pair_copies(tracer_ref, x_ref, x_sems, first, pairs)
@@ -511,9 +511,10 @@
             out_shape=[
                 jax.ShapeDtypeStruct(tracers.shape, f32),
                 jax.ShapeDtypeStruct((OWN * SIDES + 1, 8 * some, LANES), f32),
+                jax.ShapeDtypeStruct((1,), jnp.int32),
             ],
             in_specs=[in_smem, in_hbm, in_hbm, in_hbm, in_hbm, in_vmem, anywhere] + [in_hbm] * len(extra),
-            out_specs=[in_hbm, in_vmem],
+            out_specs=[in_hbm, in_vmem, in_smem],
             scratch_shapes=[
                 pltpu.VMEM((8 * some, CELLS), f32),
                 pltpu.VMEM((8 * some, CELLS), f32),
@@ -530,10 +531,11 @@
                 dma((2,)),
             ],
             input_output_aliases={7: 0} if extra else {},
+            compiler_params=limit,
             cost_estimate=pl.CostEstimate(flops=4_000_000 * some, bytes_accessed=800_000 * some, transcendentals=0),
         )(my_index, tracers, velocity, kmt, kappa, codes, after, *extra)
 
-    base, edge_a = bulk(0, FIRST_PAIRS, pack, None)
+    base, edge_a, part = bulk(0, FIRST_PAIRS, pack, None)
 
     routed_rows = PARTS * slot_count
     routed = pl.pallas_call(
@@ -544,13 +546,12 @@
             in_smem,
             pl.BlockSpec((routed_rows, 6), lambda step: (step, 0)),
             pl.BlockSpec((slot_total, LANES), lambda step: (0, 0)),
-            anywhere,
         ],
         out_specs=pl.BlockSpec((routed_rows, LANES), lambda step: (step, 0)),
         compiler_params=limit,
-    )(my_index, codes, held, edge_a)
-
-    base, edge_b = bulk(FIRST_PAIRS, pairs - FIRST_PAIRS, routed, base)
+    )(part, codes, held)
+
+    base, edge_b, _ = bulk(FIRST_PAIRS, pairs - FIRST_PAIRS, routed, base)
     halo = exchanged(routed)[: PARTS * slot_count]
 
     return pl.pallas_call(

time: 39.2 us -> 36.4 us (0.929)
  waiting for transfers between devices: 3.13 us -> 6.44 us
  Pallas kernels: 20.2 us -> 17.4 us
  local copies, waits for them, and re-layouts: 2.72 us -> 1.08 us
  starting transfers between devices: 11.8 us -> 10.3 us
    pallas_call x2, Pallas kernels: 12.3 us -> 8.73 us  [bulk(): pl.pallas_call(kernel, out_shape=[jax.ShapeDtypeStruct(tracers.shape, f32...]
    all_to_all x2, waiting for transfers between devices: 3.13 us -> 6.44 us  [exchanged(): lax.all_to_all(pieces, axes, 0, 0, tiled=True).reshape(slot_total, LANES)]
    all_to_all x2, starting transfers between devices: 11.8 us -> 10.3 us  [exchanged(): lax.all_to_all(pieces, axes, 0, 0, tiled=True).reshape(slot_total, LANES)]
    unnamed x14 -> x16, local copies, waits for them, and re-layouts: 1.92 us -> 0.94 us
    pallas_call x1, Pallas kernels: 1.37 us -> 2.05 us  [per_device(): pl.pallas_call(route_kernel, grid=(device_count // PARTS,), out_shape=jax...]
    reduce_max x1, local copies, waits for them, and re-layouts: 0.8 us -> 0.14 us  [route_codes(): return jnp.max(jnp.where(hits[:, :, None], link_slots[None], -1), axis=1)]
  transfers between devices with their start and end apart: 2 -> 2, of which waited for: 2 -> 2; matrix products, arithmetic and copies ran while one was open for 4% -> 3% of each run, Pallas kernels for 32% -> 24%
where the time goes in v7:
time: 36.4 us; the launch traced here: 36.2 us
  Pallas kernels  17.4 us (48%)
  starting transfers between devices  10.3 us (28%)
  waiting for transfers between devices  6.44 us (18%)
  local copies, waits for them, and re-layouts  1.08 us (3%)
  other arithmetic  0.79 us (2%)
    all_to_all x2, starting transfers between devices, exchanged(): lax.all_to_all(pieces, axes, 0, 0, tiled=True).reshape(slot_total, LANES)  10.3 us
    pallas_call x2, Pallas kernels, bulk(): pl.pallas_call(kernel, out_shape=[jax.ShapeDtypeStruct(tracers.shape, f32...  8.73 us
    all_to_all x2, waiting for transfers between devices, exchanged(): lax.all_to_all(pieces, axes, 0, 0, tiled=True).reshape(slot_total, LANES)  6.44 us
    pallas_call x1, Pallas kernels, per_device(): pl.pallas_call(pack_kernel, out_shape=jax.ShapeDtypeStruct((slot_total, L...  3.84 us
    pallas_call x1, Pallas kernels, per_device(): pl.pallas_call(finish_kernel, out_shape=jax.ShapeDtypeStruct(tracers.shap...  2.77 us
    pallas_call x1, Pallas kernels, per_device(): pl.pallas_call(route_kernel, grid=(device_count // PARTS,), out_shape=jax...  2.05 us
    unnamed x16, local copies, waits for them, and re-layouts  0.94 us
  transfers between devices with their start and end apart: 2, of which 2 were waited for; matrix products, arithmetic and copies ran while one was open for 3% of the time, Pallas kernels for 24%

profile of v7, /device:TPU:0, one launch (start us, length us, event | category | flops | bytes accessed | tf_op | source)
XLA Modules:
  0.0 36.2 jit_solution(3999440493911533890)
XLA Ops:
  0.0 0.0 copy-start.7
  0.0 0.0 copy-start.6
  0.0 0.0 copy-start.5
  0.0 0.0 copy-start
  0.0 0.0 copy-start.1
  0.0 3.8 %shard_map.73.after_ref = f32[320,128]{1,0:T(8,128)} custom-call(f32[10,4,5400]{2,1,0:T(4,128)} %refs_1_.1, f32[10,4,5400]{2,1,0:T(4,128)} %refs_2_.1, f32[10,5400]{1,0:T(8,128)} %refs_3_.1), custom_call_target="tpu_custom_call" | custom-call | flops 4000000 | bytes 2400000 | tf_op jit(solution)/shard_map/pallas_call | solution.py:485
  3.9 0.0 copy-start.2
  3.9 0.0 copy-start.4
  3.9 7.3 %all-to-all-start = ((f32[32,10,1,128]{3,2,1,0:T(1,128)}), f32[32,10,1,128]{3,2,1,0:T(1,128)S(1)}, u32[]{:S(2)}, u32[]{:S(2)}) async-start(f32[32,10,1,128]{3,2,1,0:T(1,128)} %bitcast.7), calls=%async_computation | async-start | bytes 327680 | tf_op jit(solution)/shard_map/all_to_all | solution.py:483
  11.2 0.0 copy-done.7
  11.2 0.0 copy-done.6
  11.3 0.0 copy-done.5
  11.3 0.4 %select_reduce_fusion.1 = s32[160,5]{0,1:T(8,128)S(1)} fusion(s32[160]{0:T(256)S(1)} %copy-done.5, s32[160,5]{0,1:T(8,128)S(1)} %pad_add_fusion), kind=kLoop, calls=%fused_computation.1 | loop fusion | flops 383200 | bytes 7040 | tf_op jit(solution)/shard_map/reduce_max | solution.py:457
  11.7 0.1 iota_compare_fusion.1
  11.8 0.3 select_reduce_fusion
  12.1 0.1 copy.17.code_ref.refs_5_
  12.2 0.0 copy-done
  12.2 0.0 copy-done.1
  12.2 0.0 copy-done.2
  12.3 0.0 copy-done.4
  12.3 0.0 copy-start.3
  12.3 0.9 %copy-done.3 = f32[320,128]{1,0:T(8,128)S(1)} copy-done((f32[320,128]{1,0:T(8,128)S(1)}, f32[320,128]{1,0:T(8,128)}, u32[]{:S(2)}) %copy-start.3) | copy-done | bytes 163864
  13.2 3.7 %shard_map.74 = (f32[10,4,5400]{2,1,0:T(4,128)}, f32[25,16,128]{2,1,0:T(8,128)S(1)}, s32[1]{0:T(128)}) custom-call(s32[1]{0:T(128)} %bitcast.my_ref.refs_0_, f32[10,4,5400]{2,1,0:T(4,128)S(1)} %copy-done, f32[10,4,5400]{2,1,0:T(4,128)S(1)} %copy-done.1, f32[10,5400]{1,0:T(8,128)S(1)} %copy-done.2, f32[10,5400]{1,0:T(8,128)S(1)} %copy-done.4, ...), custom_call_target="tpu_custom_call" | custom-call | flops 8000000 | bytes 1600000 | tf_op jit(solution)/shard_map/pallas_call | solution.py:509
  16.9 2.9 %all-to-all-done = f32[32,10,1,128]{3,2,1,0:T(1,128)S(1)} async-done(((f32[32,10,1,128]{3,2,1,0:T(1,128)}), f32[32,10,1,128]{3,2,1,0:T(1,128)S(1)}, u32[]{:S(2)}, u32[]{:S(2)}) %all-to-all-start) | async-done | bytes 163872 | tf_op jit(solution)/shard_map/all_to_all | solution.py:483
  19.8 2.0 %shard_map.75.refs_6_ = f32[320,128]{1,0:T(8,128)} custom-call(s32[1]{0:T(128)} %get-tuple-element.10.part_ref, s32[320,6]{1,0:T(8,128)S(1)} %copy.17.code_ref.refs_5_, f32[320,128]{1,0:T(8,128)S(1)} %bitcast.9), custom_call_target="tpu_custom_call" | custom-call | tf_op jit(solution)/shard_map/pallas_call | solution.py:541
  21.8 3.0 %all-to-all-start.1 = ((f32[32,10,1,128]{3,2,1,0:T(1,128)}), f32[32,10,1,128]{3,2,1,0:T(1,128)S(1)}, u32[]{:S(2)}, u32[]{:S(2)}) async-start(f32[32,10,1,128]{3,2,1,0:T(1,128)} %bitcast.5), calls=%async_computation.1 | async-start | bytes 327680 | tf_op jit(solution)/shard_map/all_to_all | solution.py:483
  24.8 5.0 %shard_map.76 = (f32[10,4,5400]{2,1,0:T(4,128)}, f32[25,24,128]{2,1,0:T(8,128)S(1)}, s32[1]{0:T(128)}) custom-call(s32[1]{0:T(128)} %bitcast.my_ref.refs_0_, f32[10,4,5400]{2,1,0:T(4,128)S(1)} %copy-done, f32[10,4,5400]{2,1,0:T(4,128)S(1)} %copy-done.1, f32[10,5400]{1,0:T(8,128)S(1)} %copy-done.2, ...), custom_call_target="tpu_custom_call", output_to_operand_aliasing={{0}: (7, {})} | custom-call | flops 12000000 | bytes 2400000 | tf_op jit(solution)/shard_map/pallas_call | solution.py:509
  29.8 3.6 %all-to-all-done.1 = f32[32,10,1,128]{3,2,1,0:T(1,128)S(1)} async-done(((f32[32,10,1,128]{3,2,1,0:T(1,128)}), f32[32,10,1,128]{3,2,1,0:T(1,128)S(1)}, u32[]{:S(2)}, u32[]{:S(2)}) %all-to-all-start.1) | async-done | bytes 163872 | tf_op jit(solution)/shard_map/all_to_all | solution.py:483
  33.4 2.8 %shard_map.77 = f32[10,4,5400]{2,1,0:T(4,128)} custom-call(f32[320,128]{1,0:T(8,128)S(1)} %bitcast.8, f32[25,16,128]{2,1,0:T(8,128)S(1)} %get-tuple-element.11.edge_a_ref, f32[25,24,128]{2,1,0:T(8,128)S(1)} %get-tuple-element.13.edge_b_ref, f32[10,4,5400]{2,1,0:T(4,128)} %get-tuple-element.14.base_ref), custom_call_target="tpu_custom_call", output_to_operand_aliasing={{}: (3, {})} | custom-call | tf_op jit(solution)/shard_map/pallas_call | solution.py:557
  (2 shorter events, 0.0 us)
Async XLA Ops:
  0.0 11.2 %copy-start.7 = (s32[160]{0:T(256)S(1)}, s32[160]{0:T(256)}, u32[]{:S(2)}) copy-start(s32[160]{0:T(256)} %param.13) | copy-start | bytes 1924
  0.0 11.2 %copy-start.6 = (s32[160,4]{0,1:T(4,128)S(1)}, s32[160,4]{0,1:T(4,128)}, u32[]{:S(2)}) copy-start(s32[160,4]{0,1:T(4,128)} %param.12) | copy-start | bytes 7684
  0.0 11.3 %copy-start.5 = (s32[160]{0:T(256)S(1)}, s32[160]{0:T(256)}, u32[]{:S(2)}) copy-start(s32[160]{0:T(256)} %param.11) | copy-start | bytes 1924
  0.0 12.2 %copy-start = (f32[10,4,5400]{2,1,0:T(4,128)S(1)}, f32[10,4,5400]{2,1,0:T(4,128)}, u32[]{:S(2)}) copy-start(f32[10,4,5400]{2,1,0:T(4,128)} %refs_1_.1) | copy-start | bytes 2592004
  0.0 12.2 %copy-start.1 = (f32[10,4,5400]{2,1,0:T(4,128)S(1)}, f32[10,4,5400]{2,1,0:T(4,128)}, u32[]{:S(2)}) copy-start(f32[10,4,5400]{2,1,0:T(4,128)} %refs_2_.1) | copy-start | bytes 2592004
  3.9 8.4 %copy-start.2 = (f32[10,5400]{1,0:T(8,128)S(1)}, f32[10,5400]{1,0:T(8,128)}, u32[]{:S(2)}) copy-start(f32[10,5400]{1,0:T(8,128)} %refs_3_.1) | copy-start | bytes 648004
  3.9 8.4 %copy-start.4 = (f32[10,5400]{1,0:T(8,128)S(1)}, f32[10,5400]{1,0:T(8,128)}, u32[]{:S(2)}) copy-start(f32[10,5400]{1,0:T(8,128)} %refs_4_.1) | copy-start | bytes 648004
  3.9 15.9 %all-to-all-start = ((f32[32,10,1,128]{3,2,1,0:T(1,128)}), f32[32,10,1,128]{3,2,1,0:T(1,128)S(1)}, u32[]{:S(2)}, u32[]{:S(2)}) async-start(f32[32,10,1,128]{3,2,1,0:T(1,128)} %bitcast.7), calls=%async_computation | async-start | bytes 327680 | tf_op jit(solution)/shard_map/all_to_all | solution.py:483
  12.3 0.9 %copy-start.3 = (f32[320,128]{1,0:T(8,128)S(1)}, f32[320,128]{1,0:T(8,128)}, u32[]{:S(2)}) copy-start(f32[320,128]{1,0:T(8,128)} %shard_map.73.after_ref) | copy-start | bytes 491524
  21.8 11.6 %all-to-all-start.1 = ((f32[32,10,1,128]{3,2,1,0:T(1,128)}), f32[32,10,1,128]{3,2,1,0:T(1,128)S(1)}, u32[]{:S(2)}, u32[]{:S(2)}) async-start(f32[32,10,1,128]{3,2,1,0:T(1,128)} %bitcast.5), calls=%async_computation.1 | async-start | bytes 327680 | tf_op jit(solution)/shard_map/all_to_all | solution.py:483

commit v8 on v6

--- a/solution.py
+++ b/solution.py
@@ -184,8 +184,7 @@
         put(20 + half, joined(d_south, d_north, half, count))
 
 
-def route_kernel(part_ref, code_ref, held_ref, after_ref, out_ref):
-    del after_ref
+def route_kernel(part_ref, code_ref, held_ref, out_ref):
     total = held_ref.shape[0]
     rows = out_ref.shape[0]
     part = part_ref[0]
@@ -207,9 +206,8 @@
     out_ref[...] = jnp.where(along_x, x_side, y_side)
 
 
-def bulk_kernel(first, my_ref, tracer_ref, velocity_ref, depth_ref, kappa_ref, code_ref, after_ref,
+def bulk_kernel(first, my_ref, tracer_ref, velocity_ref, depth_ref, kappa_ref, code_ref,
                 base_ref, edge_ref, y_ref, x_ref, v_ref, d_ref, k_ref, d8_ref, k8_ref, w_ref, z_ref, x_sems, v_sems, y_sems, d_sems):
-    del after_ref
     count = depth_ref.shape[0]
     pairs = edge_ref.shape[1] // 8
     x_copies = pair_copies(tracer_ref, x_ref, x_sems, first, pairs)
@@ -501,18 +499,18 @@
     held = exchanged(pack)
     codes = route_codes(block_owner, neighbours, fold_partner, slot_total)
 
-    def bulk(first, some, after, base):
+    def bulk(first, some, codes, base):
         kernel = functools.partial(bulk_kernel, first)
         extra = [] if base is None else [base]
         if extra:
-            kernel = lambda *refs: bulk_kernel(first, *refs[:7], *refs[8:])
+            kernel = lambda *refs: bulk_kernel(first, *refs[:6], *refs[7:])
         return pl.pallas_call(
             kernel,
             out_shape=[
                 jax.ShapeDtypeStruct(tracers.shape, f32),
                 jax.ShapeDtypeStruct((OWN * SIDES + 1, 8 * some, LANES), f32),
             ],
-            in_specs=[in_smem, in_hbm, in_hbm, in_hbm, in_hbm, in_vmem, anywhere] + [in_hbm] * len(extra),
+            in_specs=[in_smem, in_hbm, in_hbm, in_hbm, in_hbm, in_vmem] + [in_hbm] * len(extra),
             out_specs=[in_hbm, in_vmem],
             scratch_shapes=[
                 pltpu.VMEM((8 * some, CELLS), f32),
@@ -529,11 +527,13 @@
                 dma((some,)),
                 dma((2,)),
             ],
-            input_output_aliases={7: 0} if extra else {},
+            input_output_aliases={6: 0} if extra else {},
+            compiler_params=limit,
             cost_estimate=pl.CostEstimate(flops=4_000_000 * some, bytes_accessed=800_000 * some, transcendentals=0),
-        )(my_index, tracers, velocity, kmt, kappa, codes, after, *extra)
-
-    base, edge_a = bulk(0, FIRST_PAIRS, pack, None)
+        )(my_index, tracers, velocity, kmt, kappa, codes, *extra)
+
+    base, edge_a = bulk(0, FIRST_PAIRS, codes, None)
+    held, edge_a = lax.optimization_barrier((held, edge_a))
 
     routed_rows = PARTS * slot_count
     routed = pl.pallas_call(
@@ -544,13 +544,13 @@
             in_smem,
             pl.BlockSpec((routed_rows, 6), lambda step: (step, 0)),
             pl.BlockSpec((slot_total, LANES), lambda step: (0, 0)),
-            anywhere,
         ],
         out_specs=pl.BlockSpec((routed_rows, LANES), lambda step: (step, 0)),
         compiler_params=limit,
-    )(my_index, codes, held, edge_a)
-
-    base, edge_b = bulk(FIRST_PAIRS, pairs - FIRST_PAIRS, routed, base)
+    )(my_index, codes, held)
+
+    routed, base = lax.optimization_barrier((routed, base))
+    base, edge_b = bulk(FIRST_PAIRS, pairs - FIRST_PAIRS, codes, base)
     halo = exchanged(routed)[: PARTS * slot_count]
 
     return pl.pallas_call(

time: 39.2 us -> 35.3 us (0.901)
  waiting for transfers between devices: 3.13 us -> 8.39 us
  Pallas kernels: 20.2 us -> 15.7 us
  local copies, waits for them, and re-layouts: 2.72 us -> 0.17 us
  starting transfers between devices: 11.8 us -> 9.89 us
    all_to_all x2, waiting for transfers between devices: 3.13 us -> 8.39 us  [exchanged(): lax.all_to_all(pieces, axes, 0, 0, tiled=True).reshape(slot_total, LANES)]
    pallas_call x2, Pallas kernels: 12.3 us -> 7.69 us  [bulk(): pl.pallas_call(kernel, out_shape=[jax.ShapeDtypeStruct(tracers.shape, f32...]
    all_to_all x2, starting transfers between devices: 11.8 us -> 9.89 us  [exchanged(): lax.all_to_all(pieces, axes, 0, 0, tiled=True).reshape(slot_total, LANES)]
    unnamed x14, local copies, waits for them, and re-layouts: 1.92 us -> 0.03 us
    reduce_max x1, local copies, waits for them, and re-layouts: 0.8 us -> 0.14 us  [route_codes(): return jnp.max(jnp.where(hits[:, :, None], link_slots[None], -1), axis=1)]
  transfers between devices with their start and end apart: 2 -> 2, of which waited for: 2 -> 2; matrix products, arithmetic and copies ran while one was open for 4% -> 3% of each run, Pallas kernels for 32% -> 22%
where the time goes in v8:
time: 35.3 us; the launch traced here: 35.1 us
  Pallas kernels  15.7 us (44%)
  starting transfers between devices  9.89 us (28%)
  waiting for transfers between devices  8.39 us (24%)
  other arithmetic  0.79 us (2%)
    all_to_all x2, starting transfers between devices, exchanged(): lax.all_to_all(pieces, axes, 0, 0, tiled=True).reshape(slot_total, LANES)  9.89 us
    all_to_all x2, waiting for transfers between devices, exchanged(): lax.all_to_all(pieces, axes, 0, 0, tiled=True).reshape(slot_total, LANES)  8.39 us
    pallas_call x2, Pallas kernels, bulk(): pl.pallas_call(kernel, out_shape=[jax.ShapeDtypeStruct(tracers.shape, f32...  7.69 us
    pallas_call x1, Pallas kernels, per_device(): pl.pallas_call(pack_kernel, out_shape=jax.ShapeDtypeStruct((slot_total, L...  3.85 us
    pallas_call x1, Pallas kernels, per_device(): pl.pallas_call(finish_kernel, out_shape=jax.ShapeDtypeStruct(tracers.shap...  2.77 us
    pallas_call x1, Pallas kernels, per_device(): pl.pallas_call(route_kernel, grid=(device_count // PARTS,), out_shape=jax...  1.36 us
  transfers between devices with their start and end apart: 2, of which 2 were waited for; matrix products, arithmetic and copies ran while one was open for 3% of the time, Pallas kernels for 22%

profile of v8, /device:TPU:0, one launch (start us, length us, event | category | flops | bytes accessed | tf_op | source)
XLA Modules:
  0.0 35.1 jit_solution(9879822499335676642)
XLA Ops:
  0.0 0.0 copy-start.6
  0.0 0.0 copy-start.5
  0.0 0.0 copy-start.4
  0.0 0.0 copy-start
  0.0 0.0 copy-start.1
  0.0 3.8 %shard_map.73 = f32[320,128]{1,0:T(8,128)} custom-call(f32[10,4,5400]{2,1,0:T(4,128)} %refs_1_.1, f32[10,4,5400]{2,1,0:T(4,128)} %refs_2_.1, f32[10,5400]{1,0:T(8,128)} %refs_3_.1), custom_call_target="tpu_custom_call" | custom-call | flops 4000000 | bytes 2400000 | tf_op jit(solution)/shard_map/pallas_call | solution.py:483
  3.9 0.0 copy-start.2
  3.9 0.0 copy-start.3
  3.9 7.3 %all-to-all-start = ((f32[32,10,1,128]{3,2,1,0:T(1,128)}), f32[32,10,1,128]{3,2,1,0:T(1,128)S(1)}, u32[]{:S(2)}, u32[]{:S(2)}) async-start(f32[32,10,1,128]{3,2,1,0:T(1,128)} %bitcast.9), calls=%async_computation | async-start | bytes 327680 | tf_op jit(solution)/shard_map/all_to_all | solution.py:481
  11.2 0.0 copy-done.6
  11.2 0.0 copy-done.5
  11.3 0.0 copy-done.4
  11.3 0.4 %select_reduce_fusion.1 = s32[160,5]{0,1:T(8,128)S(1)} fusion(s32[160]{0:T(256)S(1)} %copy-done.4, s32[160,5]{0,1:T(8,128)S(1)} %pad_add_fusion), kind=kLoop, calls=%fused_computation.1 | loop fusion | flops 383200 | bytes 7040 | tf_op jit(solution)/shard_map/reduce_max | solution.py:455
  11.7 0.1 iota_compare_fusion.1
  11.8 0.3 select_reduce_fusion
  12.1 0.1 copy.19.code_ref.refs_5_
  12.2 0.0 copy-done
  12.2 0.0 copy-done.1
  12.2 0.0 copy-done.2
  12.3 0.0 copy-done.3
  12.3 3.2 %shard_map.74 = (f32[10,4,5400]{2,1,0:T(4,128)}, f32[25,16,128]{2,1,0:T(8,128)S(1)}) custom-call(s32[1]{0:T(128)} %bitcast.my_ref.part_ref.refs_0_, f32[10,4,5400]{2,1,0:T(4,128)S(1)} %copy-done, f32[10,4,5400]{2,1,0:T(4,128)S(1)} %copy-done.1, f32[10,5400]{1,0:T(8,128)S(1)} %copy-done.2, f32[10,5400]{1,0:T(8,128)S(1)} %copy-done.3, ...), custom_call_target="tpu_custom_call" | custom-call | flops 8000000 | bytes 1600000 | tf_op jit(solution)/shard_map/pallas_call | solution.py:507
  15.5 4.3 %all-to-all-done = f32[32,10,1,128]{3,2,1,0:T(1,128)S(1)} async-done(((f32[32,10,1,128]{3,2,1,0:T(1,128)}), f32[32,10,1,128]{3,2,1,0:T(1,128)S(1)}, u32[]{:S(2)}, u32[]{:S(2)}) %all-to-all-start) | async-done | bytes 163872 | tf_op jit(solution)/shard_map/all_to_all | solution.py:481
  19.8 1.4 %shard_map.75 = f32[320,128]{1,0:T(8,128)} custom-call(s32[1]{0:T(128)} %bitcast.my_ref.part_ref.refs_0_, s32[320,6]{1,0:T(8,128)S(1)} %copy.19.code_ref.refs_5_, f32[320,128]{1,0:T(8,128)S(1)} %bitcast.8), custom_call_target="tpu_custom_call" | custom-call | tf_op jit(solution)/shard_map/pallas_call | solution.py:539
  21.2 2.6 %all-to-all-start.1 = ((f32[32,10,1,128]{3,2,1,0:T(1,128)}), f32[32,10,1,128]{3,2,1,0:T(1,128)S(1)}, u32[]{:S(2)}, u32[]{:S(2)}) async-start(f32[32,10,1,128]{3,2,1,0:T(1,128)} %bitcast.5), calls=%async_computation.1 | async-start | bytes 327680 | tf_op jit(solution)/shard_map/all_to_all | solution.py:481
  23.7 4.5 %shard_map.76 = (f32[10,4,5400]{2,1,0:T(4,128)}, f32[25,24,128]{2,1,0:T(8,128)S(1)}) custom-call(s32[1]{0:T(128)} %bitcast.my_ref.part_ref.refs_0_, f32[10,4,5400]{2,1,0:T(4,128)S(1)} %copy-done, f32[10,4,5400]{2,1,0:T(4,128)S(1)} %copy-done.1, f32[10,5400]{1,0:T(8,128)S(1)} %copy-done.2, f32[10,5400]{1,0:T(8,128)S(1)} %copy-done.3, ...), custom_call_target="tpu_custom_call", output_to_operand_aliasing={{0}: (6, {})} | custom-call | flops 12000000 | bytes 2400000 | tf_op jit(solution)/shard_map/pallas_call | solution.py:507
  28.2 4.1 %all-to-all-done.1 = f32[32,10,1,128]{3,2,1,0:T(1,128)S(1)} async-done(((f32[32,10,1,128]{3,2,1,0:T(1,128)}), f32[32,10,1,128]{3,2,1,0:T(1,128)S(1)}, u32[]{:S(2)}, u32[]{:S(2)}) %all-to-all-start.1) | async-done | bytes 163872 | tf_op jit(solution)/shard_map/all_to_all | solution.py:481
  32.3 2.8 %shard_map.77 = f32[10,4,5400]{2,1,0:T(4,128)} custom-call(f32[320,128]{1,0:T(8,128)S(1)} %bitcast.7, f32[25,16,128]{2,1,0:T(8,128)S(1)} %get-tuple-element.17.edge_a_ref, f32[25,24,128]{2,1,0:T(8,128)S(1)} %get-tuple-element.19.edge_b_ref, f32[10,4,5400]{2,1,0:T(4,128)} %get-tuple-element.20.base_ref), custom_call_target="tpu_custom_call", output_to_operand_aliasing={{}: (3, {})} | custom-call | tf_op jit(solution)/shard_map/pallas_call | solution.py:556
  (2 shorter events, 0.0 us)
Async XLA Ops:
  0.0 11.2 %copy-start.6 = (s32[160]{0:T(256)S(1)}, s32[160]{0:T(256)}, u32[]{:S(2)}) copy-start(s32[160]{0:T(256)} %param.13) | copy-start | bytes 1924
  0.0 11.2 %copy-start.5 = (s32[160,4]{0,1:T(4,128)S(1)}, s32[160,4]{0,1:T(4,128)}, u32[]{:S(2)}) copy-start(s32[160,4]{0,1:T(4,128)} %param.12) | copy-start | bytes 7684
  0.0 11.3 %copy-start.4 = (s32[160]{0:T(256)S(1)}, s32[160]{0:T(256)}, u32[]{:S(2)}) copy-start(s32[160]{0:T(256)} %param.11) | copy-start | bytes 1924
  0.0 12.2 %copy-start = (f32[10,4,5400]{2,1,0:T(4,128)S(1)}, f32[10,4,5400]{2,1,0:T(4,128)}, u32[]{:S(2)}) copy-start(f32[10,4,5400]{2,1,0:T(4,128)} %refs_1_.1) | copy-start | bytes 2592004
  0.0 12.2 %copy-start.1 = (f32[10,4,5400]{2,1,0:T(4,128)S(1)}, f32[10,4,5400]{2,1,0:T(4,128)}, u32[]{:S(2)}) copy-start(f32[10,4,5400]{2,1,0:T(4,128)} %refs_2_.1) | copy-start | bytes 2592004
  3.9 8.4 %copy-start.2 = (f32[10,5400]{1,0:T(8,128)S(1)}, f32[10,5400]{1,0:T(8,128)}, u32[]{:S(2)}) copy-start(f32[10,5400]{1,0:T(8,128)} %refs_3_.1) | copy-start | bytes 648004
  3.9 8.4 %copy-start.3 = (f32[10,5400]{1,0:T(8,128)S(1)}, f32[10,5400]{1,0:T(8,128)}, u32[]{:S(2)}) copy-start(f32[10,5400]{1,0:T(8,128)} %refs_4_.1) | copy-start | bytes 648004
  3.9 15.9 %all-to-all-start = ((f32[32,10,1,128]{3,2,1,0:T(1,128)}), f32[32,10,1,128]{3,2,1,0:T(1,128)S(1)}, u32[]{:S(2)}, u32[]{:S(2)}) async-start(f32[32,10,1,128]{3,2,1,0:T(1,128)} %bitcast.9), calls=%async_computation | async-start | bytes 327680 | tf_op jit(solution)/shard_map/all_to_all | solution.py:481
  21.2 11.2 %all-to-all-start.1 = ((f32[32,10,1,128]{3,2,1,0:T(1,128)}), f32[32,10,1,128]{3,2,1,0:T(1,128)S(1)}, u32[]{:S(2)}, u32[]{:S(2)}) async-start(f32[32,10,1,128]{3,2,1,0:T(1,128)} %bitcast.5), calls=%async_computation.1 | async-start | bytes 327680 | tf_op jit(solution)/shard_map/all_to_all | solution.py:481

commit v9 on v8

--- a/solution.py
+++ b/solution.py
@@ -125,7 +125,7 @@
     return copies
 
 
-def pack_kernel(tracer_ref, velocity_ref, depth_ref, out_ref, x_ref, v_ref, d_ref, strip_ref, x_sems, v_sems, d_sem):
+def pack_kernel(blk_count, sub_count, tracer_ref, velocity_ref, depth_ref, out_ref, x_ref, v_ref, d_ref, strip_ref, x_sems, v_sems, d_sem):
     count = depth_ref.shape[0]
     pairs = count // 2
     x_copies = pair_copies(tracer_ref, x_ref, x_sems, 0, pairs)
@@ -154,8 +154,7 @@
 
     d_copy.wait()
     if out_ref.shape[0] > PARTS * count:
-        rest = out_ref.shape[0] - PARTS * count
-        out_ref[PARTS * count :, :] = jnp.zeros((rest, LANES), jnp.float32)
+        out_ref[...] = jnp.zeros(out_ref.shape, jnp.float32)
     slot_lane = lane_of(count)
     get_d = tile_getter(d_ref, slice(None), count)
     d_south, d_north = window(get_d, 0, count), window(get_d, CELLS - IB, count)
@@ -163,7 +162,8 @@
     spare = (slot_lane >= SPARE) & (slot_lane < SPARE + PIECE)
 
     def put(part, value):
-        out_ref[part * count : (part + 1) * count, :] = value
+        at = (part % sub_count * blk_count + part // sub_count) * count
+        out_ref[at : at + count, :] = value
 
     for chan in range(4):
         rows = pl.ds(chan, count, stride=4)
@@ -182,6 +182,14 @@
             put(X_PART + 8 + chan, strip_ref[8, rows, :])
     for half in range(2):
         put(20 + half, joined(d_south, d_north, half, count))
+
+
+def regroup_kernel(outer, inner, in_ref, out_ref):
+    size = in_ref.shape[0] // (outer * inner)
+    for major in range(outer):
+        for minor in range(inner):
+            source, target = (major * inner + minor) * size, (minor * outer + major) * size
+            out_ref[target : target + size, :] = in_ref[source : source + size, :]
 
 
 def route_kernel(part_ref, code_ref, held_ref, out_ref):
@@ -447,9 +455,9 @@
         copy.wait()
 
 
-def route_codes(block_owner, neighbours, fold_partner, slot_total):
+def route_codes(block_owner, neighbours, fold_partner, slots):
     block_count = block_owner.shape[0]
-    hits = block_owner[None, :] == jnp.arange(slot_total, dtype=jnp.int32)[:, None]
+    hits = block_owner[None, :] == slots[:, None]
     links = jnp.concatenate([neighbours, fold_partner[:, None]], axis=1)
     linked = links[:, :, None] == jnp.arange(block_count, dtype=jnp.int32)[None, None, :]
     link_slots = jnp.max(jnp.where(linked, block_owner[None, None, :], -1), axis=2)
@@ -459,12 +467,12 @@
 
 def per_device(tracers, velocity, kappa, kmt, block_owner, neighbours, fold_partner):
     slot_count, chans = tracers.shape[:2]
-    sub_count = lax.axis_size("sub")
-    device_count = lax.axis_size("blk") * sub_count
+    blk_count, sub_count = lax.axis_size("blk"), lax.axis_size("sub")
+    device_count = blk_count * sub_count
     if device_count % PARTS or chans != 4 or slot_count % 2 or slot_count < 2 * FIRST_PAIRS + 2:
         raise ValueError("unsupported sizes")
     my_index = (lax.axis_index("blk") * sub_count + lax.axis_index("sub")).astype(jnp.int32).reshape(1)
-    axes = ("blk", "sub")
+    my_place = (lax.axis_index("sub") * blk_count + lax.axis_index("blk")).astype(jnp.int32).reshape(1)
     pairs = slot_count // 2
     slot_total = device_count * slot_count
     state_rows = 4 * slot_count
@@ -477,11 +485,18 @@
     limit = pltpu.CompilerParams(vmem_limit_bytes=32 * 1024 * 1024)
 
     def exchanged(pieces):
-        pieces = pieces.reshape(device_count, slot_count, 1, LANES)
-        return lax.all_to_all(pieces, axes, 0, 0, tiled=True).reshape(slot_total, LANES)
+        width = slot_count * LANES
+        pieces = lax.all_to_all(pieces.reshape(sub_count, 1, blk_count * width), "sub", 0, 0, tiled=True)
+        pieces = pl.pallas_call(
+            functools.partial(regroup_kernel, sub_count, blk_count),
+            out_shape=jax.ShapeDtypeStruct((slot_total, LANES), f32),
+            compiler_params=limit,
+        )(pieces.reshape(slot_total, LANES))
+        pieces = lax.all_to_all(pieces.reshape(blk_count, 1, sub_count * width), "blk", 0, 0, tiled=True)
+        return pieces.reshape(slot_total, LANES)
 
     pack = pl.pallas_call(
-        pack_kernel,
+        functools.partial(pack_kernel, blk_count, sub_count),
         out_shape=jax.ShapeDtypeStruct((slot_total, LANES), f32),
         in_specs=[in_hbm, in_hbm, in_hbm],
         out_specs=in_vmem,
@@ -497,7 +512,8 @@
         cost_estimate=pl.CostEstimate(flops=4_000_000, bytes_accessed=2_400_000, transcendentals=0),
     )(tracers, velocity, kmt)
     held = exchanged(pack)
-    codes = route_codes(block_owner, neighbours, fold_partner, slot_total)
+    slots = jnp.arange(slot_total, dtype=jnp.int32).reshape(blk_count, sub_count, slot_count)
+    codes = route_codes(block_owner, neighbours, fold_partner, slots.transpose(1, 0, 2).reshape(-1))
 
     def bulk(first, some, codes, base):
         kernel = functools.partial(bulk_kernel, first)
@@ -530,7 +546,7 @@
             input_output_aliases={6: 0} if extra else {},
             compiler_params=limit,
             cost_estimate=pl.CostEstimate(flops=4_000_000 * some, bytes_accessed=800_000 * some, transcendentals=0),
-        )(my_index, tracers, velocity, kmt, kappa, codes, *extra)
+        )(my_place, tracers, velocity, kmt, kappa, codes, *extra)
 
     base, edge_a = bulk(0, FIRST_PAIRS, codes, None)
     held, edge_a = lax.optimization_barrier((held, edge_a))

time: 35.3 us -> 51 us (1.44)
  blocking collectives: 0 us -> 7.34 us
  starting transfers between devices: 9.89 us -> 14.1 us
  waiting for transfers between devices: 8.39 us -> 11.5 us
  Pallas kernels: 15.7 us -> 16.3 us
    all_to_all x0 -> x1, blocking collectives: none -> 7.34 us  [exchanged(): lax.all_to_all(pieces.reshape(sub_count, 1, blk_count * width), 'sub', 0,...]
    all_to_all x2 -> x3, starting transfers between devices: 9.89 us -> 14.1 us  [the longest x2 9.77 us: exchanged(): lax.all_to_all(pieces.reshape(blk_count, 1, sub_count * width), 'blk', 0,...]
    all_to_all x2 -> x3, waiting for transfers between devices: 8.39 us -> 11.5 us  [the longest x2 6.75 us: exchanged(): lax.all_to_all(pieces.reshape(blk_count, 1, sub_count * width), 'blk', 0,...]
    pallas_call x1 -> x3, Pallas kernels: 3.85 us -> 5.17 us  [the longest x1 3.83 us: per_device(): pl.pallas_call(functools.partial(pack_kernel, blk_count, sub_count), out_...]
    pallas_call x1, Pallas kernels: 1.36 us -> 0.7 us  [per_device(): pl.pallas_call(route_kernel, grid=(device_count // PARTS,), out_shape=jax...]
  transfers between devices with their start and end apart: 2 -> 3, of which waited for: 2 -> 3; matrix products, arithmetic and copies ran while one was open for 3% -> 2% of each run, Pallas kernels for 22% -> 15%
where the time goes in v9:
time: 51 us; the launch traced here: 50.5 us
  Pallas kernels  16.3 us (32%)
  starting transfers between devices  14.1 us (28%)
  waiting for transfers between devices  11.5 us (23%)
  blocking collectives  7.34 us (14%)
  other arithmetic  0.79 us (2%)
    all_to_all x2, starting transfers between devices, exchanged(): lax.all_to_all(pieces.reshape(blk_count, 1, sub_count * width), 'blk', 0,...  9.77 us
    pallas_call x2, Pallas kernels, bulk(): pl.pallas_call(kernel, out_shape=[jax.ShapeDtypeStruct(tracers.shape, f32...  7.69 us
    all_to_all x1, blocking collectives, exchanged(): lax.all_to_all(pieces.reshape(sub_count, 1, blk_count * width), 'sub', 0,...  7.34 us
    all_to_all x2, waiting for transfers between devices, exchanged(): lax.all_to_all(pieces.reshape(blk_count, 1, sub_count * width), 'blk', 0,...  6.75 us
    all_to_all x1, waiting for transfers between devices, exchanged(): lax.all_to_all(pieces.reshape(sub_count, 1, blk_count * width), 'sub', 0,...  4.72 us
    all_to_all x1, starting transfers between devices, exchanged(): lax.all_to_all(pieces.reshape(sub_count, 1, blk_count * width), 'sub', 0,...  4.37 us
    pallas_call x1, Pallas kernels, per_device(): pl.pallas_call(functools.partial(pack_kernel, blk_count, sub_count), out_...  3.83 us
    pallas_call x1, Pallas kernels, per_device(): pl.pallas_call(finish_kernel, out_shape=jax.ShapeDtypeStruct(tracers.shap...  2.77 us
  transfers between devices with their start and end apart: 3, of which 3 were waited for; matrix products, arithmetic and copies ran while one was open for 2% of the time, Pallas kernels for 15%

profile of v9, /device:TPU:0, one launch (start us, length us, event | category | flops | bytes accessed | tf_op | source)
XLA Modules:
  0.0 50.5 jit_solution(17249965590917457867)
XLA Ops:
  0.0 0.0 copy-start.4
  0.0 0.0 copy-start.6
  0.0 0.0 copy-start.5
  0.0 0.0 copy-start.1
  0.0 3.8 %shard_map.73 = f32[320,128]{1,0:T(8,128)} custom-call(f32[10,4,5400]{2,1,0:T(4,128)} %refs_1_.1, f32[10,4,5400]{2,1,0:T(4,128)} %refs_2_.1, f32[10,5400]{1,0:T(8,128)} %refs_3_.1), custom_call_target="tpu_custom_call" | custom-call | flops 4000000 | bytes 2400000 | tf_op jit(solution)/shard_map/pallas_call | solution.py:498
  3.9 0.0 copy-start
  3.9 0.0 copy-start.2
  3.9 4.4 %all-to-all-start = ((f32[4,1,10240]{2,1,0:T(1,128)}), f32[4,1,10240]{2,1,0:T(1,128)S(1)}, u32[]{:S(2)}, u32[]{:S(2)}) async-start(f32[4,1,10240]{2,1,0:T(1,128)} %bitcast.17), calls=%async_computation | async-start | bytes 327680 | tf_op jit(solution)/shard_map/all_to_all | solution.py:489
  8.2 0.1 reshape.109
  8.4 0.0 copy-done.4
  8.4 0.1 broadcast_compare_fusion
  8.5 0.0 copy-done.6
  8.5 0.0 copy-done.5
  8.5 4.7 %all-to-all-done = f32[4,1,10240]{2,1,0:T(1,128)S(1)} async-done(((f32[4,1,10240]{2,1,0:T(1,128)}), f32[4,1,10240]{2,1,0:T(1,128)S(1)}, u32[]{:S(2)}, u32[]{:S(2)}) %all-to-all-start) | async-done | bytes 163872 | tf_op jit(solution)/shard_map/all_to_all | solution.py:489
  13.2 0.7 %shard_map.74 = f32[320,128]{1,0:T(8,128)} custom-call(f32[320,128]{1,0:T(8,128)S(1)} %bitcast.14), custom_call_target="tpu_custom_call" | custom-call | tf_op jit(solution)/shard_map/pallas_call | solution.py:490
  13.9 6.4 %all-to-all-start.1 = ((f32[8,1,5120]{2,1,0:T(1,128)}), f32[8,1,5120]{2,1,0:T(1,128)S(1)}, u32[]{:S(2)}, u32[]{:S(2)}) async-start(f32[8,1,5120]{2,1,0:T(1,128)} %bitcast.5), calls=%async_computation.1 | async-start | bytes 327680 | tf_op jit(solution)/shard_map/all_to_all | solution.py:495
  20.3 0.4 select_reduce_fusion.1
  20.7 0.3 select_reduce_fusion
  21.0 0.1 copy.22.code_ref.refs_5_
  21.1 0.0 copy-done.1
  21.2 0.0 copy-done.3
  21.2 0.0 copy-done
  21.2 0.0 copy-done.2
  21.2 3.2 %shard_map.75 = (f32[10,4,5400]{2,1,0:T(4,128)}, f32[25,16,128]{2,1,0:T(8,128)S(1)}) custom-call(s32[1]{0:T(128)} %bitcast.7.my_ref.refs_0_, f32[10,4,5400]{2,1,0:T(4,128)S(1)} %copy-done, f32[10,4,5400]{2,1,0:T(4,128)S(1)} %copy-done.1, f32[10,5400]{1,0:T(8,128)S(1)} %copy-done.2, f32[10,5400]{1,0:T(8,128)S(1)} %copy-done.3, s32[320,6]{1,0:T(8,128)S(1)} %copy.22.code_ref.refs_5_), custom_call_target="tpu_custom_call" | custom-call | flops 8000000 | bytes 1600000 | tf_op jit(solution)/shard_map/pallas_call | solution.py:523
  24.4 3.5 %all-to-all-done.1 = f32[8,1,5120]{2,1,0:T(1,128)S(1)} async-done(((f32[8,1,5120]{2,1,0:T(1,128)}), f32[8,1,5120]{2,1,0:T(1,128)S(1)}, u32[]{:S(2)}, u32[]{:S(2)}) %all-to-all-start.1) | async-done | bytes 163872 | tf_op jit(solution)/shard_map/all_to_all | solution.py:495
  27.9 0.7 %shard_map.76 = f32[320,128]{1,0:T(8,128)S(1)} custom-call(s32[1]{0:T(128)} %bitcast.part_ref, s32[320,6]{1,0:T(8,128)S(1)} %copy.22.code_ref.refs_5_, f32[320,128]{1,0:T(8,128)S(1)} %bitcast.13), custom_call_target="tpu_custom_call" | custom-call | tf_op jit(solution)/shard_map/pallas_call | solution.py:555
  28.6 7.3 %all_to_all.20 = f32[4,1,10240]{2,1,0:T(1,128)S(1)} all-to-all(f32[4,1,10240]{2,1,0:T(1,128)S(1)} %bitcast.15), channel_id=1, replica_groups=mesh['blk'=8,'sub'=4] {'sub'}, dimensions={0} | all-to-all | bytes 327680 | tf_op jit(solution)/shard_map/all_to_all | solution.py:489
  35.9 0.7 %shard_map.77 = f32[320,128]{1,0:T(8,128)} custom-call(f32[320,128]{1,0:T(8,128)S(1)} %bitcast.16), custom_call_target="tpu_custom_call" | custom-call | tf_op jit(solution)/shard_map/pallas_call | solution.py:490
  36.6 3.4 %all-to-all-start.3 = ((f32[8,1,5120]{2,1,0:T(1,128)}), f32[8,1,5120]{2,1,0:T(1,128)S(1)}, u32[]{:S(2)}, u32[]{:S(2)}) async-start(f32[8,1,5120]{2,1,0:T(1,128)} %bitcast.10), calls=%async_computation.3 | async-start | bytes 327680 | tf_op jit(solution)/shard_map/all_to_all | solution.py:495
  40.0 4.5 %shard_map.78 = (f32[10,4,5400]{2,1,0:T(4,128)}, f32[25,24,128]{2,1,0:T(8,128)S(1)}) custom-call(s32[1]{0:T(128)} %bitcast.7.my_ref.refs_0_, f32[10,4,5400]{2,1,0:T(4,128)S(1)} %copy-done, f32[10,4,5400]{2,1,0:T(4,128)S(1)} %copy-done.1, f32[10,5400]{1,0:T(8,128)S(1)} %copy-done.2, f32[10,5400]{1,0:T(8,128)S(1)} %copy-done.3, ...), custom_call_target="tpu_custom_call", output_to_operand_aliasing={{0}: (6, {})} | custom-call | flops 12000000 | bytes 2400000 | tf_op jit(solution)/shard_map/pallas_call | solution.py:523
  44.5 3.3 %all-to-all-done.3 = f32[8,1,5120]{2,1,0:T(1,128)S(1)} async-done(((f32[8,1,5120]{2,1,0:T(1,128)}), f32[8,1,5120]{2,1,0:T(1,128)S(1)}, u32[]{:S(2)}, u32[]{:S(2)}) %all-to-all-start.3) | async-done | bytes 163872 | tf_op jit(solution)/shard_map/all_to_all | solution.py:495
  47.8 2.8 %shard_map.79 = f32[10,4,5400]{2,1,0:T(4,128)} custom-call(f32[320,128]{1,0:T(8,128)S(1)} %bitcast.12, f32[25,16,128]{2,1,0:T(8,128)S(1)} %get-tuple-element.17.edge_a_ref, f32[25,24,128]{2,1,0:T(8,128)S(1)} %get-tuple-element.19.edge_b_ref, f32[10,4,5400]{2,1,0:T(4,128)} %get-tuple-element.20.base_ref), custom_call_target="tpu_custom_call", output_to_operand_aliasing={{}: (3, {})} | custom-call | tf_op jit(solution)/shard_map/pallas_call | solution.py:572
  (4 shorter events, 0.0 us)
Async XLA Ops:
  0.0 8.4 %copy-start.4 = (s32[160]{0:T(256)S(1)}, s32[160]{0:T(256)}, u32[]{:S(2)}) copy-start(s32[160]{0:T(256)} %param.11) | copy-start | bytes 1924
  0.0 8.5 %copy-start.6 = (s32[160]{0:T(256)S(1)}, s32[160]{0:T(256)}, u32[]{:S(2)}) copy-start(s32[160]{0:T(256)} %param.13) | copy-start | bytes 1924
  0.0 8.5 %copy-start.5 = (s32[160,4]{0,1:T(4,128)S(1)}, s32[160,4]{0,1:T(4,128)}, u32[]{:S(2)}) copy-start(s32[160,4]{0,1:T(4,128)} %param.12) | copy-start | bytes 7684
  0.0 21.1 %copy-start.1 = (f32[10,4,5400]{2,1,0:T(4,128)S(1)}, f32[10,4,5400]{2,1,0:T(4,128)}, u32[]{:S(2)}) copy-start(f32[10,4,5400]{2,1,0:T(4,128)} %refs_2_.1) | copy-start | bytes 2592004
  0.0 21.1 %copy-start.3 = (f32[10,5400]{1,0:T(8,128)S(1)}, f32[10,5400]{1,0:T(8,128)}, u32[]{:S(2)}) copy-start(f32[10,5400]{1,0:T(8,128)} %refs_4_.1) | copy-start | bytes 648004
  3.9 17.3 %copy-start = (f32[10,4,5400]{2,1,0:T(4,128)S(1)}, f32[10,4,5400]{2,1,0:T(4,128)}, u32[]{:S(2)}) copy-start(f32[10,4,5400]{2,1,0:T(4,128)} %refs_1_.1) | copy-start | bytes 2592004
  3.9 17.3 %copy-start.2 = (f32[10,5400]{1,0:T(8,128)S(1)}, f32[10,5400]{1,0:T(8,128)}, u32[]{:S(2)}) copy-start(f32[10,5400]{1,0:T(8,128)} %refs_3_.1) | copy-start | bytes 648004
  3.9 9.4 %all-to-all-start = ((f32[4,1,10240]{2,1,0:T(1,128)}), f32[4,1,10240]{2,1,0:T(1,128)S(1)}, u32[]{:S(2)}, u32[]{:S(2)}) async-start(f32[4,1,10240]{2,1,0:T(1,128)} %bitcast.17), calls=%async_computation | async-start | bytes 327680 | tf_op jit(solution)/shard_map/all_to_all | solution.py:489
  13.9 14.0 %all-to-all-start.1 = ((f32[8,1,5120]{2,1,0:T(1,128)}), f32[8,1,5120]{2,1,0:T(1,128)S(1)}, u32[]{:S(2)}, u32[]{:S(2)}) async-start(f32[8,1,5120]{2,1,0:T(1,128)} %bitcast.5), calls=%async_computation.1 | async-start | bytes 327680 | tf_op jit(solution)/shard_map/all_to_all | solution.py:495
  36.6 11.2 %all-to-all-start.3 = ((f32[8,1,5120]{2,1,0:T(1,128)}), f32[8,1,5120]{2,1,0:T(1,128)S(1)}, u32[]{:S(2)}, u32[]{:S(2)}) async-start(f32[8,1,5120]{2,1,0:T(1,128)} %bitcast.10), calls=%async_computation.3 | async-start | bytes 327680 | tf_op jit(solution)/shard_map/all_to_all | solution.py:495

commit v10 on v8

--- a/solution.py
+++ b/solution.py
@@ -24,6 +24,7 @@
 SIDES = 3
 OWN = 8
 FIRST_PAIRS = 2
+CHAIN = 8
 
 
 def lane_of(rows):
@@ -77,12 +78,15 @@
     result = []
     for at in range(0, GAPS, held):
         value = jnp.zeros((rows, LANES), jnp.float32)
-        for gap in range(at, min(at + held, GAPS)):
-            start = IB * gap + first
-            place = (gap - at) * wide
-            for tile in range(max(start, 0) // LANES, min(start + wide - 1, CELLS - 1) // LANES + 1):
-                low = max(start, tile * LANES, 0)
-                value = jnp.where(lane >= place + low - start, rot(get(tile), place - start + tile * LANES), value)
+        for chain in range(at, min(at + held, GAPS), CHAIN):
+            link = jnp.zeros((rows, LANES), jnp.float32)
+            for gap in range(chain, min(chain + CHAIN, at + held, GAPS)):
+                start = IB * gap + first
+                place = (gap - at) * wide
+                for tile in range(max(start, 0) // LANES, min(start + wide - 1, CELLS - 1) // LANES + 1):
+                    low = max(start, tile * LANES, 0)
+                    link = jnp.where(lane >= place + low - start, rot(get(tile), place - start + tile * LANES), link)
+            value = jnp.where(lane >= (chain - at) * wide, link, value)
         result.append(value)
     return result
 
@@ -131,10 +135,15 @@
     x_copies = pair_copies(tracer_ref, x_ref, x_sems, 0, pairs)
     v_copies = pair_copies(velocity_ref, v_ref, v_sems, 0, pairs)
     d_copy = pltpu.make_async_copy(depth_ref, d_ref, d_sem)
+    d_copy.start()
     for pair in range(pairs):
         x_copies[pair].start()
         v_copies[pair].start()
-    d_copy.start()
+    d_copy.wait()
+    slot_lane = lane_of(count)
+    get_d = tile_getter(d_ref, slice(None), count)
+    d_south, d_north = window(get_d, 0, count), window(get_d, CELLS - IB, count)
+    d_gaps = gap_groups(get_d, -1, 2, count)[0]
     for pair in range(pairs):
         rows = pl.ds(8 * pair, 8)
         x_copies[pair].wait()
@@ -152,14 +161,9 @@
         for index, strip in enumerate(strips):
             strip_ref[index, rows, :] = strip
 
-    d_copy.wait()
     if out_ref.shape[0] > PARTS * count:
         rest = out_ref.shape[0] - PARTS * count
         out_ref[PARTS * count :, :] = jnp.zeros((rest, LANES), jnp.float32)
-    slot_lane = lane_of(count)
-    get_d = tile_getter(d_ref, slice(None), count)
-    d_south, d_north = window(get_d, 0, count), window(get_d, CELLS - IB, count)
-    d_gaps = gap_groups(get_d, -1, 2, count)[0]
     spare = (slot_lane >= SPARE) & (slot_lane < SPARE + PIECE)
 
     def put(part, value):
@@ -350,18 +354,19 @@
         pltpu.make_async_copy(rows, base_ref.at[slots], y_sems.at[pair]).wait()
 
 
-def finish_kernel(halo_ref, edge_a_ref, edge_b_ref, base_ref, out_ref,
-                  y_ref, own_ref, raw_ref, delta_ref, own_sems, in_sems, out_sems):
+def finish_kernel(arrived_ref, edge_a_ref, edge_b_ref, base_ref, out_ref,
+                  halo_ref, y_ref, own_ref, raw_ref, delta_ref, own_sems, in_sems, out_sems):
     count = out_ref.shape[0]
     pairs = count // 2
     rows = 4 * count
     split = edge_a_ref.shape[1]
+    halo_copy = pltpu.make_async_copy(arrived_ref, halo_ref, own_sems.at[2])
     own_copies = [
         pltpu.make_async_copy(edge_a_ref, own_ref.at[:, pl.ds(0, split)], own_sems.at[0]),
         pltpu.make_async_copy(edge_b_ref, own_ref.at[:, pl.ds(split, rows - split)], own_sems.at[1]),
     ]
     in_copies = pair_copies(base_ref, y_ref, in_sems, 0, pairs)
-    for copy in own_copies + in_copies:
+    for copy in [halo_copy] + in_copies + own_copies:
         copy.start()
     lane = lane_of(rows)
     level = (lax.broadcasted_iota(jnp.int32, (rows, LANES), 0) % 2).astype(jnp.float32)
@@ -376,6 +381,7 @@
 
     mirror = jnp.where(lane < IB, IB - 1 - lane, lane)
     slot_lane = lane_of(count)
+    halo_copy.wait()
     depth_x = rot(part(0), -SPARE)
     for index in range(1, 8):
         depth_x = jnp.where(slot_lane >= PIECE * index, rot(part(index), PIECE * index - SPARE), depth_x)
@@ -556,14 +562,15 @@
     return pl.pallas_call(
         finish_kernel,
         out_shape=jax.ShapeDtypeStruct(tracers.shape, f32),
-        in_specs=[in_vmem, anywhere, anywhere, in_hbm],
+        in_specs=[anywhere, anywhere, anywhere, in_hbm],
         out_specs=in_hbm,
         scratch_shapes=[
+            pltpu.VMEM((PARTS * slot_count, LANES), f32),
             pltpu.VMEM((state_rows, CELLS), f32),
             pltpu.VMEM((OWN * SIDES + 1, state_rows, LANES), f32),
             pltpu.VMEM((12, state_rows, LANES), f32),
             pltpu.VMEM((2 * SIDES, state_rows, LANES), f32),
-            dma((2,)),
+            dma((3,)),
             dma((pairs,)),
             dma((pairs,)),
         ],

time: 35.3 us -> 35.5 us (level)
  no operation moved by 1% of the time
where the time goes in v10:
time: 35.5 us; the launch traced here: 35.3 us
  Pallas kernels  15.9 us (45%)
  starting transfers between devices  9.89 us (28%)
  waiting for transfers between devices  8.39 us (24%)
  other arithmetic  0.79 us (2%)
    all_to_all x2, starting transfers between devices, exchanged(): lax.all_to_all(pieces, axes, 0, 0, tiled=True).reshape(slot_total, LANES)  9.89 us
    all_to_all x2, waiting for transfers between devices, exchanged(): lax.all_to_all(pieces, axes, 0, 0, tiled=True).reshape(slot_total, LANES)  8.39 us
    pallas_call x2, Pallas kernels, bulk(): pl.pallas_call(kernel, out_shape=[jax.ShapeDtypeStruct(tracers.shape, f32...  7.69 us
    pallas_call x1, Pallas kernels, per_device(): pl.pallas_call(pack_kernel, out_shape=jax.ShapeDtypeStruct((slot_total, L...  3.86 us
    pallas_call x1, Pallas kernels, per_device(): pl.pallas_call(finish_kernel, out_shape=jax.ShapeDtypeStruct(tracers.shap...  2.93 us
    pallas_call x1, Pallas kernels, per_device(): pl.pallas_call(route_kernel, grid=(device_count // PARTS,), out_shape=jax...  1.37 us
  transfers between devices with their start and end apart: 2, of which 2 were waited for; matrix products, arithmetic and copies ran while one was open for 3% of the time, Pallas kernels for 22%

profile of v10, /device:TPU:0, one launch (start us, length us, event | category | flops | bytes accessed | tf_op | source)
XLA Modules:
  0.0 35.3 jit_solution(8775794388657821506)
XLA Ops:
  0.0 0.0 copy-start.6
  0.0 0.0 copy-start.5
  0.0 0.0 copy-start.4
  0.0 0.0 copy-start
  0.0 0.0 copy-start.1
  0.0 3.9 %shard_map.73 = f32[320,128]{1,0:T(8,128)} custom-call(f32[10,4,5400]{2,1,0:T(4,128)} %refs_1_.1, f32[10,4,5400]{2,1,0:T(4,128)} %refs_2_.1, f32[10,5400]{1,0:T(8,128)} %refs_3_.1), custom_call_target="tpu_custom_call" | custom-call | flops 4000000 | bytes 2400000 | tf_op jit(solution)/shard_map/pallas_call | solution.py:489
  3.9 0.0 copy-start.2
  3.9 0.0 copy-start.3
  3.9 7.3 %all-to-all-start = ((f32[32,10,1,128]{3,2,1,0:T(1,128)}), f32[32,10,1,128]{3,2,1,0:T(1,128)S(1)}, u32[]{:S(2)}, u32[]{:S(2)}) async-start(f32[32,10,1,128]{3,2,1,0:T(1,128)} %bitcast.9), calls=%async_computation | async-start | bytes 327680 | tf_op jit(solution)/shard_map/all_to_all | solution.py:487
  11.2 0.0 copy-done.6
  11.2 0.0 copy-done.5
  11.3 0.0 copy-done.4
  11.3 0.4 %select_reduce_fusion.1 = s32[160,5]{0,1:T(8,128)S(1)} fusion(s32[160]{0:T(256)S(1)} %copy-done.4, s32[160,5]{0,1:T(8,128)S(1)} %pad_add_fusion), kind=kLoop, calls=%fused_computation.1 | loop fusion | flops 383200 | bytes 7040 | tf_op jit(solution)/shard_map/reduce_max | solution.py:461
  11.7 0.1 iota_compare_fusion.1
  11.8 0.3 select_reduce_fusion
  12.1 0.1 copy.19.code_ref.refs_5_
  12.2 0.0 copy-done
  12.3 0.0 copy-done.1
  12.3 0.0 copy-done.2
  12.3 0.0 copy-done.3
  12.3 3.2 %shard_map.74 = (f32[10,4,5400]{2,1,0:T(4,128)}, f32[25,16,128]{2,1,0:T(8,128)S(1)}) custom-call(s32[1]{0:T(128)} %bitcast.my_ref.part_ref.refs_0_, f32[10,4,5400]{2,1,0:T(4,128)S(1)} %copy-done, f32[10,4,5400]{2,1,0:T(4,128)S(1)} %copy-done.1, f32[10,5400]{1,0:T(8,128)S(1)} %copy-done.2, f32[10,5400]{1,0:T(8,128)S(1)} %copy-done.3, ...), custom_call_target="tpu_custom_call" | custom-call | flops 8000000 | bytes 1600000 | tf_op jit(solution)/shard_map/pallas_call | solution.py:513
  15.5 4.3 %all-to-all-done = f32[32,10,1,128]{3,2,1,0:T(1,128)S(1)} async-done(((f32[32,10,1,128]{3,2,1,0:T(1,128)}), f32[32,10,1,128]{3,2,1,0:T(1,128)S(1)}, u32[]{:S(2)}, u32[]{:S(2)}) %all-to-all-start) | async-done | bytes 163872 | tf_op jit(solution)/shard_map/all_to_all | solution.py:487
  19.8 1.4 %shard_map.75 = f32[320,128]{1,0:T(8,128)} custom-call(s32[1]{0:T(128)} %bitcast.my_ref.part_ref.refs_0_, s32[320,6]{1,0:T(8,128)S(1)} %copy.19.code_ref.refs_5_, f32[320,128]{1,0:T(8,128)S(1)} %bitcast.8), custom_call_target="tpu_custom_call" | custom-call | tf_op jit(solution)/shard_map/pallas_call | solution.py:545
  21.2 2.6 %all-to-all-start.1 = ((f32[32,10,1,128]{3,2,1,0:T(1,128)}), f32[32,10,1,128]{3,2,1,0:T(1,128)S(1)}, u32[]{:S(2)}, u32[]{:S(2)}) async-start(f32[32,10,1,128]{3,2,1,0:T(1,128)} %bitcast.5), calls=%async_computation.1 | async-start | bytes 327680 | tf_op jit(solution)/shard_map/all_to_all | solution.py:487
  23.8 4.5 %shard_map.76 = (f32[10,4,5400]{2,1,0:T(4,128)}, f32[25,24,128]{2,1,0:T(8,128)S(1)}) custom-call(s32[1]{0:T(128)} %bitcast.my_ref.part_ref.refs_0_, f32[10,4,5400]{2,1,0:T(4,128)S(1)} %copy-done, f32[10,4,5400]{2,1,0:T(4,128)S(1)} %copy-done.1, f32[10,5400]{1,0:T(8,128)S(1)} %copy-done.2, f32[10,5400]{1,0:T(8,128)S(1)} %copy-done.3, ...), custom_call_target="tpu_custom_call", output_to_operand_aliasing={{0}: (6, {})} | custom-call | flops 12000000 | bytes 2400000 | tf_op jit(solution)/shard_map/pallas_call | solution.py:513
  28.3 4.1 %all-to-all-done.1 = f32[32,10,1,128]{3,2,1,0:T(1,128)S(1)} async-done(((f32[32,10,1,128]{3,2,1,0:T(1,128)}), f32[32,10,1,128]{3,2,1,0:T(1,128)S(1)}, u32[]{:S(2)}, u32[]{:S(2)}) %all-to-all-start.1) | async-done | bytes 163872 | tf_op jit(solution)/shard_map/all_to_all | solution.py:487
  32.3 2.9 %shard_map.77 = f32[10,4,5400]{2,1,0:T(4,128)} custom-call(f32[320,128]{1,0:T(8,128)S(1)} %bitcast.7, f32[25,16,128]{2,1,0:T(8,128)S(1)} %get-tuple-element.17.edge_a_ref, f32[25,24,128]{2,1,0:T(8,128)S(1)} %get-tuple-element.19.edge_b_ref, f32[10,4,5400]{2,1,0:T(4,128)} %get-tuple-element.20.base_ref), custom_call_target="tpu_custom_call", output_to_operand_aliasing={{}: (3, {})} | custom-call | tf_op jit(solution)/shard_map/pallas_call | solution.py:562
  (2 shorter events, 0.0 us)
Async XLA Ops:
  0.0 11.2 %copy-start.6 = (s32[160]{0:T(256)S(1)}, s32[160]{0:T(256)}, u32[]{:S(2)}) copy-start(s32[160]{0:T(256)} %param.13) | copy-start | bytes 1924
  0.0 11.2 %copy-start.5 = (s32[160,4]{0,1:T(4,128)S(1)}, s32[160,4]{0,1:T(4,128)}, u32[]{:S(2)}) copy-start(s32[160,4]{0,1:T(4,128)} %param.12) | copy-start | bytes 7684
  0.0 11.3 %copy-start.4 = (s32[160]{0:T(256)S(1)}, s32[160]{0:T(256)}, u32[]{:S(2)}) copy-start(s32[160]{0:T(256)} %param.11) | copy-start | bytes 1924
  0.0 12.2 %copy-start = (f32[10,4,5400]{2,1,0:T(4,128)S(1)}, f32[10,4,5400]{2,1,0:T(4,128)}, u32[]{:S(2)}) copy-start(f32[10,4,5400]{2,1,0:T(4,128)} %refs_1_.1) | copy-start | bytes 2592004
  0.0 12.2 %copy-start.1 = (f32[10,4,5400]{2,1,0:T(4,128)S(1)}, f32[10,4,5400]{2,1,0:T(4,128)}, u32[]{:S(2)}) copy-start(f32[10,4,5400]{2,1,0:T(4,128)} %refs_2_.1) | copy-start | bytes 2592004
  3.9 8.4 %copy-start.2 = (f32[10,5400]{1,0:T(8,128)S(1)}, f32[10,5400]{1,0:T(8,128)}, u32[]{:S(2)}) copy-start(f32[10,5400]{1,0:T(8,128)} %refs_3_.1) | copy-start | bytes 648004
  3.9 8.4 %copy-start.3 = (f32[10,5400]{1,0:T(8,128)S(1)}, f32[10,5400]{1,0:T(8,128)}, u32[]{:S(2)}) copy-start(f32[10,5400]{1,0:T(8,128)} %refs_4_.1) | copy-start | bytes 648004
  3.9 15.9 %all-to-all-start = ((f32[32,10,1,128]{3,2,1,0:T(1,128)}), f32[32,10,1,128]{3,2,1,0:T(1,128)S(1)}, u32[]{:S(2)}, u32[]{:S(2)}) async-start(f32[32,10,1,128]{3,2,1,0:T(1,128)} %bitcast.9), calls=%async_computation | async-start | bytes 327680 | tf_op jit(solution)/shard_map/all_to_all | solution.py:487
  21.2 11.2 %all-to-all-start.1 = ((f32[32,10,1,128]{3,2,1,0:T(1,128)}), f32[32,10,1,128]{3,2,1,0:T(1,128)S(1)}, u32[]{:S(2)}, u32[]{:S(2)}) async-start(f32[32,10,1,128]{3,2,1,0:T(1,128)} %bitcast.5), calls=%async_computation.1 | async-start | bytes 327680 | tf_op jit(solution)/shard_map/all_to_all | solution.py:487

commit v11 on v8

--- a/solution.py
+++ b/solution.py
@@ -111,6 +111,23 @@
     return lane_pick(groups, 4 * (lane // 2) + 1 + lane % 2), lane_pick(groups, 4 * (lane // 2) + 3 * (lane % 2))
 
 
+def slots_getter(ref, pair):
+    def get(tile):
+        columns = slice(tile * LANES, min((tile + 1) * LANES, CELLS))
+        both = jnp.concatenate([ref[2 * pair, :, columns], ref[2 * pair + 1, :, columns]], axis=0)
+        if tile + 1 < TILES:
+            return both
+        return jnp.concatenate([both, jnp.zeros((8, WIDE - CELLS), jnp.float32)], axis=1)
+
+    return once(get)
+
+
+def slot_copies(source, target, sems):
+    count = source.shape[0]
+    return [pltpu.make_async_copy(source.at[pl.ds(at, 2)], target.at[pl.ds(at, 2)], sems.at[at // 2])
+            for at in range(0, count, 2)]
+
+
 def joined(south, north, half, rows):
     if half == 0:
         return jnp.where(lane_of(rows) < 64, south, rot(north, 64))
@@ -128,8 +145,8 @@
 def pack_kernel(tracer_ref, velocity_ref, depth_ref, out_ref, x_ref, v_ref, d_ref, strip_ref, x_sems, v_sems, d_sem):
     count = depth_ref.shape[0]
     pairs = count // 2
-    x_copies = pair_copies(tracer_ref, x_ref, x_sems, 0, pairs)
-    v_copies = pair_copies(velocity_ref, v_ref, v_sems, 0, pairs)
+    x_copies = slot_copies(tracer_ref, x_ref, x_sems)
+    v_copies = slot_copies(velocity_ref, v_ref, v_sems)
     d_copy = pltpu.make_async_copy(depth_ref, d_ref, d_sem)
     for pair in range(pairs):
         x_copies[pair].start()
@@ -138,12 +155,12 @@
     for pair in range(pairs):
         rows = pl.ds(8 * pair, 8)
         x_copies[pair].wait()
-        get_x = tile_getter(x_ref, rows, 8)
+        get_x = slots_getter(x_ref, pair)
         near, far = across_pair(get_x)
         south = [window(get_x, 0, 8), window(get_x, IB, 8)]
         north = [window(get_x, CELLS - IB, 8), window(get_x, CELLS - 2 * IB, 8)]
         v_copies[pair].wait()
-        get_v = tile_getter(v_ref, rows, 8)
+        get_v = slots_getter(v_ref, pair)
         v_south, v_north = window(get_v, 0, 8), window(get_v, CELLS - IB, 8)
         strips = [joined(south[0], north[0], half, 8) for half in range(2)]
         strips += [joined(south[1], north[1], half, 8) for half in range(2)]
@@ -360,7 +377,7 @@
         pltpu.make_async_copy(edge_a_ref, own_ref.at[:, pl.ds(0, split)], own_sems.at[0]),
         pltpu.make_async_copy(edge_b_ref, own_ref.at[:, pl.ds(split, rows - split)], own_sems.at[1]),
     ]
-    in_copies = pair_copies(base_ref, y_ref, in_sems, 0, pairs)
+    in_copies = slot_copies(base_ref, y_ref, in_sems)
     for copy in own_copies + in_copies:
         copy.start()
     lane = lane_of(rows)
@@ -417,7 +434,7 @@
             delta_ref[2 * side + place] = change + share * (other - change)
 
     lane = lane_of(8)
-    out_copies = []
+    out_copies = slot_copies(y_ref, out_ref, out_sems)
     for pair in range(pairs):
         mine = pl.ds(8 * pair, 8)
         in_copies[pair].wait()
@@ -438,11 +455,11 @@
                 if low < high:
                     inside = (lane >= low - at) & (lane < high - at)
                     change += jnp.where(inside, rot(source, start - at - origin), 0.0)
-            y_ref[mine, at:stop] = y_ref[mine, at:stop] + change[:, : stop - at]
-        copy = pltpu.make_async_copy(
-            y_ref.at[mine].reshape(2, 4, CELLS), out_ref.at[pl.ds(2 * pair, 2)], out_sems.at[pair])
-        copy.start()
-        out_copies.append(copy)
+            for slot in range(2):
+                index = 2 * pair + slot
+                part_of = change[4 * slot : 4 * slot + 4, : stop - at]
+                y_ref[index, :, at:stop] = y_ref[index, :, at:stop] + part_of
+        out_copies[pair].start()
     for copy in out_copies:
         copy.wait()
 
@@ -486,8 +503,8 @@
         in_specs=[in_hbm, in_hbm, in_hbm],
         out_specs=in_vmem,
         scratch_shapes=[
-            pltpu.VMEM((state_rows, CELLS), f32),
-            pltpu.VMEM((state_rows, CELLS), f32),
+            pltpu.VMEM(tracers.shape, f32),
+            pltpu.VMEM(tracers.shape, f32),
             pltpu.VMEM((slot_count, CELLS), f32),
             pltpu.VMEM((9, state_rows, LANES), f32),
             dma((pairs,)),
@@ -559,7 +576,7 @@
         in_specs=[in_vmem, anywhere, anywhere, in_hbm],
         out_specs=in_hbm,
         scratch_shapes=[
-            pltpu.VMEM((state_rows, CELLS), f32),
+            pltpu.VMEM(tracers.shape, f32),
             pltpu.VMEM((OWN * SIDES + 1, state_rows, LANES), f32),
             pltpu.VMEM((12, state_rows, LANES), f32),
             pltpu.VMEM((2 * SIDES, state_rows, LANES), f32),

time: 35.3 us -> 35.4 us (level)
  no operation moved by 1% of the time
where the time goes in v11:
time: 35.4 us; the launch traced here: 35.1 us
  Pallas kernels  15.7 us (44%)
  starting transfers between devices  9.89 us (28%)
  waiting for transfers between devices  8.39 us (24%)
  other arithmetic  0.79 us (2%)
    all_to_all x2, starting transfers between devices, exchanged(): lax.all_to_all(pieces, axes, 0, 0, tiled=True).reshape(slot_total, LANES)  9.89 us
    all_to_all x2, waiting for transfers between devices, exchanged(): lax.all_to_all(pieces, axes, 0, 0, tiled=True).reshape(slot_total, LANES)  8.39 us
    pallas_call x2, Pallas kernels, bulk(): pl.pallas_call(kernel, out_shape=[jax.ShapeDtypeStruct(tracers.shape, f32...  7.69 us
    pallas_call x1, Pallas kernels, per_device(): pl.pallas_call(pack_kernel, out_shape=jax.ShapeDtypeStruct((slot_total, L...  3.86 us
    pallas_call x1, Pallas kernels, per_device(): pl.pallas_call(finish_kernel, out_shape=jax.ShapeDtypeStruct(tracers.shap...  2.8 us
    pallas_call x1, Pallas kernels, per_device(): pl.pallas_call(route_kernel, grid=(device_count // PARTS,), out_shape=jax...  1.36 us
  transfers between devices with their start and end apart: 2, of which 2 were waited for; matrix products, arithmetic and copies ran while one was open for 3% of the time, Pallas kernels for 22%

profile of v11, /device:TPU:0, one launch (start us, length us, event | category | flops | bytes accessed | tf_op | source)
XLA Modules:
  0.0 35.1 jit_solution(5716062197612516865)
XLA Ops:
  0.0 0.0 copy-start.6
  0.0 0.0 copy-start.5
  0.0 0.0 copy-start.4
  0.0 0.0 copy-start
  0.0 0.0 copy-start.1
  0.0 3.9 %shard_map.73 = f32[320,128]{1,0:T(8,128)} custom-call(f32[10,4,5400]{2,1,0:T(4,128)} %refs_1_.1, f32[10,4,5400]{2,1,0:T(4,128)} %refs_2_.1, f32[10,5400]{1,0:T(8,128)} %refs_3_.1), custom_call_target="tpu_custom_call" | custom-call | flops 4000000 | bytes 2400000 | tf_op jit(solution)/shard_map/pallas_call | solution.py:500
  3.9 0.0 copy-start.2
  3.9 0.0 copy-start.3
  3.9 7.3 %all-to-all-start = ((f32[32,10,1,128]{3,2,1,0:T(1,128)}), f32[32,10,1,128]{3,2,1,0:T(1,128)S(1)}, u32[]{:S(2)}, u32[]{:S(2)}) async-start(f32[32,10,1,128]{3,2,1,0:T(1,128)} %bitcast.9), calls=%async_computation | async-start | bytes 327680 | tf_op jit(solution)/shard_map/all_to_all | solution.py:498
  11.2 0.0 copy-done.6
  11.2 0.0 copy-done.5
  11.3 0.0 copy-done.4
  11.3 0.4 %select_reduce_fusion.1 = s32[160,5]{0,1:T(8,128)S(1)} fusion(s32[160]{0:T(256)S(1)} %copy-done.4, s32[160,5]{0,1:T(8,128)S(1)} %pad_add_fusion), kind=kLoop, calls=%fused_computation.1 | loop fusion | flops 383200 | bytes 7040 | tf_op jit(solution)/shard_map/reduce_max | solution.py:472
  11.7 0.1 iota_compare_fusion.1
  11.8 0.3 select_reduce_fusion
  12.1 0.1 copy.19.code_ref.refs_5_
  12.2 0.0 copy-done
  12.2 0.0 copy-done.1
  12.3 0.0 copy-done.2
  12.3 0.0 copy-done.3
  12.3 3.2 %shard_map.74 = (f32[10,4,5400]{2,1,0:T(4,128)}, f32[25,16,128]{2,1,0:T(8,128)S(1)}) custom-call(s32[1]{0:T(128)} %bitcast.my_ref.part_ref.refs_0_, f32[10,4,5400]{2,1,0:T(4,128)S(1)} %copy-done, f32[10,4,5400]{2,1,0:T(4,128)S(1)} %copy-done.1, f32[10,5400]{1,0:T(8,128)S(1)} %copy-done.2, f32[10,5400]{1,0:T(8,128)S(1)} %copy-done.3, ...), custom_call_target="tpu_custom_call" | custom-call | flops 8000000 | bytes 1600000 | tf_op jit(solution)/shard_map/pallas_call | solution.py:524
  15.5 4.3 %all-to-all-done = f32[32,10,1,128]{3,2,1,0:T(1,128)S(1)} async-done(((f32[32,10,1,128]{3,2,1,0:T(1,128)}), f32[32,10,1,128]{3,2,1,0:T(1,128)S(1)}, u32[]{:S(2)}, u32[]{:S(2)}) %all-to-all-start) | async-done | bytes 163872 | tf_op jit(solution)/shard_map/all_to_all | solution.py:498
  19.8 1.4 %shard_map.75 = f32[320,128]{1,0:T(8,128)} custom-call(s32[1]{0:T(128)} %bitcast.my_ref.part_ref.refs_0_, s32[320,6]{1,0:T(8,128)S(1)} %copy.19.code_ref.refs_5_, f32[320,128]{1,0:T(8,128)S(1)} %bitcast.8), custom_call_target="tpu_custom_call" | custom-call | tf_op jit(solution)/shard_map/pallas_call | solution.py:556
  21.2 2.6 %all-to-all-start.1 = ((f32[32,10,1,128]{3,2,1,0:T(1,128)}), f32[32,10,1,128]{3,2,1,0:T(1,128)S(1)}, u32[]{:S(2)}, u32[]{:S(2)}) async-start(f32[32,10,1,128]{3,2,1,0:T(1,128)} %bitcast.5), calls=%async_computation.1 | async-start | bytes 327680 | tf_op jit(solution)/shard_map/all_to_all | solution.py:498
  23.7 4.5 %shard_map.76 = (f32[10,4,5400]{2,1,0:T(4,128)}, f32[25,24,128]{2,1,0:T(8,128)S(1)}) custom-call(s32[1]{0:T(128)} %bitcast.my_ref.part_ref.refs_0_, f32[10,4,5400]{2,1,0:T(4,128)S(1)} %copy-done, f32[10,4,5400]{2,1,0:T(4,128)S(1)} %copy-done.1, f32[10,5400]{1,0:T(8,128)S(1)} %copy-done.2, f32[10,5400]{1,0:T(8,128)S(1)} %copy-done.3, ...), custom_call_target="tpu_custom_call", output_to_operand_aliasing={{0}: (6, {})} | custom-call | flops 12000000 | bytes 2400000 | tf_op jit(solution)/shard_map/pallas_call | solution.py:524
  28.2 4.1 %all-to-all-done.1 = f32[32,10,1,128]{3,2,1,0:T(1,128)S(1)} async-done(((f32[32,10,1,128]{3,2,1,0:T(1,128)}), f32[32,10,1,128]{3,2,1,0:T(1,128)S(1)}, u32[]{:S(2)}, u32[]{:S(2)}) %all-to-all-start.1) | async-done | bytes 163872 | tf_op jit(solution)/shard_map/all_to_all | solution.py:498
  32.3 2.8 %shard_map.77 = f32[10,4,5400]{2,1,0:T(4,128)} custom-call(f32[320,128]{1,0:T(8,128)S(1)} %bitcast.7, f32[25,16,128]{2,1,0:T(8,128)S(1)} %get-tuple-element.17.edge_a_ref, f32[25,24,128]{2,1,0:T(8,128)S(1)} %get-tuple-element.19.edge_b_ref, f32[10,4,5400]{2,1,0:T(4,128)} %get-tuple-element.20.base_ref), custom_call_target="tpu_custom_call", output_to_operand_aliasing={{}: (3, {})} | custom-call | tf_op jit(solution)/shard_map/pallas_call | solution.py:573
  (2 shorter events, 0.0 us)
Async XLA Ops:
  0.0 11.2 %copy-start.6 = (s32[160]{0:T(256)S(1)}, s32[160]{0:T(256)}, u32[]{:S(2)}) copy-start(s32[160]{0:T(256)} %param.13) | copy-start | bytes 1924
  0.0 11.2 %copy-start.5 = (s32[160,4]{0,1:T(4,128)S(1)}, s32[160,4]{0,1:T(4,128)}, u32[]{:S(2)}) copy-start(s32[160,4]{0,1:T(4,128)} %param.12) | copy-start | bytes 7684
  0.0 11.3 %copy-start.4 = (s32[160]{0:T(256)S(1)}, s32[160]{0:T(256)}, u32[]{:S(2)}) copy-start(s32[160]{0:T(256)} %param.11) | copy-start | bytes 1924
  0.0 12.2 %copy-start = (f32[10,4,5400]{2,1,0:T(4,128)S(1)}, f32[10,4,5400]{2,1,0:T(4,128)}, u32[]{:S(2)}) copy-start(f32[10,4,5400]{2,1,0:T(4,128)} %refs_1_.1) | copy-start | bytes 2592004
  0.0 12.2 %copy-start.1 = (f32[10,4,5400]{2,1,0:T(4,128)S(1)}, f32[10,4,5400]{2,1,0:T(4,128)}, u32[]{:S(2)}) copy-start(f32[10,4,5400]{2,1,0:T(4,128)} %refs_2_.1) | copy-start | bytes 2592004
  3.9 8.4 %copy-start.2 = (f32[10,5400]{1,0:T(8,128)S(1)}, f32[10,5400]{1,0:T(8,128)}, u32[]{:S(2)}) copy-start(f32[10,5400]{1,0:T(8,128)} %refs_3_.1) | copy-start | bytes 648004
  3.9 8.4 %copy-start.3 = (f32[10,5400]{1,0:T(8,128)S(1)}, f32[10,5400]{1,0:T(8,128)}, u32[]{:S(2)}) copy-start(f32[10,5400]{1,0:T(8,128)} %refs_4_.1) | copy-start | bytes 648004
  3.9 15.9 %all-to-all-start = ((f32[32,10,1,128]{3,2,1,0:T(1,128)}), f32[32,10,1,128]{3,2,1,0:T(1,128)S(1)}, u32[]{:S(2)}, u32[]{:S(2)}) async-start(f32[32,10,1,128]{3,2,1,0:T(1,128)} %bitcast.9), calls=%async_computation | async-start | bytes 327680 | tf_op jit(solution)/shard_map/all_to_all | solution.py:498
  21.2 11.2 %all-to-all-start.1 = ((f32[32,10,1,128]{3,2,1,0:T(1,128)}), f32[32,10,1,128]{3,2,1,0:T(1,128)S(1)}, u32[]{:S(2)}, u32[]{:S(2)}) async-start(f32[32,10,1,128]{3,2,1,0:T(1,128)} %bitcast.5), calls=%async_computation.1 | async-start | bytes 327680 | tf_op jit(solution)/shard_map/all_to_all | solution.py:498

commit v12 on v8

--- a/solution.py
+++ b/solution.py
@@ -496,6 +496,7 @@
         ],
         cost_estimate=pl.CostEstimate(flops=4_000_000, bytes_accessed=2_400_000, transcendentals=0),
     )(tracers, velocity, kmt)
+    pack, *later = lax.optimization_barrier((pack, tracers, velocity, kmt, kappa))
     held = exchanged(pack)
     codes = route_codes(block_owner, neighbours, fold_partner, slot_total)
 
@@ -530,7 +531,7 @@
             input_output_aliases={6: 0} if extra else {},
             compiler_params=limit,
             cost_estimate=pl.CostEstimate(flops=4_000_000 * some, bytes_accessed=800_000 * some, transcendentals=0),
-        )(my_index, tracers, velocity, kmt, kappa, codes, *extra)
+        )(my_index, *later, codes, *extra)
 
     base, edge_a = bulk(0, FIRST_PAIRS, codes, None)
     held, edge_a = lax.optimization_barrier((held, edge_a))

time: 35.3 us -> 35.3 us (level)
  no operation moved by 1% of the time
where the time goes in v12:
time: 35.3 us; the launch traced here: 35.1 us
  Pallas kernels  15.7 us (44%)
  starting transfers between devices  9.89 us (28%)
  waiting for transfers between devices  8.39 us (24%)
  other arithmetic  0.79 us (2%)
    all_to_all x2, starting transfers between devices, exchanged(): lax.all_to_all(pieces, axes, 0, 0, tiled=True).reshape(slot_total, LANES)  9.89 us
    all_to_all x2, waiting for transfers between devices, exchanged(): lax.all_to_all(pieces, axes, 0, 0, tiled=True).reshape(slot_total, LANES)  8.39 us
    pallas_call x2, Pallas kernels, bulk(): pl.pallas_call(kernel, out_shape=[jax.ShapeDtypeStruct(tracers.shape, f32...  7.69 us
    pallas_call x1, Pallas kernels, per_device(): pl.pallas_call(pack_kernel, out_shape=jax.ShapeDtypeStruct((slot_total, L...  3.85 us
    pallas_call x1, Pallas kernels, per_device(): pl.pallas_call(finish_kernel, out_shape=jax.ShapeDtypeStruct(tracers.shap...  2.77 us
    pallas_call x1, Pallas kernels, per_device(): pl.pallas_call(route_kernel, grid=(device_count // PARTS,), out_shape=jax...  1.36 us
  transfers between devices with their start and end apart: 2, of which 2 were waited for; matrix products, arithmetic and copies ran while one was open for 3% of the time, Pallas kernels for 22%

profile of v12, /device:TPU:0, one launch (start us, length us, event | category | flops | bytes accessed | tf_op | source)
XLA Modules:
  0.0 35.1 jit_solution(9879822499335676642)
XLA Ops:
  0.0 0.0 copy-start.6
  0.0 0.0 copy-start.5
  0.0 0.0 copy-start.4
  0.0 0.0 copy-start
  0.0 0.0 copy-start.1
  0.0 3.8 %shard_map.73 = f32[320,128]{1,0:T(8,128)} custom-call(f32[10,4,5400]{2,1,0:T(4,128)} %refs_1_, f32[10,4,5400]{2,1,0:T(4,128)} %refs_2_, f32[10,5400]{1,0:T(8,128)} %refs_3_), custom_call_target="tpu_custom_call" | custom-call | flops 4000000 | bytes 2400000 | tf_op jit(solution)/shard_map/pallas_call | solution.py:483
  3.9 0.0 copy-start.2
  3.9 0.0 copy-start.3
  3.9 7.3 %all-to-all-start = ((f32[32,10,1,128]{3,2,1,0:T(1,128)}), f32[32,10,1,128]{3,2,1,0:T(1,128)S(1)}, u32[]{:S(2)}, u32[]{:S(2)}) async-start(f32[32,10,1,128]{3,2,1,0:T(1,128)} %bitcast.9), calls=%async_computation | async-start | bytes 327680 | tf_op jit(solution)/shard_map/all_to_all | solution.py:481
  11.2 0.0 copy-done.6
  11.2 0.0 copy-done.5
  11.3 0.0 copy-done.4
  11.3 0.4 %select_reduce_fusion.1 = s32[160,5]{0,1:T(8,128)S(1)} fusion(s32[160]{0:T(256)S(1)} %copy-done.4, s32[160,5]{0,1:T(8,128)S(1)} %pad_add_fusion), kind=kLoop, calls=%fused_computation.1 | loop fusion | flops 383200 | bytes 7040 | tf_op jit(solution)/shard_map/reduce_max | solution.py:455
  11.7 0.1 iota_compare_fusion.1
  11.8 0.3 select_reduce_fusion
  12.1 0.1 copy.19.code_ref.refs_5_
  12.2 0.0 copy-done
  12.2 0.0 copy-done.1
  12.2 0.0 copy-done.2
  12.3 0.0 copy-done.3
  12.3 3.2 %shard_map.74 = (f32[10,4,5400]{2,1,0:T(4,128)}, f32[25,16,128]{2,1,0:T(8,128)S(1)}) custom-call(s32[1]{0:T(128)} %bitcast.my_ref.part_ref.refs_0_, f32[10,4,5400]{2,1,0:T(4,128)S(1)} %copy-done, f32[10,4,5400]{2,1,0:T(4,128)S(1)} %copy-done.1, f32[10,5400]{1,0:T(8,128)S(1)} %copy-done.2, f32[10,5400]{1,0:T(8,128)S(1)} %copy-done.3, ...), custom_call_target="tpu_custom_call" | custom-call | flops 8000000 | bytes 1600000 | tf_op jit(solution)/shard_map/pallas_call | solution.py:508
  15.5 4.3 %all-to-all-done = f32[32,10,1,128]{3,2,1,0:T(1,128)S(1)} async-done(((f32[32,10,1,128]{3,2,1,0:T(1,128)}), f32[32,10,1,128]{3,2,1,0:T(1,128)S(1)}, u32[]{:S(2)}, u32[]{:S(2)}) %all-to-all-start) | async-done | bytes 163872 | tf_op jit(solution)/shard_map/all_to_all | solution.py:481
  19.8 1.4 %shard_map.75 = f32[320,128]{1,0:T(8,128)} custom-call(s32[1]{0:T(128)} %bitcast.my_ref.part_ref.refs_0_, s32[320,6]{1,0:T(8,128)S(1)} %copy.19.code_ref.refs_5_, f32[320,128]{1,0:T(8,128)S(1)} %bitcast.8), custom_call_target="tpu_custom_call" | custom-call | tf_op jit(solution)/shard_map/pallas_call | solution.py:540
  21.2 2.6 %all-to-all-start.1 = ((f32[32,10,1,128]{3,2,1,0:T(1,128)}), f32[32,10,1,128]{3,2,1,0:T(1,128)S(1)}, u32[]{:S(2)}, u32[]{:S(2)}) async-start(f32[32,10,1,128]{3,2,1,0:T(1,128)} %bitcast.5), calls=%async_computation.1 | async-start | bytes 327680 | tf_op jit(solution)/shard_map/all_to_all | solution.py:481
  23.7 4.5 %shard_map.76 = (f32[10,4,5400]{2,1,0:T(4,128)}, f32[25,24,128]{2,1,0:T(8,128)S(1)}) custom-call(s32[1]{0:T(128)} %bitcast.my_ref.part_ref.refs_0_, f32[10,4,5400]{2,1,0:T(4,128)S(1)} %copy-done, f32[10,4,5400]{2,1,0:T(4,128)S(1)} %copy-done.1, f32[10,5400]{1,0:T(8,128)S(1)} %copy-done.2, f32[10,5400]{1,0:T(8,128)S(1)} %copy-done.3, ...), custom_call_target="tpu_custom_call", output_to_operand_aliasing={{0}: (6, {})} | custom-call | flops 12000000 | bytes 2400000 | tf_op jit(solution)/shard_map/pallas_call | solution.py:508
  28.2 4.1 %all-to-all-done.1 = f32[32,10,1,128]{3,2,1,0:T(1,128)S(1)} async-done(((f32[32,10,1,128]{3,2,1,0:T(1,128)}), f32[32,10,1,128]{3,2,1,0:T(1,128)S(1)}, u32[]{:S(2)}, u32[]{:S(2)}) %all-to-all-start.1) | async-done | bytes 163872 | tf_op jit(solution)/shard_map/all_to_all | solution.py:481
  32.3 2.8 %shard_map.77 = f32[10,4,5400]{2,1,0:T(4,128)} custom-call(f32[320,128]{1,0:T(8,128)S(1)} %bitcast.7, f32[25,16,128]{2,1,0:T(8,128)S(1)} %get-tuple-element.27.edge_a_ref, f32[25,24,128]{2,1,0:T(8,128)S(1)} %get-tuple-element.29.edge_b_ref, f32[10,4,5400]{2,1,0:T(4,128)} %get-tuple-element.30.base_ref), custom_call_target="tpu_custom_call", output_to_operand_aliasing={{}: (3, {})} | custom-call | tf_op jit(solution)/shard_map/pallas_call | solution.py:557
  (2 shorter events, 0.0 us)
Async XLA Ops:
  0.0 11.2 %copy-start.6 = (s32[160]{0:T(256)S(1)}, s32[160]{0:T(256)}, u32[]{:S(2)}) copy-start(s32[160]{0:T(256)} %param.13) | copy-start | bytes 1924
  0.0 11.2 %copy-start.5 = (s32[160,4]{0,1:T(4,128)S(1)}, s32[160,4]{0,1:T(4,128)}, u32[]{:S(2)}) copy-start(s32[160,4]{0,1:T(4,128)} %param.12) | copy-start | bytes 7684
  0.0 11.3 %copy-start.4 = (s32[160]{0:T(256)S(1)}, s32[160]{0:T(256)}, u32[]{:S(2)}) copy-start(s32[160]{0:T(256)} %param.11) | copy-start | bytes 1924
  0.0 12.2 %copy-start = (f32[10,4,5400]{2,1,0:T(4,128)S(1)}, f32[10,4,5400]{2,1,0:T(4,128)}, u32[]{:S(2)}) copy-start(f32[10,4,5400]{2,1,0:T(4,128)} %refs_1_) | copy-start | bytes 2592004
  0.0 12.2 %copy-start.1 = (f32[10,4,5400]{2,1,0:T(4,128)S(1)}, f32[10,4,5400]{2,1,0:T(4,128)}, u32[]{:S(2)}) copy-start(f32[10,4,5400]{2,1,0:T(4,128)} %refs_2_) | copy-start | bytes 2592004
  3.9 8.4 %copy-start.2 = (f32[10,5400]{1,0:T(8,128)S(1)}, f32[10,5400]{1,0:T(8,128)}, u32[]{:S(2)}) copy-start(f32[10,5400]{1,0:T(8,128)} %refs_3_) | copy-start | bytes 648004
  3.9 8.4 %copy-start.3 = (f32[10,5400]{1,0:T(8,128)S(1)}, f32[10,5400]{1,0:T(8,128)}, u32[]{:S(2)}) copy-start(f32[10,5400]{1,0:T(8,128)} %refs_4_) | copy-start | bytes 648004
  3.9 15.9 %all-to-all-start = ((f32[32,10,1,128]{3,2,1,0:T(1,128)}), f32[32,10,1,128]{3,2,1,0:T(1,128)S(1)}, u32[]{:S(2)}, u32[]{:S(2)}) async-start(f32[32,10,1,128]{3,2,1,0:T(1,128)} %bitcast.9), calls=%async_computation | async-start | bytes 327680 | tf_op jit(solution)/shard_map/all_to_all | solution.py:481
  21.2 11.2 %all-to-all-start.1 = ((f32[32,10,1,128]{3,2,1,0:T(1,128)}), f32[32,10,1,128]{3,2,1,0:T(1,128)S(1)}, u32[]{:S(2)}, u32[]{:S(2)}) async-start(f32[32,10,1,128]{3,2,1,0:T(1,128)} %bitcast.5), calls=%async_computation.1 | async-start | bytes 327680 | tf_op jit(solution)/shard_map/all_to_all | solution.py:481

commit v13 on v8

--- a/solution.py
+++ b/solution.py
@@ -494,6 +494,7 @@
             dma((pairs,)),
             dma,
         ],
+        compiler_params=pltpu.CompilerParams(vmem_limit_bytes=127 * 512 * 1024),
         cost_estimate=pl.CostEstimate(flops=4_000_000, bytes_accessed=2_400_000, transcendentals=0),
     )(tracers, velocity, kmt)
     held = exchanged(pack)

time: 35.3 us -> 36.6 us (1.037)
  waiting for transfers between devices: 8.39 us -> 6.05 us
  local copies, waits for them, and re-layouts: 0.17 us -> 2.49 us
  starting transfers between devices: 9.89 us -> 11.2 us
    all_to_all x2, waiting for transfers between devices: 8.39 us -> 6.05 us  [exchanged(): lax.all_to_all(pieces, axes, 0, 0, tiled=True).reshape(slot_total, LANES)]
    unnamed x14 -> x18, local copies, waits for them, and re-layouts: 0.03 us -> 2.36 us
    all_to_all x2, starting transfers between devices: 9.89 us -> 11.2 us  [exchanged(): lax.all_to_all(pieces, axes, 0, 0, tiled=True).reshape(slot_total, LANES)]
  transfers between devices with their start and end apart: 2 -> 2, of which waited for: 2 -> 2; matrix products, arithmetic and copies ran while one was open for 3% -> 3% of each run, Pallas kernels for 22% -> 21%
where the time goes in v13:
time: 36.6 us; the launch traced here: 36.3 us
  Pallas kernels  15.6 us (43%)
  starting transfers between devices  11.2 us (31%)
  waiting for transfers between devices  6.05 us (17%)
  local copies, waits for them, and re-layouts  2.49 us (7%)
  other arithmetic  0.79 us (2%)
    all_to_all x2, starting transfers between devices, exchanged(): lax.all_to_all(pieces, axes, 0, 0, tiled=True).reshape(slot_total, LANES)  11.2 us
    pallas_call x2, Pallas kernels, bulk(): pl.pallas_call(kernel, out_shape=[jax.ShapeDtypeStruct(tracers.shape, f32...  7.69 us
    all_to_all x2, waiting for transfers between devices, exchanged(): lax.all_to_all(pieces, axes, 0, 0, tiled=True).reshape(slot_total, LANES)  6.05 us
    pallas_call x1, Pallas kernels, per_device(): pl.pallas_call(pack_kernel, out_shape=jax.ShapeDtypeStruct((slot_total, L...  3.75 us
    pallas_call x1, Pallas kernels, per_device(): pl.pallas_call(finish_kernel, out_shape=jax.ShapeDtypeStruct(tracers.shap...  2.77 us
    unnamed x18, local copies, waits for them, and re-layouts  2.36 us
    pallas_call x1, Pallas kernels, per_device(): pl.pallas_call(route_kernel, grid=(device_count // PARTS,), out_shape=jax...  1.37 us
  transfers between devices with their start and end apart: 2, of which 2 were waited for; matrix products, arithmetic and copies ran while one was open for 3% of the time, Pallas kernels for 21%

profile of v13, /device:TPU:0, one launch (start us, length us, event | category | flops | bytes accessed | tf_op | source)
XLA Modules:
  0.0 36.3 jit_solution(1643958438691512620)
XLA Ops:
  0.0 0.0 copy-start.8
  0.0 0.0 copy-start.7
  0.0 0.0 copy-start.6
  0.0 3.8 %shard_map.73 = f32[320,128]{1,0:T(8,128)} custom-call(f32[10,4,5400]{2,1,0:T(4,128)} %refs_1_.1, f32[10,4,5400]{2,1,0:T(4,128)} %refs_2_.1, f32[10,5400]{1,0:T(8,128)} %refs_3_.1), custom_call_target="tpu_custom_call" | custom-call | flops 4000000 | bytes 2400000 | tf_op jit(solution)/shard_map/pallas_call | solution.py:483
  3.8 0.0 copy-start.4
  3.8 0.0 copy-start.5
  3.8 7.3 %all-to-all-start = ((f32[32,10,1,128]{3,2,1,0:T(1,128)}), f32[32,10,1,128]{3,2,1,0:T(1,128)S(1)}, u32[]{:S(2)}, u32[]{:S(2)}) async-start(f32[32,10,1,128]{3,2,1,0:T(1,128)} %bitcast.9), calls=%async_computation | async-start | bytes 327680 | tf_op jit(solution)/shard_map/all_to_all | solution.py:481
  11.1 0.0 copy-done.8
  11.1 0.0 copy-done.7
  11.1 0.0 copy-done.6
  11.2 0.4 %select_reduce_fusion.1 = s32[160,5]{0,1:T(8,128)S(1)} fusion(s32[160]{0:T(256)S(1)} %copy-done.6, s32[160,5]{0,1:T(8,128)S(1)} %pad_add_fusion), kind=kLoop, calls=%fused_computation.1 | loop fusion | flops 383200 | bytes 7040 | tf_op jit(solution)/shard_map/reduce_max | solution.py:455
  11.6 0.1 iota_compare_fusion.1
  11.7 0.3 select_reduce_fusion
  12.0 0.1 copy.19.code_ref.refs_5_
  12.1 0.0 copy-done.4
  12.1 0.0 copy-done.5
  12.1 0.0 copy-start
  12.1 1.2 %copy-done = f32[10,4,5400]{2,1,0:T(4,128)S(1)} copy-done((f32[10,4,5400]{2,1,0:T(4,128)S(1)}, f32[10,4,5400]{2,1,0:T(4,128)}, u32[]{:S(2)}) %copy-start) | copy-done | bytes 864024
  13.3 0.0 copy-start.2
  13.3 1.2 %copy-done.2 = f32[10,4,5400]{2,1,0:T(4,128)S(1)} copy-done((f32[10,4,5400]{2,1,0:T(4,128)S(1)}, f32[10,4,5400]{2,1,0:T(4,128)}, u32[]{:S(2)}) %copy-start.2) | copy-done | bytes 864024
  14.5 0.0 copy-start.1
  14.5 0.0 copy-start.3
  14.5 3.2 %shard_map.74 = (f32[10,4,5400]{2,1,0:T(4,128)}, f32[25,16,128]{2,1,0:T(8,128)S(1)}) custom-call(s32[1]{0:T(128)} %bitcast.my_ref.part_ref.refs_0_, f32[10,4,5400]{2,1,0:T(4,128)S(1)} %copy-done, f32[10,4,5400]{2,1,0:T(4,128)S(1)} %copy-done.2, f32[10,5400]{1,0:T(8,128)S(1)} %copy-done.4, f32[10,5400]{1,0:T(8,128)S(1)} %copy-done.5, ...), custom_call_target="tpu_custom_call" | custom-call | flops 8000000 | bytes 1600000 | tf_op jit(solution)/shard_map/pallas_call | solution.py:508
  17.7 2.0 %all-to-all-done = f32[32,10,1,128]{3,2,1,0:T(1,128)S(1)} async-done(((f32[32,10,1,128]{3,2,1,0:T(1,128)}), f32[32,10,1,128]{3,2,1,0:T(1,128)S(1)}, u32[]{:S(2)}, u32[]{:S(2)}) %all-to-all-start) | async-done | bytes 163872 | tf_op jit(solution)/shard_map/all_to_all | solution.py:481
  19.7 1.4 %shard_map.75 = f32[320,128]{1,0:T(8,128)} custom-call(s32[1]{0:T(128)} %bitcast.my_ref.part_ref.refs_0_, s32[320,6]{1,0:T(8,128)S(1)} %copy.19.code_ref.refs_5_, f32[320,128]{1,0:T(8,128)S(1)} %bitcast.8), custom_call_target="tpu_custom_call" | custom-call | tf_op jit(solution)/shard_map/pallas_call | solution.py:540
  21.0 3.9 %all-to-all-start.1 = ((f32[32,10,1,128]{3,2,1,0:T(1,128)}), f32[32,10,1,128]{3,2,1,0:T(1,128)S(1)}, u32[]{:S(2)}, u32[]{:S(2)}) async-start(f32[32,10,1,128]{3,2,1,0:T(1,128)} %bitcast.5), calls=%async_computation.1 | async-start | bytes 327680 | tf_op jit(solution)/shard_map/all_to_all | solution.py:481
  24.9 0.0 copy-done.1
  24.9 0.0 copy-done.3
  24.9 4.5 %shard_map.76 = (f32[10,4,5400]{2,1,0:T(4,128)}, f32[25,24,128]{2,1,0:T(8,128)S(1)}) custom-call(s32[1]{0:T(128)} %bitcast.my_ref.part_ref.refs_0_, f32[10,4,5400]{2,1,0:T(4,128)S(1)} %copy-done.1, f32[10,4,5400]{2,1,0:T(4,128)S(1)} %copy-done.3, f32[10,5400]{1,0:T(8,128)S(1)} %copy-done.4, ...), custom_call_target="tpu_custom_call", output_to_operand_aliasing={{0}: (6, {})} | custom-call | flops 12000000 | bytes 2400000 | tf_op jit(solution)/shard_map/pallas_call | solution.py:508
  29.4 4.1 %all-to-all-done.1 = f32[32,10,1,128]{3,2,1,0:T(1,128)S(1)} async-done(((f32[32,10,1,128]{3,2,1,0:T(1,128)}), f32[32,10,1,128]{3,2,1,0:T(1,128)S(1)}, u32[]{:S(2)}, u32[]{:S(2)}) %all-to-all-start.1) | async-done | bytes 163872 | tf_op jit(solution)/shard_map/all_to_all | solution.py:481
  33.5 2.8 %shard_map.77 = f32[10,4,5400]{2,1,0:T(4,128)} custom-call(f32[320,128]{1,0:T(8,128)S(1)} %bitcast.7, f32[25,16,128]{2,1,0:T(8,128)S(1)} %get-tuple-element.17.edge_a_ref, f32[25,24,128]{2,1,0:T(8,128)S(1)} %get-tuple-element.19.edge_b_ref, f32[10,4,5400]{2,1,0:T(4,128)} %get-tuple-element.20.base_ref), custom_call_target="tpu_custom_call", output_to_operand_aliasing={{}: (3, {})} | custom-call | tf_op jit(solution)/shard_map/pallas_call | solution.py:557
  (2 shorter events, 0.0 us)
Async XLA Ops:
  0.0 11.1 %copy-start.8 = (s32[160]{0:T(256)S(1)}, s32[160]{0:T(256)}, u32[]{:S(2)}) copy-start(s32[160]{0:T(256)} %param.13) | copy-start | bytes 1924
  0.0 11.1 %copy-start.7 = (s32[160,4]{0,1:T(4,128)S(1)}, s32[160,4]{0,1:T(4,128)}, u32[]{:S(2)}) copy-start(s32[160,4]{0,1:T(4,128)} %param.12) | copy-start | bytes 7684
  0.0 11.1 %copy-start.6 = (s32[160]{0:T(256)S(1)}, s32[160]{0:T(256)}, u32[]{:S(2)}) copy-start(s32[160]{0:T(256)} %param.11) | copy-start | bytes 1924
  3.8 8.3 %copy-start.4 = (f32[10,5400]{1,0:T(8,128)S(1)}, f32[10,5400]{1,0:T(8,128)}, u32[]{:S(2)}) copy-start(f32[10,5400]{1,0:T(8,128)} %refs_3_.1) | copy-start | bytes 648004
  3.8 8.3 %copy-start.5 = (f32[10,5400]{1,0:T(8,128)S(1)}, f32[10,5400]{1,0:T(8,128)}, u32[]{:S(2)}) copy-start(f32[10,5400]{1,0:T(8,128)} %refs_4_.1) | copy-start | bytes 648004
  3.8 15.9 %all-to-all-start = ((f32[32,10,1,128]{3,2,1,0:T(1,128)}), f32[32,10,1,128]{3,2,1,0:T(1,128)S(1)}, u32[]{:S(2)}, u32[]{:S(2)}) async-start(f32[32,10,1,128]{3,2,1,0:T(1,128)} %bitcast.9), calls=%async_computation | async-start | bytes 327680 | tf_op jit(solution)/shard_map/all_to_all | solution.py:481
  12.1 1.2 %copy-start = (f32[10,4,5400]{2,1,0:T(4,128)S(1)}, f32[10,4,5400]{2,1,0:T(4,128)}, u32[]{:S(2)}) copy-start(f32[10,4,5400]{2,1,0:T(4,128)} %refs_1_.1) | copy-start | bytes 2592004
  13.3 1.2 %copy-start.2 = (f32[10,4,5400]{2,1,0:T(4,128)S(1)}, f32[10,4,5400]{2,1,0:T(4,128)}, u32[]{:S(2)}) copy-start(f32[10,4,5400]{2,1,0:T(4,128)} %refs_2_.1) | copy-start | bytes 2592004
  14.5 10.4 %copy-start.1 = (f32[10,4,5400]{2,1,0:T(4,128)S(1)}, f32[10,4,5400]{2,1,0:T(4,128)}, u32[]{:S(2)}) copy-start(f32[10,4,5400]{2,1,0:T(4,128)} %refs_1_.1) | copy-start | bytes 2592004
  14.5 10.5 %copy-start.3 = (f32[10,4,5400]{2,1,0:T(4,128)S(1)}, f32[10,4,5400]{2,1,0:T(4,128)}, u32[]{:S(2)}) copy-start(f32[10,4,5400]{2,1,0:T(4,128)} %refs_2_.1) | copy-start | bytes 2592004
  21.0 12.4 %all-to-all-start.1 = ((f32[32,10,1,128]{3,2,1,0:T(1,128)}), f32[32,10,1,128]{3,2,1,0:T(1,128)S(1)}, u32[]{:S(2)}, u32[]{:S(2)}) async-start(f32[32,10,1,128]{3,2,1,0:T(1,128)} %bitcast.5), calls=%async_computation.1 | async-start | bytes 327680 | tf_op jit(solution)/shard_map/all_to_all | solution.py:481

commit v14 on v8

--- a/solution.py
+++ b/solution.py
@@ -71,28 +71,35 @@
     return jnp.where(lane_of(rows) < LANES - offset, head, rot(get(tile + 1), -offset))
 
 
-def gap_groups(get, first, wide, rows):
+def gap_strip(get, offset, wide, rows):
     lane = lane_of(rows)
-    held = LANES // wide
-    result = []
-    for at in range(0, GAPS, held):
-        value = jnp.zeros((rows, LANES), jnp.float32)
-        for gap in range(at, min(at + held, GAPS)):
-            start = IB * gap + first
-            place = (gap - at) * wide
-            for tile in range(max(start, 0) // LANES, min(start + wide - 1, CELLS - 1) // LANES + 1):
-                low = max(start, tile * LANES, 0)
-                value = jnp.where(lane >= place + low - start, rot(get(tile), place - start + tile * LANES), value)
-        result.append(value)
-    return result
+    place = 1 if wide == 1 and offset > 0 else 0
+    value = jnp.zeros((rows, LANES), jnp.float32)
+    for turn in range(16):
+        cells = []
+        for gap in range(turn, GAPS, 16):
+            cell = IB * gap + offset
+            if cell + wide > 0:
+                cells.append((max(cell, 0) % LANES, max(cell, 0) // LANES))
+        cells.sort()
+        merged = get(cells[0][1])
+        for at, tile in cells[1:]:
+            merged = jnp.where(lane >= at, get(tile), merged)
+        moved = rot(merged, 2 * turn + place - IB * turn - offset)
+        value = jnp.where(lane % 32 >= 2 * turn + place, moved, value)
+    return value
+
+
+def edge_strip(get, rows):
+    return jnp.where(lane_of(rows) == 0, 0.0, gap_strip(get, -1, 2, rows))
+
+
+def inner_strip(get, rows):
+    return jnp.where(lane_of(rows) % 2 == 0, gap_strip(get, -2, 1, rows), gap_strip(get, 1, 1, rows))
 
 
 def lane_take(value, index):
     return jnp.take_along_axis(value, index, axis=1, mode="promise_in_bounds")
-
-
-def lane_pick(pair, index):
-    return jnp.where(index < LANES, lane_take(pair[0], index % LANES), lane_take(pair[1], index % LANES))
 
 
 def tile_getter(ref, rows, count):
@@ -103,12 +110,6 @@
         return jnp.concatenate([ref[rows, tile * LANES : CELLS], rest], axis=1)
 
     return get
-
-
-def across_pair(get):
-    lane = lane_of(8)
-    groups = gap_groups(get, -2, 4, 8)
-    return lane_pick(groups, 4 * (lane // 2) + 1 + lane % 2), lane_pick(groups, 4 * (lane // 2) + 3 * (lane % 2))
 
 
 def joined(south, north, half, rows):
@@ -139,7 +140,7 @@
         rows = pl.ds(8 * pair, 8)
         x_copies[pair].wait()
         get_x = tile_getter(x_ref, rows, 8)
-        near, far = across_pair(get_x)
+        near, far = edge_strip(get_x, 8), inner_strip(get_x, 8)
         south = [window(get_x, 0, 8), window(get_x, IB, 8)]
         north = [window(get_x, CELLS - IB, 8), window(get_x, CELLS - 2 * IB, 8)]
         v_copies[pair].wait()
@@ -148,7 +149,7 @@
         strips = [joined(south[0], north[0], half, 8) for half in range(2)]
         strips += [joined(south[1], north[1], half, 8) for half in range(2)]
         strips += [joined(v_south, v_north, half, 8) for half in range(2)]
-        strips += [near, far, gap_groups(get_v, -1, 2, 8)[0]]
+        strips += [near, far, edge_strip(get_v, 8)]
         for index, strip in enumerate(strips):
             strip_ref[index, rows, :] = strip
 
@@ -159,7 +160,7 @@
     slot_lane = lane_of(count)
     get_d = tile_getter(d_ref, slice(None), count)
     d_south, d_north = window(get_d, 0, count), window(get_d, CELLS - IB, count)
-    d_gaps = gap_groups(get_d, -1, 2, count)[0]
+    d_gaps = edge_strip(get_d, count)
     spare = (slot_lane >= SPARE) & (slot_lane < SPARE + PIECE)
 
     def put(part, value):
@@ -319,16 +320,14 @@
         pltpu.make_async_copy(
             y_ref.at[rows].reshape(2, 4, CELLS), base_ref.at[pl.ds(slot, 2)], y_sems.at[pair]).start()
         get_w, get_z = [lambda tile, ref=ref: ref[:, tile * LANES : (tile + 1) * LANES] for ref in (w_ref, z_ref)]
-        groups = gap_groups(get_z, -2, 4, 8)
         east = lane % 2 == 0
-        near, far = across_pair(state)
-        normal = gap_groups(velocity, -1, 2, 8)[0]
+        near, far, normal = edge_strip(state, 8), inner_strip(state, 8), edge_strip(velocity, 8)
+        outer, inner = edge_strip(get_z, 8), inner_strip(get_z, 8)
         normal = jnp.where(x_row, normal, sublanes(normal, 2))
-        rim_speed = lane_pick(groups, 4 * (lane // 2) + 2 * (lane % 2))
+        rim_speed = jnp.where(east, inner, outer)
         rim_speed = jnp.where(x_row, rim_speed, sublanes(rim_speed, 2))
         sides = [(
-            near, far, jnp.where(east, -normal, normal), jnp.where(east, -rim_speed, rim_speed),
-            lane_pick(groups, 4 * (lane // 2) + 1 + lane % 2), lane_pick(groups, 4 * (lane // 2) + 3 * (lane % 2)),
+            near, far, jnp.where(east, -normal, normal), jnp.where(east, -rim_speed, rim_speed), outer, inner,
         )]
         for outer, inner, edge, sign in ((0, IB, 0, 1.0), (CELLS - IB, CELLS - 2 * IB, CELLS - 2 * IB, -1.0)):
             normal, rim_speed = window(velocity, outer, 8), window(get_w, edge, 8)

time: 35.3 us -> 34.8 us (0.986)
  Pallas kernels: 15.7 us -> 14.8 us
    pallas_call x1, Pallas kernels: 3.85 us -> 3.35 us  [per_device(): pl.pallas_call(pack_kernel, out_shape=jax.ShapeDtypeStruct((slot_total, L...]
  transfers between devices with their start and end apart: 2 -> 2, of which waited for: 2 -> 2; matrix products, arithmetic and copies ran while one was open for 3% -> 3% of each run, Pallas kernels for 22% -> 21%
where the time goes in v14:
time: 34.8 us; the launch traced here: 34.6 us
  Pallas kernels  14.8 us (43%)
  starting transfers between devices  9.89 us (28%)
  waiting for transfers between devices  8.73 us (25%)
  other arithmetic  0.79 us (2%)
    all_to_all x2, starting transfers between devices, exchanged(): lax.all_to_all(pieces, axes, 0, 0, tiled=True).reshape(slot_total, LANES)  9.89 us
    all_to_all x2, waiting for transfers between devices, exchanged(): lax.all_to_all(pieces, axes, 0, 0, tiled=True).reshape(slot_total, LANES)  8.73 us
    pallas_call x2, Pallas kernels, bulk(): pl.pallas_call(kernel, out_shape=[jax.ShapeDtypeStruct(tracers.shape, f32...  7.35 us
    pallas_call x1, Pallas kernels, per_device(): pl.pallas_call(pack_kernel, out_shape=jax.ShapeDtypeStruct((slot_total, L...  3.35 us
    pallas_call x1, Pallas kernels, per_device(): pl.pallas_call(finish_kernel, out_shape=jax.ShapeDtypeStruct(tracers.shap...  2.77 us
    pallas_call x1, Pallas kernels, per_device(): pl.pallas_call(route_kernel, grid=(device_count // PARTS,), out_shape=jax...  1.37 us
  transfers between devices with their start and end apart: 2, of which 2 were waited for; matrix products, arithmetic and copies ran while one was open for 3% of the time, Pallas kernels for 21%

profile of v14, /device:TPU:0, one launch (start us, length us, event | category | flops | bytes accessed | tf_op | source)
XLA Modules:
  0.0 34.6 jit_solution(1103669803234230236)
XLA Ops:
  0.0 0.0 copy-start.6
  0.0 0.0 copy-start.5
  0.0 0.0 copy-start.4
  0.0 0.0 copy-start
  0.0 0.0 copy-start.1
  0.0 3.3 %shard_map.73 = f32[320,128]{1,0:T(8,128)} custom-call(f32[10,4,5400]{2,1,0:T(4,128)} %refs_1_.1, f32[10,4,5400]{2,1,0:T(4,128)} %refs_2_.1, f32[10,5400]{1,0:T(8,128)} %refs_3_.1), custom_call_target="tpu_custom_call" | custom-call | flops 4000000 | bytes 2400000 | tf_op jit(solution)/shard_map/pallas_call | solution.py:482
  3.4 0.0 copy-start.2
  3.4 0.0 copy-start.3
  3.4 7.3 %all-to-all-start = ((f32[32,10,1,128]{3,2,1,0:T(1,128)}), f32[32,10,1,128]{3,2,1,0:T(1,128)S(1)}, u32[]{:S(2)}, u32[]{:S(2)}) async-start(f32[32,10,1,128]{3,2,1,0:T(1,128)} %bitcast.9), calls=%async_computation | async-start | bytes 327680 | tf_op jit(solution)/shard_map/all_to_all | solution.py:480
  10.7 0.0 copy-done.6
  10.7 0.0 copy-done.5
  10.8 0.0 copy-done.4
  10.8 0.4 %select_reduce_fusion.1 = s32[160,5]{0,1:T(8,128)S(1)} fusion(s32[160]{0:T(256)S(1)} %copy-done.4, s32[160,5]{0,1:T(8,128)S(1)} %pad_add_fusion), kind=kLoop, calls=%fused_computation.1 | loop fusion | flops 383200 | bytes 7040 | tf_op jit(solution)/shard_map/reduce_max | solution.py:454
  11.2 0.1 iota_compare_fusion.1
  11.3 0.3 select_reduce_fusion
  11.6 0.1 copy.19.code_ref.refs_5_
  11.7 0.0 copy-done
  11.7 0.0 copy-done.1
  11.7 0.0 copy-done.2
  11.8 0.0 copy-done.3
  11.8 3.1 %shard_map.74 = (f32[10,4,5400]{2,1,0:T(4,128)}, f32[25,16,128]{2,1,0:T(8,128)S(1)}) custom-call(s32[1]{0:T(128)} %bitcast.my_ref.part_ref.refs_0_, f32[10,4,5400]{2,1,0:T(4,128)S(1)} %copy-done, f32[10,4,5400]{2,1,0:T(4,128)S(1)} %copy-done.1, f32[10,5400]{1,0:T(8,128)S(1)} %copy-done.2, f32[10,5400]{1,0:T(8,128)S(1)} %copy-done.3, ...), custom_call_target="tpu_custom_call" | custom-call | flops 8000000 | bytes 1600000 | tf_op jit(solution)/shard_map/pallas_call | solution.py:506
  14.9 4.4 %all-to-all-done = f32[32,10,1,128]{3,2,1,0:T(1,128)S(1)} async-done(((f32[32,10,1,128]{3,2,1,0:T(1,128)}), f32[32,10,1,128]{3,2,1,0:T(1,128)S(1)}, u32[]{:S(2)}, u32[]{:S(2)}) %all-to-all-start) | async-done | bytes 163872 | tf_op jit(solution)/shard_map/all_to_all | solution.py:480
  19.3 1.4 %shard_map.75 = f32[320,128]{1,0:T(8,128)} custom-call(s32[1]{0:T(128)} %bitcast.my_ref.part_ref.refs_0_, s32[320,6]{1,0:T(8,128)S(1)} %copy.19.code_ref.refs_5_, f32[320,128]{1,0:T(8,128)S(1)} %bitcast.8), custom_call_target="tpu_custom_call" | custom-call | tf_op jit(solution)/shard_map/pallas_call | solution.py:538
  20.7 2.6 %all-to-all-start.1 = ((f32[32,10,1,128]{3,2,1,0:T(1,128)}), f32[32,10,1,128]{3,2,1,0:T(1,128)S(1)}, u32[]{:S(2)}, u32[]{:S(2)}) async-start(f32[32,10,1,128]{3,2,1,0:T(1,128)} %bitcast.5), calls=%async_computation.1 | async-start | bytes 327680 | tf_op jit(solution)/shard_map/all_to_all | solution.py:480
  23.2 4.2 %shard_map.76 = (f32[10,4,5400]{2,1,0:T(4,128)}, f32[25,24,128]{2,1,0:T(8,128)S(1)}) custom-call(s32[1]{0:T(128)} %bitcast.my_ref.part_ref.refs_0_, f32[10,4,5400]{2,1,0:T(4,128)S(1)} %copy-done, f32[10,4,5400]{2,1,0:T(4,128)S(1)} %copy-done.1, f32[10,5400]{1,0:T(8,128)S(1)} %copy-done.2, f32[10,5400]{1,0:T(8,128)S(1)} %copy-done.3, ...), custom_call_target="tpu_custom_call", output_to_operand_aliasing={{0}: (6, {})} | custom-call | flops 12000000 | bytes 2400000 | tf_op jit(solution)/shard_map/pallas_call | solution.py:506
  27.5 4.3 %all-to-all-done.1 = f32[32,10,1,128]{3,2,1,0:T(1,128)S(1)} async-done(((f32[32,10,1,128]{3,2,1,0:T(1,128)}), f32[32,10,1,128]{3,2,1,0:T(1,128)S(1)}, u32[]{:S(2)}, u32[]{:S(2)}) %all-to-all-start.1) | async-done | bytes 163872 | tf_op jit(solution)/shard_map/all_to_all | solution.py:480
  31.8 2.8 %shard_map.77 = f32[10,4,5400]{2,1,0:T(4,128)} custom-call(f32[320,128]{1,0:T(8,128)S(1)} %bitcast.7, f32[25,16,128]{2,1,0:T(8,128)S(1)} %get-tuple-element.17.edge_a_ref, f32[25,24,128]{2,1,0:T(8,128)S(1)} %get-tuple-element.19.edge_b_ref, f32[10,4,5400]{2,1,0:T(4,128)} %get-tuple-element.20.base_ref), custom_call_target="tpu_custom_call", output_to_operand_aliasing={{}: (3, {})} | custom-call | tf_op jit(solution)/shard_map/pallas_call | solution.py:555
  (2 shorter events, 0.0 us)
Async XLA Ops:
  0.0 10.7 %copy-start.6 = (s32[160]{0:T(256)S(1)}, s32[160]{0:T(256)}, u32[]{:S(2)}) copy-start(s32[160]{0:T(256)} %param.13) | copy-start | bytes 1924
  0.0 10.7 %copy-start.5 = (s32[160,4]{0,1:T(4,128)S(1)}, s32[160,4]{0,1:T(4,128)}, u32[]{:S(2)}) copy-start(s32[160,4]{0,1:T(4,128)} %param.12) | copy-start | bytes 7684
  0.0 10.8 %copy-start.4 = (s32[160]{0:T(256)S(1)}, s32[160]{0:T(256)}, u32[]{:S(2)}) copy-start(s32[160]{0:T(256)} %param.11) | copy-start | bytes 1924
  0.0 11.7 %copy-start = (f32[10,4,5400]{2,1,0:T(4,128)S(1)}, f32[10,4,5400]{2,1,0:T(4,128)}, u32[]{:S(2)}) copy-start(f32[10,4,5400]{2,1,0:T(4,128)} %refs_1_.1) | copy-start | bytes 2592004
  0.0 11.7 %copy-start.1 = (f32[10,4,5400]{2,1,0:T(4,128)S(1)}, f32[10,4,5400]{2,1,0:T(4,128)}, u32[]{:S(2)}) copy-start(f32[10,4,5400]{2,1,0:T(4,128)} %refs_2_.1) | copy-start | bytes 2592004
  3.4 8.4 %copy-start.2 = (f32[10,5400]{1,0:T(8,128)S(1)}, f32[10,5400]{1,0:T(8,128)}, u32[]{:S(2)}) copy-start(f32[10,5400]{1,0:T(8,128)} %refs_3_.1) | copy-start | bytes 648004
  3.4 8.4 %copy-start.3 = (f32[10,5400]{1,0:T(8,128)S(1)}, f32[10,5400]{1,0:T(8,128)}, u32[]{:S(2)}) copy-start(f32[10,5400]{1,0:T(8,128)} %refs_4_.1) | copy-start | bytes 648004
  3.4 15.9 %all-to-all-start = ((f32[32,10,1,128]{3,2,1,0:T(1,128)}), f32[32,10,1,128]{3,2,1,0:T(1,128)S(1)}, u32[]{:S(2)}, u32[]{:S(2)}) async-start(f32[32,10,1,128]{3,2,1,0:T(1,128)} %bitcast.9), calls=%async_computation | async-start | bytes 327680 | tf_op jit(solution)/shard_map/all_to_all | solution.py:480
  20.7 11.2 %all-to-all-start.1 = ((f32[32,10,1,128]{3,2,1,0:T(1,128)}), f32[32,10,1,128]{3,2,1,0:T(1,128)S(1)}, u32[]{:S(2)}, u32[]{:S(2)}) async-start(f32[32,10,1,128]{3,2,1,0:T(1,128)} %bitcast.5), calls=%async_computation.1 | async-start | bytes 327680 | tf_op jit(solution)/shard_map/all_to_all | solution.py:480

commit v15 on v14

--- a/solution.py
+++ b/solution.py
@@ -65,10 +65,10 @@
 
 def window(get, start, rows):
     tile, offset = start // LANES, start % LANES
-    head = rot(get(tile), -offset)
-    if offset == 0 or tile + 1 >= TILES:
-        return head
-    return jnp.where(lane_of(rows) < LANES - offset, head, rot(get(tile + 1), -offset))
+    value = get(tile)
+    if offset > 0 and tile + 1 < TILES:
+        value = jnp.where(lane_of(rows) < offset, get(tile + 1), value)
+    return rot(value, -offset)
 
 
 def gap_strip(get, offset, wide, rows):
@@ -189,21 +189,23 @@
     total = held_ref.shape[0]
     rows = out_ref.shape[0]
     part = part_ref[0]
-    picked = [jnp.zeros((rows, 2 * LANES), jnp.float32) for _ in range(5)]
+    fold = code_ref[:, 4:5]
+    wanted = [code_ref[:, side : side + 1] for side in range(3)] + [jnp.maximum(code_ref[:, 3:4], fold)]
+    picked = [jnp.zeros((rows, 2 * LANES), jnp.float32) for _ in wanted]
     for start in range(0, total, rows):
         held = held_ref[start : start + rows, :]
         high = held.astype(jnp.bfloat16)
         low = (held - high.astype(jnp.float32)).astype(jnp.bfloat16)
         halves = jnp.concatenate([high, low], axis=1)
         source = lax.broadcasted_iota(jnp.int32, (rows, rows), 1) + start
-        for side in range(5):
-            one_hot = jnp.where(code_ref[:, side : side + 1] == source, 1.0, 0.0).astype(jnp.bfloat16)
+        for side, code in enumerate(wanted):
+            one_hot = jnp.where(code == source, 1.0, 0.0).astype(jnp.bfloat16)
             picked[side] += jnp.dot(one_hot, halves, preferred_element_type=jnp.float32)
-    west, east, south, north, fold = [value[:, :LANES] + value[:, LANES:] for value in picked]
+    west, east, south, north = [value[:, :LANES] + value[:, LANES:] for value in picked]
     lane = lane_of(rows)
     along_x = (part >= X_PART) | ((part < 8) & (lane >= SPARE) & (lane < SPARE + PIECE))
     x_side = jnp.where(lane % 2 == 0, west, east)
-    y_side = jnp.where(lane < 64, north + rot(fold, 64), south)
+    y_side = jnp.where(lane < 64, jnp.where(fold >= 0, rot(north, 64), north), south)
     out_ref[...] = jnp.where(along_x, x_side, y_side)
 
 
@@ -349,18 +351,19 @@
         pltpu.make_async_copy(rows, base_ref.at[slots], y_sems.at[pair]).wait()
 
 
-def finish_kernel(halo_ref, edge_a_ref, edge_b_ref, base_ref, out_ref,
-                  y_ref, own_ref, raw_ref, delta_ref, own_sems, in_sems, out_sems):
+def finish_kernel(arrived_ref, edge_a_ref, edge_b_ref, base_ref, out_ref,
+                  halo_ref, y_ref, own_ref, raw_ref, delta_ref, own_sems, in_sems, out_sems):
     count = out_ref.shape[0]
     pairs = count // 2
     rows = 4 * count
     split = edge_a_ref.shape[1]
+    halo_copy = pltpu.make_async_copy(arrived_ref, halo_ref, own_sems.at[2])
     own_copies = [
         pltpu.make_async_copy(edge_a_ref, own_ref.at[:, pl.ds(0, split)], own_sems.at[0]),
         pltpu.make_async_copy(edge_b_ref, own_ref.at[:, pl.ds(split, rows - split)], own_sems.at[1]),
     ]
     in_copies = pair_copies(base_ref, y_ref, in_sems, 0, pairs)
-    for copy in own_copies + in_copies:
+    for copy in [halo_copy] + own_copies + in_copies:
         copy.start()
     lane = lane_of(rows)
     level = (lax.broadcasted_iota(jnp.int32, (rows, LANES), 0) % 2).astype(jnp.float32)
@@ -375,6 +378,7 @@
 
     mirror = jnp.where(lane < IB, IB - 1 - lane, lane)
     slot_lane = lane_of(count)
+    halo_copy.wait()
     depth_x = rot(part(0), -SPARE)
     for index in range(1, 8):
         depth_x = jnp.where(slot_lane >= PIECE * index, rot(part(index), PIECE * index - SPARE), depth_x)
@@ -555,14 +559,15 @@
     return pl.pallas_call(
         finish_kernel,
         out_shape=jax.ShapeDtypeStruct(tracers.shape, f32),
-        in_specs=[in_vmem, anywhere, anywhere, in_hbm],
+        in_specs=[anywhere, anywhere, anywhere, in_hbm],
         out_specs=in_hbm,
         scratch_shapes=[
+            pltpu.VMEM((PARTS * slot_count, LANES), f32),
             pltpu.VMEM((state_rows, CELLS), f32),
             pltpu.VMEM((OWN * SIDES + 1, state_rows, LANES), f32),
             pltpu.VMEM((12, state_rows, LANES), f32),
             pltpu.VMEM((2 * SIDES, state_rows, LANES), f32),
-            dma((2,)),
+            dma((3,)),
             dma((pairs,)),
             dma((pairs,)),
         ],

time: 34.8 us -> 35 us (level)
  no operation moved by 1% of the time
where the time goes in v15:
time: 35 us; the launch traced here: 34.8 us
  Pallas kernels  15 us (43%)
  starting transfers between devices  9.89 us (28%)
  waiting for transfers between devices  8.73 us (25%)
  other arithmetic  0.79 us (2%)
    all_to_all x2, starting transfers between devices, exchanged(): lax.all_to_all(pieces, axes, 0, 0, tiled=True).reshape(slot_total, LANES)  9.89 us
    all_to_all x2, waiting for transfers between devices, exchanged(): lax.all_to_all(pieces, axes, 0, 0, tiled=True).reshape(slot_total, LANES)  8.73 us
    pallas_call x2, Pallas kernels, bulk(): pl.pallas_call(kernel, out_shape=[jax.ShapeDtypeStruct(tracers.shape, f32...  7.35 us
    pallas_call x1, Pallas kernels, per_device(): pl.pallas_call(pack_kernel, out_shape=jax.ShapeDtypeStruct((slot_total, L...  3.31 us
    pallas_call x1, Pallas kernels, per_device(): pl.pallas_call(finish_kernel, out_shape=jax.ShapeDtypeStruct(tracers.shap...  2.96 us
    pallas_call x1, Pallas kernels, per_device(): pl.pallas_call(route_kernel, grid=(device_count // PARTS,), out_shape=jax...  1.37 us
  transfers between devices with their start and end apart: 2, of which 2 were waited for; matrix products, arithmetic and copies ran while one was open for 3% of the time, Pallas kernels for 21%

profile of v15, /device:TPU:0, one launch (start us, length us, event | category | flops | bytes accessed | tf_op | source)
XLA Modules:
  0.0 34.8 jit_solution(8579578806795944002)
XLA Ops:
  0.0 0.0 copy-start.6
  0.0 0.0 copy-start.5
  0.0 0.0 copy-start.4
  0.0 0.0 copy-start
  0.0 0.0 copy-start.1
  0.0 3.3 %shard_map.73 = f32[320,128]{1,0:T(8,128)} custom-call(f32[10,4,5400]{2,1,0:T(4,128)} %refs_1_.1, f32[10,4,5400]{2,1,0:T(4,128)} %refs_2_.1, f32[10,5400]{1,0:T(8,128)} %refs_3_.1), custom_call_target="tpu_custom_call" | custom-call | flops 4000000 | bytes 2400000 | tf_op jit(solution)/shard_map/pallas_call | solution.py:486
  3.3 0.0 copy-start.2
  3.3 0.0 copy-start.3
  3.4 7.3 %all-to-all-start = ((f32[32,10,1,128]{3,2,1,0:T(1,128)}), f32[32,10,1,128]{3,2,1,0:T(1,128)S(1)}, u32[]{:S(2)}, u32[]{:S(2)}) async-start(f32[32,10,1,128]{3,2,1,0:T(1,128)} %bitcast.9), calls=%async_computation | async-start | bytes 327680 | tf_op jit(solution)/shard_map/all_to_all | solution.py:484
  10.7 0.0 copy-done.6
  10.7 0.0 copy-done.5
  10.7 0.0 copy-done.4
  10.7 0.4 %select_reduce_fusion.1 = s32[160,5]{0,1:T(8,128)S(1)} fusion(s32[160]{0:T(256)S(1)} %copy-done.4, s32[160,5]{0,1:T(8,128)S(1)} %pad_add_fusion), kind=kLoop, calls=%fused_computation.1 | loop fusion | flops 383200 | bytes 7040 | tf_op jit(solution)/shard_map/reduce_max | solution.py:458
  11.2 0.1 iota_compare_fusion.1
  11.3 0.3 select_reduce_fusion
  11.5 0.1 copy.19.code_ref.refs_5_
  11.7 0.0 copy-done
  11.7 0.0 copy-done.1
  11.7 0.0 copy-done.2
  11.7 0.0 copy-done.3
  11.7 3.1 %shard_map.74 = (f32[10,4,5400]{2,1,0:T(4,128)}, f32[25,16,128]{2,1,0:T(8,128)S(1)}) custom-call(s32[1]{0:T(128)} %bitcast.my_ref.part_ref.refs_0_, f32[10,4,5400]{2,1,0:T(4,128)S(1)} %copy-done, f32[10,4,5400]{2,1,0:T(4,128)S(1)} %copy-done.1, f32[10,5400]{1,0:T(8,128)S(1)} %copy-done.2, f32[10,5400]{1,0:T(8,128)S(1)} %copy-done.3, ...), custom_call_target="tpu_custom_call" | custom-call | flops 8000000 | bytes 1600000 | tf_op jit(solution)/shard_map/pallas_call | solution.py:510
  14.8 4.4 %all-to-all-done = f32[32,10,1,128]{3,2,1,0:T(1,128)S(1)} async-done(((f32[32,10,1,128]{3,2,1,0:T(1,128)}), f32[32,10,1,128]{3,2,1,0:T(1,128)S(1)}, u32[]{:S(2)}, u32[]{:S(2)}) %all-to-all-start) | async-done | bytes 163872 | tf_op jit(solution)/shard_map/all_to_all | solution.py:484
  19.3 1.4 %shard_map.75 = f32[320,128]{1,0:T(8,128)} custom-call(s32[1]{0:T(128)} %bitcast.my_ref.part_ref.refs_0_, s32[320,6]{1,0:T(8,128)S(1)} %copy.19.code_ref.refs_5_, f32[320,128]{1,0:T(8,128)S(1)} %bitcast.8), custom_call_target="tpu_custom_call" | custom-call | tf_op jit(solution)/shard_map/pallas_call | solution.py:542
  20.6 2.6 %all-to-all-start.1 = ((f32[32,10,1,128]{3,2,1,0:T(1,128)}), f32[32,10,1,128]{3,2,1,0:T(1,128)S(1)}, u32[]{:S(2)}, u32[]{:S(2)}) async-start(f32[32,10,1,128]{3,2,1,0:T(1,128)} %bitcast.5), calls=%async_computation.1 | async-start | bytes 327680 | tf_op jit(solution)/shard_map/all_to_all | solution.py:484
  23.2 4.2 %shard_map.76 = (f32[10,4,5400]{2,1,0:T(4,128)}, f32[25,24,128]{2,1,0:T(8,128)S(1)}) custom-call(s32[1]{0:T(128)} %bitcast.my_ref.part_ref.refs_0_, f32[10,4,5400]{2,1,0:T(4,128)S(1)} %copy-done, f32[10,4,5400]{2,1,0:T(4,128)S(1)} %copy-done.1, f32[10,5400]{1,0:T(8,128)S(1)} %copy-done.2, f32[10,5400]{1,0:T(8,128)S(1)} %copy-done.3, ...), custom_call_target="tpu_custom_call", output_to_operand_aliasing={{0}: (6, {})} | custom-call | flops 12000000 | bytes 2400000 | tf_op jit(solution)/shard_map/pallas_call | solution.py:510
  27.5 4.3 %all-to-all-done.1 = f32[32,10,1,128]{3,2,1,0:T(1,128)S(1)} async-done(((f32[32,10,1,128]{3,2,1,0:T(1,128)}), f32[32,10,1,128]{3,2,1,0:T(1,128)S(1)}, u32[]{:S(2)}, u32[]{:S(2)}) %all-to-all-start.1) | async-done | bytes 163872 | tf_op jit(solution)/shard_map/all_to_all | solution.py:484
  31.8 3.0 %shard_map.77 = f32[10,4,5400]{2,1,0:T(4,128)} custom-call(f32[320,128]{1,0:T(8,128)S(1)} %bitcast.7, f32[25,16,128]{2,1,0:T(8,128)S(1)} %get-tuple-element.17.edge_a_ref, f32[25,24,128]{2,1,0:T(8,128)S(1)} %get-tuple-element.19.edge_b_ref, f32[10,4,5400]{2,1,0:T(4,128)} %get-tuple-element.20.base_ref), custom_call_target="tpu_custom_call", output_to_operand_aliasing={{}: (3, {})} | custom-call | tf_op jit(solution)/shard_map/pallas_call | solution.py:559
  (2 shorter events, 0.0 us)
Async XLA Ops:
  0.0 10.7 %copy-start.6 = (s32[160]{0:T(256)S(1)}, s32[160]{0:T(256)}, u32[]{:S(2)}) copy-start(s32[160]{0:T(256)} %param.13) | copy-start | bytes 1924
  0.0 10.7 %copy-start.5 = (s32[160,4]{0,1:T(4,128)S(1)}, s32[160,4]{0,1:T(4,128)}, u32[]{:S(2)}) copy-start(s32[160,4]{0,1:T(4,128)} %param.12) | copy-start | bytes 7684
  0.0 10.7 %copy-start.4 = (s32[160]{0:T(256)S(1)}, s32[160]{0:T(256)}, u32[]{:S(2)}) copy-start(s32[160]{0:T(256)} %param.11) | copy-start | bytes 1924
  0.0 11.7 %copy-start = (f32[10,4,5400]{2,1,0:T(4,128)S(1)}, f32[10,4,5400]{2,1,0:T(4,128)}, u32[]{:S(2)}) copy-start(f32[10,4,5400]{2,1,0:T(4,128)} %refs_1_.1) | copy-start | bytes 2592004
  0.0 11.7 %copy-start.1 = (f32[10,4,5400]{2,1,0:T(4,128)S(1)}, f32[10,4,5400]{2,1,0:T(4,128)}, u32[]{:S(2)}) copy-start(f32[10,4,5400]{2,1,0:T(4,128)} %refs_2_.1) | copy-start | bytes 2592004
  3.3 8.4 %copy-start.2 = (f32[10,5400]{1,0:T(8,128)S(1)}, f32[10,5400]{1,0:T(8,128)}, u32[]{:S(2)}) copy-start(f32[10,5400]{1,0:T(8,128)} %refs_3_.1) | copy-start | bytes 648004
  3.3 8.4 %copy-start.3 = (f32[10,5400]{1,0:T(8,128)S(1)}, f32[10,5400]{1,0:T(8,128)}, u32[]{:S(2)}) copy-start(f32[10,5400]{1,0:T(8,128)} %refs_4_.1) | copy-start | bytes 648004
  3.4 15.9 %all-to-all-start = ((f32[32,10,1,128]{3,2,1,0:T(1,128)}), f32[32,10,1,128]{3,2,1,0:T(1,128)S(1)}, u32[]{:S(2)}, u32[]{:S(2)}) async-start(f32[32,10,1,128]{3,2,1,0:T(1,128)} %bitcast.9), calls=%async_computation | async-start | bytes 327680 | tf_op jit(solution)/shard_map/all_to_all | solution.py:484
  20.6 11.2 %all-to-all-start.1 = ((f32[32,10,1,128]{3,2,1,0:T(1,128)}), f32[32,10,1,128]{3,2,1,0:T(1,128)S(1)}, u32[]{:S(2)}, u32[]{:S(2)}) async-start(f32[32,10,1,128]{3,2,1,0:T(1,128)} %bitcast.5), calls=%async_computation.1 | async-start | bytes 327680 | tf_op jit(solution)/shard_map/all_to_all | solution.py:484

commit v16 on v15

--- a/solution.py
+++ b/solution.py
@@ -351,20 +351,18 @@
         pltpu.make_async_copy(rows, base_ref.at[slots], y_sems.at[pair]).wait()
 
 
-def finish_kernel(arrived_ref, edge_a_ref, edge_b_ref, base_ref, out_ref,
-                  halo_ref, y_ref, own_ref, raw_ref, delta_ref, own_sems, in_sems, out_sems):
+def finish_kernel(halo_ref, edge_a_ref, edge_b_ref, base_ref, out_ref,
+                  y_ref, raw_ref, delta_ref, in_sems, out_sems):
     count = out_ref.shape[0]
     pairs = count // 2
     rows = 4 * count
-    split = edge_a_ref.shape[1]
-    halo_copy = pltpu.make_async_copy(arrived_ref, halo_ref, own_sems.at[2])
-    own_copies = [
-        pltpu.make_async_copy(edge_a_ref, own_ref.at[:, pl.ds(0, split)], own_sems.at[0]),
-        pltpu.make_async_copy(edge_b_ref, own_ref.at[:, pl.ds(split, rows - split)], own_sems.at[1]),
-    ]
     in_copies = pair_copies(base_ref, y_ref, in_sems, 0, pairs)
-    for copy in [halo_copy] + own_copies + in_copies:
+    for copy in in_copies:
         copy.start()
+
+    def own(index):
+        return jnp.concatenate([edge_a_ref[index], edge_b_ref[index]], axis=0)
+
     lane = lane_of(rows)
     level = (lax.broadcasted_iota(jnp.int32, (rows, LANES), 0) % 2).astype(jnp.float32)
 
@@ -378,7 +376,6 @@
 
     mirror = jnp.where(lane < IB, IB - 1 - lane, lane)
     slot_lane = lane_of(count)
-    halo_copy.wait()
     depth_x = rot(part(0), -SPARE)
     for index in range(1, 8):
         depth_x = jnp.where(slot_lane >= PIECE * index, rot(part(index), PIECE * index - SPARE), depth_x)
@@ -393,9 +390,7 @@
                          for half in range(2)]
         south_halo.append(jnp.where(lane < HALF, rot(first, 64), rot(second, 64 + HALF)))
         north_raw.append(jnp.where(lane < HALF, first, rot(second, HALF)))
-    for copy in own_copies:
-        copy.wait()
-    folded = own_ref[OWN * SIDES] > 0.0
+    folded = own(OWN * SIDES) > 0.0
     north_halo = []
     for kind, raw in enumerate(north_raw):
         turned = lane_take(raw, mirror)
@@ -403,7 +398,7 @@
 
     for side, (out_near, out_far, out_normal, out_depth) in enumerate((x_halo, south_halo, north_halo)):
         near, far, normal, rim_speed, wet, inner_wet, ratio, inner_ratio = [
-            own_ref[OWN * side + index] for index in range(OWN)]
+            own(OWN * side + index) for index in range(OWN)]
         if side == 0:
             out_normal = jnp.where(lane % 2 == 0, -out_normal, out_normal)
             beyond = out_near - jnp.where(lane % 2 == 0, rot(near, -1), rot(near, 1))
@@ -473,7 +468,6 @@
     state_rows = 4 * slot_count
     f32 = jnp.float32
     in_hbm = pl.BlockSpec(memory_space=pltpu.HBM)
-    anywhere = pl.BlockSpec(memory_space=pl.ANY)
     in_vmem = pl.BlockSpec(memory_space=pltpu.VMEM)
     in_smem = pl.BlockSpec(memory_space=pltpu.SMEM)
     dma = pltpu.SemaphoreType.DMA
@@ -539,19 +533,23 @@
     held, edge_a = lax.optimization_barrier((held, edge_a))
 
     routed_rows = PARTS * slot_count
+    blocks = dict(in_specs=[in_smem, in_vmem, in_vmem], out_specs=in_vmem)
+    if device_count > PARTS:
+        blocks = dict(
+            grid=(device_count // PARTS,),
+            in_specs=[
+                in_smem,
+                pl.BlockSpec((routed_rows, 6), lambda step: (step, 0)),
+                pl.BlockSpec((slot_total, LANES), lambda step: (0, 0)),
+            ],
+            out_specs=pl.BlockSpec((routed_rows, LANES), lambda step: (step, 0)),
+        )
     routed = pl.pallas_call(
         route_kernel,
-        grid=(device_count // PARTS,),
         out_shape=jax.ShapeDtypeStruct((slot_total, LANES), f32),
-        in_specs=[
-            in_smem,
-            pl.BlockSpec((routed_rows, 6), lambda step: (step, 0)),
-            pl.BlockSpec((slot_total, LANES), lambda step: (0, 0)),
-        ],
-        out_specs=pl.BlockSpec((routed_rows, LANES), lambda step: (step, 0)),
         compiler_params=limit,
+        **blocks,
     )(my_index, codes, held)
-
     routed, base = lax.optimization_barrier((routed, base))
     base, edge_b = bulk(FIRST_PAIRS, pairs - FIRST_PAIRS, codes, base)
     halo = exchanged(routed)[: PARTS * slot_count]
@@ -559,15 +557,12 @@
     return pl.pallas_call(
         finish_kernel,
         out_shape=jax.ShapeDtypeStruct(tracers.shape, f32),
-        in_specs=[anywhere, anywhere, anywhere, in_hbm],
+        in_specs=[in_vmem, in_vmem, in_vmem, in_hbm],
         out_specs=in_hbm,
         scratch_shapes=[
-            pltpu.VMEM((PARTS * slot_count, LANES), f32),
             pltpu.VMEM((state_rows, CELLS), f32),
-            pltpu.VMEM((OWN * SIDES + 1, state_rows, LANES), f32),
             pltpu.VMEM((12, state_rows, LANES), f32),
             pltpu.VMEM((2 * SIDES, state_rows, LANES), f32),
-            dma((3,)),
             dma((pairs,)),
             dma((pairs,)),
         ],

time: 35 us -> 34.8 us (level)
  no operation moved by 1% of the time
where the time goes in v16:
time: 34.8 us; the launch traced here: 34.5 us
  Pallas kernels  14.8 us (43%)
  starting transfers between devices  9.89 us (28%)
  waiting for transfers between devices  8.73 us (25%)
  other arithmetic  0.79 us (2%)
    all_to_all x2, starting transfers between devices, exchanged(): lax.all_to_all(pieces, axes, 0, 0, tiled=True).reshape(slot_total, LANES)  9.89 us
    all_to_all x2, waiting for transfers between devices, exchanged(): lax.all_to_all(pieces, axes, 0, 0, tiled=True).reshape(slot_total, LANES)  8.73 us
    pallas_call x2, Pallas kernels, bulk(): pl.pallas_call(kernel, out_shape=[jax.ShapeDtypeStruct(tracers.shape, f32...  7.35 us
    pallas_call x1, Pallas kernels, per_device(): pl.pallas_call(pack_kernel, out_shape=jax.ShapeDtypeStruct((slot_total, L...  3.31 us
    pallas_call x1, Pallas kernels, per_device(): pl.pallas_call(finish_kernel, out_shape=jax.ShapeDtypeStruct(tracers.shap...  2.72 us
    pallas_call x1, Pallas kernels, per_device(): pl.pallas_call(route_kernel, out_shape=jax.ShapeDtypeStruct((slot_total,...  1.37 us
  transfers between devices with their start and end apart: 2, of which 2 were waited for; matrix products, arithmetic and copies ran while one was open for 3% of the time, Pallas kernels for 21%

profile of v16, /device:TPU:0, one launch (start us, length us, event | category | flops | bytes accessed | tf_op | source)
XLA Modules:
  0.0 34.5 jit_solution(18061176099076819892)
XLA Ops:
  0.0 0.0 copy-start.6
  0.0 0.0 copy-start.5
  0.0 0.0 copy-start.4
  0.0 0.0 copy-start
  0.0 0.0 copy-start.1
  0.0 3.3 %shard_map.73 = f32[320,128]{1,0:T(8,128)} custom-call(f32[10,4,5400]{2,1,0:T(4,128)} %refs_1_.1, f32[10,4,5400]{2,1,0:T(4,128)} %refs_2_.1, f32[10,5400]{1,0:T(8,128)} %refs_3_.1), custom_call_target="tpu_custom_call" | custom-call | flops 4000000 | bytes 2400000 | tf_op jit(solution)/shard_map/pallas_call | solution.py:480
  3.3 0.0 copy-start.2
  3.3 0.0 copy-start.3
  3.4 7.3 %all-to-all-start = ((f32[32,10,1,128]{3,2,1,0:T(1,128)}), f32[32,10,1,128]{3,2,1,0:T(1,128)S(1)}, u32[]{:S(2)}, u32[]{:S(2)}) async-start(f32[32,10,1,128]{3,2,1,0:T(1,128)} %bitcast.9), calls=%async_computation | async-start | bytes 327680 | tf_op jit(solution)/shard_map/all_to_all | solution.py:478
  10.7 0.0 copy-done.6
  10.7 0.0 copy-done.5
  10.7 0.0 copy-done.4
  10.7 0.4 %select_reduce_fusion.1 = s32[160,5]{0,1:T(8,128)S(1)} fusion(s32[160]{0:T(256)S(1)} %copy-done.4, s32[160,5]{0,1:T(8,128)S(1)} %pad_add_fusion), kind=kLoop, calls=%fused_computation.1 | loop fusion | flops 383200 | bytes 7040 | tf_op jit(solution)/shard_map/reduce_max | solution.py:453
  11.2 0.1 iota_compare_fusion.1
  11.3 0.3 select_reduce_fusion
  11.5 0.1 copy.19.code_ref.refs_5_
  11.7 0.0 copy-done
  11.7 0.0 copy-done.1
  11.7 0.0 copy-done.2
  11.7 0.0 copy-done.3
  11.7 3.1 %shard_map.74 = (f32[10,4,5400]{2,1,0:T(4,128)}, f32[25,16,128]{2,1,0:T(8,128)S(1)}) custom-call(s32[1]{0:T(128)} %bitcast.my_ref.part_ref.refs_0_, f32[10,4,5400]{2,1,0:T(4,128)S(1)} %copy-done, f32[10,4,5400]{2,1,0:T(4,128)S(1)} %copy-done.1, f32[10,5400]{1,0:T(8,128)S(1)} %copy-done.2, f32[10,5400]{1,0:T(8,128)S(1)} %copy-done.3, ...), custom_call_target="tpu_custom_call" | custom-call | flops 8000000 | bytes 1600000 | tf_op jit(solution)/shard_map/pallas_call | solution.py:504
  14.8 4.4 %all-to-all-done = f32[32,10,1,128]{3,2,1,0:T(1,128)S(1)} async-done(((f32[32,10,1,128]{3,2,1,0:T(1,128)}), f32[32,10,1,128]{3,2,1,0:T(1,128)S(1)}, u32[]{:S(2)}, u32[]{:S(2)}) %all-to-all-start) | async-done | bytes 163872 | tf_op jit(solution)/shard_map/all_to_all | solution.py:478
  19.3 1.4 %shard_map.75 = f32[320,128]{1,0:T(8,128)} custom-call(s32[1]{0:T(128)} %bitcast.my_ref.part_ref.refs_0_, s32[320,6]{1,0:T(8,128)S(1)} %copy.19.code_ref.refs_5_, f32[320,128]{1,0:T(8,128)S(1)} %bitcast.8), custom_call_target="tpu_custom_call" | custom-call | tf_op jit(solution)/shard_map/pallas_call | solution.py:547
  20.6 2.6 %all-to-all-start.1 = ((f32[32,10,1,128]{3,2,1,0:T(1,128)}), f32[32,10,1,128]{3,2,1,0:T(1,128)S(1)}, u32[]{:S(2)}, u32[]{:S(2)}) async-start(f32[32,10,1,128]{3,2,1,0:T(1,128)} %bitcast.5), calls=%async_computation.1 | async-start | bytes 327680 | tf_op jit(solution)/shard_map/all_to_all | solution.py:478
  23.2 4.2 %shard_map.76 = (f32[10,4,5400]{2,1,0:T(4,128)}, f32[25,24,128]{2,1,0:T(8,128)S(1)}) custom-call(s32[1]{0:T(128)} %bitcast.my_ref.part_ref.refs_0_, f32[10,4,5400]{2,1,0:T(4,128)S(1)} %copy-done, f32[10,4,5400]{2,1,0:T(4,128)S(1)} %copy-done.1, f32[10,5400]{1,0:T(8,128)S(1)} %copy-done.2, f32[10,5400]{1,0:T(8,128)S(1)} %copy-done.3, ...), custom_call_target="tpu_custom_call", output_to_operand_aliasing={{0}: (6, {})} | custom-call | flops 12000000 | bytes 2400000 | tf_op jit(solution)/shard_map/pallas_call | solution.py:504
  27.5 4.3 %all-to-all-done.1 = f32[32,10,1,128]{3,2,1,0:T(1,128)S(1)} async-done(((f32[32,10,1,128]{3,2,1,0:T(1,128)}), f32[32,10,1,128]{3,2,1,0:T(1,128)S(1)}, u32[]{:S(2)}, u32[]{:S(2)}) %all-to-all-start.1) | async-done | bytes 163872 | tf_op jit(solution)/shard_map/all_to_all | solution.py:478
  31.8 2.7 %shard_map.77 = f32[10,4,5400]{2,1,0:T(4,128)} custom-call(f32[320,128]{1,0:T(8,128)S(1)} %bitcast.7, f32[25,16,128]{2,1,0:T(8,128)S(1)} %get-tuple-element.17.edge_a_ref, f32[25,24,128]{2,1,0:T(8,128)S(1)} %get-tuple-element.19.edge_b_ref, f32[10,4,5400]{2,1,0:T(4,128)} %get-tuple-element.20.base_ref), custom_call_target="tpu_custom_call", output_to_operand_aliasing={{}: (3, {})} | custom-call | tf_op jit(solution)/shard_map/pallas_call | solution.py:557
  (2 shorter events, 0.0 us)
Async XLA Ops:
  0.0 10.7 %copy-start.6 = (s32[160]{0:T(256)S(1)}, s32[160]{0:T(256)}, u32[]{:S(2)}) copy-start(s32[160]{0:T(256)} %param.13) | copy-start | bytes 1924
  0.0 10.7 %copy-start.5 = (s32[160,4]{0,1:T(4,128)S(1)}, s32[160,4]{0,1:T(4,128)}, u32[]{:S(2)}) copy-start(s32[160,4]{0,1:T(4,128)} %param.12) | copy-start | bytes 7684
  0.0 10.7 %copy-start.4 = (s32[160]{0:T(256)S(1)}, s32[160]{0:T(256)}, u32[]{:S(2)}) copy-start(s32[160]{0:T(256)} %param.11) | copy-start | bytes 1924
  0.0 11.7 %copy-start = (f32[10,4,5400]{2,1,0:T(4,128)S(1)}, f32[10,4,5400]{2,1,0:T(4,128)}, u32[]{:S(2)}) copy-start(f32[10,4,5400]{2,1,0:T(4,128)} %refs_1_.1) | copy-start | bytes 2592004
  0.0 11.7 %copy-start.1 = (f32[10,4,5400]{2,1,0:T(4,128)S(1)}, f32[10,4,5400]{2,1,0:T(4,128)}, u32[]{:S(2)}) copy-start(f32[10,4,5400]{2,1,0:T(4,128)} %refs_2_.1) | copy-start | bytes 2592004
  3.3 8.4 %copy-start.2 = (f32[10,5400]{1,0:T(8,128)S(1)}, f32[10,5400]{1,0:T(8,128)}, u32[]{:S(2)}) copy-start(f32[10,5400]{1,0:T(8,128)} %refs_3_.1) | copy-start | bytes 648004
  3.3 8.4 %copy-start.3 = (f32[10,5400]{1,0:T(8,128)S(1)}, f32[10,5400]{1,0:T(8,128)}, u32[]{:S(2)}) copy-start(f32[10,5400]{1,0:T(8,128)} %refs_4_.1) | copy-start | bytes 648004
  3.4 15.9 %all-to-all-start = ((f32[32,10,1,128]{3,2,1,0:T(1,128)}), f32[32,10,1,128]{3,2,1,0:T(1,128)S(1)}, u32[]{:S(2)}, u32[]{:S(2)}) async-start(f32[32,10,1,128]{3,2,1,0:T(1,128)} %bitcast.9), calls=%async_computation | async-start | bytes 327680 | tf_op jit(solution)/shard_map/all_to_all | solution.py:478
  20.6 11.2 %all-to-all-start.1 = ((f32[32,10,1,128]{3,2,1,0:T(1,128)}), f32[32,10,1,128]{3,2,1,0:T(1,128)S(1)}, u32[]{:S(2)}, u32[]{:S(2)}) async-start(f32[32,10,1,128]{3,2,1,0:T(1,128)} %bitcast.5), calls=%async_computation.1 | async-start | bytes 327680 | tf_op jit(solution)/shard_map/all_to_all | solution.py:478

commit v17 on v16

--- a/solution.py
+++ b/solution.py
@@ -24,6 +24,7 @@
 SIDES = 3
 OWN = 8
 FIRST_PAIRS = 2
+AHEAD = 3
 
 
 def lane_of(rows):
@@ -352,7 +353,7 @@
 
 
 def finish_kernel(halo_ref, edge_a_ref, edge_b_ref, base_ref, out_ref,
-                  y_ref, raw_ref, delta_ref, in_sems, out_sems):
+                  y_ref, ahead_ref, raw_ref, delta_ref, in_sems, out_sems):
     count = out_ref.shape[0]
     pairs = count // 2
     rows = 4 * count
@@ -415,10 +416,8 @@
             delta_ref[2 * side + place] = change + share * (other - change)
 
     lane = lane_of(8)
-    out_copies = []
-    for pair in range(pairs):
+    def spread(pair):
         mine = pl.ds(8 * pair, 8)
-        in_copies[pair].wait()
         near, deep, south, south_in, north, north_in = [delta_ref[index, mine, :] for index in range(2 * SIDES)]
         groups = []
         for at in range(2):
@@ -436,7 +435,22 @@
                 if low < high:
                     inside = (lane >= low - at) & (lane < high - at)
                     change += jnp.where(inside, rot(source, start - at - origin), 0.0)
-            y_ref[mine, at:stop] = y_ref[mine, at:stop] + change[:, : stop - at]
+            yield at, stop, change[:, : stop - at]
+
+    for pair in range(AHEAD):
+        for at, stop, change in spread(pair):
+            ahead_ref[pl.ds(8 * pair, 8), at:stop] = change
+    out_copies = []
+    for pair in range(pairs):
+        mine = pl.ds(8 * pair, 8)
+        in_copies[pair].wait()
+        if pair < AHEAD:
+            for at in range(0, CELLS, LANES):
+                stop = min(at + LANES, CELLS)
+                y_ref[mine, at:stop] = y_ref[mine, at:stop] + ahead_ref[mine, at:stop]
+        else:
+            for at, stop, change in spread(pair):
+                y_ref[mine, at:stop] = y_ref[mine, at:stop] + change
         copy = pltpu.make_async_copy(
             y_ref.at[mine].reshape(2, 4, CELLS), out_ref.at[pl.ds(2 * pair, 2)], out_sems.at[pair])
         copy.start()
@@ -561,6 +575,7 @@
         out_specs=in_hbm,
         scratch_shapes=[
             pltpu.VMEM((state_rows, CELLS), f32),
+            pltpu.VMEM((8 * AHEAD, CELLS), f32),
             pltpu.VMEM((12, state_rows, LANES), f32),
             pltpu.VMEM((2 * SIDES, state_rows, LANES), f32),
             dma((pairs,)),

time: 34.8 us -> 34.4 us (0.989)
  Pallas kernels: 14.8 us -> 14.4 us
    pallas_call x1, Pallas kernels: 2.72 us -> 2.35 us  [per_device(): pl.pallas_call(finish_kernel, out_shape=jax.ShapeDtypeStruct(tracers.shap...]
  transfers between devices with their start and end apart: 2 -> 2, of which waited for: 2 -> 2; matrix products, arithmetic and copies ran while one was open for 3% -> 3% of each run, Pallas kernels for 21% -> 22%
where the time goes in v17:
time: 34.4 us; the launch traced here: 34.1 us
  Pallas kernels  14.4 us (42%)
  starting transfers between devices  9.89 us (29%)
  waiting for transfers between devices  8.73 us (25%)
  other arithmetic  0.79 us (2%)
    all_to_all x2, starting transfers between devices, exchanged(): lax.all_to_all(pieces, axes, 0, 0, tiled=True).reshape(slot_total, LANES)  9.89 us
    all_to_all x2, waiting for transfers between devices, exchanged(): lax.all_to_all(pieces, axes, 0, 0, tiled=True).reshape(slot_total, LANES)  8.73 us
    pallas_call x2, Pallas kernels, bulk(): pl.pallas_call(kernel, out_shape=[jax.ShapeDtypeStruct(tracers.shape, f32...  7.35 us
    pallas_call x1, Pallas kernels, per_device(): pl.pallas_call(pack_kernel, out_shape=jax.ShapeDtypeStruct((slot_total, L...  3.31 us
    pallas_call x1, Pallas kernels, per_device(): pl.pallas_call(finish_kernel, out_shape=jax.ShapeDtypeStruct(tracers.shap...  2.35 us
    pallas_call x1, Pallas kernels, per_device(): pl.pallas_call(route_kernel, out_shape=jax.ShapeDtypeStruct((slot_total,...  1.37 us
  transfers between devices with their start and end apart: 2, of which 2 were waited for; matrix products, arithmetic and copies ran while one was open for 3% of the time, Pallas kernels for 22%

profile of v17, /device:TPU:0, one launch (start us, length us, event | category | flops | bytes accessed | tf_op | source)
XLA Modules:
  0.0 34.1 jit_solution(3539545096388599352)
XLA Ops:
  0.0 0.0 copy-start.6
  0.0 0.0 copy-start.5
  0.0 0.0 copy-start.4
  0.0 0.0 copy-start
  0.0 0.0 copy-start.1
  0.0 3.3 %shard_map.73 = f32[320,128]{1,0:T(8,128)} custom-call(f32[10,4,5400]{2,1,0:T(4,128)} %refs_1_.1, f32[10,4,5400]{2,1,0:T(4,128)} %refs_2_.1, f32[10,5400]{1,0:T(8,128)} %refs_3_.1), custom_call_target="tpu_custom_call" | custom-call | flops 4000000 | bytes 2400000 | tf_op jit(solution)/shard_map/pallas_call | solution.py:494
  3.3 0.0 copy-start.2
  3.3 0.0 copy-start.3
  3.4 7.3 %all-to-all-start = ((f32[32,10,1,128]{3,2,1,0:T(1,128)}), f32[32,10,1,128]{3,2,1,0:T(1,128)S(1)}, u32[]{:S(2)}, u32[]{:S(2)}) async-start(f32[32,10,1,128]{3,2,1,0:T(1,128)} %bitcast.9), calls=%async_computation | async-start | bytes 327680 | tf_op jit(solution)/shard_map/all_to_all | solution.py:492
  10.7 0.0 copy-done.6
  10.7 0.0 copy-done.5
  10.7 0.0 copy-done.4
  10.7 0.4 %select_reduce_fusion.1 = s32[160,5]{0,1:T(8,128)S(1)} fusion(s32[160]{0:T(256)S(1)} %copy-done.4, s32[160,5]{0,1:T(8,128)S(1)} %pad_add_fusion), kind=kLoop, calls=%fused_computation.1 | loop fusion | flops 383200 | bytes 7040 | tf_op jit(solution)/shard_map/reduce_max | solution.py:467
  11.2 0.1 iota_compare_fusion.1
  11.3 0.3 select_reduce_fusion
  11.5 0.1 copy.19.code_ref.refs_5_
  11.7 0.0 copy-done
  11.7 0.0 copy-done.1
  11.7 0.0 copy-done.2
  11.7 0.0 copy-done.3
  11.7 3.1 %shard_map.74 = (f32[10,4,5400]{2,1,0:T(4,128)}, f32[25,16,128]{2,1,0:T(8,128)S(1)}) custom-call(s32[1]{0:T(128)} %bitcast.my_ref.part_ref.refs_0_, f32[10,4,5400]{2,1,0:T(4,128)S(1)} %copy-done, f32[10,4,5400]{2,1,0:T(4,128)S(1)} %copy-done.1, f32[10,5400]{1,0:T(8,128)S(1)} %copy-done.2, f32[10,5400]{1,0:T(8,128)S(1)} %copy-done.3, ...), custom_call_target="tpu_custom_call" | custom-call | flops 8000000 | bytes 1600000 | tf_op jit(solution)/shard_map/pallas_call | solution.py:518
  14.8 4.4 %all-to-all-done = f32[32,10,1,128]{3,2,1,0:T(1,128)S(1)} async-done(((f32[32,10,1,128]{3,2,1,0:T(1,128)}), f32[32,10,1,128]{3,2,1,0:T(1,128)S(1)}, u32[]{:S(2)}, u32[]{:S(2)}) %all-to-all-start) | async-done | bytes 163872 | tf_op jit(solution)/shard_map/all_to_all | solution.py:492
  19.3 1.4 %shard_map.75 = f32[320,128]{1,0:T(8,128)} custom-call(s32[1]{0:T(128)} %bitcast.my_ref.part_ref.refs_0_, s32[320,6]{1,0:T(8,128)S(1)} %copy.19.code_ref.refs_5_, f32[320,128]{1,0:T(8,128)S(1)} %bitcast.8), custom_call_target="tpu_custom_call" | custom-call | tf_op jit(solution)/shard_map/pallas_call | solution.py:561
  20.6 2.6 %all-to-all-start.1 = ((f32[32,10,1,128]{3,2,1,0:T(1,128)}), f32[32,10,1,128]{3,2,1,0:T(1,128)S(1)}, u32[]{:S(2)}, u32[]{:S(2)}) async-start(f32[32,10,1,128]{3,2,1,0:T(1,128)} %bitcast.5), calls=%async_computation.1 | async-start | bytes 327680 | tf_op jit(solution)/shard_map/all_to_all | solution.py:492
  23.2 4.2 %shard_map.76 = (f32[10,4,5400]{2,1,0:T(4,128)}, f32[25,24,128]{2,1,0:T(8,128)S(1)}) custom-call(s32[1]{0:T(128)} %bitcast.my_ref.part_ref.refs_0_, f32[10,4,5400]{2,1,0:T(4,128)S(1)} %copy-done, f32[10,4,5400]{2,1,0:T(4,128)S(1)} %copy-done.1, f32[10,5400]{1,0:T(8,128)S(1)} %copy-done.2, f32[10,5400]{1,0:T(8,128)S(1)} %copy-done.3, ...), custom_call_target="tpu_custom_call", output_to_operand_aliasing={{0}: (6, {})} | custom-call | flops 12000000 | bytes 2400000 | tf_op jit(solution)/shard_map/pallas_call | solution.py:518
  27.5 4.3 %all-to-all-done.1 = f32[32,10,1,128]{3,2,1,0:T(1,128)S(1)} async-done(((f32[32,10,1,128]{3,2,1,0:T(1,128)}), f32[32,10,1,128]{3,2,1,0:T(1,128)S(1)}, u32[]{:S(2)}, u32[]{:S(2)}) %all-to-all-start.1) | async-done | bytes 163872 | tf_op jit(solution)/shard_map/all_to_all | solution.py:492
  31.8 2.4 %shard_map.77 = f32[10,4,5400]{2,1,0:T(4,128)} custom-call(f32[320,128]{1,0:T(8,128)S(1)} %bitcast.7, f32[25,16,128]{2,1,0:T(8,128)S(1)} %get-tuple-element.17.edge_a_ref, f32[25,24,128]{2,1,0:T(8,128)S(1)} %get-tuple-element.19.edge_b_ref, f32[10,4,5400]{2,1,0:T(4,128)} %get-tuple-element.20.base_ref), custom_call_target="tpu_custom_call", output_to_operand_aliasing={{}: (3, {})} | custom-call | tf_op jit(solution)/shard_map/pallas_call | solution.py:571
  (2 shorter events, 0.0 us)
Async XLA Ops:
  0.0 10.7 %copy-start.6 = (s32[160]{0:T(256)S(1)}, s32[160]{0:T(256)}, u32[]{:S(2)}) copy-start(s32[160]{0:T(256)} %param.13) | copy-start | bytes 1924
  0.0 10.7 %copy-start.5 = (s32[160,4]{0,1:T(4,128)S(1)}, s32[160,4]{0,1:T(4,128)}, u32[]{:S(2)}) copy-start(s32[160,4]{0,1:T(4,128)} %param.12) | copy-start | bytes 7684
  0.0 10.7 %copy-start.4 = (s32[160]{0:T(256)S(1)}, s32[160]{0:T(256)}, u32[]{:S(2)}) copy-start(s32[160]{0:T(256)} %param.11) | copy-start | bytes 1924
  0.0 11.7 %copy-start = (f32[10,4,5400]{2,1,0:T(4,128)S(1)}, f32[10,4,5400]{2,1,0:T(4,128)}, u32[]{:S(2)}) copy-start(f32[10,4,5400]{2,1,0:T(4,128)} %refs_1_.1) | copy-start | bytes 2592004
  0.0 11.7 %copy-start.1 = (f32[10,4,5400]{2,1,0:T(4,128)S(1)}, f32[10,4,5400]{2,1,0:T(4,128)}, u32[]{:S(2)}) copy-start(f32[10,4,5400]{2,1,0:T(4,128)} %refs_2_.1) | copy-start | bytes 2592004
  3.3 8.4 %copy-start.2 = (f32[10,5400]{1,0:T(8,128)S(1)}, f32[10,5400]{1,0:T(8,128)}, u32[]{:S(2)}) copy-start(f32[10,5400]{1,0:T(8,128)} %refs_3_.1) | copy-start | bytes 648004
  3.3 8.4 %copy-start.3 = (f32[10,5400]{1,0:T(8,128)S(1)}, f32[10,5400]{1,0:T(8,128)}, u32[]{:S(2)}) copy-start(f32[10,5400]{1,0:T(8,128)} %refs_4_.1) | copy-start | bytes 648004
  3.4 15.9 %all-to-all-start = ((f32[32,10,1,128]{3,2,1,0:T(1,128)}), f32[32,10,1,128]{3,2,1,0:T(1,128)S(1)}, u32[]{:S(2)}, u32[]{:S(2)}) async-start(f32[32,10,1,128]{3,2,1,0:T(1,128)} %bitcast.9), calls=%async_computation | async-start | bytes 327680 | tf_op jit(solution)/shard_map/all_to_all | solution.py:492
  20.6 11.2 %all-to-all-start.1 = ((f32[32,10,1,128]{3,2,1,0:T(1,128)}), f32[32,10,1,128]{3,2,1,0:T(1,128)S(1)}, u32[]{:S(2)}, u32[]{:S(2)}) async-start(f32[32,10,1,128]{3,2,1,0:T(1,128)} %bitcast.5), calls=%async_computation.1 | async-start | bytes 327680 | tf_op jit(solution)/shard_map/all_to_all | solution.py:492

commit v18 on v17

--- a/solution.py
+++ b/solution.py
@@ -139,12 +139,14 @@
     d_copy.start()
     for pair in range(pairs):
         rows = pl.ds(8 * pair, 8)
-        x_copies[pair].wait()
+        if pair == 0 or pair % 2 == 1:
+            for arrived in range(pair, min(pair + 1 + pair % 2, pairs)):
+                x_copies[arrived].wait()
+                v_copies[arrived].wait()
         get_x = tile_getter(x_ref, rows, 8)
         near, far = edge_strip(get_x, 8), inner_strip(get_x, 8)
         south = [window(get_x, 0, 8), window(get_x, IB, 8)]
         north = [window(get_x, CELLS - IB, 8), window(get_x, CELLS - 2 * IB, 8)]
-        v_copies[pair].wait()
         get_v = tile_getter(v_ref, rows, 8)
         v_south, v_north = window(get_v, 0, 8), window(get_v, CELLS - IB, 8)
         strips = [joined(south[0], north[0], half, 8) for half in range(2)]
@@ -192,17 +194,17 @@
     part = part_ref[0]
     fold = code_ref[:, 4:5]
     wanted = [code_ref[:, side : side + 1] for side in range(3)] + [jnp.maximum(code_ref[:, 3:4], fold)]
-    picked = [jnp.zeros((rows, 2 * LANES), jnp.float32) for _ in wanted]
+    picked = jnp.zeros((len(wanted) * rows, 2 * LANES), jnp.float32)
     for start in range(0, total, rows):
         held = held_ref[start : start + rows, :]
         high = held.astype(jnp.bfloat16)
         low = (held - high.astype(jnp.float32)).astype(jnp.bfloat16)
         halves = jnp.concatenate([high, low], axis=1)
         source = lax.broadcasted_iota(jnp.int32, (rows, rows), 1) + start
-        for side, code in enumerate(wanted):
-            one_hot = jnp.where(code == source, 1.0, 0.0).astype(jnp.bfloat16)
-            picked[side] += jnp.dot(one_hot, halves, preferred_element_type=jnp.float32)
-    west, east, south, north = [value[:, :LANES] + value[:, LANES:] for value in picked]
+        one_hots = [jnp.where(code == source, 1.0, 0.0).astype(jnp.bfloat16) for code in wanted]
+        picked += jnp.dot(jnp.concatenate(one_hots, axis=0), halves, preferred_element_type=jnp.float32)
+    picked = picked[:, :LANES] + picked[:, LANES:]
+    west, east, south, north = [picked[side * rows : (side + 1) * rows] for side in range(4)]
     lane = lane_of(rows)
     along_x = (part >= X_PART) | ((part < 8) & (lane >= SPARE) & (lane < SPARE + PIECE))
     x_side = jnp.where(lane % 2 == 0, west, east)

time: 34.4 us -> 33.9 us (0.985)
  Pallas kernels: 14.4 us -> 13.9 us
    pallas_call x1, Pallas kernels: 3.31 us -> 2.94 us  [per_device(): pl.pallas_call(pack_kernel, out_shape=jax.ShapeDtypeStruct((slot_total, L...]
where the time goes in v18:
time: 33.9 us; the launch traced here: 33.7 us
  Pallas kernels  13.9 us (41%)
  starting transfers between devices  9.89 us (29%)
  waiting for transfers between devices  8.73 us (26%)
  other arithmetic  0.79 us (2%)
    all_to_all x2, starting transfers between devices, exchanged(): lax.all_to_all(pieces, axes, 0, 0, tiled=True).reshape(slot_total, LANES)  9.89 us
    all_to_all x2, waiting for transfers between devices, exchanged(): lax.all_to_all(pieces, axes, 0, 0, tiled=True).reshape(slot_total, LANES)  8.73 us
    pallas_call x2, Pallas kernels, bulk(): pl.pallas_call(kernel, out_shape=[jax.ShapeDtypeStruct(tracers.shape, f32...  7.35 us
    pallas_call x1, Pallas kernels, per_device(): pl.pallas_call(pack_kernel, out_shape=jax.ShapeDtypeStruct((slot_total, L...  2.94 us
    pallas_call x1, Pallas kernels, per_device(): pl.pallas_call(finish_kernel, out_shape=jax.ShapeDtypeStruct(tracers.shap...  2.35 us
    pallas_call x1, Pallas kernels, per_device(): pl.pallas_call(route_kernel, out_shape=jax.ShapeDtypeStruct((slot_total,...  1.29 us
  transfers between devices with their start and end apart: 2, of which 2 were waited for; matrix products, arithmetic and copies ran while one was open for 3% of the time, Pallas kernels for 22%

profile of v18, /device:TPU:0, one launch (start us, length us, event | category | flops | bytes accessed | tf_op | source)
XLA Modules:
  0.0 33.7 jit_solution(16083864188928467868)
XLA Ops:
  0.0 0.0 copy-start.6
  0.0 0.0 copy-start.5
  0.0 0.0 copy-start.4
  0.0 0.0 copy-start
  0.0 0.0 copy-start.1
  0.0 2.9 %shard_map.73 = f32[320,128]{1,0:T(8,128)} custom-call(f32[10,4,5400]{2,1,0:T(4,128)} %refs_1_.1, f32[10,4,5400]{2,1,0:T(4,128)} %refs_2_.1, f32[10,5400]{1,0:T(8,128)} %refs_3_.1), custom_call_target="tpu_custom_call" | custom-call | flops 4000000 | bytes 2400000 | tf_op jit(solution)/shard_map/pallas_call | solution.py:496
  3.0 0.0 copy-start.2
  3.0 0.0 copy-start.3
  3.0 7.3 %all-to-all-start = ((f32[32,10,1,128]{3,2,1,0:T(1,128)}), f32[32,10,1,128]{3,2,1,0:T(1,128)S(1)}, u32[]{:S(2)}, u32[]{:S(2)}) async-start(f32[32,10,1,128]{3,2,1,0:T(1,128)} %bitcast.9), calls=%async_computation | async-start | bytes 327680 | tf_op jit(solution)/shard_map/all_to_all | solution.py:494
  10.3 0.0 copy-done.6
  10.3 0.0 copy-done.5
  10.4 0.0 copy-done.4
  10.4 0.4 %select_reduce_fusion.1 = s32[160,5]{0,1:T(8,128)S(1)} fusion(s32[160]{0:T(256)S(1)} %copy-done.4, s32[160,5]{0,1:T(8,128)S(1)} %pad_add_fusion), kind=kLoop, calls=%fused_computation.1 | loop fusion | flops 383200 | bytes 7040 | tf_op jit(solution)/shard_map/reduce_max | solution.py:469
  10.8 0.1 iota_compare_fusion.1
  10.9 0.3 select_reduce_fusion
  11.2 0.1 copy.19.code_ref.refs_5_
  11.3 0.0 copy-done
  11.3 0.0 copy-done.1
  11.3 0.0 copy-done.2
  11.4 0.0 copy-done.3
  11.4 3.1 %shard_map.74 = (f32[10,4,5400]{2,1,0:T(4,128)}, f32[25,16,128]{2,1,0:T(8,128)S(1)}) custom-call(s32[1]{0:T(128)} %bitcast.my_ref.part_ref.refs_0_, f32[10,4,5400]{2,1,0:T(4,128)S(1)} %copy-done, f32[10,4,5400]{2,1,0:T(4,128)S(1)} %copy-done.1, f32[10,5400]{1,0:T(8,128)S(1)} %copy-done.2, f32[10,5400]{1,0:T(8,128)S(1)} %copy-done.3, ...), custom_call_target="tpu_custom_call" | custom-call | flops 8000000 | bytes 1600000 | tf_op jit(solution)/shard_map/pallas_call | solution.py:520
  14.5 4.4 %all-to-all-done = f32[32,10,1,128]{3,2,1,0:T(1,128)S(1)} async-done(((f32[32,10,1,128]{3,2,1,0:T(1,128)}), f32[32,10,1,128]{3,2,1,0:T(1,128)S(1)}, u32[]{:S(2)}, u32[]{:S(2)}) %all-to-all-start) | async-done | bytes 163872 | tf_op jit(solution)/shard_map/all_to_all | solution.py:494
  18.9 1.3 %shard_map.75 = f32[320,128]{1,0:T(8,128)} custom-call(s32[1]{0:T(128)} %bitcast.my_ref.part_ref.refs_0_, s32[320,6]{1,0:T(8,128)S(1)} %copy.19.code_ref.refs_5_, f32[320,128]{1,0:T(8,128)S(1)} %bitcast.8), custom_call_target="tpu_custom_call" | custom-call | tf_op jit(solution)/shard_map/pallas_call | solution.py:563
  20.2 2.6 %all-to-all-start.1 = ((f32[32,10,1,128]{3,2,1,0:T(1,128)}), f32[32,10,1,128]{3,2,1,0:T(1,128)S(1)}, u32[]{:S(2)}, u32[]{:S(2)}) async-start(f32[32,10,1,128]{3,2,1,0:T(1,128)} %bitcast.5), calls=%async_computation.1 | async-start | bytes 327680 | tf_op jit(solution)/shard_map/all_to_all | solution.py:494
  22.8 4.2 %shard_map.76 = (f32[10,4,5400]{2,1,0:T(4,128)}, f32[25,24,128]{2,1,0:T(8,128)S(1)}) custom-call(s32[1]{0:T(128)} %bitcast.my_ref.part_ref.refs_0_, f32[10,4,5400]{2,1,0:T(4,128)S(1)} %copy-done, f32[10,4,5400]{2,1,0:T(4,128)S(1)} %copy-done.1, f32[10,5400]{1,0:T(8,128)S(1)} %copy-done.2, f32[10,5400]{1,0:T(8,128)S(1)} %copy-done.3, ...), custom_call_target="tpu_custom_call", output_to_operand_aliasing={{0}: (6, {})} | custom-call | flops 12000000 | bytes 2400000 | tf_op jit(solution)/shard_map/pallas_call | solution.py:520
  27.0 4.3 %all-to-all-done.1 = f32[32,10,1,128]{3,2,1,0:T(1,128)S(1)} async-done(((f32[32,10,1,128]{3,2,1,0:T(1,128)}), f32[32,10,1,128]{3,2,1,0:T(1,128)S(1)}, u32[]{:S(2)}, u32[]{:S(2)}) %all-to-all-start.1) | async-done | bytes 163872 | tf_op jit(solution)/shard_map/all_to_all | solution.py:494
  31.3 2.4 %shard_map.77 = f32[10,4,5400]{2,1,0:T(4,128)} custom-call(f32[320,128]{1,0:T(8,128)S(1)} %bitcast.7, f32[25,16,128]{2,1,0:T(8,128)S(1)} %get-tuple-element.17.edge_a_ref, f32[25,24,128]{2,1,0:T(8,128)S(1)} %get-tuple-element.19.edge_b_ref, f32[10,4,5400]{2,1,0:T(4,128)} %get-tuple-element.20.base_ref), custom_call_target="tpu_custom_call", output_to_operand_aliasing={{}: (3, {})} | custom-call | tf_op jit(solution)/shard_map/pallas_call | solution.py:573
  (2 shorter events, 0.0 us)
Async XLA Ops:
  0.0 10.3 %copy-start.6 = (s32[160]{0:T(256)S(1)}, s32[160]{0:T(256)}, u32[]{:S(2)}) copy-start(s32[160]{0:T(256)} %param.13) | copy-start | bytes 1924
  0.0 10.3 %copy-start.5 = (s32[160,4]{0,1:T(4,128)S(1)}, s32[160,4]{0,1:T(4,128)}, u32[]{:S(2)}) copy-start(s32[160,4]{0,1:T(4,128)} %param.12) | copy-start | bytes 7684
  0.0 10.4 %copy-start.4 = (s32[160]{0:T(256)S(1)}, s32[160]{0:T(256)}, u32[]{:S(2)}) copy-start(s32[160]{0:T(256)} %param.11) | copy-start | bytes 1924
  0.0 11.3 %copy-start = (f32[10,4,5400]{2,1,0:T(4,128)S(1)}, f32[10,4,5400]{2,1,0:T(4,128)}, u32[]{:S(2)}) copy-start(f32[10,4,5400]{2,1,0:T(4,128)} %refs_1_.1) | copy-start | bytes 2592004
  0.0 11.3 %copy-start.1 = (f32[10,4,5400]{2,1,0:T(4,128)S(1)}, f32[10,4,5400]{2,1,0:T(4,128)}, u32[]{:S(2)}) copy-start(f32[10,4,5400]{2,1,0:T(4,128)} %refs_2_.1) | copy-start | bytes 2592004
  3.0 8.4 %copy-start.2 = (f32[10,5400]{1,0:T(8,128)S(1)}, f32[10,5400]{1,0:T(8,128)}, u32[]{:S(2)}) copy-start(f32[10,5400]{1,0:T(8,128)} %refs_3_.1) | copy-start | bytes 648004
  3.0 8.4 %copy-start.3 = (f32[10,5400]{1,0:T(8,128)S(1)}, f32[10,5400]{1,0:T(8,128)}, u32[]{:S(2)}) copy-start(f32[10,5400]{1,0:T(8,128)} %refs_4_.1) | copy-start | bytes 648004
  3.0 15.9 %all-to-all-start = ((f32[32,10,1,128]{3,2,1,0:T(1,128)}), f32[32,10,1,128]{3,2,1,0:T(1,128)S(1)}, u32[]{:S(2)}, u32[]{:S(2)}) async-start(f32[32,10,1,128]{3,2,1,0:T(1,128)} %bitcast.9), calls=%async_computation | async-start | bytes 327680 | tf_op jit(solution)/shard_map/all_to_all | solution.py:494
  20.2 11.2 %all-to-all-start.1 = ((f32[32,10,1,128]{3,2,1,0:T(1,128)}), f32[32,10,1,128]{3,2,1,0:T(1,128)S(1)}, u32[]{:S(2)}, u32[]{:S(2)}) async-start(f32[32,10,1,128]{3,2,1,0:T(1,128)} %bitcast.5), calls=%async_computation.1 | async-start | bytes 327680 | tf_op jit(solution)/shard_map/all_to_all | solution.py:494

commit v19 on v18

--- a/solution.py
+++ b/solution.py
@@ -139,10 +139,12 @@
     d_copy.start()
     for pair in range(pairs):
         rows = pl.ds(8 * pair, 8)
-        if pair == 0 or pair % 2 == 1:
-            for arrived in range(pair, min(pair + 1 + pair % 2, pairs)):
+        if pair in (0, FIRST_PAIRS):
+            for arrived in range(pair, FIRST_PAIRS if pair == 0 else pairs):
                 x_copies[arrived].wait()
                 v_copies[arrived].wait()
+            if pair > 0:
+                d_copy.wait()
         get_x = tile_getter(x_ref, rows, 8)
         near, far = edge_strip(get_x, 8), inner_strip(get_x, 8)
         south = [window(get_x, 0, 8), window(get_x, IB, 8)]
@@ -156,7 +158,6 @@
         for index, strip in enumerate(strips):
             strip_ref[index, rows, :] = strip
 
-    d_copy.wait()
     if out_ref.shape[0] > PARTS * count:
         rest = out_ref.shape[0] - PARTS * count
         out_ref[PARTS * count :, :] = jnp.zeros((rest, LANES), jnp.float32)
@@ -445,7 +446,9 @@
     out_copies = []
     for pair in range(pairs):
         mine = pl.ds(8 * pair, 8)
-        in_copies[pair].wait()
+        if pair <= AHEAD:
+            for arrived in range(pair, pair + 1 if pair < AHEAD else pairs):
+                in_copies[arrived].wait()
         if pair < AHEAD:
             for at in range(0, CELLS, LANES):
                 stop = min(at + LANES, CELLS)
@@ -453,10 +456,12 @@
         else:
             for at, stop, change in spread(pair):
                 y_ref[mine, at:stop] = y_ref[mine, at:stop] + change
-        copy = pltpu.make_async_copy(
-            y_ref.at[mine].reshape(2, 4, CELLS), out_ref.at[pl.ds(2 * pair, 2)], out_sems.at[pair])
+        out_copies.append(pltpu.make_async_copy(
+            y_ref.at[mine].reshape(2, 4, CELLS), out_ref.at[pl.ds(2 * pair, 2)], out_sems.at[pair]))
+        if pair < AHEAD:
+            out_copies[pair].start()
+    for copy in out_copies[AHEAD:]:
         copy.start()
-        out_copies.append(copy)
     for copy in out_copies:
         copy.wait()
 

time: 33.9 us -> 34.1 us (level)
  no operation moved by 1% of the time
where the time goes in v19:
time: 34.1 us; the launch traced here: 33.9 us
  Pallas kernels  14.1 us (41%)
  starting transfers between devices  9.89 us (29%)
  waiting for transfers between devices  8.73 us (26%)
  other arithmetic  0.79 us (2%)
    all_to_all x2, starting transfers between devices, exchanged(): lax.all_to_all(pieces, axes, 0, 0, tiled=True).reshape(slot_total, LANES)  9.89 us
    all_to_all x2, waiting for transfers between devices, exchanged(): lax.all_to_all(pieces, axes, 0, 0, tiled=True).reshape(slot_total, LANES)  8.73 us
    pallas_call x2, Pallas kernels, bulk(): pl.pallas_call(kernel, out_shape=[jax.ShapeDtypeStruct(tracers.shape, f32...  7.35 us
    pallas_call x1, Pallas kernels, per_device(): pl.pallas_call(pack_kernel, out_shape=jax.ShapeDtypeStruct((slot_total, L...  3.09 us
    pallas_call x1, Pallas kernels, per_device(): pl.pallas_call(finish_kernel, out_shape=jax.ShapeDtypeStruct(tracers.shap...  2.39 us
    pallas_call x1, Pallas kernels, per_device(): pl.pallas_call(route_kernel, out_shape=jax.ShapeDtypeStruct((slot_total,...  1.28 us
  transfers between devices with their start and end apart: 2, of which 2 were waited for; matrix products, arithmetic and copies ran while one was open for 3% of the time, Pallas kernels for 22%

profile of v19, /device:TPU:0, one launch (start us, length us, event | category | flops | bytes accessed | tf_op | source)
XLA Modules:
  0.0 33.9 jit_solution(2243910826768288411)
XLA Ops:
  0.0 0.0 copy-start.6
  0.0 0.0 copy-start.5
  0.0 0.0 copy-start.4
  0.0 0.0 copy-start
  0.0 0.0 copy-start.1
  0.0 3.1 %shard_map.73 = f32[320,128]{1,0:T(8,128)} custom-call(f32[10,4,5400]{2,1,0:T(4,128)} %refs_1_.1, f32[10,4,5400]{2,1,0:T(4,128)} %refs_2_.1, f32[10,5400]{1,0:T(8,128)} %refs_3_.1), custom_call_target="tpu_custom_call" | custom-call | flops 4000000 | bytes 2400000 | tf_op jit(solution)/shard_map/pallas_call | solution.py:501
  3.1 0.0 copy-start.2
  3.1 0.0 copy-start.3
  3.1 7.3 %all-to-all-start = ((f32[32,10,1,128]{3,2,1,0:T(1,128)}), f32[32,10,1,128]{3,2,1,0:T(1,128)S(1)}, u32[]{:S(2)}, u32[]{:S(2)}) async-start(f32[32,10,1,128]{3,2,1,0:T(1,128)} %bitcast.9), calls=%async_computation | async-start | bytes 327680 | tf_op jit(solution)/shard_map/all_to_all | solution.py:499
  10.5 0.0 copy-done.6
  10.5 0.0 copy-done.5
  10.5 0.0 copy-done.4
  10.5 0.4 %select_reduce_fusion.1 = s32[160,5]{0,1:T(8,128)S(1)} fusion(s32[160]{0:T(256)S(1)} %copy-done.4, s32[160,5]{0,1:T(8,128)S(1)} %pad_add_fusion), kind=kLoop, calls=%fused_computation.1 | loop fusion | flops 383200 | bytes 7040 | tf_op jit(solution)/shard_map/reduce_max | solution.py:474
  10.9 0.1 iota_compare_fusion.1
  11.0 0.3 select_reduce_fusion
  11.3 0.1 copy.19.code_ref.refs_5_
  11.5 0.0 copy-done
  11.5 0.0 copy-done.1
  11.5 0.0 copy-done.2
  11.5 0.0 copy-done.3
  11.5 3.1 %shard_map.74 = (f32[10,4,5400]{2,1,0:T(4,128)}, f32[25,16,128]{2,1,0:T(8,128)S(1)}) custom-call(s32[1]{0:T(128)} %bitcast.my_ref.part_ref.refs_0_, f32[10,4,5400]{2,1,0:T(4,128)S(1)} %copy-done, f32[10,4,5400]{2,1,0:T(4,128)S(1)} %copy-done.1, f32[10,5400]{1,0:T(8,128)S(1)} %copy-done.2, f32[10,5400]{1,0:T(8,128)S(1)} %copy-done.3, ...), custom_call_target="tpu_custom_call" | custom-call | flops 8000000 | bytes 1600000 | tf_op jit(solution)/shard_map/pallas_call | solution.py:525
  14.6 4.4 %all-to-all-done = f32[32,10,1,128]{3,2,1,0:T(1,128)S(1)} async-done(((f32[32,10,1,128]{3,2,1,0:T(1,128)}), f32[32,10,1,128]{3,2,1,0:T(1,128)S(1)}, u32[]{:S(2)}, u32[]{:S(2)}) %all-to-all-start) | async-done | bytes 163872 | tf_op jit(solution)/shard_map/all_to_all | solution.py:499
  19.0 1.3 %shard_map.75 = f32[320,128]{1,0:T(8,128)} custom-call(s32[1]{0:T(128)} %bitcast.my_ref.part_ref.refs_0_, s32[320,6]{1,0:T(8,128)S(1)} %copy.19.code_ref.refs_5_, f32[320,128]{1,0:T(8,128)S(1)} %bitcast.8), custom_call_target="tpu_custom_call" | custom-call | tf_op jit(solution)/shard_map/pallas_call | solution.py:568
  20.3 2.6 %all-to-all-start.1 = ((f32[32,10,1,128]{3,2,1,0:T(1,128)}), f32[32,10,1,128]{3,2,1,0:T(1,128)S(1)}, u32[]{:S(2)}, u32[]{:S(2)}) async-start(f32[32,10,1,128]{3,2,1,0:T(1,128)} %bitcast.5), calls=%async_computation.1 | async-start | bytes 327680 | tf_op jit(solution)/shard_map/all_to_all | solution.py:499
  22.9 4.2 %shard_map.76 = (f32[10,4,5400]{2,1,0:T(4,128)}, f32[25,24,128]{2,1,0:T(8,128)S(1)}) custom-call(s32[1]{0:T(128)} %bitcast.my_ref.part_ref.refs_0_, f32[10,4,5400]{2,1,0:T(4,128)S(1)} %copy-done, f32[10,4,5400]{2,1,0:T(4,128)S(1)} %copy-done.1, f32[10,5400]{1,0:T(8,128)S(1)} %copy-done.2, f32[10,5400]{1,0:T(8,128)S(1)} %copy-done.3, ...), custom_call_target="tpu_custom_call", output_to_operand_aliasing={{0}: (6, {})} | custom-call | flops 12000000 | bytes 2400000 | tf_op jit(solution)/shard_map/pallas_call | solution.py:525
  27.2 4.3 %all-to-all-done.1 = f32[32,10,1,128]{3,2,1,0:T(1,128)S(1)} async-done(((f32[32,10,1,128]{3,2,1,0:T(1,128)}), f32[32,10,1,128]{3,2,1,0:T(1,128)S(1)}, u32[]{:S(2)}, u32[]{:S(2)}) %all-to-all-start.1) | async-done | bytes 163872 | tf_op jit(solution)/shard_map/all_to_all | solution.py:499
  31.5 2.4 %shard_map.77 = f32[10,4,5400]{2,1,0:T(4,128)} custom-call(f32[320,128]{1,0:T(8,128)S(1)} %bitcast.7, f32[25,16,128]{2,1,0:T(8,128)S(1)} %get-tuple-element.17.edge_a_ref, f32[25,24,128]{2,1,0:T(8,128)S(1)} %get-tuple-element.19.edge_b_ref, f32[10,4,5400]{2,1,0:T(4,128)} %get-tuple-element.20.base_ref), custom_call_target="tpu_custom_call", output_to_operand_aliasing={{}: (3, {})} | custom-call | tf_op jit(solution)/shard_map/pallas_call | solution.py:578
  (2 shorter events, 0.0 us)
Async XLA Ops:
  0.0 10.5 %copy-start.6 = (s32[160]{0:T(256)S(1)}, s32[160]{0:T(256)}, u32[]{:S(2)}) copy-start(s32[160]{0:T(256)} %param.13) | copy-start | bytes 1924
  0.0 10.5 %copy-start.5 = (s32[160,4]{0,1:T(4,128)S(1)}, s32[160,4]{0,1:T(4,128)}, u32[]{:S(2)}) copy-start(s32[160,4]{0,1:T(4,128)} %param.12) | copy-start | bytes 7684
  0.0 10.5 %copy-start.4 = (s32[160]{0:T(256)S(1)}, s32[160]{0:T(256)}, u32[]{:S(2)}) copy-start(s32[160]{0:T(256)} %param.11) | copy-start | bytes 1924
  0.0 11.5 %copy-start = (f32[10,4,5400]{2,1,0:T(4,128)S(1)}, f32[10,4,5400]{2,1,0:T(4,128)}, u32[]{:S(2)}) copy-start(f32[10,4,5400]{2,1,0:T(4,128)} %refs_1_.1) | copy-start | bytes 2592004
  0.0 11.5 %copy-start.1 = (f32[10,4,5400]{2,1,0:T(4,128)S(1)}, f32[10,4,5400]{2,1,0:T(4,128)}, u32[]{:S(2)}) copy-start(f32[10,4,5400]{2,1,0:T(4,128)} %refs_2_.1) | copy-start | bytes 2592004
  3.1 8.4 %copy-start.2 = (f32[10,5400]{1,0:T(8,128)S(1)}, f32[10,5400]{1,0:T(8,128)}, u32[]{:S(2)}) copy-start(f32[10,5400]{1,0:T(8,128)} %refs_3_.1) | copy-start | bytes 648004
  3.1 8.4 %copy-start.3 = (f32[10,5400]{1,0:T(8,128)S(1)}, f32[10,5400]{1,0:T(8,128)}, u32[]{:S(2)}) copy-start(f32[10,5400]{1,0:T(8,128)} %refs_4_.1) | copy-start | bytes 648004
  3.1 15.9 %all-to-all-start = ((f32[32,10,1,128]{3,2,1,0:T(1,128)}), f32[32,10,1,128]{3,2,1,0:T(1,128)S(1)}, u32[]{:S(2)}, u32[]{:S(2)}) async-start(f32[32,10,1,128]{3,2,1,0:T(1,128)} %bitcast.9), calls=%async_computation | async-start | bytes 327680 | tf_op jit(solution)/shard_map/all_to_all | solution.py:499
  20.3 11.2 %all-to-all-start.1 = ((f32[32,10,1,128]{3,2,1,0:T(1,128)}), f32[32,10,1,128]{3,2,1,0:T(1,128)S(1)}, u32[]{:S(2)}, u32[]{:S(2)}) async-start(f32[32,10,1,128]{3,2,1,0:T(1,128)} %bitcast.5), calls=%async_computation.1 | async-start | bytes 327680 | tf_op jit(solution)/shard_map/all_to_all | solution.py:499
